TPU v7x, 32 devices: a whole 2x2x4 slice. The times are simulated.
32 devices in a mesh: seq: 8 (over z, x), tp: 4 (over y, core).
Axes of the slice: x: 2, y: 2, z: 4, core: 2. Of those that a mesh axis runs over, the one named last changes fastest.
Arguments:
- queries: bfloat16 [2048, 8192], P('seq', 'tp'), may hold values from -1000 to 1000
- states: bfloat16 [4096, 4096], P('seq', 'tp'), may hold values from -18 to 18
- state_doc: int32 [4096], replicated, may hold values from 0 to 7, as said below
- state_pos: int32 [4096], replicated, may hold values from 0 to 511, as said below
- lengths: int32 [8], replicated, may hold values from 64 to 512, as said below
- offsets: int32 [8], replicated, may hold values from 0 to 256
- key_weight: bfloat16 [4096, 8192], P(None, 'tp'), may hold values from -1 to 1
- value_weight: bfloat16 [4096, 8192], P(None, 'tp'), may hold values from -1 to 1
- context_grad: bfloat16 [2048, 8192], P('seq', 'tp'), may hold values from -6 to 6
Outputs:
- query_grad: bfloat16 [2048, 8192], P('seq', 'tp')
- key_weight_grad: bfloat16 [4096, 8192], P('seq', 'tp')
- value_weight_grad: bfloat16 [4096, 8192], P('seq', 'tp')
Inputs may be any that keep to these rules, and one draw needn't show every extreme that they name: `state_doc`: each document has exactly 512 state rows. The 512 rows held by one index of seq name any one document at most 80 times, and in every draw some device's rows name some document exactly 80 times. `state_pos`: within one document the state rows carry each position from 0 to 511 exactly once. `lengths`: some document has length 512.
All inputs are finite; a program needn't handle non-finite values.
Results may differ from a plain program's by a relative error of at most 0.017.
Values may be sent and summed in bfloat16 or wider, within the bound.
No kernel may reach another device: no remote copies, remote signals or barrier semaphores. Data moves between devices by JAX's collectives and lax.ppermute only.
A program may use at most 128 MiB of HBM per device.

v0:
```python
import jax
import jax.numpy as jnp
from jax import lax
from jax.sharding import PartitionSpec as P

HEAD_DIM = 128


def attend(query_rows, key_rows, value_rows, grad_rows, length, offset):
    query_count = query_rows.shape[0]
    state_count = key_rows.shape[0]
    head_count = query_rows.shape[1] // HEAD_DIM
    query_heads = query_rows.reshape(query_count, head_count, HEAD_DIM)
    key_heads = key_rows.reshape(state_count, head_count, HEAD_DIM)
    value_heads = value_rows.reshape(state_count, head_count, HEAD_DIM)
    grad_heads = grad_rows.reshape(query_count, head_count, HEAD_DIM)
    score_scale = HEAD_DIM ** (-0.5)
    scores = (
        jnp.einsum("qhd,khd->hqk", query_heads, key_heads, preferred_element_type=jnp.float32)
        * score_scale
    )
    query_index = jnp.arange(query_count)
    positions = jnp.arange(state_count)
    visible = (positions[None, :] <= offset + query_index[:, None]) & (positions[None, :] < length)
    scores = jnp.where(visible[None], scores, -jnp.inf)
    row_top = jnp.max(scores, axis=-1, keepdims=True)
    weights = jnp.exp(scores - row_top)
    probabilities = weights / jnp.sum(weights, axis=-1, keepdims=True)
    probs_low = probabilities.astype(jnp.bfloat16)
    context = jnp.einsum("hqk,khd->qhd", probs_low, value_heads, preferred_element_type=jnp.float32)
    delta_rows = jnp.sum(grad_heads.astype(jnp.float32) * context, axis=-1)
    prob_grad = jnp.einsum(
        "qhd,khd->hqk", grad_heads, value_heads, preferred_element_type=jnp.float32
    )
    score_grad = (probabilities * (prob_grad - delta_rows.T[:, :, None]) * score_scale).astype(
        jnp.bfloat16
    )
    query_grad = jnp.einsum(
        "hqk,khd->qhd", score_grad, key_heads, preferred_element_type=jnp.float32
    )
    key_grad = jnp.einsum(
        "hqk,qhd->khd", score_grad, query_heads, preferred_element_type=jnp.float32
    )
    value_grad = jnp.einsum(
        "hqk,qhd->khd", probs_low, grad_heads, preferred_element_type=jnp.float32
    )
    width = query_rows.shape[1]
    return (
        query_grad.astype(jnp.bfloat16).reshape(query_count, width),
        key_grad.astype(jnp.bfloat16).reshape(state_count, width),
        value_grad.astype(jnp.bfloat16).reshape(state_count, width),
    )


def shards(
    queries, states, state_doc, state_pos, lengths, offsets, key_weight, value_weight, context_grad
):
    seq_count = lax.axis_size("seq")
    device = lax.axis_index("seq")
    row_count = states.shape[0]
    capacity = 3 * row_count // (4 * seq_count) + row_count // 16
    docs_all = state_doc.reshape(seq_count, row_count)
    positions_all = state_pos.reshape(seq_count, row_count)
    onehot = (docs_all[:, :, None] == jnp.arange(seq_count)[None, None, :]).astype(jnp.int32)
    earlier = jnp.cumsum(onehot, axis=1) - onehot
    slots_all = jnp.sum(earlier * onehot, axis=2)
    own_docs = lax.dynamic_index_in_dim(docs_all, device, 0, keepdims=False)
    own_slots = lax.dynamic_index_in_dim(slots_all, device, 0, keepdims=False)
    targets = own_docs * capacity + own_slots
    source_row = jnp.full((seq_count * capacity,), row_count, jnp.int32)
    source_row = source_row.at[targets].set(jnp.arange(row_count, dtype=jnp.int32))
    arrival_index = jnp.arange(seq_count, dtype=jnp.int32)[:, None] * capacity + slots_all
    placed = jnp.where(docs_all == device, positions_all, row_count)
    order_slot = jnp.zeros((row_count,), jnp.int32)
    order_slot = order_slot.at[placed.reshape(-1)].set(arrival_index.reshape(-1), mode="drop")
    padded = jnp.concatenate([states, jnp.zeros((1, states.shape[1]), states.dtype)], axis=0)
    arrived = lax.all_to_all(
        jnp.take(padded, source_row, axis=0), "seq", split_axis=0, concat_axis=0, tiled=True
    )
    doc_states = lax.all_gather(jnp.take(arrived, order_slot, axis=0), "tp", axis=1, tiled=True)
    key_rows = jnp.dot(doc_states, key_weight, preferred_element_type=jnp.float32).astype(
        jnp.bfloat16
    )
    value_rows = jnp.dot(doc_states, value_weight, preferred_element_type=jnp.float32).astype(
        jnp.bfloat16
    )
    length = lax.dynamic_index_in_dim(lengths, device, 0, keepdims=False)
    offset = lax.dynamic_index_in_dim(offsets, device, 0, keepdims=False)
    query_grad, key_grad, value_grad = attend(
        queries, key_rows, value_rows, context_grad, length, offset
    )
    both_grads = jnp.concatenate([key_grad, value_grad], axis=1)
    summed = lax.psum_scatter(
        lax.dot_general(
            doc_states, both_grads, (((0,), (0,)), ((), ())), preferred_element_type=jnp.float32
        ).astype(jnp.bfloat16),
        "seq",
        scatter_dimension=0,
        tiled=True,
    ).astype(jnp.float32)
    head_width = key_weight.shape[1]
    return (
        query_grad,
        summed[:, :head_width].astype(jnp.bfloat16),
        summed[:, head_width:].astype(jnp.bfloat16),
    )


def solution(mesh):
    in_specs = (
        P("seq", "tp"),
        P("seq", "tp"),
        P(),
        P(),
        P(),
        P(),
        P(None, "tp"),
        P(None, "tp"),
        P("seq", "tp"),
    )
    out_specs = (P("seq", "tp"), P("seq", "tp"), P("seq", "tp"))
    return jax.shard_map(shards, mesh=mesh, in_specs=in_specs, out_specs=out_specs, check_vma=False)
```

profile of v0, /device:TPU:0, one launch (start us, length us, event | category | flops | bytes accessed | tf_op | source)
XLA Modules:
  0.0 732.8 jit_solution(5535529215156652583)
XLA Ops:
  7.2 0.7 eq.34
  7.9 0.7 fusion.17
  8.6 9.0 %reduce-window.6 = s32[8,8,4,128]{3,1,2,0:T(8,128)S(1)} reduce-window(s32[8,8,4,128]{3,1,2,0:T(8,128)S(1)} %fusion.17, s32[]{:T(128)} %constant.34.clone.1), window={size=1x1x1x128 pad=0_0x0_0x0_0x127_0}, to_apply=%region_0.0 | reduce-window | flops 4161536 | bytes 262148 | tf_op jit(solution)/shard_map/reduce-window
  17.6 0.1 slice.22
  17.7 0.3 copy.25
  18.0 0.1 fusion.18
  18.1 0.1 fusion.16
  18.3 2.4 scatter_custom_fusion.1
  20.8 0.1 broadcast_in_dim.63
  20.9 1.3 concatenate.6
  22.2 2.8 gather_fusion
  25.1 1.2 broadcast_select_fusion
  26.3 7.3 all-to-all-start
  33.6 0.0 all-gather.2.cloned.1.call-start
  33.6 0.1 add_bitcast_fusion
  33.7 15.5 %scatter_custom_fusion = s32[512]{0:T(512)S(1)} fusion(s32[4096]{0:T(1024)S(1)} %compare_select_fusion, s32[4096]{0:T(1024)S(1)} %bitcast.95, s32[]{:T(128)} %constant.34.clone.1), kind=kCustom, calls=%fused_computation.53 | custom fusion | bytes 2052 | tf_op jit(solution)/shard_map/scatter | solution.py:75
  49.3 15.7 %all-to-all-done = bf16[8,80,1024]{2,1,0:T(8,128)(2,1)S(1)} async-done(((bf16[8,80,1024]{2,1,0:T(8,128)(2,1)}), bf16[8,80,1024]{2,1,0:T(8,128)(2,1)S(1)}, u32[]{:S(2)}, u32[]{:S(2)}) %all-to-all-start) | async-done | bytes 1310752 | tf_op jit(solution)/shard_map/all_to_all | solution.py:77
  65.0 2.0 gather_fusion.1
  67.0 1.1 broadcast_select_fusion.1
  68.2 0.0 all-gather.2.cloned.1.call-update
  68.2 0.2 reduce-scatter.2.cloned.1.call-start
  68.4 0.6 dynamic_slice.16
  69.0 0.6 dynamic_slice.17
  69.6 1.5 copy.46
  71.1 1.4 copy.29
  72.5 0.7 iota_compare_fusion.3
  73.1 0.7 iota_add_fusion
  73.8 0.1 fusion.14
  73.9 28.0 %all-gather.2.cloned.1.call-done = bf16[512,4096]{1,0:T(8,128)(2,1)} async-done(((bf16[512,1024]{1,0:T(8,128)(2,1)}), bf16[512,4096]{1,0:T(8,128)(2,1)}) %all-gather.2.cloned.1.call-update) | async-done | bytes 4194320 | tf_op jit(solution)/shard_map/all_gather | solution.py:80
  101.9 13.6 %convolution_convert_fusion.1 = bf16[512,2048]{1,0:T(8,128)(2,1)S(1)} fusion(bf16[512,4096]{1,0:T(8,128)(2,1)} %all-gather.2.cloned.1.call-done, bf16[4096,2048]{1,0:T(8,128)(2,1)} %param.16), kind=kOutput, calls=%fused_computation.20 | convolution fusion | flops 8590983168 | bytes 23068672 | tf_op jit(solution)/shard_map/dot_general | solution.py:84
  115.5 2.5 copy.47
  118.0 14.5 %convolution_convert_fusion.2 = bf16[512,2048]{1,0:T(8,128)(2,1)} fusion(bf16[512,4096]{1,0:T(8,128)(2,1)} %all-gather.2.cloned.1.call-done, bf16[4096,2048]{1,0:T(8,128)(2,1)} %param.15), kind=kOutput, calls=%fused_computation.21 | convolution fusion | flops 8590983168 | bytes 23068672 | tf_op jit(solution)/shard_map/dot_general | solution.py:81
  132.6 2.9 copy.45
  135.4 5.1 fusion.28
  140.5 4.4 fusion.10
  144.9 1.5 convolution_convert_fusion.3
  146.4 0.1 copy-done.2
  146.5 0.9 fusion.11
  147.3 0.5 slice-done.1
  147.8 2.0 fusion.2
  149.8 1.9 copy-done
  151.8 2.8 convolution_convert_fusion.4
  154.6 23.5 %convolution_convert_fusion = bf16[4096,4096]{1,0:T(8,128)(2,1)} fusion(bf16[512,4096]{1,0:T(8,128)(2,1)} %all-gather.2.cloned.1.call-done, bf16[512,2048]{0,1:T(8,128)(2,1)S(1)} %bitcast.90, bf16[512,2048]{0,1:T(8,128)(2,1)} %bitcast.91), kind=kOutput, calls=%fused_computation.5 | convolution fusion | flops 17205035008 | bytes 41943040 | tf_op jit(solution)/shard_map/dot_general | solution.py:94
  178.0 0.0 reduce-scatter.2.cloned.1.call-update
  178.1 2.9 convolution_convert_fusion.5
  181.0 1.4 copy.39
  182.4 538.7 %reduce-scatter.2.cloned.1.call-done = bf16[512,4096]{1,0:T(8,128)(2,1)} async-done(((bf16[4096,4096]{1,0:T(8,128)(2,1)}), bf16[512,4096]{1,0:T(8,128)(2,1)}) %reduce-scatter.2.cloned.1.call-update) | async-done | bytes 4194320 | tf_op jit(solution)/shard_map/reduce_scatter | solution.py:93
  721.1 4.8 fusion.27
  (31 shorter events, 0.1 us)
Async XLA Ops:
  25.0 8.7 %copy-start.4 = (s32[4096]{0:T(1024)S(1)}, s32[4096]{0:T(1024)}, u32[]{:S(2)}) copy-start(s32[4096]{0:T(1024)} %param.11) | copy-start | bytes 49156
  25.1 8.7 %copy-start.5 = (s32[4096]{0:T(1024)S(1)}, s32[4096]{0:T(1024)}, u32[]{:S(2)}) copy-start(s32[4096]{0:T(1024)} %param.12) | copy-start | bytes 49156
  26.3 38.6 %all-to-all-start = ((bf16[8,80,1024]{2,1,0:T(8,128)(2,1)}), bf16[8,80,1024]{2,1,0:T(8,128)(2,1)S(1)}, u32[]{:S(2)}, u32[]{:S(2)}) async-start(bf16[8,80,1024]{2,1,0:T(8,128)(2,1)} %broadcast_select_fusion), calls=%async_computation | async-start | bytes 2621440 | tf_op jit(solution)/shard_map/all_to_all | solution.py:77
  33.6 68.3 %all-gather.2.cloned.1.call-start = ((), (), s32[]{:S(2)}) async-start(), calls=%async_computation.2 | async-start | bytes 5242880 | tf_op jit(solution)/shard_map/all_gather | solution.py:80
  64.9 3.5 copy-start.6
  65.0 4.1 copy-start.7
  67.0 4.1 copy-start.3
  68.2 653.0 %reduce-scatter.2.cloned.1.call-start = ((), (), s32[]{:S(2)}) async-start(), calls=%async_computation.3 | async-start | bytes 37748736 | tf_op jit(solution)/shard_map/reduce_scatter | solution.py:93
  140.5 4.4 copy-start.1
  140.5 6.9 slice-start
  144.9 1.6 copy-start.2
  144.9 2.9 slice-start.1
  149.8 1.9 copy-start
Sparse Core Ops, SparseCore 0:
  68.3 33.5 all-gather.1
  178.2 542.9 reduce-scatter.1
where the time goes:
time: 733 us
  waiting for transfers between devices  582 us (79%)
  matrix products  66.7 us (9%)
  local copies, waits for them, and re-layouts  43.5 us (6%)
  other arithmetic  18.3 us (2%)
  between operations  14.4 us (2%)
  starting transfers between devices  7.51 us (1%)
    reduce_scatter x1, waiting for transfers between devices, shards(): lax.psum_scatter(lax.dot_general(doc_states, both_grads, (((0,), (0,)), (...  539 us
    all_gather x1, waiting for transfers between devices, shards(): lax.all_gather(jnp.take(arrived, order_slot, axis=0), 'tp', axis=1, tiled...  28 us
    dot_general x1, matrix products, shards(): lax.dot_general(doc_states, both_grads, (((0,), (0,)), ((), ())), preferr...  23.5 us
    all_to_all x1, waiting for transfers between devices, shards(): lax.all_to_all(jnp.take(padded, source_row, axis=0), 'seq', split_axis=0,...  15.7 us
    scatter x1, local copies, waits for them, and re-layouts, shards(): order_slot.at[placed.reshape(-1)]  15.5 us
  transfers between devices with their start and end apart: 3, of which 3 were waited for; matrix products, arithmetic and copies ran while one was open for 3% of the time, Pallas kernels for 0%

commit v1 on v0

v1 whole, which is shorter than its diff:
```python
import jax
import jax.numpy as jnp
from jax import lax
from jax.experimental import pallas as pl
from jax.experimental.pallas import tpu as pltpu
from jax.sharding import PartitionSpec as P

HEAD_DIM = 128
LOW = jnp.bfloat16
WIDE = jnp.float32


def attend_kernel(info_ref, query_ref, key_ref, value_ref, grad_ref, query_grad_ref, rows_grad_ref):
    head = pl.program_id(0)
    length = info_ref[0]
    offset = info_ref[1]
    scale = HEAD_DIM ** (-0.5)
    query, key, value, grad = query_ref[...], key_ref[...], value_ref[...], grad_ref[...]
    across = (((1,), (1,)), ((), ()))
    down = (((0,), (0,)), ((), ()))
    scores = lax.dot_general(query, key, across, preferred_element_type=WIDE) * scale
    position = lax.broadcasted_iota(jnp.int32, scores.shape, 1)
    limit = jnp.minimum(
        lax.broadcasted_iota(jnp.int32, (scores.shape[0], 1), 0) + (offset + 1), length
    )
    scores = jnp.where(position < limit, scores, -1e30)
    weights = jnp.exp(scores - jnp.max(scores, axis=-1, keepdims=True))
    probs = weights * (1.0 / jnp.sum(weights, axis=-1, keepdims=True))
    probs_low = probs.astype(LOW)
    context = jnp.dot(probs_low, value, preferred_element_type=WIDE)
    delta = jnp.sum(grad.astype(WIDE) * context, axis=-1, keepdims=True)
    prob_grad = lax.dot_general(grad, value, across, preferred_element_type=WIDE)
    score_grad = (probs * (prob_grad - delta) * scale).astype(LOW)
    query_grad_ref[...] = jnp.dot(score_grad, key, preferred_element_type=WIDE).astype(LOW)
    key_grad = lax.dot_general(score_grad, query, down, preferred_element_type=WIDE)
    value_grad = lax.dot_general(probs_low, grad, down, preferred_element_type=WIDE)
    half = rows_grad_ref.shape[1] // 2
    start = pl.multiple_of(head * HEAD_DIM, HEAD_DIM)
    rows_grad_ref[:, pl.ds(start, HEAD_DIM)] = key_grad.astype(LOW)
    rows_grad_ref[:, pl.ds(half + start, HEAD_DIM)] = value_grad.astype(LOW)


def attend(info, queries, key_rows, value_rows, grads, first, heads):
    query_count = queries.shape[0]
    state_count = key_rows.shape[0]
    width = heads * HEAD_DIM
    flops = 12 * query_count * state_count * width
    return pl.pallas_call(
        attend_kernel,
        grid=(heads,),
        in_specs=[
            pl.BlockSpec(memory_space=pltpu.SMEM),
            pl.BlockSpec((query_count, HEAD_DIM), lambda h: (0, first + h)),
            pl.BlockSpec((state_count, HEAD_DIM), lambda h: (0, h)),
            pl.BlockSpec((state_count, HEAD_DIM), lambda h: (0, h)),
            pl.BlockSpec((query_count, HEAD_DIM), lambda h: (0, first + h)),
        ],
        out_specs=[
            pl.BlockSpec((query_count, HEAD_DIM), lambda h: (0, h)),
            pl.BlockSpec((state_count, 2 * width), lambda h: (0, 0)),
        ],
        out_shape=[
            jax.ShapeDtypeStruct((query_count, width), LOW),
            jax.ShapeDtypeStruct((state_count, 2 * width), LOW),
        ],
        compiler_params=pltpu.CompilerParams(vmem_limit_bytes=24 * 1024 * 1024),
        cost_estimate=pl.CostEstimate(
            flops=4 * flops, bytes_accessed=12 * state_count * width, transcendentals=query_count * state_count * heads
        ),
    )(info, queries, key_rows, value_rows, grads)


def down_dot(left, right):
    return lax.dot_general(left, right, (((0,), (0,)), ((), ())), preferred_element_type=WIDE)


def line_shape(seq_count):
    minor = 1
    while (2 * minor) ** 2 <= seq_count and seq_count % (2 * minor) == 0:
        minor *= 2
    return seq_count // minor, minor


def route(states, state_doc, state_pos):
    seq_count = lax.axis_size("seq")
    device = lax.axis_index("seq")
    row_count = states.shape[0]
    capacity = 3 * row_count // (4 * seq_count) + row_count // 16
    docs_all = state_doc.reshape(seq_count, row_count)
    positions_all = state_pos.reshape(seq_count, row_count)
    before = (
        lax.broadcasted_iota(jnp.int32, (row_count, row_count), 0)
        < lax.broadcasted_iota(jnp.int32, (row_count, row_count), 1)
    ).astype(LOW)
    own_docs = lax.dynamic_index_in_dim(docs_all, device, 0, keepdims=False)
    doc_ids = jnp.arange(seq_count, dtype=jnp.int32)
    own_hot = own_docs[None, :] == doc_ids[:, None]
    mine = docs_all == device
    ranks = jnp.dot(
        jnp.concatenate([own_hot, mine], axis=0).astype(LOW), before, preferred_element_type=WIDE
    ).astype(jnp.int32)
    own_ranks = jnp.sum(jnp.where(own_hot, ranks[:seq_count], 0), axis=0)
    targets = own_docs * capacity + own_ranks
    slots = jnp.arange(seq_count * capacity, dtype=jnp.int32)
    send_hot = (targets[None, :] == slots[:, None]).astype(LOW)
    sent = jnp.dot(send_hot, states, preferred_element_type=WIDE).astype(LOW)
    arrived = lax.all_to_all(sent, "seq", split_axis=0, concat_axis=0, tiled=True)
    arrival = jnp.where(mine, ranks[seq_count:], capacity)
    hit = arrival[:, None, :] == jnp.arange(capacity, dtype=jnp.int32)[None, :, None]
    slot_position = jnp.max(jnp.where(hit, positions_all[:, None, :], -1), axis=2).reshape(-1)
    place_hot = (
        slot_position[None, :] == jnp.arange(row_count, dtype=jnp.int32)[:, None]
    ).astype(LOW)
    return jnp.dot(place_hot, arrived, preferred_element_type=WIDE).astype(LOW)


def shards(
    queries, states, state_doc, state_pos, lengths, offsets, key_weight, value_weight, context_grad
):
    seq_count = lax.axis_size("seq")
    tp_count = lax.axis_size("tp")
    device = lax.axis_index("seq")
    part = lax.axis_index("tp")
    major, minor = line_shape(seq_count)
    z, x = device // minor, device % minor
    row_count = states.shape[0]
    feature_count = key_weight.shape[0]
    slice_width = feature_count // seq_count
    quarter = row_count // tp_count
    head_count = key_weight.shape[1] // HEAD_DIM
    group_count = 4
    heads = head_count // group_count
    width = heads * HEAD_DIM

    def at(major_index, minor_index):
        return major_index * minor + minor_index

    def step_up(value, first, last):
        pairs = [(at(i, j), at(i + 1, j)) for i in range(first, last) for j in range(minor)]
        return lax.ppermute(value, "seq", pairs)

    def step_down(value, first, last):
        pairs = [(at(i, j), at(i - 1, j)) for i in range(first, last) for j in range(minor)]
        return lax.ppermute(value, "seq", pairs)

    def turn(value, shift):
        pairs = [(at(i, j), at(i, (j + shift) % minor)) for i in range(major) for j in range(minor)]
        return lax.ppermute(value, "seq", pairs)

    with jax.named_scope("route"):
        doc_part = route(states, state_doc, state_pos)
    with jax.named_scope("gather_states"):
        doc_states = lax.all_gather(doc_part, "tp", axis=1, tiled=True)
    own_rows = lax.dynamic_slice_in_dim(doc_states, part * quarter, quarter, 0)

    with jax.named_scope("line_states"):
        blocks = own_rows.reshape(quarter, major, minor * slice_width).transpose(1, 0, 2)
        groups = [[at(i, j) for i in range(major)] for j in range(minor)]
        blocks = lax.all_to_all(
            blocks, "seq", split_axis=0, concat_axis=0, axis_index_groups=groups, tiled=True
        )
        order = (z - jnp.arange(major)) % major
        blocks = jnp.take(blocks, order, axis=0)
        line_states = lax.all_gather(blocks, "tp", axis=0, tiled=False)
        line_states = line_states.reshape(tp_count * major * quarter, minor * slice_width)

    with jax.named_scope("side_states"):
        sides = own_rows.reshape(quarter, major, minor, slice_width)
        gathered = []
        for shift in range(1, minor):
            wanted = lax.dynamic_index_in_dim(sides, (x + shift) % minor, 2, keepdims=False)
            got = turn(wanted.transpose(1, 0, 2), shift)
            gathered.append(lax.all_gather(got, "tp", axis=1, tiled=True))
        own_side = lax.dynamic_index_in_dim(
            doc_states.reshape(row_count, major, minor, slice_width), x, 2, keepdims=False
        ).transpose(1, 0, 2)
        side_states = jnp.concatenate([own_side] + gathered, axis=1)

    info = jnp.stack(
        [
            lax.dynamic_index_in_dim(lengths, device, 0, keepdims=False),
            lax.dynamic_index_in_dim(offsets, device, 0, keepdims=False),
        ]
    )
    query_grads, rows_grads = [], []
    for group in range(group_count):
        with jax.named_scope(f"attend_{group}"):
            columns = slice(group * width, (group + 1) * width)
            key_rows = jnp.dot(doc_states, key_weight[:, columns], preferred_element_type=WIDE)
            value_rows = jnp.dot(doc_states, value_weight[:, columns], preferred_element_type=WIDE)
            query_grad, rows_grad = attend(
                info, queries, key_rows.astype(LOW), value_rows.astype(LOW), context_grad,
                group * heads, heads,
            )
            query_grads.append(query_grad)
            rows_grads.append(rows_grad)

    even = [rows_grads[0], rows_grads[2]]
    odd = [rows_grads[1], rows_grads[3]]
    rows_up, rows_down = [[g] for g in even], [[g] for g in even]
    odd_rows = [None, None]
    sums_up, sums_down = [None, None], [None, None]

    def side_product(index, dest):
        return down_dot(
            lax.dynamic_index_in_dim(side_states, dest, 0, keepdims=False), odd_rows[index]
        )

    for step in range(major):
        distance = major - step
        for index in range(2):
            with jax.named_scope(f"rows_{step}_{index}"):
                if step < major - 1:
                    rows_up[index].append(step_up(rows_up[index][-1], step, major - 1))
                    rows_down[index].append(step_down(rows_down[index][-1], 1, major - step))
            with jax.named_scope(f"sums_{step}_{index}"):
                if step == 0:
                    odd_rows[index] = jnp.concatenate(
                        [odd[index]] + [turn(odd[index], shift) for shift in range(1, minor)], axis=0
                    )
                else:
                    if 2 * distance >= major:
                        up_product = down_product = side_product(
                            index, jnp.where(z + distance < major, z + distance, jnp.maximum(z - distance, 0))
                        )
                    else:
                        up_product = side_product(index, jnp.minimum(z + distance, major - 1))
                        down_product = side_product(index, jnp.maximum(z - distance, 0))
                    if sums_up[index] is not None:
                        up_product = up_product + sums_up[index].astype(WIDE)
                        down_product = down_product + sums_down[index].astype(WIDE)
                    sums_up[index] = step_up(up_product.astype(LOW), 0, major - distance)
                    sums_down[index] = step_down(down_product.astype(LOW), distance, major)

    results = [None] * group_count
    for index in range(2):
        with jax.named_scope(f"even_{index}"):
            pieces = [even[index]]
            for j in range(1, major):
                pieces.append(jnp.where(z >= j, rows_up[index][j], rows_down[index][major - j]))
            line_rows = jnp.concatenate(
                [piece.reshape(tp_count, 1, quarter, 2 * width) for piece in pieces], axis=1
            ).reshape(tp_count * major * quarter, 2 * width)

            def line_product(dest):
                chosen = lax.dynamic_slice_in_dim(line_states, dest * slice_width, slice_width, 1)
                return down_dot(chosen, line_rows)

            arrivals = [
                turn(line_product((x + shift) % minor).astype(LOW), shift) for shift in range(1, minor)
            ]
            total = line_product(x)
            for arrival in arrivals:
                total = total + arrival.astype(WIDE)
            results[2 * index] = total.astype(LOW)
        with jax.named_scope(f"odd_{index}"):
            total = side_product(index, z)
            total = total + sums_up[index].astype(WIDE) + sums_down[index].astype(WIDE)
            results[2 * index + 1] = total.astype(LOW)

    return (
        jnp.concatenate(query_grads, axis=1),
        jnp.concatenate([result[:, :width] for result in results], axis=1),
        jnp.concatenate([result[:, width:] for result in results], axis=1),
    )


def solution(mesh):
    in_specs = (
        P("seq", "tp"),
        P("seq", "tp"),
        P(),
        P(),
        P(),
        P(),
        P(None, "tp"),
        P(None, "tp"),
        P("seq", "tp"),
    )
    out_specs = (P("seq", "tp"), P("seq", "tp"), P("seq", "tp"))
    return jax.shard_map(shards, mesh=mesh, in_specs=in_specs, out_specs=out_specs, check_vma=False)
```

time: 733 us -> 465 us (0.63)
  waiting for transfers between devices: 582 us -> 203 us
  starting transfers between devices: 7.51 us -> 84.8 us
  Pallas kernels: 0 us -> 21.6 us
  matrix products: 66.7 us -> 80.3 us
  local copies, waits for them, and re-layouts: 43.5 us -> 31.5 us
    reduce_scatter x1 -> x0, waiting for transfers between devices: 539 us -> none  [shards(): lax.psum_scatter(lax.dot_general(doc_states, both_grads, (((0,), (0,)), (...]
    ppermute x0 -> x29, waiting for transfers between devices: none -> 141 us  [the longest x12 63.4 us: step_up(): return lax.ppermute(value, 'seq', pairs)]
    ppermute x0 -> x29, starting transfers between devices: none -> 59 us  [the longest x12 39.9 us: step_up(): return lax.ppermute(value, 'seq', pairs)]
    pallas_call x0 -> x4, Pallas kernels: none -> 21.6 us  [attend(): pl.pallas_call(attend_kernel, grid=(heads,), in_specs=[pl.BlockSpec(memor...]
    dot_general x8 -> x25, matrix products: 61.6 us -> 80.3 us  [the longest x14 35.1 us: down_dot(): lax.dot_general(left, right, (((0,), (0,)), ((), ())), preferred_element_...]
    scatter x2 -> x0, local copies, waits for them, and re-layouts: 17.9 us -> none  [the longest x1 15.5 us: shards(): order_slot.at[placed.reshape(-1)]]
    all_to_all x1 -> x2, waiting for transfers between devices: 15.7 us -> 31 us  [the longest x1 31 us: route(): lax.all_to_all(sent, 'seq', split_axis=0, concat_axis=0, tiled=True)]
    all_gather x1 -> x3, starting transfers between devices: 0.04 us -> 12.6 us  [the longest x1 12.6 us: shards(): gathered.append(lax.all_gather(got, 'tp', axis=1, tiled=True))]
  transfers between devices with their start and end apart: 3 -> 34, of which waited for: 3 -> 15; matrix products, arithmetic and copies ran while one was open for 3% -> 24% of each run, Pallas kernels for 0% -> 3%
where the time goes in v1:
time: 465 us; the launch traced here: 462 us
  waiting for transfers between devices  203 us (44%)
  starting transfers between devices  84.8 us (18%)
  matrix products  80.3 us (17%)
  local copies, waits for them, and re-layouts  31.5 us (7%)
  other arithmetic  25.5 us (5%)
  Pallas kernels  21.6 us (5%)
  between operations  14.9 us (3%)
    ppermute x12, waiting for transfers between devices, step_up(): return lax.ppermute(value, 'seq', pairs)  63.4 us
    ppermute x12, waiting for transfers between devices, step_down(): return lax.ppermute(value, 'seq', pairs)  40.8 us
    ppermute x12, starting transfers between devices, step_up(): return lax.ppermute(value, 'seq', pairs)  39.9 us
    ppermute x5, waiting for transfers between devices, turn(): return lax.ppermute(value, 'seq', pairs)  37 us
    dot_general x14, matrix products, down_dot(): lax.dot_general(left, right, (((0,), (0,)), ((), ())), preferred_element_...  35.1 us
    all_gather x1, waiting for transfers between devices, shards(): doc_states = lax.all_gather(doc_part, 'tp', axis=1, tiled=True)  31.1 us
    all_to_all x1, waiting for transfers between devices, route(): lax.all_to_all(sent, 'seq', split_axis=0, concat_axis=0, tiled=True)  31 us
    dot_general x4, matrix products, shards(): jnp.dot(doc_states, key_weight[:, columns], preferred_element_type=WIDE)  22.3 us
  transfers between devices with their start and end apart: 34, of which 15 were waited for; matrix products, arithmetic and copies ran while one was open for 24% of the time, Pallas kernels for 3%

profile of v1, /device:TPU:0, one launch (start us, length us, event | category | flops | bytes accessed | tf_op | source)
XLA Modules:
  0.0 462.0 jit_solution(14623258388106990402)
XLA Ops:
  10.3 7.4 %all-to-all-start = ((bf16[8,80,1024]{2,1,0:T(8,128)(2,1)}), bf16[8,80,1024]{2,1,0:T(8,128)(2,1)S(1)}, u32[]{:S(2)}, u32[]{:S(2)}) async-start(bf16[8,80,1024]{2,1,0:T(8,128)(2,1)} %bitcast.119), calls=%async_computation | async-start | bytes 2621440 | tf_op jit(solution)/shard_map/route/all_to_all | solution.py:107
  18.1 31.0 %all-to-all-done = bf16[8,80,1024]{2,1,0:T(8,128)(2,1)S(1)} async-done(((bf16[8,80,1024]{2,1,0:T(8,128)(2,1)}), bf16[8,80,1024]{2,1,0:T(8,128)(2,1)S(1)}, u32[]{:S(2)}, u32[]{:S(2)}) %all-to-all-start) | async-done | bytes 1310752 | tf_op jit(solution)/shard_map/route/all_to_all | solution.py:107
  53.8 31.1 %all-gather.4.cloned.1.call-done = bf16[512,4096]{1,0:T(8,128)(2,1)} async-done(((bf16[512,1024]{1,0:T(8,128)(2,1)}), bf16[512,4096]{1,0:T(8,128)(2,1)}) %all-gather.4.cloned.1.call-update) | async-done | bytes 4194320 | tf_op jit(solution)/shard_map/gather_states/all_gather | solution.py:153
  84.8 5.9 %fusion.46.key_ref = bf16[512,512]{1,0:T(8,128)(2,1)S(1)} fusion(bf16[512,4096]{1,0:T(8,128)(2,1)} %all-gather.4.cloned.1.call-done, bf16[4096,2048]{1,0:T(8,128)(2,1)} %param.15), kind=kOutput, calls=%fused_computation.66 | convolution fusion | flops 2147745792 | bytes 8912896 | tf_op jit(solution)/shard_map/attend_2/dot_general | solution.py:189
  90.8 4.7 %fusion.49.value_ref = bf16[512,512]{1,0:T(8,128)(2,1)S(1)} fusion(bf16[512,4096]{1,0:T(8,128)(2,1)S(1)} %copy-done.19, bf16[4096,2048]{1,0:T(8,128)(2,1)} %param.16), kind=kOutput, calls=%fused_computation.67 | convolution fusion | flops 2147745792 | bytes 8912896 | tf_op jit(solution)/shard_map/attend_2/dot_general | solution.py:190
  95.5 6.2 %attend_2.1 = (bf16[256,512]{1,0:T(8,128)(2,1)S(1)}, bf16[512,1024]{1,0:T(8,128)(2,1)}) custom-call(s32[2]{0:T(128)S(1)} %pad_add_fusion.info_ref, bf16[256,2048]{1,0:T(8,128)(2,1)S(1)} %copy-done.8, bf16[512,512]{1,0:T(8,128)(2,1)S(1)} %fusion.46.key_ref, bf16[512,512]{1,0:T(8,128)(2,1)S(1)} %fusion.49.value_ref, bf16[256,2048]{1,0:T(8,128)(2,1)S(1)} %copy-done.11), custom_call_target="tpu_custom_call" | custom-call | flops 3221225472 | bytes 3145728 | tf_op jit(solution)/shard_map/attend_2/pallas_call | solution.py:48
  101.7 4.4 collective-permute-start.15
  107.3 4.5 fusion.34.key_ref
  111.9 4.5 fusion.37.value_ref
  116.4 5.1 %attend_0.1 = (bf16[256,512]{1,0:T(8,128)(2,1)S(1)}, bf16[512,1024]{1,0:T(8,128)(2,1)S(1)}) custom-call(s32[2]{0:T(128)S(1)} %pad_add_fusion.info_ref, bf16[256,2048]{1,0:T(8,128)(2,1)S(1)} %copy-done.8, bf16[512,512]{1,0:T(8,128)(2,1)S(1)} %fusion.34.key_ref, bf16[512,512]{1,0:T(8,128)(2,1)S(1)} %fusion.37.value_ref, bf16[256,2048]{1,0:T(8,128)(2,1)S(1)} %copy-done.11), custom_call_target="tpu_custom_call" | custom-call | flops 3221225472 | bytes 3145728 | tf_op jit(solution)/shard_map/attend_0/pallas_call | solution.py:48
  122.3 5.6 %collective-permute-start = (bf16[512,1024]{1,0:T(8,128)(2,1)S(1)}, bf16[512,1024]{1,0:T(8,128)(2,1)}, u32[]{:S(2)}, u32[]{:S(2)}) collective-permute-start(bf16[512,1024]{1,0:T(8,128)(2,1)S(1)} %get-tuple-element.15), channel_id=1, source_target_pairs={{0,8},{4,12},{8,16},{12,20},{16,24},{20,28},{1,9},{5,13},{9,17},{1... | collective-permute-start | bytes 3145736 | tf_op jit(solution)/shard_map/rows_0_0/ppermute | solution.py:140
  133.7 5.8 %all-to-all-start.1 = ((bf16[4,128,1024]{2,1,0:T(8,128)(2,1)}), bf16[4,128,1024]{2,1,0:T(8,128)(2,1)}, u32[]{:S(2)}, u32[]{:S(2)}) async-start(bf16[4,128,1024]{2,1,0:T(8,128)(2,1)} %bitcast.6), calls=%async_computation.1 | async-start | bytes 2097152 | tf_op jit(solution)/shard_map/line_states/all_to_all | solution.py:159
  139.5 12.6 %all-gather.8.cloned.1.call-start = ((), (), s32[]{:S(2)}) async-start(), calls=%async_computation.4 | async-start | bytes 2621440 | tf_op jit(solution)/shard_map/side_states/all_gather | solution.py:173
  152.1 5.9 %fusion.52.key_ref = bf16[512,512]{1,0:T(8,128)(2,1)S(1)} fusion(bf16[512,4096]{1,0:T(8,128)(2,1)} %all-gather.4.cloned.1.call-done, bf16[4096,2048]{1,0:T(8,128)(2,1)} %param.15), kind=kOutput, calls=%fused_computation.68 | convolution fusion | flops 2147745792 | bytes 8912896 | tf_op jit(solution)/shard_map/attend_3/dot_general | solution.py:189
  158.1 4.7 %fusion.55.value_ref = bf16[512,512]{1,0:T(8,128)(2,1)S(1)} fusion(bf16[512,4096]{1,0:T(8,128)(2,1)S(1)} %copy-done.20, bf16[4096,2048]{1,0:T(8,128)(2,1)} %param.16), kind=kOutput, calls=%fused_computation.69 | convolution fusion | flops 2147745792 | bytes 8912896 | tf_op jit(solution)/shard_map/attend_3/dot_general | solution.py:190
  162.8 5.1 %attend_3.1 = (bf16[256,512]{1,0:T(8,128)(2,1)S(1)}, bf16[512,1024]{1,0:T(8,128)(2,1)S(1)}) custom-call(s32[2]{0:T(128)S(1)} %pad_add_fusion.info_ref, bf16[256,2048]{1,0:T(8,128)(2,1)S(1)} %copy-done.9, bf16[512,512]{1,0:T(8,128)(2,1)S(1)} %fusion.52.key_ref, bf16[512,512]{1,0:T(8,128)(2,1)S(1)} %fusion.55.value_ref, bf16[256,2048]{1,0:T(8,128)(2,1)S(1)} %copy-done.12), custom_call_target="tpu_custom_call" | custom-call | flops 3221225472 | bytes 3145728 | tf_op jit(solution)/shard_map/attend_3/pallas_call | solution.py:48
  168.9 5.9 %fusion.40.key_ref = bf16[512,512]{1,0:T(8,128)(2,1)S(1)} fusion(bf16[512,4096]{1,0:T(8,128)(2,1)} %all-gather.4.cloned.1.call-done, bf16[4096,2048]{1,0:T(8,128)(2,1)} %param.15), kind=kOutput, calls=%fused_computation.64 | convolution fusion | flops 2147745792 | bytes 8912896 | tf_op jit(solution)/shard_map/attend_1/dot_general | solution.py:189
  174.9 5.0 %fusion.43.value_ref = bf16[512,512]{1,0:T(8,128)(2,1)S(1)} fusion(bf16[512,4096]{1,0:T(8,128)(2,1)S(1)} %copy-done.21, bf16[4096,2048]{1,0:T(8,128)(2,1)} %param.16), kind=kOutput, calls=%fused_computation.65 | convolution fusion | flops 2147745792 | bytes 8912896 | tf_op jit(solution)/shard_map/attend_1/dot_general | solution.py:190
  181.5 5.1 %attend_1.1 = (bf16[256,512]{1,0:T(8,128)(2,1)S(1)}, bf16[512,1024]{1,0:T(8,128)(2,1)S(1)}) custom-call(s32[2]{0:T(128)S(1)} %pad_add_fusion.info_ref, bf16[256,2048]{1,0:T(8,128)(2,1)S(1)} %copy-done.10, bf16[512,512]{1,0:T(8,128)(2,1)S(1)} %fusion.40.key_ref, bf16[512,512]{1,0:T(8,128)(2,1)S(1)} %fusion.43.value_ref, bf16[256,2048]{1,0:T(8,128)(2,1)S(1)} %copy-done.13), custom_call_target="tpu_custom_call" | custom-call | flops 3221225472 | bytes 3145728 | tf_op jit(solution)/shard_map/attend_1/pallas_call | solution.py:48
  187.4 7.9 %reshape.128 = bf16[512,4,2,512]{3,2,1,0:T(2,128)(2,1)} reshape(bf16[512,4096]{1,0:T(8,128)(2,1)} %all-gather.4.cloned.1.call-done) | data formatting | bytes 8388608 | tf_op jit(solution)/shard_map/side_states/reshape | solution.py:175
  196.6 8.5 %constant_dynamic-slice_fusion.1 = bf16[512,4,1,512]{3,2,1,0:T(2,128)(2,1)} fusion(bf16[512,4,2,512]{3,2,1,0:T(2,128)(2,1)} %reshape.128, s32[]{:T(128)S(6)} %select_n.180), kind=kLoop, calls=%fused_computation.108 | loop fusion | bytes 4194308 | tf_op jit(solution)/shard_map/side_states/jit(dynamic_index_in_dim)/dynamic_slice | solution.py:174
  210.7 2.5 copy.62
  222.9 13.2 %collective-permute-done.17 = bf16[512,1024]{1,0:T(8,128)(2,1)} collective-permute-done((bf16[512,1024]{1,0:T(8,128)(2,1)}, bf16[512,1024]{1,0:T(8,128)(2,1)}, u32[]{:S(2)}, u32[]{:S(2)}) %collective-permute-start.17) | collective-permute-done | bytes 1048608 | tf_op jit(solution)/shard_map/rows_1_1/ppermute | solution.py:144
  237.3 2.5 broadcast_select_fusion.2
  241.5 17.0 %collective-permute-done.2 = bf16[512,1024]{1,0:T(8,128)(2,1)} collective-permute-done((bf16[512,1024]{1,0:T(8,128)(2,1)}, bf16[512,1024]{1,0:T(8,128)(2,1)}, u32[]{:S(2)}, u32[]{:S(2)}) %collective-permute-start.2) | collective-permute-done | bytes 1048608 | tf_op jit(solution)/shard_map/rows_1_0/ppermute | solution.py:144
  259.8 2.4 broadcast_select_fusion.3
  262.2 2.5 broadcast_select_fusion
  264.7 3.1 convolution_convert_fusion.1
  267.8 5.7 %collective-permute-start.23 = (bf16[512,1024]{1,0:T(8,128)(2,1)S(1)}, bf16[512,1024]{1,0:T(8,128)(2,1)S(1)}, u32[]{:S(2)}, u32[]{:S(2)}) collective-permute-start(bf16[512,1024]{1,0:T(8,128)(2,1)S(1)} %convolution_convert_fusion.1), channel_id=1, source_target_pairs={{0,8},{4,12},{1,9},{5,13},{2,10},{6,14},{3,11},{7,15}} | collective-permute-start | bytes 3145736 | tf_op jit(solution)/shard_map/sums_1_1/ppermute | solution.py:140
  274.2 6.8 %collective-permute-done.18 = bf16[512,1024]{1,0:T(8,128)(2,1)} collective-permute-done((bf16[512,1024]{1,0:T(8,128)(2,1)}, bf16[512,1024]{1,0:T(8,128)(2,1)}, u32[]{:S(2)}, u32[]{:S(2)}) %collective-permute-start.18) | collective-permute-done | bytes 1048608 | tf_op jit(solution)/shard_map/rows_2_1/ppermute | solution.py:144
  282.4 3.5 pad_maximum_fusion.1
  285.8 2.9 convolution_convert_fusion.2
  296.0 3.9 collective-permute-done.3
  302.9 13.5 %collective-permute-done.9 = bf16[512,1024]{1,0:T(8,128)(2,1)S(1)} collective-permute-done((bf16[512,1024]{1,0:T(8,128)(2,1)S(1)}, bf16[512,1024]{1,0:T(8,128)(2,1)S(1)}, u32[]{:S(2)}, u32[]{:S(2)}) %collective-permute-start.9) | collective-permute-done | bytes 1048608 | tf_op jit(solution)/shard_map/sums_1_0/ppermute | solution.py:140
  316.4 3.0 add_convert_fusion.10
  322.5 5.0 %collective-permute-start.10 = (bf16[512,1024]{1,0:T(8,128)(2,1)S(1)}, bf16[512,1024]{1,0:T(8,128)(2,1)S(1)}, u32[]{:S(2)}, u32[]{:S(2)}) collective-permute-start(bf16[512,1024]{1,0:T(8,128)(2,1)S(1)} %get-tuple-element.19), channel_id=1, source_target_pairs={{0,8},{4,12},{8,16},{12,20},{1,9},{5,13},{9,17},{13,21},{2,10},{6,... | collective-permute-start | bytes 3145736 | tf_op jit(solution)/shard_map/sums_2_0/ppermute | solution.py:140
  330.1 8.8 %collective-permute-done.24 = bf16[512,1024]{1,0:T(8,128)(2,1)S(1)} collective-permute-done((bf16[512,1024]{1,0:T(8,128)(2,1)S(1)}, bf16[512,1024]{1,0:T(8,128)(2,1)S(1)}, u32[]{:S(2)}, u32[]{:S(2)}) %collective-permute-start.24) | collective-permute-done | bytes 1048608 | tf_op jit(solution)/shard_map/sums_2_1/ppermute | solution.py:140
  340.2 4.5 collective-permute-start.25
  344.6 2.9 add_convert_fusion.7
  348.8 12.5 %collective-permute-done.10 = bf16[512,1024]{1,0:T(8,128)(2,1)S(1)} collective-permute-done((bf16[512,1024]{1,0:T(8,128)(2,1)S(1)}, bf16[512,1024]{1,0:T(8,128)(2,1)S(1)}, u32[]{:S(2)}, u32[]{:S(2)}) %collective-permute-start.10) | collective-permute-done | bytes 1048608 | tf_op jit(solution)/shard_map/sums_2_0/ppermute | solution.py:140
  361.3 2.9 add_convert_fusion.9
  364.2 4.6 %collective-permute-start.11 = (bf16[512,1024]{1,0:T(8,128)(2,1)S(1)}, bf16[512,1024]{1,0:T(8,128)(2,1)S(1)}, u32[]{:S(2)}, u32[]{:S(2)}) collective-permute-start(bf16[512,1024]{1,0:T(8,128)(2,1)S(1)} %add_convert_fusion.9), channel_id=1, source_target_pairs={{0,8},{4,12},{8,16},{12,20},{16,24},{20,28},{1,9},{5,13},{9,17},{1... | collective-permute-start | bytes 3145736 | tf_op jit(solution)/shard_map/sums_3_0/ppermute | solution.py:140
  370.1 2.9 fusion.92
  373.0 10.8 %collective-permute-done.25 = bf16[512,1024]{1,0:T(8,128)(2,1)S(1)} collective-permute-done((bf16[512,1024]{1,0:T(8,128)(2,1)S(1)}, bf16[512,1024]{1,0:T(8,128)(2,1)S(1)}, u32[]{:S(2)}, u32[]{:S(2)}) %collective-permute-start.25) | collective-permute-done | bytes 1048608 | tf_op jit(solution)/shard_map/sums_3_1/ppermute | solution.py:140
  384.4 16.7 %collective-permute-done.11 = bf16[512,1024]{1,0:T(8,128)(2,1)S(1)} collective-permute-done((bf16[512,1024]{1,0:T(8,128)(2,1)S(1)}, bf16[512,1024]{1,0:T(8,128)(2,1)S(1)}, u32[]{:S(2)}, u32[]{:S(2)}) %collective-permute-start.11) | collective-permute-done | bytes 1048608 | tf_op jit(solution)/shard_map/sums_3_0/ppermute | solution.py:140
  401.7 5.3 %fusion.27 = bf16[512,1024]{1,0:T(8,128)(2,1)S(1)} fusion(bf16[2048,1024]{1,0:T(8,128)(2,1)} %bitcast.108, bf16[2048,1024]{1,0:T(8,128)(2,1)} %bitcast.125, s32[]{:T(128)S(6)} %select_n.179), kind=kOutput, calls=%fused_computation.54 | convolution fusion | flops 2148007936 | bytes 7340036 | tf_op jit(solution)/shard_map/even_1/dot_general | solution.py:74
  411.8 21.5 %collective-permute-done.21 = bf16[512,1024]{1,0:T(8,128)(2,1)S(1)} collective-permute-done((bf16[512,1024]{1,0:T(8,128)(2,1)S(1)}, bf16[512,1024]{1,0:T(8,128)(2,1)S(1)}, u32[]{:S(2)}, u32[]{:S(2)}) %collective-permute-start.21) | collective-permute-done | bytes 1048608 | tf_op jit(solution)/shard_map/even_1/ppermute | solution.py:148
  435.7 13.9 %collective-permute-done.6 = bf16[512,1024]{1,0:T(8,128)(2,1)S(1)} collective-permute-done((bf16[512,1024]{1,0:T(8,128)(2,1)S(1)}, bf16[512,1024]{1,0:T(8,128)(2,1)S(1)}, u32[]{:S(2)}, u32[]{:S(2)}) %collective-permute-start.6) | collective-permute-done | bytes 1048608 | tf_op jit(solution)/shard_map/even_0/ppermute | solution.py:148
  (161 shorter events, 75.8 us)
Async XLA Ops:
  10.3 7.4 %copy-start.28 = (s32[4096]{0:T(1024)S(1)}, s32[4096]{0:T(1024)}, u32[]{:S(2)}) copy-start(s32[4096]{0:T(1024)} %param.12) | copy-start | bytes 49156
  10.3 38.8 %all-to-all-start = ((bf16[8,80,1024]{2,1,0:T(8,128)(2,1)}), bf16[8,80,1024]{2,1,0:T(8,128)(2,1)S(1)}, u32[]{:S(2)}, u32[]{:S(2)}) async-start(bf16[8,80,1024]{2,1,0:T(8,128)(2,1)} %bitcast.119), calls=%async_computation | async-start | bytes 2621440 | tf_op jit(solution)/shard_map/route/all_to_all | solution.py:107
  17.7 67.1 %all-gather.4.cloned.1.call-start = ((), (), s32[]{:S(2)}) async-start(), calls=%async_computation.2 | async-start | bytes 5242880 | tf_op jit(solution)/shard_map/gather_states/all_gather | solution.py:153
  101.7 78.2 %collective-permute-start.15 = (bf16[512,1024]{1,0:T(8,128)(2,1)}, bf16[512,1024]{1,0:T(8,128)(2,1)}, u32[]{:S(2)}, u32[]{:S(2)}) collective-permute-start(bf16[512,1024]{1,0:T(8,128)(2,1)} %get-tuple-element.17), channel_id=1, source_target_pairs={{0,8},{4,12},{8,16},{12,20},{16,24},{20,28},{1,9},{5,13},{9,17},{1... | collective-permute-start | bytes 3145736 | tf_op jit(solution)/shard_map/rows_0_1/ppermute | solution.py:140
  106.0 99.0 %collective-permute-start.16 = (bf16[512,1024]{1,0:T(8,128)(2,1)}, bf16[512,1024]{1,0:T(8,128)(2,1)}, u32[]{:S(2)}, u32[]{:S(2)}) collective-permute-start(bf16[512,1024]{1,0:T(8,128)(2,1)} %get-tuple-element.17), channel_id=1, source_target_pairs={{8,0},{12,4},{16,8},{20,12},{24,16},{28,20},{9,1},{13,5},{17,9},{2... | collective-permute-start | bytes 3145736 | tf_op jit(solution)/shard_map/rows_0_1/ppermute | solution.py:144
  122.3 85.2 %collective-permute-start = (bf16[512,1024]{1,0:T(8,128)(2,1)S(1)}, bf16[512,1024]{1,0:T(8,128)(2,1)}, u32[]{:S(2)}, u32[]{:S(2)}) collective-permute-start(bf16[512,1024]{1,0:T(8,128)(2,1)S(1)} %get-tuple-element.15), channel_id=1, source_target_pairs={{0,8},{4,12},{8,16},{12,20},{16,24},{20,28},{1,9},{5,13},{9,17},{1... | collective-permute-start | bytes 3145736 | tf_op jit(solution)/shard_map/rows_0_0/ppermute | solution.py:140
  127.8 81.5 %collective-permute-start.1 = (bf16[512,1024]{1,0:T(8,128)(2,1)S(1)}, bf16[512,1024]{1,0:T(8,128)(2,1)}, u32[]{:S(2)}, u32[]{:S(2)}) collective-permute-start(bf16[512,1024]{1,0:T(8,128)(2,1)S(1)} %get-tuple-element.15), channel_id=1, source_target_pairs={{8,0},{12,4},{16,8},{20,12},{24,16},{28,20},{9,1},{13,5},{17,9},{2... | collective-permute-start | bytes 3145736 | tf_op jit(solution)/shard_map/rows_0_0/ppermute | solution.py:144
  131.0 37.0 %collective-permute-start.7 = (bf16[4,128,512]{2,1,0:T(8,128)(2,1)}, bf16[4,128,512]{2,1,0:T(8,128)(2,1)S(1)}, u32[]{:S(2)}, u32[]{:S(2)}) collective-permute-start(bf16[4,128,512]{2,1,0:T(8,128)(2,1)} %bitcast.120), channel_id=1, source_target_pairs={{0,4},{4,0},{8,12},{12,8},{16,20},{20,16},{24,28},{28,24},{1,5},{5... | collective-permute-start | bytes 1572872 | tf_op jit(solution)/shard_map/side_states/ppermute | solution.py:148
  133.7 86.1 %all-to-all-start.1 = ((bf16[4,128,1024]{2,1,0:T(8,128)(2,1)}), bf16[4,128,1024]{2,1,0:T(8,128)(2,1)}, u32[]{:S(2)}, u32[]{:S(2)}) async-start(bf16[4,128,1024]{2,1,0:T(8,128)(2,1)} %bitcast.6), calls=%async_computation.1 | async-start | bytes 2097152 | tf_op jit(solution)/shard_map/line_states/all_to_all | solution.py:159
  139.5 125.2 %all-gather.8.cloned.1.call-start = ((), (), s32[]{:S(2)}) async-start(), calls=%async_computation.4 | async-start | bytes 2621440 | tf_op jit(solution)/shard_map/side_states/all_gather | solution.py:173
  167.9 6.9 %copy-start.4 = (bf16[256,512]{1,0:T(8,128)(2,1)}, bf16[256,512]{1,0:T(8,128)(2,1)S(1)}, u32[]{:S(2)}) copy-start(bf16[256,512]{1,0:T(8,128)(2,1)S(1)} %get-tuple-element.14) | copy-start | bytes 786436
  168.0 27.3 %collective-permute-start.22 = (bf16[512,1024]{1,0:T(8,128)(2,1)S(1)}, bf16[512,1024]{1,0:T(8,128)(2,1)}, u32[]{:S(2)}, u32[]{:S(2)}) collective-permute-start(bf16[512,1024]{1,0:T(8,128)(2,1)S(1)} %get-tuple-element.18), channel_id=1, source_target_pairs={{0,4},{4,0},{8,12},{12,8},{16,20},{20,16},{24,28},{28,24},{1,5},{5... | collective-permute-start | bytes 3145736 | tf_op jit(solution)/shard_map/sums_0_1/ppermute | solution.py:148
  168.8 232.9 %all-gather.6.cloned.1.call-start = ((), (), s32[]{:S(2)}) async-start(), calls=%async_computation.3 | async-start | bytes 5242880 | tf_op jit(solution)/shard_map/line_states/all_gather | solution.py:164
  168.9 6.0 %copy-start.21 = (bf16[512,4096]{1,0:T(8,128)(2,1)S(1)}, bf16[512,4096]{1,0:T(8,128)(2,1)}, u32[]{:S(2)}) copy-start(bf16[512,4096]{1,0:T(8,128)(2,1)} %all-gather.4.cloned.1.call-done) | copy-start | bytes 12582916
  174.9 6.7 %copy-start.10 = (bf16[256,2048]{1,0:T(8,128)(2,1)S(1)}, bf16[256,2048]{1,0:T(8,128)(2,1)}, u32[]{:S(2)}) copy-start(bf16[256,2048]{1,0:T(8,128)(2,1)} %query_ref.7) | copy-start | bytes 3145732
  174.9 6.7 %copy-start.13 = (bf16[256,2048]{1,0:T(8,128)(2,1)S(1)}, bf16[256,2048]{1,0:T(8,128)(2,1)}, u32[]{:S(2)}) copy-start(bf16[256,2048]{1,0:T(8,128)(2,1)} %grad_ref.7) | copy-start | bytes 3145732
  179.9 34.4 %collective-permute-start.19 = (bf16[512,1024]{1,0:T(8,128)(2,1)}, bf16[512,1024]{1,0:T(8,128)(2,1)}, u32[]{:S(2)}, u32[]{:S(2)}) collective-permute-start(bf16[512,1024]{1,0:T(8,128)(2,1)} %collective-permute-done.15), channel_id=1, source_target_pairs={{8,16},{12,20},{16,24},{20,28},{9,17},{13,21},{17,25},{21,29},{10,... | collective-permute-start | bytes 3145736 | tf_op jit(solution)/shard_map/rows_1_1/ppermute | solution.py:140
  195.2 11.2 %copy-start.3 = (bf16[256,512]{1,0:T(8,128)(2,1)S(1)}, bf16[256,512]{1,0:T(8,128)(2,1)}, u32[]{:S(2)}) copy-start(bf16[256,512]{1,0:T(8,128)(2,1)} %copy-done.2) | copy-start | bytes 786436
  195.2 11.2 %copy-start.5 = (bf16[256,512]{1,0:T(8,128)(2,1)S(1)}, bf16[256,512]{1,0:T(8,128)(2,1)}, u32[]{:S(2)}) copy-start(bf16[256,512]{1,0:T(8,128)(2,1)} %copy-done.4) | copy-start | bytes 786436
  195.2 11.2 %copy-start.7 = (bf16[256,512]{1,0:T(8,128)(2,1)S(1)}, bf16[256,512]{1,0:T(8,128)(2,1)}, u32[]{:S(2)}) copy-start(bf16[256,512]{1,0:T(8,128)(2,1)} %copy-done.6) | copy-start | bytes 786436
  195.3 23.5 %collective-permute-start.8 = (bf16[512,1024]{1,0:T(8,128)(2,1)S(1)}, bf16[512,1024]{1,0:T(8,128)(2,1)S(1)}, u32[]{:S(2)}, u32[]{:S(2)}) collective-permute-start(bf16[512,1024]{1,0:T(8,128)(2,1)S(1)} %get-tuple-element.16), channel_id=1, source_target_pairs={{0,4},{4,0},{8,12},{12,8},{16,20},{20,16},{24,28},{28,24},{1,5},{5... | collective-permute-start | bytes 3145736 | tf_op jit(solution)/shard_map/sums_0_0/ppermute | solution.py:148
  205.1 31.0 %collective-permute-start.17 = (bf16[512,1024]{1,0:T(8,128)(2,1)}, bf16[512,1024]{1,0:T(8,128)(2,1)}, u32[]{:S(2)}, u32[]{:S(2)}) collective-permute-start(bf16[512,1024]{1,0:T(8,128)(2,1)} %collective-permute-done.16), channel_id=1, source_target_pairs={{8,0},{12,4},{16,8},{20,12},{9,1},{13,5},{17,9},{21,13},{10,2},{14... | collective-permute-start | bytes 3145736 | tf_op jit(solution)/shard_map/rows_1_1/ppermute | solution.py:144
  207.5 32.3 %collective-permute-start.4 = (bf16[512,1024]{1,0:T(8,128)(2,1)}, bf16[512,1024]{1,0:T(8,128)(2,1)}, u32[]{:S(2)}, u32[]{:S(2)}) collective-permute-start(bf16[512,1024]{1,0:T(8,128)(2,1)} %collective-permute-done), channel_id=1, source_target_pairs={{8,16},{12,20},{16,24},{20,28},{9,17},{13,21},{17,25},{21,29},{10,... | collective-permute-start | bytes 3145736 | tf_op jit(solution)/shard_map/rows_1_0/ppermute | solution.py:140
  209.3 49.2 %collective-permute-start.2 = (bf16[512,1024]{1,0:T(8,128)(2,1)}, bf16[512,1024]{1,0:T(8,128)(2,1)}, u32[]{:S(2)}, u32[]{:S(2)}) collective-permute-start(bf16[512,1024]{1,0:T(8,128)(2,1)} %collective-permute-done.1), channel_id=1, source_target_pairs={{8,0},{12,4},{16,8},{20,12},{9,1},{13,5},{17,9},{21,13},{10,2},{14... | collective-permute-start | bytes 3145736 | tf_op jit(solution)/shard_map/rows_1_0/ppermute | solution.py:144
  214.2 48.0 %collective-permute-start.20 = (bf16[512,1024]{1,0:T(8,128)(2,1)}, bf16[512,1024]{1,0:T(8,128)(2,1)}, u32[]{:S(2)}, u32[]{:S(2)}) collective-permute-start(bf16[512,1024]{1,0:T(8,128)(2,1)} %collective-permute-done.19), channel_id=1, source_target_pairs={{16,24},{20,28},{17,25},{21,29},{18,26},{22,30},{19,27},{23,31}} | collective-permute-start | bytes 3145736 | tf_op jit(solution)/shard_map/rows_2_1/ppermute | solution.py:140
  236.0 44.9 %collective-permute-start.18 = (bf16[512,1024]{1,0:T(8,128)(2,1)}, bf16[512,1024]{1,0:T(8,128)(2,1)}, u32[]{:S(2)}, u32[]{:S(2)}) collective-permute-start(bf16[512,1024]{1,0:T(8,128)(2,1)} %collective-permute-done.17), channel_id=1, source_target_pairs={{8,0},{12,4},{9,1},{13,5},{10,2},{14,6},{11,3},{15,7}} | collective-permute-start | bytes 3145736 | tf_op jit(solution)/shard_map/rows_2_1/ppermute | solution.py:144
  239.8 50.5 %collective-permute-start.5 = (bf16[512,1024]{1,0:T(8,128)(2,1)}, bf16[512,1024]{1,0:T(8,128)(2,1)}, u32[]{:S(2)}, u32[]{:S(2)}) collective-permute-start(bf16[512,1024]{1,0:T(8,128)(2,1)} %collective-permute-done.4), channel_id=1, source_target_pairs={{16,24},{20,28},{17,25},{21,29},{18,26},{22,30},{19,27},{23,31}} | collective-permute-start | bytes 3145736 | tf_op jit(solution)/shard_map/rows_2_0/ppermute | solution.py:140
  258.5 41.4 %collective-permute-start.3 = (bf16[512,1024]{1,0:T(8,128)(2,1)}, bf16[512,1024]{1,0:T(8,128)(2,1)}, u32[]{:S(2)}, u32[]{:S(2)}) collective-permute-start(bf16[512,1024]{1,0:T(8,128)(2,1)} %collective-permute-done.2), channel_id=1, source_target_pairs={{8,0},{12,4},{9,1},{13,5},{10,2},{14,6},{11,3},{15,7}} | collective-permute-start | bytes 3145736 | tf_op jit(solution)/shard_map/rows_2_0/ppermute | solution.py:144
  267.8 14.5 %copy-start.25 = (bf16[512,1024]{1,0:T(8,128)(2,1)S(1)}, bf16[512,1024]{1,0:T(8,128)(2,1)}, u32[]{:S(2)}) copy-start(bf16[512,1024]{1,0:T(8,128)(2,1)} %broadcast_select_fusion.2) | copy-start | bytes 3145732
  267.8 14.5 %copy-start.26 = (bf16[512,1024]{1,0:T(8,128)(2,1)S(1)}, bf16[512,1024]{1,0:T(8,128)(2,1)}, u32[]{:S(2)}) copy-start(bf16[512,1024]{1,0:T(8,128)(2,1)} %broadcast_select_fusion) | copy-start | bytes 3145732
  267.8 26.1 %collective-permute-start.23 = (bf16[512,1024]{1,0:T(8,128)(2,1)S(1)}, bf16[512,1024]{1,0:T(8,128)(2,1)S(1)}, u32[]{:S(2)}, u32[]{:S(2)}) collective-permute-start(bf16[512,1024]{1,0:T(8,128)(2,1)S(1)} %convolution_convert_fusion.1), channel_id=1, source_target_pairs={{0,8},{4,12},{1,9},{5,13},{2,10},{6,14},{3,11},{7,15}} | collective-permute-start | bytes 3145736 | tf_op jit(solution)/shard_map/sums_1_1/ppermute | solution.py:140
  273.5 20.4 %collective-permute-start.26 = (bf16[512,1024]{1,0:T(8,128)(2,1)S(1)}, bf16[512,1024]{1,0:T(8,128)(2,1)S(1)}, u32[]{:S(2)}, u32[]{:S(2)}) collective-permute-start(bf16[512,1024]{1,0:T(8,128)(2,1)S(1)} %convolution_convert_fusion.1), channel_id=1, source_target_pairs={{24,16},{28,20},{25,17},{29,21},{26,18},{30,22},{27,19},{31,23}} | collective-permute-start | bytes 3145736 | tf_op jit(solution)/shard_map/sums_1_1/ppermute | solution.py:144
  288.7 27.7 %collective-permute-start.9 = (bf16[512,1024]{1,0:T(8,128)(2,1)S(1)}, bf16[512,1024]{1,0:T(8,128)(2,1)S(1)}, u32[]{:S(2)}, u32[]{:S(2)}) collective-permute-start(bf16[512,1024]{1,0:T(8,128)(2,1)S(1)} %convolution_convert_fusion.2), channel_id=1, source_target_pairs={{0,8},{4,12},{1,9},{5,13},{2,10},{6,14},{3,11},{7,15}} | collective-permute-start | bytes 3145736 | tf_op jit(solution)/shard_map/sums_1_0/ppermute | solution.py:140
  290.4 26.0 %collective-permute-start.12 = (bf16[512,1024]{1,0:T(8,128)(2,1)S(1)}, bf16[512,1024]{1,0:T(8,128)(2,1)S(1)}, u32[]{:S(2)}, u32[]{:S(2)}) collective-permute-start(bf16[512,1024]{1,0:T(8,128)(2,1)S(1)} %convolution_convert_fusion.2), channel_id=1, source_target_pairs={{24,16},{28,20},{25,17},{29,21},{26,18},{30,22},{27,19},{31,23}} | collective-permute-start | bytes 3145736 | tf_op jit(solution)/shard_map/sums_1_0/ppermute | solution.py:144
  295.3 32.2 %collective-permute-start.27 = (bf16[512,1024]{1,0:T(8,128)(2,1)S(1)}, bf16[512,1024]{1,0:T(8,128)(2,1)S(1)}, u32[]{:S(2)}, u32[]{:S(2)}) collective-permute-start(bf16[512,1024]{1,0:T(8,128)(2,1)S(1)} %get-tuple-element.22), channel_id=1, source_target_pairs={{16,8},{20,12},{24,16},{28,20},{17,9},{21,13},{25,17},{29,21},{18,... | collective-permute-start | bytes 3145736 | tf_op jit(solution)/shard_map/sums_2_1/ppermute | solution.py:144
  301.3 18.9 %copy-start.24 = (bf16[512,1024]{1,0:T(8,128)(2,1)S(1)}, bf16[512,1024]{1,0:T(8,128)(2,1)}, u32[]{:S(2)}) copy-start(bf16[512,1024]{1,0:T(8,128)(2,1)} %broadcast_select_fusion.3) | copy-start | bytes 3145732
  301.3 37.6 %collective-permute-start.24 = (bf16[512,1024]{1,0:T(8,128)(2,1)S(1)}, bf16[512,1024]{1,0:T(8,128)(2,1)S(1)}, u32[]{:S(2)}, u32[]{:S(2)}) collective-permute-start(bf16[512,1024]{1,0:T(8,128)(2,1)S(1)} %get-tuple-element.21), channel_id=1, source_target_pairs={{0,8},{4,12},{8,16},{12,20},{1,9},{5,13},{9,17},{13,21},{2,10},{6,... | collective-permute-start | bytes 3145736 | tf_op jit(solution)/shard_map/sums_2_1/ppermute | solution.py:140
  319.4 25.2 %collective-permute-start.13 = (bf16[512,1024]{1,0:T(8,128)(2,1)S(1)}, bf16[512,1024]{1,0:T(8,128)(2,1)S(1)}, u32[]{:S(2)}, u32[]{:S(2)}) collective-permute-start(bf16[512,1024]{1,0:T(8,128)(2,1)S(1)} %get-tuple-element.20), channel_id=1, source_target_pairs={{16,8},{20,12},{24,16},{28,20},{17,9},{21,13},{25,17},{29,21},{18,... | collective-permute-start | bytes 3145736 | tf_op jit(solution)/shard_map/sums_2_0/ppermute | solution.py:144
  322.5 38.8 %collective-permute-start.10 = (bf16[512,1024]{1,0:T(8,128)(2,1)S(1)}, bf16[512,1024]{1,0:T(8,128)(2,1)S(1)}, u32[]{:S(2)}, u32[]{:S(2)}) collective-permute-start(bf16[512,1024]{1,0:T(8,128)(2,1)S(1)} %get-tuple-element.19), channel_id=1, source_target_pairs={{0,8},{4,12},{8,16},{12,20},{1,9},{5,13},{9,17},{13,21},{2,10},{6,... | collective-permute-start | bytes 3145736 | tf_op jit(solution)/shard_map/sums_2_0/ppermute | solution.py:140
  328.8 44.2 %collective-permute-start.28 = (bf16[512,1024]{1,0:T(8,128)(2,1)S(1)}, bf16[512,1024]{1,0:T(8,128)(2,1)S(1)}, u32[]{:S(2)}, u32[]{:S(2)}) collective-permute-start(bf16[512,1024]{1,0:T(8,128)(2,1)S(1)} %add_convert_fusion.1), channel_id=1, source_target_pairs={{8,0},{12,4},{16,8},{20,12},{24,16},{28,20},{9,1},{13,5},{17,9},{2... | collective-permute-start | bytes 3145736 | tf_op jit(solution)/shard_map/sums_3_1/ppermute | solution.py:144
  340.2 43.7 %collective-permute-start.25 = (bf16[512,1024]{1,0:T(8,128)(2,1)S(1)}, bf16[512,1024]{1,0:T(8,128)(2,1)S(1)}, u32[]{:S(2)}, u32[]{:S(2)}) collective-permute-start(bf16[512,1024]{1,0:T(8,128)(2,1)S(1)} %add_convert_fusion.3), channel_id=1, source_target_pairs={{0,8},{4,12},{8,16},{12,20},{16,24},{20,28},{1,9},{5,13},{9,17},{1... | collective-permute-start | bytes 3145736 | tf_op jit(solution)/shard_map/sums_3_1/ppermute | solution.py:140
  347.5 36.9 %collective-permute-start.14 = (bf16[512,1024]{1,0:T(8,128)(2,1)S(1)}, bf16[512,1024]{1,0:T(8,128)(2,1)S(1)}, u32[]{:S(2)}, u32[]{:S(2)}) collective-permute-start(bf16[512,1024]{1,0:T(8,128)(2,1)S(1)} %add_convert_fusion.7), channel_id=1, source_target_pairs={{8,0},{12,4},{16,8},{20,12},{24,16},{28,20},{9,1},{13,5},{17,9},{2... | collective-permute-start | bytes 3145736 | tf_op jit(solution)/shard_map/sums_3_0/ppermute | solution.py:144
  364.2 36.9 %collective-permute-start.11 = (bf16[512,1024]{1,0:T(8,128)(2,1)S(1)}, bf16[512,1024]{1,0:T(8,128)(2,1)S(1)}, u32[]{:S(2)}, u32[]{:S(2)}) collective-permute-start(bf16[512,1024]{1,0:T(8,128)(2,1)S(1)} %add_convert_fusion.9), channel_id=1, source_target_pairs={{0,8},{4,12},{8,16},{12,20},{16,24},{20,28},{1,9},{5,13},{9,17},{1... | collective-permute-start | bytes 3145736 | tf_op jit(solution)/shard_map/sums_3_0/ppermute | solution.py:140
  401.7 6.9 %copy-start.23 = (bf16[4,4,128,1024]{3,2,1,0:T(8,128)(2,1)S(1)}, bf16[4,4,128,1024]{3,2,1,0:T(8,128)(2,1)}, u32[]{:S(2)}) copy-start(bf16[4,4,128,1024]{3,2,1,0:T(8,128)(2,1)} %pad_maximum_fusion) | copy-start | bytes 12582916
  401.7 6.9 %copy-start.29 = (bf16[4,4,128,1024]{3,2,1,0:T(8,128)(2,1)S(1)}, bf16[4,4,128,1024]{3,2,1,0:T(8,128)(2,1)}, u32[]{:S(2)}) copy-start(bf16[4,4,128,1024]{3,2,1,0:T(8,128)(2,1)} %all-gather.6.cloned.1.call-done) | copy-start | bytes 12582916
  407.1 26.2 %collective-permute-start.21 = (bf16[512,1024]{1,0:T(8,128)(2,1)S(1)}, bf16[512,1024]{1,0:T(8,128)(2,1)S(1)}, u32[]{:S(2)}, u32[]{:S(2)}) collective-permute-start(bf16[512,1024]{1,0:T(8,128)(2,1)S(1)} %fusion.27), channel_id=1, source_target_pairs={{0,4},{4,0},{8,12},{12,8},{16,20},{20,16},{24,28},{28,24},{1,5},{5... | collective-permute-start | bytes 3145736 | tf_op jit(solution)/shard_map/even_1/ppermute | solution.py:148
  408.6 24.6 %copy-start.22 = (bf16[4,4,128,1024]{3,2,1,0:T(8,128)(2,1)S(1)}, bf16[4,4,128,1024]{3,2,1,0:T(8,128)(2,1)}, u32[]{:S(2)}) copy-start(bf16[4,4,128,1024]{3,2,1,0:T(8,128)(2,1)} %pad_maximum_fusion.1) | copy-start | bytes 12582916
  411.0 38.6 %collective-permute-start.6 = (bf16[512,1024]{1,0:T(8,128)(2,1)S(1)}, bf16[512,1024]{1,0:T(8,128)(2,1)S(1)}, u32[]{:S(2)}, u32[]{:S(2)}) collective-permute-start(bf16[512,1024]{1,0:T(8,128)(2,1)S(1)} %fusion.24), channel_id=1, source_target_pairs={{0,4},{4,0},{8,12},{12,8},{16,20},{20,16},{24,28},{28,24},{1,5},{5... | collective-permute-start | bytes 3145736 | tf_op jit(solution)/shard_map/even_0/ppermute | solution.py:148
  (18 other events, 57.8 us)
Sparse Core Ops, SparseCore 0:
  51.2 33.5 all-gather.3
  169.0 22.8 all-gather.7
  223.0 43.5 all-gather.5

commit v2 on v1

v2 whole, which is shorter than its diff:
```python
import jax
import jax.numpy as jnp
from jax import lax
from jax.experimental import pallas as pl
from jax.experimental.pallas import tpu as pltpu
from jax.sharding import PartitionSpec as P

HEAD_DIM = 128
VMEM_LIMIT = 60 * 1024 * 1024


def cost(rank):
    return pl.CostEstimate(flops=0, bytes_accessed=rank * 2**19, transcendentals=0)
LOW = jnp.bfloat16
WIDE = jnp.float32


def attend_kernel(
    info_ref, states_ref, key_weight_ref, value_weight_ref, query_ref, grad_ref, query_grad_ref, rows_grad_ref
):
    length = info_ref[0]
    offset = info_ref[1]
    scale = HEAD_DIM ** (-0.5)
    across = (((1,), (1,)), ((), ()))
    down = (((0,), (0,)), ((), ()))
    query_count, block = query_ref.shape
    state_count = states_ref.shape[0]
    key_rows = jnp.dot(states_ref[...], key_weight_ref[...], preferred_element_type=WIDE).astype(LOW)
    value_rows = jnp.dot(states_ref[...], value_weight_ref[...], preferred_element_type=WIDE).astype(LOW)
    position = lax.broadcasted_iota(jnp.int32, (query_count, state_count), 1)
    limit = jnp.minimum(
        lax.broadcasted_iota(jnp.int32, (query_count, 1), 0) + (offset + 1), length
    )
    visible = position < limit
    for head in range(block // HEAD_DIM):
        columns = slice(head * HEAD_DIM, (head + 1) * HEAD_DIM)
        query, grad = query_ref[:, columns], grad_ref[:, columns]
        key, value = key_rows[:, columns], value_rows[:, columns]
        scores = lax.dot_general(query, key, across, preferred_element_type=WIDE) * scale
        scores = jnp.where(visible, scores, -1e30)
        weights = jnp.exp(scores - jnp.max(scores, axis=-1, keepdims=True))
        probs = weights * (1.0 / jnp.sum(weights, axis=-1, keepdims=True))
        probs_low = probs.astype(LOW)
        context = jnp.dot(probs_low, value, preferred_element_type=WIDE)
        delta = jnp.sum(grad.astype(WIDE) * context, axis=-1, keepdims=True)
        prob_grad = lax.dot_general(grad, value, across, preferred_element_type=WIDE)
        score_grad = (probs * (prob_grad - delta) * scale).astype(LOW)
        query_grad_ref[:, columns] = jnp.dot(score_grad, key, preferred_element_type=WIDE).astype(LOW)
        key_grad = lax.dot_general(score_grad, query, down, preferred_element_type=WIDE)
        value_grad = lax.dot_general(probs_low, grad, down, preferred_element_type=WIDE)
        rows_grad_ref[:, columns] = key_grad.astype(LOW)
        value_columns = slice(block + head * HEAD_DIM, block + (head + 1) * HEAD_DIM)
        rows_grad_ref[:, value_columns] = value_grad.astype(LOW)


def attend(rank, info, doc_states, key_weight, value_weight, queries, grads, first, heads):
    query_count = queries.shape[0]
    state_count, feature_count = doc_states.shape
    pair = 2 if heads % 2 == 0 and first % 2 == 0 else 1
    block = pair * HEAD_DIM
    width = heads * HEAD_DIM
    return pl.pallas_call(
        attend_kernel,
        grid=(heads // pair,),
        in_specs=[
            pl.BlockSpec(memory_space=pltpu.SMEM),
            pl.BlockSpec((state_count, feature_count), lambda h: (0, 0), pipeline_mode=pl.Buffered(1)),
            pl.BlockSpec((feature_count, block), lambda h: (0, first // pair + h)),
            pl.BlockSpec((feature_count, block), lambda h: (0, first // pair + h)),
            pl.BlockSpec((query_count, block), lambda h: (0, first // pair + h)),
            pl.BlockSpec((query_count, block), lambda h: (0, first // pair + h)),
        ],
        out_specs=[
            pl.BlockSpec((query_count, block), lambda h: (0, h)),
            pl.BlockSpec((state_count, 2 * block), lambda h: (0, h)),
        ],
        out_shape=[
            jax.ShapeDtypeStruct((query_count, width), LOW),
            jax.ShapeDtypeStruct((state_count, 2 * width), LOW),
        ],
        compiler_params=pltpu.CompilerParams(vmem_limit_bytes=40 * 1024 * 1024),
        cost_estimate=cost(rank),
    )(info, doc_states, key_weight, value_weight, queries, grads)


def products(rank, scalars, z_slot, count, terms, rows, slice_width, block):
    columns = terms[0][2][0][0].shape[1]
    arrays, specs = [], []
    for left, place, rights, _ in terms:
        for k in range(count):
            arrays.append(left)
            specs.append(pl.BlockSpec((rows, slice_width), lambda c, s, k=k, place=place: place(k, s)))
        for right, row in rights:
            arrays.append(right)
            specs.append(pl.BlockSpec((rows, block), lambda c, s, row=row: (row, c)))

    def body(scalar_ref, *refs):
        refs = list(refs)
        totals = [None] * count
        for _, _, rights, limit in terms:
            lefts = [refs.pop(0) for _ in range(count)]
            right = refs.pop(0)[...]
            if len(rights) == 2:
                right = jnp.where(scalar_ref[z_slot] >= limit, right, refs.pop(0)[...])
            for k in range(count):
                product = lax.dot_general(
                    lefts[k][...], right, (((0,), (0,)), ((), ())), preferred_element_type=WIDE
                )
                totals[k] = product if totals[k] is None else totals[k] + product
        for k in range(count):
            refs[k][...] = totals[k].astype(LOW)

    return pl.pallas_call(
        body,
        grid_spec=pltpu.PrefetchScalarGridSpec(
            num_scalar_prefetch=1,
            grid=(columns // block,),
            in_specs=specs,
            out_specs=[pl.BlockSpec((slice_width, block), lambda c, s: (0, c))] * count,
        ),
        out_shape=[jax.ShapeDtypeStruct((slice_width, columns), LOW)] * count,
        compiler_params=pltpu.CompilerParams(vmem_limit_bytes=VMEM_LIMIT),
        cost_estimate=cost(rank),
    )(scalars, *arrays)


def add_arrivals(rank, scalars, bases, arrivals, block):
    slice_width, columns = bases[0].shape
    count = len(bases)

    def body(scalar_ref, *refs):
        for base_ref, ref, out_ref in zip(refs[:count], refs[count:], refs[2 * count :]):
            out_ref[...] = (base_ref[...].astype(WIDE) + ref[...].astype(WIDE)).astype(LOW)

    flat = pl.BlockSpec((slice_width, block), lambda c, s: (0, c))
    return pl.pallas_call(
        body,
        grid_spec=pltpu.PrefetchScalarGridSpec(
            num_scalar_prefetch=1,
            grid=(columns // block,),
            in_specs=[flat] * (2 * count),
            out_specs=[flat] * count,
        ),
        out_shape=[jax.ShapeDtypeStruct((slice_width, columns), LOW)] * count,
        compiler_params=pltpu.CompilerParams(vmem_limit_bytes=VMEM_LIMIT),
        cost_estimate=cost(rank),
    )(scalars, *bases, *arrivals)


def choose(rank, scalars, z_slot, limit, up, down, block):
    rows, columns = up.shape

    def body(scalar_ref, up_ref, down_ref, out_ref):
        out_ref[...] = jnp.where(scalar_ref[z_slot] >= limit, up_ref[...], down_ref[...])

    spec = pl.BlockSpec((rows, block), lambda c, s: (0, c))
    return pl.pallas_call(
        body,
        grid_spec=pltpu.PrefetchScalarGridSpec(
            num_scalar_prefetch=1, grid=(columns // block,), in_specs=[spec] * 2, out_specs=spec
        ),
        out_shape=jax.ShapeDtypeStruct(up.shape, LOW),
        compiler_params=pltpu.CompilerParams(vmem_limit_bytes=VMEM_LIMIT),
        cost_estimate=cost(rank),
    )(scalars, up, down)


def finish(rank, scalars, addends, results, shape, first, block):
    slice_width, columns = addends[0].shape
    arrays = list(addends)
    specs = [pl.BlockSpec((slice_width, block), lambda c, s: (0, c))] * len(addends)
    aliases = {}
    if results is not None:
        aliases = {1 + len(arrays): 0, 2 + len(arrays): 1}
        arrays += list(results)
        specs += [pl.BlockSpec(memory_space=pl.ANY)] * 2

    def body(scalar_ref, *refs):
        total = refs[0][...].astype(WIDE)
        for ref in refs[1 : len(addends)]:
            total = total + ref[...].astype(WIDE)
        half = total.shape[1] // 2
        refs[-2][...] = total[:, :half].astype(LOW)
        refs[-1][...] = total[:, half:].astype(LOW)

    return pl.pallas_call(
        body,
        grid_spec=pltpu.PrefetchScalarGridSpec(
            num_scalar_prefetch=1,
            grid=(columns // block,),
            in_specs=specs,
            out_specs=[pl.BlockSpec((slice_width, block // 2), lambda c, s: (0, first + c))] * 2,
        ),
        out_shape=[jax.ShapeDtypeStruct(shape, LOW)] * 2,
        input_output_aliases=aliases,
        compiler_params=pltpu.CompilerParams(vmem_limit_bytes=VMEM_LIMIT),
        cost_estimate=cost(rank),
    )(scalars, *arrays)


def line_shape(seq_count):
    minor = 1
    while (2 * minor) ** 2 <= seq_count and seq_count % (2 * minor) == 0:
        minor *= 2
    return seq_count // minor, minor


def route(states, state_doc, state_pos):
    seq_count = lax.axis_size("seq")
    device = lax.axis_index("seq")
    row_count = states.shape[0]
    capacity = 3 * row_count // (4 * seq_count) + row_count // 16
    docs_all = state_doc.reshape(seq_count, row_count)
    positions_all = state_pos.reshape(seq_count, row_count)
    before = (
        lax.broadcasted_iota(jnp.int32, (row_count, row_count), 0)
        < lax.broadcasted_iota(jnp.int32, (row_count, row_count), 1)
    ).astype(LOW)
    own_docs = lax.dynamic_index_in_dim(docs_all, device, 0, keepdims=False)
    doc_ids = jnp.arange(seq_count, dtype=jnp.int32)
    own_hot = own_docs[None, :] == doc_ids[:, None]
    mine = docs_all == device
    ranks = jnp.dot(
        jnp.concatenate([own_hot, mine], axis=0).astype(LOW), before, preferred_element_type=WIDE
    ).astype(jnp.int32)
    own_ranks = jnp.sum(jnp.where(own_hot, ranks[:seq_count], 0), axis=0)
    targets = own_docs * capacity + own_ranks
    slots = jnp.arange(seq_count * capacity, dtype=jnp.int32)
    send_hot = (targets[None, :] == slots[:, None]).astype(LOW)
    sent = jnp.dot(send_hot, states, preferred_element_type=WIDE).astype(LOW)
    arrived = lax.all_to_all(sent, "seq", split_axis=0, concat_axis=0, tiled=True)
    arrival = jnp.where(mine, ranks[seq_count:], capacity)
    hit = arrival[:, None, :] == jnp.arange(capacity, dtype=jnp.int32)[None, :, None]
    slot_position = jnp.max(jnp.where(hit, positions_all[:, None, :], -1), axis=2).reshape(-1)
    place_hot = (
        slot_position[None, :] == jnp.arange(row_count, dtype=jnp.int32)[:, None]
    ).astype(LOW)
    return jnp.dot(place_hot, arrived, preferred_element_type=WIDE).astype(LOW)


def shards(
    queries, states, state_doc, state_pos, lengths, offsets, key_weight, value_weight, context_grad
):
    seq_count = lax.axis_size("seq")
    tp_count = lax.axis_size("tp")
    device = lax.axis_index("seq")
    part = lax.axis_index("tp")
    major, minor = line_shape(seq_count)
    z, x = device // minor, device % minor
    row_count = states.shape[0]
    feature_count = key_weight.shape[0]
    slice_width = feature_count // seq_count
    quarter = row_count // tp_count
    head_count = key_weight.shape[1] // HEAD_DIM
    group_count = 4
    heads = head_count // group_count
    width = heads * HEAD_DIM

    def at(major_index, minor_index):
        return major_index * minor + minor_index

    def step_up(value, first, last):
        pairs = [(at(i, j), at(i + 1, j)) for i in range(first, last) for j in range(minor)]
        return lax.ppermute(value, "seq", pairs)

    def step_down(value, first, last):
        pairs = [(at(i, j), at(i - 1, j)) for i in range(first, last) for j in range(minor)]
        return lax.ppermute(value, "seq", pairs)

    def turn(value, shift):
        pairs = [(at(i, j), at(i, (j + shift) % minor)) for i in range(major) for j in range(minor)]
        return lax.ppermute(value, "seq", pairs)

    with jax.named_scope("route"):
        doc_part = route(states, state_doc, state_pos)

    with jax.named_scope("line_states"):
        ratio = tp_count // major
        slots = [i for i in range(0, major, 2)] + [i for i in range(1, major, 2)]
        pairs = []
        for i in range(major):
            for j in range(minor):
                for t in range(tp_count):
                    to = t // ratio
                    slot = slots.index((to - i) % major) * ratio + t % ratio
                    pairs.append((at(i, j) * tp_count + t, at(to, j) * tp_count + slot))
        moved = lax.ppermute(doc_part, ("seq", "tp"), pairs)
    side_parts = []
    if ratio == 1:
        with jax.named_scope("side_states"):
            for shift in range(1, minor):
                wanted = lax.dynamic_slice_in_dim(
                    doc_part, ((x + shift) % minor) * slice_width, slice_width, 1
                )
                side_parts.append(turn(wanted, shift))
    with jax.named_scope("gather_states"):
        doc_states = lax.all_gather(doc_part, "tp", axis=1, tiled=True)
    doc_states, moved, *side_parts = lax.optimization_barrier((doc_states, moved, *side_parts))
    with jax.named_scope("side_states"):
        if ratio == 1:
            side_states = [
                lax.all_gather(piece, "tp", axis=0, tiled=True) for piece in side_parts
            ]
        else:
            own_rows = lax.dynamic_slice_in_dim(doc_states, part * quarter, quarter, 0)
            side_states = []
            for shift in range(1, minor):
                wanted = jnp.concatenate(
                    [
                        lax.dynamic_slice_in_dim(
                            own_rows, at(i, (x + shift) % minor) * slice_width, slice_width, 1
                        )
                        for i in range(major)
                    ],
                    axis=1,
                )
                side_states.append(lax.all_gather(turn(wanted, shift), "tp", axis=0, tiled=True))
    with jax.named_scope("line_states"):
        line_states = lax.all_gather(moved, "tp", axis=0, tiled=True)
        if ratio > 1:
            line_states = line_states.reshape(major, ratio, row_count, -1).transpose(0, 2, 1, 3)
        line_states = line_states.reshape(major * row_count, minor * slice_width)

    def nearest(distance):
        return jnp.where(z + distance < major, z + distance, jnp.maximum(z - distance, 0))

    def dests_from(step):
        found = []
        for distance in range(major - step, 0, -1):
            if 2 * distance >= major:
                found.append(nearest(distance))
            else:
                found += [jnp.minimum(z + distance, major - 1), jnp.maximum(z - distance, 0)]
        return found + [z]

    first_dests, later_dests = [nearest(major - 1)], dests_from(2)
    side_dests = [(x + shift) % minor for shift in range(1, minor)] + [x]
    table = [
        lax.dynamic_index_in_dim(lengths, device, 0, keepdims=False),
        lax.dynamic_index_in_dim(offsets, device, 0, keepdims=False),
        z,
    ]
    z_slot = 2
    first_slot = len(table)
    table += [at(dest, x) for dest in first_dests] + first_dests
    later_slot = len(table)
    table += [at(dest, x) for dest in later_dests] + later_dests
    side_slot = len(table)
    table += side_dests
    table = jnp.stack([jnp.asarray(value, jnp.int32) for value in table])

    latest, pending, rank = None, [], 0

    def scalars():
        nonlocal rank
        rank += 1
        others = [] if latest is None else [latest]
        others += pending
        pending.clear()
        return lax.optimization_barrier((table, *others))[0]

    query_grads = [None] * group_count

    def attend_group(group):
        nonlocal latest
        with jax.named_scope(f"attend_{group}"):
            info = scalars()
            query_grads[group], latest = attend(
                rank, info, doc_states, key_weight, value_weight, queries, context_grad,
                group * heads, heads,
            )
            return latest

    even, odd = [None, None], [None, None]
    rows_up, rows_down = [[], []], [[], []]
    odd_rows = [None, None]
    sums_up, sums_down = [None, None], [None, None]
    side_own = [None, None]
    side_ahead, line_ahead, even_sums = [None, None], [None, None], [None, None]
    block = 4 * HEAD_DIM if heads % 2 == 0 else 2 * HEAD_DIM

    def send_first(index):
        with jax.named_scope(f"rows_0_{index}"):
            rows_up[index] = [(even[index], 0), (step_up(even[index], 0, major - 1), 0)]
            rows_down[index] = [(even[index], 0), (step_down(even[index], 1, major), 0)]

    def first_arrives(index):
        pending.extend([rows_up[index][1][0], rows_down[index][1][0]])

    def send_rows(step, index, before):
        nonlocal latest
        with jax.named_scope(f"rows_{step}_{index}"):
            up, down = rows_up[index][step][0], rows_down[index][step][0]
            others = [rows_up[before[1]][before[0] + 1][0], rows_down[before[1]][before[0] + 1][0]]
            if 2 * step < major:
                up, down = lax.optimization_barrier((up, down, latest, *others))[:2]
                up, down = step_up(up, step, major - 1), step_down(down, 1, major - step)
            else:
                pending.extend(others)
                info = scalars()
                latest = both = choose(rank, info, z_slot, step, up, down, block)
                pairs = [(at(i, j), at(i + 1, j)) for i in range(step, major - 1) for j in range(minor)]
                pairs += [(at(i, j), at(i - 1, j)) for i in range(1, major - step) for j in range(minor)]
                up = down = lax.ppermute(both, "seq", pairs)
            rows_up[index].append((up, 0))
            rows_down[index].append((down, 0))

    def send_odd(index):
        with jax.named_scope(f"side_rows_{index}"):
            odd_rows[index] = [odd[index]] + [turn(odd[index], shift) for shift in range(1, minor)]

    def side_products(index, slot, total, skip, count, free=False):
        nonlocal latest
        terms = [(doc_states, lambda k, s: (0, s[slot + skip + k]), [(odd_rows[index][0], 0)], None)]
        for states_of, rows_of in zip(side_states, odd_rows[index][1:]):
            if ratio == 1:
                place = lambda k, s: (s[slot + total + skip + k], 0)
            else:
                place = lambda k, s: (0, s[slot + total + skip + k])
            terms.append((states_of, place, [(rows_of, 0)], None))
        info = scalars()
        found = products(0 if free else rank, info, z_slot, count, terms, row_count, slice_width, block)
        latest = found[-1]
        return found

    def send_sums(step, index):
        nonlocal latest
        distance = major - step
        up_pairs = [(at(i, j), at(i + 1, j)) for i in range(major - distance) for j in range(minor)]
        down_pairs = [(at(i, j), at(i - 1, j)) for i in range(distance, major) for j in range(minor)]
        with jax.named_scope(f"sums_{step}_{index}"):
            if step == 1:
                up = down = side_products(index, first_slot, 1, 0, 1)[0]
            else:
                place = len(later_dests) - len(dests_from(step))
                info = scalars()
                up, down = sums_up[index], sums_down[index]
                if up is down and 2 * distance >= major:
                    (up,) = add_arrivals(rank, info, [side_ahead[index][place]], [up], block)
                    down = up
                else:
                    bases = [side_ahead[index][place], side_ahead[index][place + (2 * distance < major)]]
                    up, down = add_arrivals(rank, info, bases, [up, down], block)
                latest = down
            if 2 * distance > major + 1 and up is down:
                sums_up[index] = sums_down[index] = lax.ppermute(up, "seq", up_pairs + down_pairs)
            else:
                sums_up[index] = lax.ppermute(up, "seq", up_pairs)
                sums_down[index] = lax.ppermute(down, "seq", down_pairs)

    def products_ahead(index):
        with jax.named_scope(f"side_ahead_{index}"):
            count = len(later_dests)
            if count > 1:
                side_ahead[index] = side_products(index, later_slot, count, 0, count - 1, True)

    def own_product(index, *awaited):
        with jax.named_scope(f"side_own_{index}"):
            pending.extend(awaited)
            count = len(later_dests)
            side_own[index] = side_products(index, later_slot, count, count - 1, 1)[0]

    def send_even(index):
        nonlocal latest
        with jax.named_scope(f"even_{index}"):
            terms = []
            for j in range(major):
                rights = [(even[index], 0)] if j == 0 else [rows_up[index][j], rows_down[index][major - j]]
                place = lambda k, s, slot=slots.index(j): (slot, s[side_slot + k])
                terms.append((line_states, place, rights, j if j else None))
            info = scalars()
            *sent, line_ahead[index] = products(
                rank, info, z_slot, minor, terms, row_count, slice_width, block
            )
            latest = line_ahead[index]
            even_sums[index] = [turn(value, shift) for shift, value in enumerate(sent, 1)]

    results = None
    steps = 2 * width // block

    def finish_group(addends, group):
        nonlocal latest, results
        with jax.named_scope(f"finish_{group}"):
            info = scalars()
            results = finish(
                rank, info, addends, results, (slice_width, key_weight.shape[1]), group * steps, block
            )
            latest = results[0]

    even[0] = attend_group(0)
    send_first(0)
    odd[0] = attend_group(2)
    send_odd(0)
    even[1] = attend_group(1)
    send_first(1)
    first_arrives(0)
    odd[1] = attend_group(3)
    send_odd(1)
    send_sums(1, 0)
    if major > 2:
        send_rows(1, 0, (0, 1))
    products_ahead(0)
    send_sums(1, 1)
    for step in range(2, major):
        if step > 2:
            send_rows(step - 1, 1, (step - 1, 0))
        send_sums(step, 0)
        if step == 2:
            send_rows(1, 1, (1, 0))
            products_ahead(1)
            own_product(1, sums_up[1], sums_down[1])
        if step < major - 1:
            send_rows(step, 0, (step - 1, 1))
        else:
            send_even(0)
        send_sums(step, 1)
        if step == 2:
            own_product(0, sums_up[0], sums_down[0])
    if major == 2:
        own_product(1)
        own_product(0)
        send_even(0)
    send_even(1)
    finish_group([side_own[0], sums_up[0], sums_down[0]], 2)
    finish_group([line_ahead[0], *even_sums[0]], 0)
    finish_group([side_own[1], sums_up[1], sums_down[1]], 3)
    finish_group([line_ahead[1], *even_sums[1]], 1)

    return (jnp.concatenate(query_grads, axis=1), *results)


def solution(mesh):
    in_specs = (
        P("seq", "tp"),
        P("seq", "tp"),
        P(),
        P(),
        P(),
        P(),
        P(None, "tp"),
        P(None, "tp"),
        P("seq", "tp"),
    )
    out_specs = (P("seq", "tp"), P("seq", "tp"), P("seq", "tp"))
    return jax.shard_map(shards, mesh=mesh, in_specs=in_specs, out_specs=out_specs, check_vma=False)
```

time: 465 us -> 343 us (0.74)
  Pallas kernels: 21.6 us -> 132 us
  waiting for transfers between devices: 203 us -> 100 us
  matrix products: 80.3 us -> 4.04 us
  other arithmetic: 25.5 us -> 1.42 us
  local copies, waits for them, and re-layouts: 31.5 us -> 11.6 us
  starting transfers between devices: 84.8 us -> 78.2 us
    pallas_call x4 -> x22, Pallas kernels: 21.6 us -> 132 us  [the longest x8 53.3 us: products(): pl.pallas_call(body, grid_spec=pltpu.PrefetchScalarGridSpec(num_scalar_pr...]
    dot_general x22 -> x0, matrix products: 76.3 us -> none  [the longest x14 35.1 us: down_dot(): lax.dot_general(left, right, (((0,), (0,)), ((), ())), preferred_element_...]
    ppermute x12 -> x4, waiting for transfers between devices: 63.4 us -> 0.01 us  [step_up(): return lax.ppermute(value, 'seq', pairs)]
    ppermute x0 -> x13, starting transfers between devices: none -> 48.8 us  [the longest x4 28.4 us: send_sums(): sums_up[index] = lax.ppermute(up, 'seq', up_pairs)]
    ppermute x12 -> x4, waiting for transfers between devices: 40.8 us -> 4.95 us  [step_down(): return lax.ppermute(value, 'seq', pairs)]
    ppermute x12 -> x4, starting transfers between devices: 39.9 us -> 10.6 us  [step_up(): return lax.ppermute(value, 'seq', pairs)]
    ppermute x5, waiting for transfers between devices: 37 us -> 15.2 us  [turn(): return lax.ppermute(value, 'seq', pairs)]
    ppermute x0 -> x13, waiting for transfers between devices: none -> 16.2 us  [the longest x4 9.32 us: send_sums(): sums_down[index] = lax.ppermute(down, 'seq', down_pairs)]
  transfers between devices with their start and end apart: 34 -> 30, of which waited for: 15 -> 11; matrix products, arithmetic and copies ran while one was open for 24% -> 1% of each run, Pallas kernels for 3% -> 38%
where the time goes in v2:
time: 343 us; the launch traced here: 342 us
  Pallas kernels  132 us (38%)
  waiting for transfers between devices  100 us (29%)
  starting transfers between devices  78.2 us (23%)
  between operations  14.2 us (4%)
  local copies, waits for them, and re-layouts  11.6 us (3%)
  matrix products  4.04 us (1%)
    pallas_call x8, Pallas kernels, products(): pl.pallas_call(body, grid_spec=pltpu.PrefetchScalarGridSpec(num_scalar_pr...  53.3 us
    pallas_call x4, Pallas kernels, attend(): pl.pallas_call(attend_kernel, grid=(heads // pair,), in_specs=[pl.BlockSp...  45.5 us
    all_gather x1, waiting for transfers between devices, shards(): doc_states = lax.all_gather(doc_part, 'tp', axis=1, tiled=True)  31.9 us
    all_to_all x1, waiting for transfers between devices, route(): lax.all_to_all(sent, 'seq', split_axis=0, concat_axis=0, tiled=True)  31 us
    ppermute x4, starting transfers between devices, send_sums(): sums_up[index] = lax.ppermute(up, 'seq', up_pairs)  28.4 us
    ppermute x5, waiting for transfers between devices, turn(): return lax.ppermute(value, 'seq', pairs)  15.2 us
    pallas_call x4, Pallas kernels, add_arrivals(): pl.pallas_call(body, grid_spec=pltpu.PrefetchScalarGridSpec(num_scalar_pr...  14.3 us
    pallas_call x4, Pallas kernels, finish(): pl.pallas_call(body, grid_spec=pltpu.PrefetchScalarGridSpec(num_scalar_pr...  13.1 us
  transfers between devices with their start and end apart: 30, of which 11 were waited for; matrix products, arithmetic and copies ran while one was open for 1% of the time, Pallas kernels for 38%

profile of v2, /device:TPU:0, one launch (start us, length us, event | category | flops | bytes accessed | tf_op | source)
XLA Modules:
  0.0 341.7 jit_solution(10603034494143491572)
XLA Ops:
  8.4 1.9 convolution_convert_fusion
  10.3 7.4 %all-to-all-start = ((bf16[8,80,1024]{2,1,0:T(8,128)(2,1)}), bf16[8,80,1024]{2,1,0:T(8,128)(2,1)S(1)}, u32[]{:S(2)}, u32[]{:S(2)}) async-start(bf16[8,80,1024]{2,1,0:T(8,128)(2,1)} %bitcast.15), calls=%async_computation | async-start | bytes 2621440 | tf_op jit(solution)/shard_map/route/all_to_all | solution.py:231
  18.1 31.0 %all-to-all-done = bf16[8,80,1024]{2,1,0:T(8,128)(2,1)S(1)} async-done(((bf16[8,80,1024]{2,1,0:T(8,128)(2,1)}), bf16[8,80,1024]{2,1,0:T(8,128)(2,1)S(1)}, u32[]{:S(2)}, u32[]{:S(2)}) %all-to-all-start) | async-done | bytes 1310752 | tf_op jit(solution)/shard_map/route/all_to_all | solution.py:231
  49.1 2.0 convolution_convert_fusion.1
  51.1 2.0 collective-permute-start
  55.7 12.6 %collective-permute-done.1 = bf16[512,512]{1,0:T(8,128)(2,1)} collective-permute-done((bf16[512,512]{1,0:T(8,128)(2,1)S(1)}, bf16[512,512]{1,0:T(8,128)(2,1)}, u32[]{:S(2)}, u32[]{:S(2)}) %collective-permute-start.1) | collective-permute-done | bytes 524320 | tf_op jit(solution)/shard_map/side_states/ppermute | solution.py:272
  68.3 31.9 %all-gather.4.cloned.1.call-done.states_ref.refs_0_.refs_1_.refs_2_ = bf16[512,4096]{1,0:T(8,128)(2,1)} async-done(((bf16[512,1024]{1,0:T(8,128)(2,1)}), bf16[512,4096]{1,0:T(8,128)(2,1)}) %all-gather.4.cloned.1.call-update) | async-done | bytes 4194320 | tf_op jit(solution)/shard_map/gather_states/all_gather | solution.py:297
  103.6 2.2 copy-done.2
  105.8 10.8 %attend_0.1 = (bf16[256,512]{1,0:T(8,128)(2,1)S(1)}, bf16[512,1024]{1,0:T(8,128)(2,1)S(1)}) custom-call(s32[15]{0:T(128)S(1)} %stack.54.info_ref.scalar_ref, bf16[512,4096]{1,0:T(8,128)(2,1)S(1)} %copy-done.2, bf16[4096,2048]{1,0:T(8,128)(2,1)} %key_weight_ref.7, bf16[4096,2048]{1,0:T(8,128)(2,1)} %value_weight_ref.7, bf16[256,2048]{1,0:T(8,128)(2,1)S(1)} %copy-done.3, ...), custom_call_target="tpu_custom_call" | custom-call | bytes 524288 | tf_op jit(solution)/shard_map/attend_0/pallas_call | solution.py:62
  116.6 1.6 collective-permute-start.2
  119.7 10.8 %attend_2.1 = (bf16[256,512]{1,0:T(8,128)(2,1)S(1)}, bf16[512,1024]{1,0:T(8,128)(2,1)S(1)}) custom-call(s32[15]{0:T(128)S(1)} %stack.54.info_ref.scalar_ref, bf16[512,4096]{1,0:T(8,128)(2,1)S(1)} %copy-done.2, bf16[4096,2048]{1,0:T(8,128)(2,1)} %key_weight_ref.7, bf16[4096,2048]{1,0:T(8,128)(2,1)} %value_weight_ref.7, bf16[256,2048]{1,0:T(8,128)(2,1)S(1)} %copy-done.3, ...), custom_call_target="tpu_custom_call" | custom-call | bytes 1048576 | tf_op jit(solution)/shard_map/attend_2/pallas_call | solution.py:62
  130.5 1.6 collective-permute-start.4
  132.1 11.8 %attend_1.1 = (bf16[256,512]{1,0:T(8,128)(2,1)S(1)}, bf16[512,1024]{1,0:T(8,128)(2,1)}) custom-call(s32[15]{0:T(128)S(1)} %stack.54.info_ref.scalar_ref, bf16[512,4096]{1,0:T(8,128)(2,1)S(1)} %copy-done.2, bf16[4096,2048]{1,0:T(8,128)(2,1)} %key_weight_ref.7, bf16[4096,2048]{1,0:T(8,128)(2,1)} %value_weight_ref.7, bf16[256,2048]{1,0:T(8,128)(2,1)S(1)} %copy-done.3, ...), custom_call_target="tpu_custom_call" | custom-call | bytes 1572864 | tf_op jit(solution)/shard_map/attend_1/pallas_call | solution.py:62
  143.9 7.5 %collective-permute-start.8 = (bf16[512,1024]{1,0:T(8,128)(2,1)}, bf16[512,1024]{1,0:T(8,128)(2,1)}, u32[]{:S(2)}, u32[]{:S(2)}) collective-permute-start(bf16[512,1024]{1,0:T(8,128)(2,1)} %get-tuple-element.69.refs_2_), channel_id=1, source_target_pairs={{0,8},{4,12},{8,16},{12,20},{16,24},{20,28},{1,9},{5,13},{9,17},{1... | collective-permute-start | bytes 3145736 | tf_op jit(solution)/shard_map/rows_0_1/ppermute | solution.py:264
  152.7 12.2 %attend_3.1 = (bf16[256,512]{1,0:T(8,128)(2,1)S(1)}, bf16[512,1024]{1,0:T(8,128)(2,1)}) custom-call(s32[15]{0:T(128)S(1)} %stack.54.info_ref.scalar_ref, bf16[512,4096]{1,0:T(8,128)(2,1)S(1)} %copy-done.2, bf16[4096,2048]{1,0:T(8,128)(2,1)} %key_weight_ref.7, bf16[4096,2048]{1,0:T(8,128)(2,1)} %value_weight_ref.7, bf16[256,2048]{1,0:T(8,128)(2,1)S(1)} %copy-done.3, ...), custom_call_target="tpu_custom_call" | custom-call | bytes 2097152 | tf_op jit(solution)/shard_map/attend_3/pallas_call | solution.py:62
  166.1 4.5 %sums_1_0.1 = bf16[512,1024]{1,0:T(8,128)(2,1)} custom-call(s32[15]{0:T(128)} %copy-done.7, bf16[512,4096]{1,0:T(8,128)(2,1)} %all-gather.4.cloned.1.call-done.states_ref.refs_0_.refs_1_.refs_2_, bf16[512,1024]{1,0:T(8,128)(2,1)} %copy-done.5, bf16[2048,512]{1,0:T(8,128)(2,1)} %all-gather.6.cloned.1.call-done.refs_2_.refs_4_.refs_5_.refs_6_, ...), custom_call_target="tpu_custom_call" | custom-call | bytes 2621440 | tf_op jit(solution)/shard_map/sums_1_0/pallas_call | solution.py:113
  170.6 5.5 %collective-permute-start.6 = (bf16[512,1024]{1,0:T(8,128)(2,1)}, bf16[512,1024]{1,0:T(8,128)(2,1)}, u32[]{:S(2)}, u32[]{:S(2)}) collective-permute-start(bf16[512,1024]{1,0:T(8,128)(2,1)} %sums_1_0.1), channel_id=1, source_target_pairs={{0,8},{4,12},{24,16},{28,20},{1,9},{5,13},{25,17},{29,21},{2,10},{... | collective-permute-start | bytes 3145736 | tf_op jit(solution)/shard_map/sums_1_0/ppermute | solution.py:446
  176.1 1.7 collective-permute-done.9.refs_14_
  178.6 1.5 collective-permute-start.11
  180.1 7.4 %side_ahead_0.1 = (bf16[512,1024]{1,0:T(8,128)(2,1)}, bf16[512,1024]{1,0:T(8,128)(2,1)}, bf16[512,1024]{1,0:T(8,128)(2,1)}) custom-call(s32[15]{0:T(128)} %copy-done.7, bf16[512,4096]{1,0:T(8,128)(2,1)} %all-gather.4.cloned.1.call-done.states_ref.refs_0_.refs_1_.refs_2_, bf16[512,4096]{1,0:T(8,128)(2,1)} %all-gather.4.cloned.1.call-done.states_ref.refs_0_.refs_1_.refs_2_, ...), custom_call_target="tpu_custom_call" | custom-call | tf_op jit(solution)/shard_map/side_ahead_0/pallas_call | solution.py:113
  187.5 2.6 collective-permute-done.5.refs_3_.refs_7_
  191.1 4.5 %sums_1_1.1 = bf16[512,1024]{1,0:T(8,128)(2,1)} custom-call(s32[15]{0:T(128)} %copy-done.7, bf16[512,4096]{1,0:T(8,128)(2,1)} %all-gather.4.cloned.1.call-done.states_ref.refs_0_.refs_1_.refs_2_, bf16[512,1024]{1,0:T(8,128)(2,1)} %get-tuple-element.72.refs_1_.refs_3_, bf16[2048,512]{1,0:T(8,128)(2,1)} %all-gather.6.cloned.1.call-done.refs_2_.refs_4_.refs_5_.refs_6_, ...), custom_call_target="tpu_custom_call" | custom-call | bytes 3670016 | tf_op jit(solution)/shard_map/sums_1_1/pallas_call | solution.py:113
  195.6 5.3 %collective-permute-start.7 = (bf16[512,1024]{1,0:T(8,128)(2,1)}, bf16[512,1024]{1,0:T(8,128)(2,1)}, u32[]{:S(2)}, u32[]{:S(2)}) collective-permute-start(bf16[512,1024]{1,0:T(8,128)(2,1)} %sums_1_1.1), channel_id=1, source_target_pairs={{0,8},{4,12},{24,16},{28,20},{1,9},{5,13},{25,17},{29,21},{2,10},{... | collective-permute-start | bytes 3145736 | tf_op jit(solution)/shard_map/sums_1_1/ppermute | solution.py:446
  200.9 3.1 sums_2_0.1
  206.9 6.0 %collective-permute-start.14 = (bf16[512,1024]{1,0:T(8,128)(2,1)}, bf16[512,1024]{1,0:T(8,128)(2,1)}, u32[]{:S(2)}, u32[]{:S(2)}) collective-permute-start(bf16[512,1024]{1,0:T(8,128)(2,1)} %sums_2_0.1), channel_id=1, source_target_pairs={{0,8},{4,12},{8,16},{12,20},{1,9},{5,13},{9,17},{13,21},{2,10},{6,... | collective-permute-start | bytes 3145736 | tf_op jit(solution)/shard_map/sums_2_0/ppermute | solution.py:448
  213.0 1.6 collective-permute-start.15
  214.6 7.4 %side_ahead_1.1 = (bf16[512,1024]{1,0:T(8,128)(2,1)}, bf16[512,1024]{1,0:T(8,128)(2,1)}, bf16[512,1024]{1,0:T(8,128)(2,1)}) custom-call(s32[15]{0:T(128)} %copy-done.7, bf16[512,4096]{1,0:T(8,128)(2,1)} %all-gather.4.cloned.1.call-done.states_ref.refs_0_.refs_1_.refs_2_, bf16[512,4096]{1,0:T(8,128)(2,1)} %all-gather.4.cloned.1.call-done.states_ref.refs_0_.refs_1_.refs_2_, ...), custom_call_target="tpu_custom_call" | custom-call | tf_op jit(solution)/shard_map/side_ahead_1/pallas_call | solution.py:113
  222.0 1.7 collective-permute-done.7.refs_1_
  223.8 4.5 %side_own_1.1.refs_0_ = bf16[512,1024]{1,0:T(8,128)(2,1)} custom-call(s32[15]{0:T(128)} %copy-done.7, bf16[512,4096]{1,0:T(8,128)(2,1)} %all-gather.4.cloned.1.call-done.states_ref.refs_0_.refs_1_.refs_2_, bf16[512,1024]{1,0:T(8,128)(2,1)} %get-tuple-element.72.refs_1_.refs_3_, ...), custom_call_target="tpu_custom_call" | custom-call | bytes 5242880 | tf_op jit(solution)/shard_map/side_own_1/pallas_call | solution.py:113
  228.3 2.3 collective-permute-done.13.down_ref.refs_10_
  231.6 3.1 rows_2_0.1
  236.0 3.2 sums_2_1.1
  239.2 8.7 %collective-permute-start.17 = (bf16[512,1024]{1,0:T(8,128)(2,1)}, bf16[512,1024]{1,0:T(8,128)(2,1)}, u32[]{:S(2)}, u32[]{:S(2)}) collective-permute-start(bf16[512,1024]{1,0:T(8,128)(2,1)} %sums_2_1.1), channel_id=1, source_target_pairs={{0,8},{4,12},{8,16},{12,20},{1,9},{5,13},{9,17},{13,21},{2,10},{6,... | collective-permute-start | bytes 3145736 | tf_op jit(solution)/shard_map/sums_2_1/ppermute | solution.py:448
  248.6 4.5 %side_own_0.1.refs_0_ = bf16[512,1024]{1,0:T(8,128)(2,1)} custom-call(s32[15]{0:T(128)} %copy-done.7, bf16[512,4096]{1,0:T(8,128)(2,1)} %all-gather.4.cloned.1.call-done.states_ref.refs_0_.refs_1_.refs_2_, bf16[512,1024]{1,0:T(8,128)(2,1)} %copy-done.5, bf16[2048,512]{1,0:T(8,128)(2,1)} %all-gather.6.cloned.1.call-done.refs_2_.refs_4_.refs_5_.refs_6_, ...), custom_call_target="tpu_custom_call" | custom-call | bytes 6815744 | tf_op jit(solution)/shard_map/side_own_0/pallas_call | solution.py:113
  253.1 5.1 %collective-permute-done.16.refs_6_.refs_13_ = bf16[512,1024]{1,0:T(8,128)(2,1)S(1)} collective-permute-done((bf16[512,1024]{1,0:T(8,128)(2,1)}, bf16[512,1024]{1,0:T(8,128)(2,1)S(1)}, u32[]{:S(2)}, u32[]{:S(2)}) %collective-permute-start.16) | collective-permute-done | bytes 1048608 | tf_op jit(solution)/shard_map/rows_2_0/ppermute | solution.py:404
  258.3 3.1 rows_2_1.1
  262.6 4.0 %sums_3_0.1 = (bf16[512,1024]{1,0:T(8,128)(2,1)}, bf16[512,1024]{1,0:T(8,128)(2,1)}) custom-call(s32[15]{0:T(128)} %copy-done.7, bf16[512,1024]{1,0:T(8,128)(2,1)} %get-tuple-element.93.refs_0_, bf16[512,1024]{1,0:T(8,128)(2,1)} %get-tuple-element.76.refs_1_, bf16[512,1024]{1,0:T(8,128)(2,1)} %collective-permute-done.14.refs_2_, ...), custom_call_target="tpu_custom_call" | custom-call | bytes 7864320 | tf_op jit(solution)/shard_map/sums_3_0/pallas_call | solution.py:136
  266.6 8.2 %collective-permute-start.20 = (bf16[512,1024]{1,0:T(8,128)(2,1)}, bf16[512,1024]{1,0:T(8,128)(2,1)}, u32[]{:S(2)}, u32[]{:S(2)}) collective-permute-start(bf16[512,1024]{1,0:T(8,128)(2,1)} %get-tuple-element.104), channel_id=1, source_target_pairs={{0,8},{4,12},{8,16},{12,20},{16,24},{20,28},{1,9},{5,13},{9,17},{1... | collective-permute-start | bytes 3145736 | tf_op jit(solution)/shard_map/sums_3_0/ppermute | solution.py:448
  276.1 10.1 %even_0.1 = (bf16[512,1024]{1,0:T(8,128)(2,1)}, bf16[512,1024]{1,0:T(8,128)(2,1)}) custom-call(s32[15]{0:T(128)} %copy-done.7, bf16[2048,1024]{1,0:T(8,128)(2,1)} %all-gather.8.cloned.1.call-done.refs_0_.refs_1_.refs_3_.refs_4_.refs_7_.refs_8_.refs_11_.refs_12_, ...), custom_call_target="tpu_custom_call" | custom-call | bytes 8388608 | tf_op jit(solution)/shard_map/even_0/pallas_call | solution.py:113
  287.9 4.0 %sums_3_1.1 = (bf16[512,1024]{1,0:T(8,128)(2,1)}, bf16[512,1024]{1,0:T(8,128)(2,1)}) custom-call(s32[15]{0:T(128)} %copy-done.7, bf16[512,1024]{1,0:T(8,128)(2,1)} %get-tuple-element.99.refs_0_, bf16[512,1024]{1,0:T(8,128)(2,1)} %get-tuple-element.81.refs_1_, bf16[512,1024]{1,0:T(8,128)(2,1)} %collective-permute-done.17.refs_2_, bf16[512,1024]{1,0:T(8,128)(2,1)} %copy-done.23), custom_call_target="tpu_custom_call" | custom-call | bytes 8912896 | tf_op jit(solution)/shard_map/sums_3_1/pallas_call | solution.py:136
  292.0 5.5 %collective-permute-start.23 = (bf16[512,1024]{1,0:T(8,128)(2,1)}, bf16[512,1024]{1,0:T(8,128)(2,1)}, u32[]{:S(2)}, u32[]{:S(2)}) collective-permute-start(bf16[512,1024]{1,0:T(8,128)(2,1)} %get-tuple-element.111), channel_id=1, source_target_pairs={{0,8},{4,12},{8,16},{12,20},{16,24},{20,28},{1,9},{5,13},{9,17},{1... | collective-permute-start | bytes 3145736 | tf_op jit(solution)/shard_map/sums_3_1/ppermute | solution.py:448
  298.9 10.2 %even_1.1 = (bf16[512,1024]{1,0:T(8,128)(2,1)}, bf16[512,1024]{1,0:T(8,128)(2,1)}) custom-call(s32[15]{0:T(128)} %copy-done.7, bf16[2048,1024]{1,0:T(8,128)(2,1)} %all-gather.8.cloned.1.call-done.refs_0_.refs_1_.refs_3_.refs_4_.refs_7_.refs_8_.refs_11_.refs_12_, ...), custom_call_target="tpu_custom_call" | custom-call | bytes 9437184 | tf_op jit(solution)/shard_map/even_1/pallas_call | solution.py:113
  311.7 2.9 collective-permute-done.21.refs_2_
  314.7 3.4 %finish_2.1 = (bf16[512,2048]{1,0:T(8,128)(2,1)}, bf16[512,2048]{1,0:T(8,128)(2,1)}) custom-call(s32[15]{0:T(128)} %copy-done.7, bf16[512,1024]{1,0:T(8,128)(2,1)} %side_own_0.1.refs_0_, bf16[512,1024]{1,0:T(8,128)(2,1)} %collective-permute-done.20.refs_1_, bf16[512,1024]{1,0:T(8,128)(2,1)} %collective-permute-done.21.refs_2_), custom_call_target="tpu_custom_call" | custom-call | bytes 9961472 | tf_op jit(solution)/shard_map/finish_2/pallas_call | solution.py:186
  319.1 3.0 finish_0.1
  322.2 6.4 %collective-permute-done.24.refs_2_ = bf16[512,1024]{1,0:T(8,128)(2,1)} collective-permute-done((bf16[512,1024]{1,0:T(8,128)(2,1)}, bf16[512,1024]{1,0:T(8,128)(2,1)}, u32[]{:S(2)}, u32[]{:S(2)}) %collective-permute-start.24) | collective-permute-done | bytes 1048608 | tf_op jit(solution)/shard_map/sums_3_1/ppermute | solution.py:449
  328.5 3.4 %finish_3.1 = (bf16[512,2048]{1,0:T(8,128)(2,1)}, bf16[512,2048]{1,0:T(8,128)(2,1)}) custom-call(s32[15]{0:T(128)} %copy-done.7, bf16[512,1024]{1,0:T(8,128)(2,1)} %side_own_1.1.refs_0_, bf16[512,1024]{1,0:T(8,128)(2,1)} %collective-permute-done.23.refs_1_, ...), custom_call_target="tpu_custom_call", output_to_operand_aliasing={{0}: (4, {}), {1}: (5, {})} | custom-call | bytes 11010048 | tf_op jit(solution)/shard_map/finish_3/pallas_call | solution.py:186
  332.0 3.2 finish_1.1
  (109 shorter events, 28.4 us)
Async XLA Ops:
  10.3 38.8 %all-to-all-start = ((bf16[8,80,1024]{2,1,0:T(8,128)(2,1)}), bf16[8,80,1024]{2,1,0:T(8,128)(2,1)S(1)}, u32[]{:S(2)}, u32[]{:S(2)}) async-start(bf16[8,80,1024]{2,1,0:T(8,128)(2,1)} %bitcast.15), calls=%async_computation | async-start | bytes 2621440 | tf_op jit(solution)/shard_map/route/all_to_all | solution.py:231
  17.7 82.5 %all-gather.4.cloned.1.call-start = ((), (), s32[]{:S(2)}) async-start(), calls=%async_computation.1 | async-start | bytes 5242880 | tf_op jit(solution)/shard_map/gather_states/all_gather | solution.py:297
  51.0 50.0 %copy-start.26 = (s32[8]{0:T(128)S(1)}, s32[8]{0:T(128)}, u32[]{:S(2)}) copy-start(s32[8]{0:T(128)} %param.13) | copy-start | bytes 100
  51.0 50.6 %copy-start.27 = (s32[8]{0:T(128)S(1)}, s32[8]{0:T(128)}, u32[]{:S(2)}) copy-start(s32[8]{0:T(128)} %param.14) | copy-start | bytes 100
  51.0 52.5 %copy-start.3 = (bf16[256,2048]{1,0:T(8,128)(2,1)S(1)}, bf16[256,2048]{1,0:T(8,128)(2,1)}, u32[]{:S(2)}) copy-start(bf16[256,2048]{1,0:T(8,128)(2,1)} %query_ref.7) | copy-start | bytes 3145732
  51.1 52.5 %copy-start.4 = (bf16[256,2048]{1,0:T(8,128)(2,1)S(1)}, bf16[256,2048]{1,0:T(8,128)(2,1)}, u32[]{:S(2)}) copy-start(bf16[256,2048]{1,0:T(8,128)(2,1)} %grad_ref.7) | copy-start | bytes 3145732
  51.1 115.0 %all-gather.6.cloned.1.call-start = ((), (), s32[]{:S(2)}) async-start(), calls=%async_computation.2 | async-start | bytes 2621440 | tf_op jit(solution)/shard_map/side_states/all_gather | solution.py:302
  51.1 17.2 %collective-permute-start = (bf16[512,1024]{1,0:T(8,128)(2,1)}, bf16[512,1024]{1,0:T(8,128)(2,1)S(1)}, u32[]{:S(2)}, u32[]{:S(2)}) collective-permute-start(bf16[512,1024]{1,0:T(8,128)(2,1)} %convolution_convert_fusion.1), channel_id=1, source_target_pairs={{0,0},{1,10},{2,17},{3,27},{4,4},{5,14},{6,21},{7,31},{8,3},{9,8},... | collective-permute-start | bytes 3145736 | tf_op jit(solution)/shard_map/line_states/ppermute | solution.py:287
  54.2 14.1 %collective-permute-start.1 = (bf16[512,512]{1,0:T(8,128)(2,1)S(1)}, bf16[512,512]{1,0:T(8,128)(2,1)}, u32[]{:S(2)}, u32[]{:S(2)}) collective-permute-start(bf16[512,512]{1,0:T(8,128)(2,1)S(1)} %constant_dynamic-slice_fusion), channel_id=1, source_target_pairs={{0,4},{4,0},{8,12},{12,8},{16,20},{20,16},{24,28},{28,24},{1,5},{5... | collective-permute-start | bytes 1572872 | tf_op jit(solution)/shard_map/side_states/ppermute | solution.py:272
  68.3 32.0 %copy-start.24 = (bf16[512,1024]{1,0:T(8,128)(2,1)}, bf16[512,1024]{1,0:T(8,128)(2,1)S(1)}, u32[]{:S(2)}) copy-start(bf16[512,1024]{1,0:T(8,128)(2,1)S(1)} %collective-permute-done) | copy-start | bytes 3145732
  100.3 175.9 %all-gather.8.cloned.1.call-start = ((), (), s32[]{:S(2)}) async-start(), calls=%async_computation.3 | async-start | bytes 5242880 | tf_op jit(solution)/shard_map/line_states/all_gather | solution.py:319
  105.8 46.9 %copy-start.7 = (s32[15]{0:T(128)}, s32[15]{0:T(128)S(1)}, u32[]{:S(2)}) copy-start(s32[15]{0:T(128)S(1)} %stack.54.info_ref.scalar_ref) | copy-start | bytes 184
  116.5 14.0 %copy-start.6 = (bf16[512,1024]{1,0:T(8,128)(2,1)}, bf16[512,1024]{1,0:T(8,128)(2,1)S(1)}, u32[]{:S(2)}) copy-start(bf16[512,1024]{1,0:T(8,128)(2,1)S(1)} %get-tuple-element.63.refs_2_) | copy-start | bytes 3145732
  116.6 36.1 %collective-permute-start.2 = (bf16[512,1024]{1,0:T(8,128)(2,1)S(1)}, bf16[512,1024]{1,0:T(8,128)(2,1)S(1)}, u32[]{:S(2)}, u32[]{:S(2)}) collective-permute-start(bf16[512,1024]{1,0:T(8,128)(2,1)S(1)} %get-tuple-element.63.refs_2_), channel_id=1, source_target_pairs={{0,8},{4,12},{8,16},{12,20},{16,24},{20,28},{1,9},{5,13},{9,17},{1... | collective-permute-start | bytes 3145736 | tf_op jit(solution)/shard_map/rows_0_0/ppermute | solution.py:264
  118.2 34.5 %collective-permute-start.3 = (bf16[512,1024]{1,0:T(8,128)(2,1)S(1)}, bf16[512,1024]{1,0:T(8,128)(2,1)S(1)}, u32[]{:S(2)}, u32[]{:S(2)}) collective-permute-start(bf16[512,1024]{1,0:T(8,128)(2,1)S(1)} %get-tuple-element.63.refs_2_), channel_id=1, source_target_pairs={{8,0},{12,4},{16,8},{20,12},{24,16},{28,20},{9,1},{13,5},{17,9},{2... | collective-permute-start | bytes 3145736 | tf_op jit(solution)/shard_map/rows_0_0/ppermute | solution.py:268
  130.5 13.4 %copy-start.5 = (bf16[512,1024]{1,0:T(8,128)(2,1)}, bf16[512,1024]{1,0:T(8,128)(2,1)S(1)}, u32[]{:S(2)}) copy-start(bf16[512,1024]{1,0:T(8,128)(2,1)S(1)} %get-tuple-element.65.refs_1_.refs_3_) | copy-start | bytes 3145732
  130.5 13.4 %copy-start.8 = (bf16[256,512]{1,0:T(8,128)(2,1)}, bf16[256,512]{1,0:T(8,128)(2,1)S(1)}, u32[]{:S(2)}) copy-start(bf16[256,512]{1,0:T(8,128)(2,1)S(1)} %get-tuple-element.68) | copy-start | bytes 786436
  130.5 35.5 %collective-permute-start.4 = (bf16[512,1024]{1,0:T(8,128)(2,1)S(1)}, bf16[512,1024]{1,0:T(8,128)(2,1)}, u32[]{:S(2)}, u32[]{:S(2)}) collective-permute-start(bf16[512,1024]{1,0:T(8,128)(2,1)S(1)} %get-tuple-element.65.refs_1_.refs_3_), channel_id=1, source_target_pairs={{0,4},{4,0},{8,12},{12,8},{16,20},{20,16},{24,28},{28,24},{1,5},{5... | collective-permute-start | bytes 3145736 | tf_op jit(solution)/shard_map/side_rows_0/ppermute | solution.py:272
  143.9 21.0 %copy-start.10 = (bf16[256,512]{1,0:T(8,128)(2,1)}, bf16[256,512]{1,0:T(8,128)(2,1)S(1)}, u32[]{:S(2)}) copy-start(bf16[256,512]{1,0:T(8,128)(2,1)S(1)} %get-tuple-element.67) | copy-start | bytes 786436
  143.9 32.2 %collective-permute-start.8 = (bf16[512,1024]{1,0:T(8,128)(2,1)}, bf16[512,1024]{1,0:T(8,128)(2,1)}, u32[]{:S(2)}, u32[]{:S(2)}) collective-permute-start(bf16[512,1024]{1,0:T(8,128)(2,1)} %get-tuple-element.69.refs_2_), channel_id=1, source_target_pairs={{0,8},{4,12},{8,16},{12,20},{16,24},{20,28},{1,9},{5,13},{9,17},{1... | collective-permute-start | bytes 3145736 | tf_op jit(solution)/shard_map/rows_0_1/ppermute | solution.py:264
  151.4 26.5 %collective-permute-start.9 = (bf16[512,1024]{1,0:T(8,128)(2,1)}, bf16[512,1024]{1,0:T(8,128)(2,1)}, u32[]{:S(2)}, u32[]{:S(2)}) collective-permute-start(bf16[512,1024]{1,0:T(8,128)(2,1)} %get-tuple-element.69.refs_2_), channel_id=1, source_target_pairs={{8,0},{12,4},{16,8},{20,12},{24,16},{28,20},{9,1},{13,5},{17,9},{2... | collective-permute-start | bytes 3145736 | tf_op jit(solution)/shard_map/rows_0_1/ppermute | solution.py:268
  152.7 25.2 %copy-start.20 = (bf16[512,1024]{1,0:T(8,128)(2,1)}, bf16[512,1024]{1,0:T(8,128)(2,1)S(1)}, u32[]{:S(2)}) copy-start(bf16[512,1024]{1,0:T(8,128)(2,1)S(1)} %collective-permute-done.2.refs_5_) | copy-start | bytes 3145732
  152.7 12.2 %copy-start.21 = (bf16[512,1024]{1,0:T(8,128)(2,1)}, bf16[512,1024]{1,0:T(8,128)(2,1)S(1)}, u32[]{:S(2)}) copy-start(bf16[512,1024]{1,0:T(8,128)(2,1)S(1)} %collective-permute-done.3.refs_14_) | copy-start | bytes 3145732
  165.6 24.5 %collective-permute-start.5 = (bf16[512,1024]{1,0:T(8,128)(2,1)}, bf16[512,1024]{1,0:T(8,128)(2,1)S(1)}, u32[]{:S(2)}, u32[]{:S(2)}) collective-permute-start(bf16[512,1024]{1,0:T(8,128)(2,1)} %get-tuple-element.72.refs_1_.refs_3_), channel_id=1, source_target_pairs={{0,4},{4,0},{8,12},{12,8},{16,20},{20,16},{24,28},{28,24},{1,5},{5... | collective-permute-start | bytes 3145736 | tf_op jit(solution)/shard_map/side_rows_1/ppermute | solution.py:272
  170.6 30.2 %collective-permute-start.6 = (bf16[512,1024]{1,0:T(8,128)(2,1)}, bf16[512,1024]{1,0:T(8,128)(2,1)}, u32[]{:S(2)}, u32[]{:S(2)}) collective-permute-start(bf16[512,1024]{1,0:T(8,128)(2,1)} %sums_1_0.1), channel_id=1, source_target_pairs={{0,8},{4,12},{24,16},{28,20},{1,9},{5,13},{25,17},{29,21},{2,10},{... | collective-permute-start | bytes 3145736 | tf_op jit(solution)/shard_map/sums_1_0/ppermute | solution.py:446
  177.8 26.2 %collective-permute-start.10 = (bf16[512,1024]{1,0:T(8,128)(2,1)S(1)}, bf16[512,1024]{1,0:T(8,128)(2,1)S(1)}, u32[]{:S(2)}, u32[]{:S(2)}) collective-permute-start(bf16[512,1024]{1,0:T(8,128)(2,1)S(1)} %collective-permute-done.2.refs_5_), channel_id=1, source_target_pairs={{8,16},{12,20},{16,24},{20,28},{9,17},{13,21},{17,25},{21,29},{10,... | collective-permute-start | bytes 3145736 | tf_op jit(solution)/shard_map/rows_1_0/ppermute | solution.py:264
  178.6 26.4 %collective-permute-start.11 = (bf16[512,1024]{1,0:T(8,128)(2,1)}, bf16[512,1024]{1,0:T(8,128)(2,1)}, u32[]{:S(2)}, u32[]{:S(2)}) collective-permute-start(bf16[512,1024]{1,0:T(8,128)(2,1)} %copy-done.21), channel_id=1, source_target_pairs={{8,0},{12,4},{16,8},{20,12},{9,1},{13,5},{17,9},{21,13},{10,2},{14... | collective-permute-start | bytes 3145736 | tf_op jit(solution)/shard_map/rows_1_0/ppermute | solution.py:268
  195.6 28.2 %collective-permute-start.7 = (bf16[512,1024]{1,0:T(8,128)(2,1)}, bf16[512,1024]{1,0:T(8,128)(2,1)}, u32[]{:S(2)}, u32[]{:S(2)}) collective-permute-start(bf16[512,1024]{1,0:T(8,128)(2,1)} %sums_1_1.1), channel_id=1, source_target_pairs={{0,8},{4,12},{24,16},{28,20},{1,9},{5,13},{25,17},{29,21},{2,10},{... | collective-permute-start | bytes 3145736 | tf_op jit(solution)/shard_map/sums_1_1/ppermute | solution.py:446
  204.0 18.0 %copy-start.19 = (bf16[512,1024]{1,0:T(8,128)(2,1)}, bf16[512,1024]{1,0:T(8,128)(2,1)S(1)}, u32[]{:S(2)}) copy-start(bf16[512,1024]{1,0:T(8,128)(2,1)S(1)} %collective-permute-done.10.up_ref.refs_9_) | copy-start | bytes 3145732
  204.9 23.4 %collective-permute-start.12 = (bf16[512,1024]{1,0:T(8,128)(2,1)}, bf16[512,1024]{1,0:T(8,128)(2,1)S(1)}, u32[]{:S(2)}, u32[]{:S(2)}) collective-permute-start(bf16[512,1024]{1,0:T(8,128)(2,1)} %collective-permute-done.8.refs_5_), channel_id=1, source_target_pairs={{8,16},{12,20},{16,24},{20,28},{9,17},{13,21},{17,25},{21,29},{10,... | collective-permute-start | bytes 3145736 | tf_op jit(solution)/shard_map/rows_1_1/ppermute | solution.py:264
  205.6 25.0 %collective-permute-start.13 = (bf16[512,1024]{1,0:T(8,128)(2,1)}, bf16[512,1024]{1,0:T(8,128)(2,1)S(1)}, u32[]{:S(2)}, u32[]{:S(2)}) collective-permute-start(bf16[512,1024]{1,0:T(8,128)(2,1)} %collective-permute-done.9.refs_14_), channel_id=1, source_target_pairs={{8,0},{12,4},{16,8},{20,12},{9,1},{13,5},{17,9},{21,13},{10,2},{14... | collective-permute-start | bytes 3145736 | tf_op jit(solution)/shard_map/rows_1_1/ppermute | solution.py:268
  206.9 41.6 %collective-permute-start.14 = (bf16[512,1024]{1,0:T(8,128)(2,1)}, bf16[512,1024]{1,0:T(8,128)(2,1)}, u32[]{:S(2)}, u32[]{:S(2)}) collective-permute-start(bf16[512,1024]{1,0:T(8,128)(2,1)} %sums_2_0.1), channel_id=1, source_target_pairs={{0,8},{4,12},{8,16},{12,20},{1,9},{5,13},{9,17},{13,21},{2,10},{6,... | collective-permute-start | bytes 3145736 | tf_op jit(solution)/shard_map/sums_2_0/ppermute | solution.py:448
  213.0 35.6 %collective-permute-start.15 = (bf16[512,1024]{1,0:T(8,128)(2,1)}, bf16[512,1024]{1,0:T(8,128)(2,1)}, u32[]{:S(2)}, u32[]{:S(2)}) collective-permute-start(bf16[512,1024]{1,0:T(8,128)(2,1)} %sums_2_0.1), channel_id=1, source_target_pairs={{16,8},{20,12},{24,16},{28,20},{17,9},{21,13},{25,17},{29,21},{18,... | collective-permute-start | bytes 3145736 | tf_op jit(solution)/shard_map/sums_2_0/ppermute | solution.py:449
  228.3 10.8 %copy-start.17 = (bf16[512,1024]{1,0:T(8,128)(2,1)}, bf16[512,1024]{1,0:T(8,128)(2,1)S(1)}, u32[]{:S(2)}) copy-start(bf16[512,1024]{1,0:T(8,128)(2,1)S(1)} %collective-permute-done.12.up_ref.refs_9_) | copy-start | bytes 3145732
  234.7 23.6 %collective-permute-start.16 = (bf16[512,1024]{1,0:T(8,128)(2,1)}, bf16[512,1024]{1,0:T(8,128)(2,1)S(1)}, u32[]{:S(2)}, u32[]{:S(2)}) collective-permute-start(bf16[512,1024]{1,0:T(8,128)(2,1)} %rows_2_0.1), channel_id=1, source_target_pairs={{16,24},{20,28},{8,0},{12,4},{17,25},{21,29},{9,1},{13,5},{18,26},... | collective-permute-start | bytes 3145736 | tf_op jit(solution)/shard_map/rows_2_0/ppermute | solution.py:404
  239.2 47.1 %collective-permute-start.17 = (bf16[512,1024]{1,0:T(8,128)(2,1)}, bf16[512,1024]{1,0:T(8,128)(2,1)}, u32[]{:S(2)}, u32[]{:S(2)}) collective-permute-start(bf16[512,1024]{1,0:T(8,128)(2,1)} %sums_2_1.1), channel_id=1, source_target_pairs={{0,8},{4,12},{8,16},{12,20},{1,9},{5,13},{9,17},{13,21},{2,10},{6,... | collective-permute-start | bytes 3145736 | tf_op jit(solution)/shard_map/sums_2_1/ppermute | solution.py:448
  247.8 39.1 %collective-permute-start.18 = (bf16[512,1024]{1,0:T(8,128)(2,1)}, bf16[512,1024]{1,0:T(8,128)(2,1)S(1)}, u32[]{:S(2)}, u32[]{:S(2)}) collective-permute-start(bf16[512,1024]{1,0:T(8,128)(2,1)} %sums_2_1.1), channel_id=1, source_target_pairs={{16,8},{20,12},{24,16},{28,20},{17,9},{21,13},{25,17},{29,21},{18,... | collective-permute-start | bytes 3145736 | tf_op jit(solution)/shard_map/sums_2_1/ppermute | solution.py:449
  258.2 8.4 %copy-start.16 = (bf16[512,1024]{1,0:T(8,128)(2,1)}, bf16[512,1024]{1,0:T(8,128)(2,1)S(1)}, u32[]{:S(2)}) copy-start(bf16[512,1024]{1,0:T(8,128)(2,1)S(1)} %collective-permute-done.16.refs_6_.refs_13_) | copy-start | bytes 3145732
  261.3 36.2 %collective-permute-start.19 = (bf16[512,1024]{1,0:T(8,128)(2,1)}, bf16[512,1024]{1,0:T(8,128)(2,1)S(1)}, u32[]{:S(2)}, u32[]{:S(2)}) collective-permute-start(bf16[512,1024]{1,0:T(8,128)(2,1)} %rows_2_1.1), channel_id=1, source_target_pairs={{16,24},{20,28},{8,0},{12,4},{17,25},{21,29},{9,1},{13,5},{18,26},... | collective-permute-start | bytes 3145736 | tf_op jit(solution)/shard_map/rows_2_1/ppermute | solution.py:404
  266.6 42.6 %collective-permute-start.20 = (bf16[512,1024]{1,0:T(8,128)(2,1)}, bf16[512,1024]{1,0:T(8,128)(2,1)}, u32[]{:S(2)}, u32[]{:S(2)}) collective-permute-start(bf16[512,1024]{1,0:T(8,128)(2,1)} %get-tuple-element.104), channel_id=1, source_target_pairs={{0,8},{4,12},{8,16},{12,20},{16,24},{20,28},{1,9},{5,13},{9,17},{1... | collective-permute-start | bytes 3145736 | tf_op jit(solution)/shard_map/sums_3_0/ppermute | solution.py:448
  274.8 39.9 %collective-permute-start.21 = (bf16[512,1024]{1,0:T(8,128)(2,1)}, bf16[512,1024]{1,0:T(8,128)(2,1)}, u32[]{:S(2)}, u32[]{:S(2)}) collective-permute-start(bf16[512,1024]{1,0:T(8,128)(2,1)} %get-tuple-element.94), channel_id=1, source_target_pairs={{8,0},{12,4},{16,8},{20,12},{24,16},{28,20},{9,1},{13,5},{17,9},{2... | collective-permute-start | bytes 3145736 | tf_op jit(solution)/shard_map/sums_3_0/ppermute | solution.py:449
  286.2 31.9 %collective-permute-start.22 = (bf16[512,1024]{1,0:T(8,128)(2,1)}, bf16[512,1024]{1,0:T(8,128)(2,1)S(1)}, u32[]{:S(2)}, u32[]{:S(2)}) collective-permute-start(bf16[512,1024]{1,0:T(8,128)(2,1)} %get-tuple-element.107), channel_id=1, source_target_pairs={{0,4},{4,0},{8,12},{12,8},{16,20},{20,16},{24,28},{28,24},{1,5},{5... | collective-permute-start | bytes 3145736 | tf_op jit(solution)/shard_map/even_0/ppermute | solution.py:272
  292.0 30.2 %collective-permute-start.23 = (bf16[512,1024]{1,0:T(8,128)(2,1)}, bf16[512,1024]{1,0:T(8,128)(2,1)}, u32[]{:S(2)}, u32[]{:S(2)}) collective-permute-start(bf16[512,1024]{1,0:T(8,128)(2,1)} %get-tuple-element.111), channel_id=1, source_target_pairs={{0,8},{4,12},{8,16},{12,20},{16,24},{20,28},{1,9},{5,13},{9,17},{1... | collective-permute-start | bytes 3145736 | tf_op jit(solution)/shard_map/sums_3_1/ppermute | solution.py:448
  297.5 13.1 %copy-start.9 = (bf16[256,512]{1,0:T(8,128)(2,1)S(1)}, bf16[256,512]{1,0:T(8,128)(2,1)}, u32[]{:S(2)}) copy-start(bf16[256,512]{1,0:T(8,128)(2,1)} %copy-done.8) | copy-start | bytes 786436
  297.5 13.1 %copy-start.11 = (bf16[256,512]{1,0:T(8,128)(2,1)S(1)}, bf16[256,512]{1,0:T(8,128)(2,1)}, u32[]{:S(2)}) copy-start(bf16[256,512]{1,0:T(8,128)(2,1)} %copy-done.10) | copy-start | bytes 786436
  297.5 13.1 %copy-start.13 = (bf16[256,512]{1,0:T(8,128)(2,1)S(1)}, bf16[256,512]{1,0:T(8,128)(2,1)}, u32[]{:S(2)}) copy-start(bf16[256,512]{1,0:T(8,128)(2,1)} %copy-done.12) | copy-start | bytes 786436
  297.5 31.0 %collective-permute-start.24 = (bf16[512,1024]{1,0:T(8,128)(2,1)}, bf16[512,1024]{1,0:T(8,128)(2,1)}, u32[]{:S(2)}, u32[]{:S(2)}) collective-permute-start(bf16[512,1024]{1,0:T(8,128)(2,1)} %get-tuple-element.100), channel_id=1, source_target_pairs={{8,0},{12,4},{16,8},{20,12},{24,16},{28,20},{9,1},{13,5},{17,9},{2... | collective-permute-start | bytes 3145736 | tf_op jit(solution)/shard_map/sums_3_1/ppermute | solution.py:449
  309.2 22.8 %collective-permute-start.25 = (bf16[512,1024]{1,0:T(8,128)(2,1)}, bf16[512,1024]{1,0:T(8,128)(2,1)}, u32[]{:S(2)}, u32[]{:S(2)}) collective-permute-start(bf16[512,1024]{1,0:T(8,128)(2,1)} %get-tuple-element.115), channel_id=1, source_target_pairs={{0,4},{4,0},{8,12},{12,8},{16,20},{20,16},{24,28},{28,24},{1,5},{5... | collective-permute-start | bytes 3145736 | tf_op jit(solution)/shard_map/even_1/ppermute | solution.py:272
  (10 other events, 20.2 us)
Sparse Core Ops, SparseCore 0:
  51.2 48.9 all-gather.3
  101.8 23.5 all-gather.5
  127.5 34.4 all-gather.7

commit v3 on v2

--- a/solution.py
+++ b/solution.py
@@ -7,6 +7,7 @@
 
 HEAD_DIM = 128
 VMEM_LIMIT = 60 * 1024 * 1024
+SMALL_LIMIT = 16 * 1024 * 1024
 
 
 def cost(rank):
@@ -15,18 +16,26 @@
 WIDE = jnp.float32
 
 
-def attend_kernel(
-    info_ref, states_ref, key_weight_ref, value_weight_ref, query_ref, grad_ref, query_grad_ref, rows_grad_ref
-):
+def attend_kernel(pieces, info_ref, *refs):
+    states_refs, key_refs, value_refs = refs[:pieces], refs[pieces : 2 * pieces], refs[2 * pieces : 3 * pieces]
+    query_ref, grad_ref, query_grad_ref, rows_grad_ref = refs[3 * pieces :]
     length = info_ref[0]
     offset = info_ref[1]
     scale = HEAD_DIM ** (-0.5)
     across = (((1,), (1,)), ((), ()))
     down = (((0,), (0,)), ((), ()))
     query_count, block = query_ref.shape
-    state_count = states_ref.shape[0]
-    key_rows = jnp.dot(states_ref[...], key_weight_ref[...], preferred_element_type=WIDE).astype(LOW)
-    value_rows = jnp.dot(states_ref[...], value_weight_ref[...], preferred_element_type=WIDE).astype(LOW)
+    state_count = states_refs[0].shape[0]
+
+    def project(weight_refs):
+        total = None
+        for states_ref, weight_ref in zip(states_refs, weight_refs):
+            weight = weight_ref[...].reshape(-1, block)
+            product = jnp.dot(states_ref[...], weight, preferred_element_type=WIDE)
+            total = product if total is None else total + product
+        return total.astype(LOW)
+
+    key_rows, value_rows = project(key_refs), project(value_refs)
     position = lax.broadcasted_iota(jnp.int32, (query_count, state_count), 1)
     limit = jnp.minimum(
         lax.broadcasted_iota(jnp.int32, (query_count, 1), 0) + (offset + 1), length
@@ -55,18 +64,29 @@
 
 def attend(rank, info, doc_states, key_weight, value_weight, queries, grads, first, heads):
     query_count = queries.shape[0]
-    state_count, feature_count = doc_states.shape
+    pieces = len(doc_states)
+    state_count, feature_count = doc_states[0].shape
+    part_count, _, part_features, _ = key_weight.shape
     pair = 2 if heads % 2 == 0 and first % 2 == 0 else 1
     block = pair * HEAD_DIM
     width = heads * HEAD_DIM
+    weight_specs = [
+        pl.BlockSpec(
+            (part_count, 1, part_features, block), lambda h, piece=piece: (0, piece, 0, first // pair + h)
+        )
+        for piece in range(pieces)
+    ]
+    states_spec = pl.BlockSpec(
+        (state_count, feature_count), lambda h: (0, 0), pipeline_mode=pl.Buffered(1)
+    )
     return pl.pallas_call(
-        attend_kernel,
+        lambda *refs: attend_kernel(pieces, *refs),
         grid=(heads // pair,),
         in_specs=[
             pl.BlockSpec(memory_space=pltpu.SMEM),
-            pl.BlockSpec((state_count, feature_count), lambda h: (0, 0), pipeline_mode=pl.Buffered(1)),
-            pl.BlockSpec((feature_count, block), lambda h: (0, first // pair + h)),
-            pl.BlockSpec((feature_count, block), lambda h: (0, first // pair + h)),
+            *[states_spec] * pieces,
+            *weight_specs,
+            *weight_specs,
             pl.BlockSpec((query_count, block), lambda h: (0, first // pair + h)),
             pl.BlockSpec((query_count, block), lambda h: (0, first // pair + h)),
         ],
@@ -80,7 +100,7 @@
         ],
         compiler_params=pltpu.CompilerParams(vmem_limit_bytes=40 * 1024 * 1024),
         cost_estimate=cost(rank),
-    )(info, doc_states, key_weight, value_weight, queries, grads)
+    )(info, *doc_states, *[key_weight] * pieces, *[value_weight] * pieces, queries, grads)
 
 
 def products(rank, scalars, z_slot, count, terms, rows, slice_width, block):
@@ -142,7 +162,7 @@
             out_specs=[flat] * count,
         ),
         out_shape=[jax.ShapeDtypeStruct((slice_width, columns), LOW)] * count,
-        compiler_params=pltpu.CompilerParams(vmem_limit_bytes=VMEM_LIMIT),
+        compiler_params=pltpu.CompilerParams(vmem_limit_bytes=SMALL_LIMIT),
         cost_estimate=cost(rank),
     )(scalars, *bases, *arrivals)
 
@@ -160,7 +180,7 @@
             num_scalar_prefetch=1, grid=(columns // block,), in_specs=[spec] * 2, out_specs=spec
         ),
         out_shape=jax.ShapeDtypeStruct(up.shape, LOW),
-        compiler_params=pltpu.CompilerParams(vmem_limit_bytes=VMEM_LIMIT),
+        compiler_params=pltpu.CompilerParams(vmem_limit_bytes=SMALL_LIMIT),
         cost_estimate=cost(rank),
     )(scalars, up, down)
 
@@ -193,7 +213,7 @@
         ),
         out_shape=[jax.ShapeDtypeStruct(shape, LOW)] * 2,
         input_output_aliases=aliases,
-        compiler_params=pltpu.CompilerParams(vmem_limit_bytes=VMEM_LIMIT),
+        compiler_params=pltpu.CompilerParams(vmem_limit_bytes=SMALL_LIMIT),
         cost_estimate=cost(rank),
     )(scalars, *arrays)
 
@@ -205,7 +225,7 @@
     return seq_count // minor, minor
 
 
-def route(states, state_doc, state_pos):
+def route(states, state_doc, state_pos, pieces, table):
     seq_count = lax.axis_size("seq")
     device = lax.axis_index("seq")
     row_count = states.shape[0]
@@ -227,15 +247,20 @@
     targets = own_docs * capacity + own_ranks
     slots = jnp.arange(seq_count * capacity, dtype=jnp.int32)
     send_hot = (targets[None, :] == slots[:, None]).astype(LOW)
-    sent = jnp.dot(send_hot, states, preferred_element_type=WIDE).astype(LOW)
-    arrived = lax.all_to_all(sent, "seq", split_axis=0, concat_axis=0, tiled=True)
+    piece_width = states.shape[1] // pieces
+    arrived = []
+    for piece in range(pieces):
+        columns = states[:, piece * piece_width : (piece + 1) * piece_width]
+        sent = jnp.dot(send_hot, columns, preferred_element_type=WIDE).astype(LOW)
+        arrived.append(lax.all_to_all(sent, "seq", split_axis=0, concat_axis=0, tiled=True))
     arrival = jnp.where(mine, ranks[seq_count:], capacity)
     hit = arrival[:, None, :] == jnp.arange(capacity, dtype=jnp.int32)[None, :, None]
     slot_position = jnp.max(jnp.where(hit, positions_all[:, None, :], -1), axis=2).reshape(-1)
     place_hot = (
         slot_position[None, :] == jnp.arange(row_count, dtype=jnp.int32)[:, None]
     ).astype(LOW)
-    return jnp.dot(place_hot, arrived, preferred_element_type=WIDE).astype(LOW)
+    arrived[0], table = lax.optimization_barrier((arrived[0], table))
+    return [jnp.dot(place_hot, piece, preferred_element_type=WIDE).astype(LOW) for piece in arrived], table
 
 
 def shards(
@@ -271,20 +296,65 @@
         pairs = [(at(i, j), at(i, (j + shift) % minor)) for i in range(major) for j in range(minor)]
         return lax.ppermute(value, "seq", pairs)
 
+    pieces = seq_count // tp_count
+    if minor % pieces or pieces > 2:
+        pieces = 1
+    def nearest(distance):
+        return jnp.where(z + distance < major, z + distance, jnp.maximum(z - distance, 0))
+
+    def dests_from(step):
+        found = []
+        for distance in range(major - step, 0, -1):
+            if 2 * distance >= major:
+                found.append(nearest(distance))
+            else:
+                found += [jnp.minimum(z + distance, major - 1), jnp.maximum(z - distance, 0)]
+        return found + [z]
+
+    first_dests, later_dests = [nearest(major - 1)], dests_from(2)
+    side_dests = [(x + shift) % minor for shift in range(1, minor)] + [x]
+    table = [
+        lax.dynamic_index_in_dim(lengths, device, 0, keepdims=False),
+        lax.dynamic_index_in_dim(offsets, device, 0, keepdims=False),
+        z,
+    ]
+    z_slot = 2
+    first_slot = len(table)
+    table += [at(dest, x) // pieces for dest in first_dests] + first_dests
+    later_slot = len(table)
+    table += [at(dest, x) // pieces for dest in later_dests] + later_dests
+    side_slot = len(table)
+    table += side_dests
+    table = jnp.stack([jnp.asarray(value, jnp.int32) for value in table])
+
     with jax.named_scope("route"):
-        doc_part = route(states, state_doc, state_pos)
-
-    with jax.named_scope("line_states"):
-        ratio = tp_count // major
-        slots = [i for i in range(0, major, 2)] + [i for i in range(1, major, 2)]
-        pairs = []
-        for i in range(major):
-            for j in range(minor):
-                for t in range(tp_count):
-                    to = t // ratio
-                    slot = slots.index((to - i) % major) * ratio + t % ratio
-                    pairs.append((at(i, j) * tp_count + t, at(to, j) * tp_count + slot))
-        moved = lax.ppermute(doc_part, ("seq", "tp"), pairs)
+        doc_pieces, table = route(states, state_doc, state_pos, pieces, table)
+        doc_part = jnp.concatenate(doc_pieces, axis=1) if pieces > 1 else doc_pieces[0]
+
+    ratio = tp_count // major
+    slots = list(range(1, major, 2)) + list(range(2, major, 2)) + [0]
+    piece_rows = row_count // ratio
+    distance = jnp.asarray(slots, jnp.int32)[part // ratio]
+
+    def send_line(states_of, piece):
+        with jax.named_scope(f"line_states_{piece}"):
+            rows = lax.dynamic_slice_in_dim(states_of, part % ratio * piece_rows, piece_rows, 0)
+            found = [
+                lax.dynamic_slice_in_dim(
+                    rows, at((z + distance) % major, j) // pieces * slice_width, slice_width, 1
+                )
+                for j in range(piece, minor, pieces)
+            ]
+            rows = jnp.concatenate(found, axis=1) if len(found) > 1 else found[0]
+            pairs = []
+            for i in range(major):
+                for j in range(minor):
+                    for t in range(tp_count):
+                        if slots[t // ratio]:
+                            to = at((i + slots[t // ratio]) % major, j)
+                            pairs.append((at(i, j) * tp_count + t, to * tp_count + t))
+            return rows, lax.ppermute(rows, ("seq", "tp"), pairs)
+
     side_parts = []
     if ratio == 1:
         with jax.named_scope("side_states"):
@@ -294,61 +364,49 @@
                 )
                 side_parts.append(turn(wanted, shift))
     with jax.named_scope("gather_states"):
-        doc_states = lax.all_gather(doc_part, "tp", axis=1, tiled=True)
-    doc_states, moved, *side_parts = lax.optimization_barrier((doc_states, moved, *side_parts))
+        doc_states = [lax.all_gather(piece, "tp", axis=1, tiled=True) for piece in doc_pieces]
+    found = [send_line(doc_states[piece], piece) for piece in range(pieces - 1)]
+    joined = lax.optimization_barrier((*doc_states, *[got for _, got in found], *side_parts))
+    doc_states, side_parts = list(joined[:pieces]), joined[2 * pieces - 1 :]
+    found = [(rows, got) for (rows, _), got in zip(found, joined[pieces : 2 * pieces - 1])]
+    found.append(send_line(doc_states[-1], pieces - 1))
+
+    def gather_line(after):
+        with jax.named_scope("line_states"):
+            arrived = lax.optimization_barrier((*[got for _, got in found], after))[:-1]
+            pieces_found = [jnp.where(distance == 0, rows, got) for (rows, _), got in zip(found, arrived)]
+            if 1 < pieces < minor:
+                rows = [rows.reshape(piece_rows, minor // pieces, 1, slice_width) for rows in pieces_found]
+                rows = jnp.concatenate(rows, axis=2).reshape(piece_rows, minor * slice_width)
+            else:
+                rows = jnp.concatenate(pieces_found, axis=1)
+            return lax.all_gather(rows, "tp", axis=0, tiled=True)
+
+    def piece_of(minor_index):
+        if pieces == 1:
+            return doc_states[0]
+        return jnp.where(minor_index % 2 == 1, doc_states[1], doc_states[0])
+
     with jax.named_scope("side_states"):
         if ratio == 1:
             side_states = [
                 lax.all_gather(piece, "tp", axis=0, tiled=True) for piece in side_parts
             ]
         else:
-            own_rows = lax.dynamic_slice_in_dim(doc_states, part * quarter, quarter, 0)
             side_states = []
             for shift in range(1, minor):
+                own_rows = lax.dynamic_slice_in_dim(piece_of(x + shift), part * quarter, quarter, 0)
                 wanted = jnp.concatenate(
                     [
                         lax.dynamic_slice_in_dim(
-                            own_rows, at(i, (x + shift) % minor) * slice_width, slice_width, 1
+                            own_rows, at(i, (x + shift) % minor) // pieces * slice_width, slice_width, 1
                         )
                         for i in range(major)
                     ],
                     axis=1,
                 )
                 side_states.append(lax.all_gather(turn(wanted, shift), "tp", axis=0, tiled=True))
-    with jax.named_scope("line_states"):
-        line_states = lax.all_gather(moved, "tp", axis=0, tiled=True)
-        if ratio > 1:
-            line_states = line_states.reshape(major, ratio, row_count, -1).transpose(0, 2, 1, 3)
-        line_states = line_states.reshape(major * row_count, minor * slice_width)
-
-    def nearest(distance):
-        return jnp.where(z + distance < major, z + distance, jnp.maximum(z - distance, 0))
-
-    def dests_from(step):
-        found = []
-        for distance in range(major - step, 0, -1):
-            if 2 * distance >= major:
-                found.append(nearest(distance))
-            else:
-                found += [jnp.minimum(z + distance, major - 1), jnp.maximum(z - distance, 0)]
-        return found + [z]
-
-    first_dests, later_dests = [nearest(major - 1)], dests_from(2)
-    side_dests = [(x + shift) % minor for shift in range(1, minor)] + [x]
-    table = [
-        lax.dynamic_index_in_dim(lengths, device, 0, keepdims=False),
-        lax.dynamic_index_in_dim(offsets, device, 0, keepdims=False),
-        z,
-    ]
-    z_slot = 2
-    first_slot = len(table)
-    table += [at(dest, x) for dest in first_dests] + first_dests
-    later_slot = len(table)
-    table += [at(dest, x) for dest in later_dests] + later_dests
-    side_slot = len(table)
-    table += side_dests
-    table = jnp.stack([jnp.asarray(value, jnp.int32) for value in table])
-
+        own_states = piece_of(x)
     latest, pending, rank = None, [], 0
 
     def scalars():
@@ -359,6 +417,8 @@
         pending.clear()
         return lax.optimization_barrier((table, *others))[0]
 
+    weight_shape = (tp_count, pieces, feature_count // (tp_count * pieces), key_weight.shape[1])
+    key_parts, value_parts = key_weight.reshape(weight_shape), value_weight.reshape(weight_shape)
     query_grads = [None] * group_count
 
     def attend_group(group):
@@ -366,7 +426,7 @@
         with jax.named_scope(f"attend_{group}"):
             info = scalars()
             query_grads[group], latest = attend(
-                rank, info, doc_states, key_weight, value_weight, queries, context_grad,
+                rank, info, doc_states, key_parts, value_parts, queries, context_grad,
                 group * heads, heads,
             )
             return latest
@@ -411,7 +471,7 @@
 
     def side_products(index, slot, total, skip, count, free=False):
         nonlocal latest
-        terms = [(doc_states, lambda k, s: (0, s[slot + skip + k]), [(odd_rows[index][0], 0)], None)]
+        terms = [(own_states, lambda k, s: (0, s[slot + skip + k]), [(odd_rows[index][0], 0)], None)]
         for states_of, rows_of in zip(side_states, odd_rows[index][1:]):
             if ratio == 1:
                 place = lambda k, s: (s[slot + total + skip + k], 0)
@@ -489,6 +549,7 @@
 
     even[0] = attend_group(0)
     send_first(0)
+    line_states = gather_line(latest)
     odd[0] = attend_group(2)
     send_odd(0)
     even[1] = attend_group(1)

time: 343 us -> 334 us (0.974)
  waiting for transfers between devices: 100 us -> 53.5 us
  blocking collectives: 0 us -> 21.4 us
  Pallas kernels: 132 us -> 123 us
  local copies, waits for them, and re-layouts: 11.6 us -> 20.4 us
  other arithmetic: 1.42 us -> 9.97 us
  starting transfers between devices: 78.2 us -> 82.3 us
    all_gather x2 -> x3, waiting for transfers between devices: 31.9 us -> 7.27 us  [the longest x2 7.25 us: shards(): lax.all_gather(piece, 'tp', axis=1, tiled=True)]
    all_to_all x0 -> x1, blocking collectives: none -> 21.4 us  [route(): lax.all_to_all(sent, 'seq', split_axis=0, concat_axis=0, tiled=True)]
    all_to_all x1, waiting for transfers between devices: 31 us -> 14.2 us  [route(): lax.all_to_all(sent, 'seq', split_axis=0, concat_axis=0, tiled=True)]
    unnamed x56 -> x82, local copies, waits for them, and re-layouts: 7.05 us -> 12.5 us
    pallas_call x4, Pallas kernels: 13.1 us -> 8.43 us  [finish(): pl.pallas_call(body, grid_spec=pltpu.PrefetchScalarGridSpec(num_scalar_pr...]
    select_n x0 -> x3, other arithmetic: none -> 4.35 us  [the longest x2 2.74 us: gather_line(): jnp.where(distance == 0, rows, got)]
    ppermute x1 -> x2, starting transfers between devices: 2.02 us -> 6.19 us  [send_line(): return (rows, lax.ppermute(rows, ('seq', 'tp'), pairs))]
    ppermute x5, waiting for transfers between devices: 15.2 us -> 11.4 us  [turn(): return lax.ppermute(value, 'seq', pairs)]
  transfers between devices with their start and end apart: 30 -> 32, of which waited for: 11 -> 10; matrix products, arithmetic and copies ran while one was open for 1% -> 6% of each run, Pallas kernels for 38% -> 36%
where the time goes in v3:
time: 334 us; the launch traced here: 332 us
  Pallas kernels  123 us (37%)
  starting transfers between devices  82.3 us (25%)
  waiting for transfers between devices  53.5 us (16%)
  blocking collectives  21.4 us (6%)
  local copies, waits for them, and re-layouts  20.4 us (6%)
  between operations  15.8 us (5%)
  other arithmetic  9.97 us (3%)
  matrix products  5.85 us (2%)
    pallas_call x8, Pallas kernels, products(): pl.pallas_call(body, grid_spec=pltpu.PrefetchScalarGridSpec(num_scalar_pr...  53.3 us
    pallas_call x4, Pallas kernels, attend(): pl.pallas_call(lambda *refs: attend_kernel(pieces, *refs), grid=(heads //...  46.3 us
    ppermute x4, starting transfers between devices, send_sums(): sums_up[index] = lax.ppermute(up, 'seq', up_pairs)  27.8 us
    all_to_all x1, blocking collectives, route(): lax.all_to_all(sent, 'seq', split_axis=0, concat_axis=0, tiled=True)  21.4 us
    all_to_all x1, waiting for transfers between devices, route(): lax.all_to_all(sent, 'seq', split_axis=0, concat_axis=0, tiled=True)  14.2 us
    unnamed x82, local copies, waits for them, and re-layouts  12.5 us
    ppermute x4, waiting for transfers between devices, send_sums(): sums_down[index] = lax.ppermute(down, 'seq', down_pairs)  12.1 us
    ppermute x4, starting transfers between devices, step_up(): return lax.ppermute(value, 'seq', pairs)  11.6 us
  transfers between devices with their start and end apart: 32, of which 10 were waited for; matrix products, arithmetic and copies ran while one was open for 6% of the time, Pallas kernels for 36%

profile of v3, /device:TPU:0, one launch (start us, length us, event | category | flops | bytes accessed | tf_op | source)
XLA Modules:
  0.0 332.2 jit_solution(18320761784317753853)
XLA Ops:
  8.2 2.4 convolution_convert_fusion.1
  10.6 7.4 %all-to-all-start = ((bf16[8,80,512]{2,1,0:T(8,128)(2,1)}), bf16[8,80,512]{2,1,0:T(8,128)(2,1)S(1)}, u32[]{:S(2)}, u32[]{:S(2)}) async-start(bf16[8,80,512]{2,1,0:T(8,128)(2,1)} %bitcast.3), calls=%async_computation | async-start | bytes 1310720 | tf_op jit(solution)/shard_map/route/all_to_all | solution.py:255
  21.1 14.2 %all-to-all-done = bf16[8,80,512]{2,1,0:T(8,128)(2,1)S(1)} async-done(((bf16[8,80,512]{2,1,0:T(8,128)(2,1)}), bf16[8,80,512]{2,1,0:T(8,128)(2,1)S(1)}, u32[]{:S(2)}, u32[]{:S(2)}) %all-to-all-start) | async-done | bytes 655392 | tf_op jit(solution)/shard_map/route/all_to_all | solution.py:255
  37.3 21.4 %all_to_all.24 = bf16[8,80,512]{2,1,0:T(8,128)(2,1)S(1)} all-to-all(bf16[8,80,512]{2,1,0:T(8,128)(2,1)S(1)} %bitcast.42), channel_id=1, replica_groups=mesh['seq'=8,'tp'=4] {'seq'}, dimensions={0} | all-to-all | bytes 1310720 | tf_op jit(solution)/shard_map/route/all_to_all | solution.py:255
  61.5 2.1 fusion.8
  63.6 2.0 constant_dynamic-slice_fusion
  65.6 2.8 collective-permute-start
  68.5 7.6 %collective-permute-done.1 = bf16[512,512]{1,0:T(8,128)(2,1)} collective-permute-done((bf16[512,512]{1,0:T(8,128)(2,1)}, bf16[512,512]{1,0:T(8,128)(2,1)}, u32[]{:S(2)}, u32[]{:S(2)}) %collective-permute-start.1) | collective-permute-done | bytes 524320 | tf_op jit(solution)/shard_map/side_states/ppermute | solution.py:297
  76.0 7.2 %all-gather.7.cloned.1.call-done.refs_2_ = bf16[512,2048]{1,0:T(8,128)(2,1)} async-done(((bf16[512,512]{1,0:T(8,128)(2,1)}), bf16[512,2048]{1,0:T(8,128)(2,1)}) %all-gather.7.cloned.1.call-update) | async-done | bytes 2097168 | tf_op jit(solution)/shard_map/gather_states/all_gather | solution.py:367
  83.4 1.9 constant_dynamic-slice_fusion.1
  85.2 3.4 %collective-permute-start.17 = (bf16[512,512]{1,0:T(8,128)(2,1)}, bf16[512,512]{1,0:T(8,128)(2,1)}, u32[]{:S(2)}, u32[]{:S(2)}) collective-permute-start(bf16[512,512]{1,0:T(8,128)(2,1)} %constant_dynamic-slice_fusion.1), channel_id=1, source_target_pairs={{0,8},{1,25},{2,18},{4,12},{5,29},{6,22},{8,16},{9,1},{10,26},{12,... | collective-permute-start | bytes 1572872 | tf_op jit(solution)/shard_map/line_states_1/ppermute | solution.py:356
  92.2 11.0 %attend_0.1 = (bf16[256,512]{1,0:T(8,128)(2,1)S(1)}, bf16[512,1024]{1,0:T(8,128)(2,1)S(1)}) custom-call(s32[15]{0:T(128)S(1)} %stack.54.refs_0_.scalar_ref, bf16[512,2048]{1,0:T(8,128)(2,1)S(1)} %copy-done, bf16[512,2048]{1,0:T(8,128)(2,1)S(1)} %copy-done.1, bf16[4,2,512,2048]{3,2,1,0:T(8,128)(2,1)} %bitcast.24, bf16[4,2,512,2048]{3,2,1,0:T(8,128)(2,1)} %bitcast.25, ...), custom_call_target="tpu_custom_call" | custom-call | bytes 524288 | tf_op jit(solution)/shard_map/attend_0/pallas_call | solution.py:82
  107.3 4.4 %collective-permute-start.2 = (bf16[512,1024]{1,0:T(8,128)(2,1)}, bf16[512,1024]{1,0:T(8,128)(2,1)}, u32[]{:S(2)}, u32[]{:S(2)}) collective-permute-start(bf16[512,1024]{1,0:T(8,128)(2,1)} %copy-done.15), channel_id=1, source_target_pairs={{0,8},{4,12},{8,16},{12,20},{16,24},{20,28},{1,9},{5,13},{9,17},{1... | collective-permute-start | bytes 3145736 | tf_op jit(solution)/shard_map/rows_0_0/ppermute | solution.py:289
  116.1 12.2 %attend_2.1 = (bf16[256,512]{1,0:T(8,128)(2,1)S(1)}, bf16[512,1024]{1,0:T(8,128)(2,1)}) custom-call(s32[15]{0:T(128)S(1)} %stack.54.refs_0_.scalar_ref, bf16[512,2048]{1,0:T(8,128)(2,1)S(1)} %copy-done, bf16[512,2048]{1,0:T(8,128)(2,1)S(1)} %copy-done.2, bf16[4,2,512,2048]{3,2,1,0:T(8,128)(2,1)} %bitcast.26, bf16[4,2,512,2048]{3,2,1,0:T(8,128)(2,1)} %bitcast.27, ...), custom_call_target="tpu_custom_call" | custom-call | bytes 1048576 | tf_op jit(solution)/shard_map/attend_2/pallas_call | solution.py:82
  130.3 11.6 %attend_1.1 = (bf16[256,512]{1,0:T(8,128)(2,1)S(1)}, bf16[512,1024]{1,0:T(8,128)(2,1)}) custom-call(s32[15]{0:T(128)S(1)} %stack.54.refs_0_.scalar_ref, bf16[512,2048]{1,0:T(8,128)(2,1)S(1)} %copy-done, bf16[512,2048]{1,0:T(8,128)(2,1)S(1)} %copy-done.2, bf16[4,2,512,2048]{3,2,1,0:T(8,128)(2,1)} %bitcast.28, bf16[4,2,512,2048]{3,2,1,0:T(8,128)(2,1)} %bitcast.29, ...), custom_call_target="tpu_custom_call" | custom-call | bytes 1572864 | tf_op jit(solution)/shard_map/attend_1/pallas_call | solution.py:82
  142.6 5.7 %collective-permute-start.8 = (bf16[512,1024]{1,0:T(8,128)(2,1)}, bf16[512,1024]{1,0:T(8,128)(2,1)}, u32[]{:S(2)}, u32[]{:S(2)}) collective-permute-start(bf16[512,1024]{1,0:T(8,128)(2,1)} %get-tuple-element.77.refs_2_), channel_id=1, source_target_pairs={{0,8},{4,12},{8,16},{12,20},{16,24},{20,28},{1,9},{5,13},{9,17},{1... | collective-permute-start | bytes 3145736 | tf_op jit(solution)/shard_map/rows_0_1/ppermute | solution.py:289
  152.3 11.5 %attend_3.1 = (bf16[256,512]{1,0:T(8,128)(2,1)S(1)}, bf16[512,1024]{1,0:T(8,128)(2,1)}) custom-call(s32[15]{0:T(128)S(1)} %stack.54.refs_0_.scalar_ref, bf16[512,2048]{1,0:T(8,128)(2,1)S(1)} %copy-done, bf16[512,2048]{1,0:T(8,128)(2,1)S(1)} %copy-done.3, bf16[4,2,512,2048]{3,2,1,0:T(8,128)(2,1)} %bitcast.30, bf16[4,2,512,2048]{3,2,1,0:T(8,128)(2,1)} %bitcast.31, ...), custom_call_target="tpu_custom_call" | custom-call | bytes 2097152 | tf_op jit(solution)/shard_map/attend_3/pallas_call | solution.py:82
  165.9 4.5 %sums_1_0.1 = bf16[512,1024]{1,0:T(8,128)(2,1)} custom-call(s32[15]{0:T(128)} %copy-done.24, bf16[512,2048]{1,0:T(8,128)(2,1)} %broadcast_select_fusion.refs_0_.refs_1_.refs_2_, bf16[512,1024]{1,0:T(8,128)(2,1)} %get-tuple-element.73.refs_1_.refs_3_, bf16[2048,512]{1,0:T(8,128)(2,1)} %all-gather.9.cloned.1.call-done.refs_2_.refs_4_.refs_5_.refs_6_, ...), custom_call_target="tpu_custom_call" | custom-call | bytes 2621440 | tf_op jit(solution)/shard_map/sums_1_0/pallas_call | solution.py:133
  170.4 4.6 %collective-permute-start.6 = (bf16[512,1024]{1,0:T(8,128)(2,1)}, bf16[512,1024]{1,0:T(8,128)(2,1)S(1)}, u32[]{:S(2)}, u32[]{:S(2)}) collective-permute-start(bf16[512,1024]{1,0:T(8,128)(2,1)} %sums_1_0.1), channel_id=1, source_target_pairs={{0,8},{4,12},{24,16},{28,20},{1,9},{5,13},{25,17},{29,21},{2,10},{... | collective-permute-start | bytes 3145736 | tf_op jit(solution)/shard_map/sums_1_0/ppermute | solution.py:506
  177.3 7.4 %side_ahead_0.1 = (bf16[512,1024]{1,0:T(8,128)(2,1)}, bf16[512,1024]{1,0:T(8,128)(2,1)}, bf16[512,1024]{1,0:T(8,128)(2,1)}) custom-call(s32[15]{0:T(128)} %copy-done.24, bf16[512,2048]{1,0:T(8,128)(2,1)} %broadcast_select_fusion.refs_0_.refs_1_.refs_2_, bf16[512,2048]{1,0:T(8,128)(2,1)} %broadcast_select_fusion.refs_0_.refs_1_.refs_2_, ...), custom_call_target="tpu_custom_call" | custom-call | tf_op jit(solution)/shard_map/side_ahead_0/pallas_call | solution.py:133
  184.7 3.8 %collective-permute-done.5.refs_3_.refs_7_ = bf16[512,1024]{1,0:T(8,128)(2,1)} collective-permute-done((bf16[512,1024]{1,0:T(8,128)(2,1)}, bf16[512,1024]{1,0:T(8,128)(2,1)}, u32[]{:S(2)}, u32[]{:S(2)}) %collective-permute-start.5) | collective-permute-done | bytes 1048608 | tf_op jit(solution)/shard_map/side_rows_1/ppermute | solution.py:297
  188.5 4.6 %sums_1_1.1 = bf16[512,1024]{1,0:T(8,128)(2,1)} custom-call(s32[15]{0:T(128)} %copy-done.24, bf16[512,2048]{1,0:T(8,128)(2,1)} %broadcast_select_fusion.refs_0_.refs_1_.refs_2_, bf16[512,1024]{1,0:T(8,128)(2,1)} %get-tuple-element.80.refs_1_.refs_3_, bf16[2048,512]{1,0:T(8,128)(2,1)} %all-gather.9.cloned.1.call-done.refs_2_.refs_4_.refs_5_.refs_6_, ...), custom_call_target="tpu_custom_call" | custom-call | bytes 3670016 | tf_op jit(solution)/shard_map/sums_1_1/pallas_call | solution.py:133
  193.1 5.3 %collective-permute-start.7 = (bf16[512,1024]{1,0:T(8,128)(2,1)}, bf16[512,1024]{1,0:T(8,128)(2,1)}, u32[]{:S(2)}, u32[]{:S(2)}) collective-permute-start(bf16[512,1024]{1,0:T(8,128)(2,1)} %sums_1_1.1), channel_id=1, source_target_pairs={{0,8},{4,12},{24,16},{28,20},{1,9},{5,13},{25,17},{29,21},{2,10},{... | collective-permute-start | bytes 3145736 | tf_op jit(solution)/shard_map/sums_1_1/ppermute | solution.py:506
  199.6 1.9 sums_2_0.1
  204.5 5.5 %collective-permute-start.14 = (bf16[512,1024]{1,0:T(8,128)(2,1)}, bf16[512,1024]{1,0:T(8,128)(2,1)}, u32[]{:S(2)}, u32[]{:S(2)}) collective-permute-start(bf16[512,1024]{1,0:T(8,128)(2,1)} %sums_2_0.1), channel_id=1, source_target_pairs={{0,8},{4,12},{8,16},{12,20},{1,9},{5,13},{9,17},{13,21},{2,10},{6,... | collective-permute-start | bytes 3145736 | tf_op jit(solution)/shard_map/sums_2_0/ppermute | solution.py:508
  211.7 7.4 %side_ahead_1.1 = (bf16[512,1024]{1,0:T(8,128)(2,1)}, bf16[512,1024]{1,0:T(8,128)(2,1)}, bf16[512,1024]{1,0:T(8,128)(2,1)}) custom-call(s32[15]{0:T(128)} %copy-done.24, bf16[512,2048]{1,0:T(8,128)(2,1)} %broadcast_select_fusion.refs_0_.refs_1_.refs_2_, bf16[512,2048]{1,0:T(8,128)(2,1)} %broadcast_select_fusion.refs_0_.refs_1_.refs_2_, ...), custom_call_target="tpu_custom_call" | custom-call | tf_op jit(solution)/shard_map/side_ahead_1/pallas_call | solution.py:133
  219.1 2.2 collective-permute-done.7.refs_1_
  221.3 4.7 %side_own_1.1.refs_0_ = bf16[512,1024]{1,0:T(8,128)(2,1)} custom-call(s32[15]{0:T(128)} %copy-done.24, bf16[512,2048]{1,0:T(8,128)(2,1)} %broadcast_select_fusion.refs_0_.refs_1_.refs_2_, bf16[512,1024]{1,0:T(8,128)(2,1)} %get-tuple-element.80.refs_1_.refs_3_, bf16[2048,512]{1,0:T(8,128)(2,1)} %all-gather.9.cloned.1.call-done.refs_2_.refs_4_.refs_5_.refs_6_, ...), custom_call_target="tpu_custom_call" | custom-call | bytes 5242880 | tf_op jit(solution)/shard_map/side_own_1/pallas_call | solution.py:133
  228.8 1.8 rows_2_0.1
  231.9 2.8 sums_2_1.1
  234.7 8.7 %collective-permute-start.18 = (bf16[512,1024]{1,0:T(8,128)(2,1)}, bf16[512,1024]{1,0:T(8,128)(2,1)}, u32[]{:S(2)}, u32[]{:S(2)}) collective-permute-start(bf16[512,1024]{1,0:T(8,128)(2,1)} %sums_2_1.1), channel_id=1, source_target_pairs={{0,8},{4,12},{8,16},{12,20},{1,9},{5,13},{9,17},{13,21},{2,10},{6,... | collective-permute-start | bytes 3145736 | tf_op jit(solution)/shard_map/sums_2_1/ppermute | solution.py:508
  245.0 4.5 %side_own_0.1.refs_0_ = bf16[512,1024]{1,0:T(8,128)(2,1)} custom-call(s32[15]{0:T(128)} %copy-done.24, bf16[512,2048]{1,0:T(8,128)(2,1)} %broadcast_select_fusion.refs_0_.refs_1_.refs_2_, bf16[512,1024]{1,0:T(8,128)(2,1)} %get-tuple-element.73.refs_1_.refs_3_, bf16[2048,512]{1,0:T(8,128)(2,1)} %all-gather.9.cloned.1.call-done.refs_2_.refs_4_.refs_5_.refs_6_, ...), custom_call_target="tpu_custom_call" | custom-call | bytes 6815744 | tf_op jit(solution)/shard_map/side_own_0/pallas_call | solution.py:133
  249.5 4.6 %collective-permute-done.16.refs_6_.refs_13_ = bf16[512,1024]{1,0:T(8,128)(2,1)} collective-permute-done((bf16[512,1024]{1,0:T(8,128)(2,1)}, bf16[512,1024]{1,0:T(8,128)(2,1)}, u32[]{:S(2)}, u32[]{:S(2)}) %collective-permute-start.16) | collective-permute-done | bytes 1048608 | tf_op jit(solution)/shard_map/rows_2_0/ppermute | solution.py:464
  254.2 1.7 rows_2_1.1
  257.2 3.3 sums_3_0.1
  260.5 9.0 %collective-permute-start.21 = (bf16[512,1024]{1,0:T(8,128)(2,1)}, bf16[512,1024]{1,0:T(8,128)(2,1)}, u32[]{:S(2)}, u32[]{:S(2)}) collective-permute-start(bf16[512,1024]{1,0:T(8,128)(2,1)} %get-tuple-element.114), channel_id=1, source_target_pairs={{0,8},{4,12},{8,16},{12,20},{16,24},{20,28},{1,9},{5,13},{9,17},{1... | collective-permute-start | bytes 3145736 | tf_op jit(solution)/shard_map/sums_3_0/ppermute | solution.py:508
  271.0 10.1 %even_0.1 = (bf16[512,1024]{1,0:T(8,128)(2,1)}, bf16[512,1024]{1,0:T(8,128)(2,1)}) custom-call(s32[15]{0:T(128)} %copy-done.24, bf16[2048,1024]{1,0:T(8,128)(2,1)} %all-gather.11.cloned.1.call-done.refs_0_.refs_1_.refs_3_.refs_4_.refs_7_.refs_8_.refs_11_.refs_12_, ...), custom_call_target="tpu_custom_call" | custom-call | bytes 8388608 | tf_op jit(solution)/shard_map/even_0/pallas_call | solution.py:133
  281.6 3.4 %sums_3_1.1 = (bf16[512,1024]{1,0:T(8,128)(2,1)}, bf16[512,1024]{1,0:T(8,128)(2,1)}) custom-call(s32[15]{0:T(128)S(1)} %copy-done.28, bf16[512,1024]{1,0:T(8,128)(2,1)S(1)} %copy-done.16, bf16[512,1024]{1,0:T(8,128)(2,1)S(1)} %copy-done.17, bf16[512,1024]{1,0:T(8,128)(2,1)} %collective-permute-done.18.refs_2_, bf16[512,1024]{1,0:T(8,128)(2,1)} %collective-permute-done.19.refs_3_), custom_call_target="tpu_custom_call" | custom-call | bytes 8912896 | tf_op jit(solution)/shard_map/sums_3_1/pallas_call | solution.py:156
  285.0 4.6 %collective-permute-start.24 = (bf16[512,1024]{1,0:T(8,128)(2,1)}, bf16[512,1024]{1,0:T(8,128)(2,1)S(1)}, u32[]{:S(2)}, u32[]{:S(2)}) collective-permute-start(bf16[512,1024]{1,0:T(8,128)(2,1)} %get-tuple-element.121), channel_id=1, source_target_pairs={{0,8},{4,12},{8,16},{12,20},{16,24},{20,28},{1,9},{5,13},{9,17},{1... | collective-permute-start | bytes 3145736 | tf_op jit(solution)/shard_map/sums_3_1/ppermute | solution.py:508
  289.6 1.7 collective-permute-start.25
  291.3 10.1 %even_1.1 = (bf16[512,1024]{1,0:T(8,128)(2,1)}, bf16[512,1024]{1,0:T(8,128)(2,1)}) custom-call(s32[15]{0:T(128)} %copy-done.24, bf16[2048,1024]{1,0:T(8,128)(2,1)} %all-gather.11.cloned.1.call-done.refs_0_.refs_1_.refs_3_.refs_4_.refs_7_.refs_8_.refs_11_.refs_12_, ...), custom_call_target="tpu_custom_call" | custom-call | bytes 9437184 | tf_op jit(solution)/shard_map/even_1/pallas_call | solution.py:133
  303.1 2.0 pad_maximum_fusion
  305.1 4.1 %collective-permute-done.22.refs_2_ = bf16[512,1024]{1,0:T(8,128)(2,1)} collective-permute-done((bf16[512,1024]{1,0:T(8,128)(2,1)}, bf16[512,1024]{1,0:T(8,128)(2,1)}, u32[]{:S(2)}, u32[]{:S(2)}) %collective-permute-start.22) | collective-permute-done | bytes 1048608 | tf_op jit(solution)/shard_map/sums_3_0/ppermute | solution.py:509
  309.3 3.0 finish_2.1
  312.3 1.7 finish_0.1
  314.1 8.0 %collective-permute-done.25.refs_2_ = bf16[512,1024]{1,0:T(8,128)(2,1)S(1)} collective-permute-done((bf16[512,1024]{1,0:T(8,128)(2,1)}, bf16[512,1024]{1,0:T(8,128)(2,1)S(1)}, u32[]{:S(2)}, u32[]{:S(2)}) %collective-permute-start.25) | collective-permute-done | bytes 1048608 | tf_op jit(solution)/shard_map/sums_3_1/ppermute | solution.py:509
  322.0 1.9 finish_3.1
  323.9 1.7 finish_1.1
  (150 shorter events, 46.8 us)
Async XLA Ops:
  7.2 12.2 %copy-start.36 = (s32[4096]{0:T(1024)S(1)}, s32[4096]{0:T(1024)}, u32[]{:S(2)}) copy-start(s32[4096]{0:T(1024)} %param.13) | copy-start | bytes 49156
  10.6 26.1 %copy-start.37 = (bf16[512,1024]{1,0:T(8,128)(2,1)S(1)}, bf16[512,1024]{1,0:T(8,128)(2,1)}, u32[]{:S(2)}) copy-start(bf16[512,1024]{1,0:T(8,128)(2,1)} %param.11) | copy-start | bytes 3145732
  10.6 24.7 %all-to-all-start = ((bf16[8,80,512]{2,1,0:T(8,128)(2,1)}), bf16[8,80,512]{2,1,0:T(8,128)(2,1)S(1)}, u32[]{:S(2)}, u32[]{:S(2)}) async-start(bf16[8,80,512]{2,1,0:T(8,128)(2,1)} %bitcast.3), calls=%async_computation | async-start | bytes 1310720 | tf_op jit(solution)/shard_map/route/all_to_all | solution.py:255
  18.0 45.6 %all-gather.5.cloned.1.call-start = ((), (), s32[]{:S(2)}) async-start(), calls=%async_computation.2 | async-start | bytes 2621440 | tf_op jit(solution)/shard_map/gather_states/all_gather | solution.py:367
  21.1 130.2 %copy-start.24 = (s32[15]{0:T(128)}, s32[15]{0:T(128)S(1)}, u32[]{:S(2)}) copy-start(s32[15]{0:T(128)S(1)} %stack.54.refs_0_.scalar_ref) | copy-start | bytes 184
  36.7 46.6 %all-gather.7.cloned.1.call-start = ((), (), s32[]{:S(2)}) async-start(), calls=%async_computation.3 | async-start | bytes 2621440 | tf_op jit(solution)/shard_map/gather_states/all_gather | solution.py:367
  37.3 22.9 %copy-start.40 = (s32[4]{0:T(128)S(1)}, s32[4]{0:T(128)}, u32[]{:S(2)}) copy-start(s32[4]{0:T(128)} %constant.152.clone) | copy-start | bytes 52
  37.3 24.2 %copy-start.35 = (bf16[512,512]{1,0:T(8,128)(2,1)S(1)}, bf16[512,512]{1,0:T(8,128)(2,1)}, u32[]{:S(2)}) copy-start(bf16[512,512]{1,0:T(8,128)(2,1)} %fusion.2) | copy-start | bytes 1572868
  60.1 105.8 %all-gather.9.cloned.1.call-start = ((), (), s32[]{:S(2)}) async-start(), calls=%async_computation.4 | async-start | bytes 2621440 | tf_op jit(solution)/shard_map/side_states/all_gather | solution.py:393
  61.5 27.8 %copy-start.4 = (bf16[256,2048]{1,0:T(8,128)(2,1)S(1)}, bf16[256,2048]{1,0:T(8,128)(2,1)}, u32[]{:S(2)}) copy-start(bf16[256,2048]{1,0:T(8,128)(2,1)} %refs_7_.7) | copy-start | bytes 3145732
  63.6 12.4 %collective-permute-start.1 = (bf16[512,512]{1,0:T(8,128)(2,1)}, bf16[512,512]{1,0:T(8,128)(2,1)}, u32[]{:S(2)}, u32[]{:S(2)}) collective-permute-start(bf16[512,512]{1,0:T(8,128)(2,1)} %fusion.8), channel_id=1, source_target_pairs={{0,4},{4,0},{8,12},{12,8},{16,20},{20,16},{24,28},{28,24},{1,5},{5... | collective-permute-start | bytes 1572872 | tf_op jit(solution)/shard_map/side_states/ppermute | solution.py:297
  63.6 25.7 %copy-start = (bf16[512,2048]{1,0:T(8,128)(2,1)S(1)}, bf16[512,2048]{1,0:T(8,128)(2,1)}, u32[]{:S(2)}) copy-start(bf16[512,2048]{1,0:T(8,128)(2,1)} %all-gather.5.cloned.1.call-done.refs_1_) | copy-start | bytes 6291460
  65.6 17.6 %collective-permute-start = (bf16[512,512]{1,0:T(8,128)(2,1)}, bf16[512,512]{1,0:T(8,128)(2,1)}, u32[]{:S(2)}, u32[]{:S(2)}) collective-permute-start(bf16[512,512]{1,0:T(8,128)(2,1)} %constant_dynamic-slice_fusion), channel_id=1, source_target_pairs={{0,8},{1,25},{2,18},{4,12},{5,29},{6,22},{8,16},{9,1},{10,26},{12,... | collective-permute-start | bytes 1572872 | tf_op jit(solution)/shard_map/line_states_0/ppermute | solution.py:356
  83.3 187.7 %all-gather.11.cloned.1.call-start = ((), (), s32[]{:S(2)}) async-start(), calls=%async_computation.5 | async-start | bytes 5242880 | tf_op jit(solution)/shard_map/line_states/all_gather | solution.py:383
  85.2 18.1 %collective-permute-start.17 = (bf16[512,512]{1,0:T(8,128)(2,1)}, bf16[512,512]{1,0:T(8,128)(2,1)}, u32[]{:S(2)}, u32[]{:S(2)}) collective-permute-start(bf16[512,512]{1,0:T(8,128)(2,1)} %constant_dynamic-slice_fusion.1), channel_id=1, source_target_pairs={{0,8},{1,25},{2,18},{4,12},{5,29},{6,22},{8,16},{9,1},{10,26},{12,... | collective-permute-start | bytes 1572872 | tf_op jit(solution)/shard_map/line_states_1/ppermute | solution.py:356
  107.3 44.0 %collective-permute-start.2 = (bf16[512,1024]{1,0:T(8,128)(2,1)}, bf16[512,1024]{1,0:T(8,128)(2,1)}, u32[]{:S(2)}, u32[]{:S(2)}) collective-permute-start(bf16[512,1024]{1,0:T(8,128)(2,1)} %copy-done.15), channel_id=1, source_target_pairs={{0,8},{4,12},{8,16},{12,20},{16,24},{20,28},{1,9},{5,13},{9,17},{1... | collective-permute-start | bytes 3145736 | tf_op jit(solution)/shard_map/rows_0_0/ppermute | solution.py:289
  111.7 39.6 %collective-permute-start.3 = (bf16[512,1024]{1,0:T(8,128)(2,1)}, bf16[512,1024]{1,0:T(8,128)(2,1)}, u32[]{:S(2)}, u32[]{:S(2)}) collective-permute-start(bf16[512,1024]{1,0:T(8,128)(2,1)} %copy-done.15), channel_id=1, source_target_pairs={{8,0},{12,4},{16,8},{20,12},{24,16},{28,20},{9,1},{13,5},{17,9},{2... | collective-permute-start | bytes 3145736 | tf_op jit(solution)/shard_map/rows_0_0/ppermute | solution.py:293
  129.0 36.9 %collective-permute-start.4 = (bf16[512,1024]{1,0:T(8,128)(2,1)}, bf16[512,1024]{1,0:T(8,128)(2,1)}, u32[]{:S(2)}, u32[]{:S(2)}) collective-permute-start(bf16[512,1024]{1,0:T(8,128)(2,1)} %get-tuple-element.73.refs_1_.refs_3_), channel_id=1, source_target_pairs={{0,4},{4,0},{8,12},{12,8},{16,20},{20,16},{24,28},{28,24},{1,5},{5... | collective-permute-start | bytes 3145736 | tf_op jit(solution)/shard_map/side_rows_0/ppermute | solution.py:297
  142.6 32.4 %collective-permute-start.8 = (bf16[512,1024]{1,0:T(8,128)(2,1)}, bf16[512,1024]{1,0:T(8,128)(2,1)}, u32[]{:S(2)}, u32[]{:S(2)}) collective-permute-start(bf16[512,1024]{1,0:T(8,128)(2,1)} %get-tuple-element.77.refs_2_), channel_id=1, source_target_pairs={{0,8},{4,12},{8,16},{12,20},{16,24},{20,28},{1,9},{5,13},{9,17},{1... | collective-permute-start | bytes 3145736 | tf_op jit(solution)/shard_map/rows_0_1/ppermute | solution.py:289
  148.3 26.7 %collective-permute-start.9 = (bf16[512,1024]{1,0:T(8,128)(2,1)}, bf16[512,1024]{1,0:T(8,128)(2,1)}, u32[]{:S(2)}, u32[]{:S(2)}) collective-permute-start(bf16[512,1024]{1,0:T(8,128)(2,1)} %get-tuple-element.77.refs_2_), channel_id=1, source_target_pairs={{8,0},{12,4},{16,8},{20,12},{24,16},{28,20},{9,1},{13,5},{17,9},{2... | collective-permute-start | bytes 3145736 | tf_op jit(solution)/shard_map/rows_0_1/ppermute | solution.py:293
  164.4 24.1 %collective-permute-start.5 = (bf16[512,1024]{1,0:T(8,128)(2,1)}, bf16[512,1024]{1,0:T(8,128)(2,1)}, u32[]{:S(2)}, u32[]{:S(2)}) collective-permute-start(bf16[512,1024]{1,0:T(8,128)(2,1)} %get-tuple-element.80.refs_1_.refs_3_), channel_id=1, source_target_pairs={{0,4},{4,0},{8,12},{12,8},{16,20},{20,16},{24,28},{28,24},{1,5},{5... | collective-permute-start | bytes 3145736 | tf_op jit(solution)/shard_map/side_rows_1/ppermute | solution.py:297
  170.4 28.0 %collective-permute-start.6 = (bf16[512,1024]{1,0:T(8,128)(2,1)}, bf16[512,1024]{1,0:T(8,128)(2,1)S(1)}, u32[]{:S(2)}, u32[]{:S(2)}) collective-permute-start(bf16[512,1024]{1,0:T(8,128)(2,1)} %sums_1_0.1), channel_id=1, source_target_pairs={{0,8},{4,12},{24,16},{28,20},{1,9},{5,13},{25,17},{29,21},{2,10},{... | collective-permute-start | bytes 3145736 | tf_op jit(solution)/shard_map/sums_1_0/ppermute | solution.py:506
  175.0 26.5 %collective-permute-start.10 = (bf16[512,1024]{1,0:T(8,128)(2,1)}, bf16[512,1024]{1,0:T(8,128)(2,1)S(1)}, u32[]{:S(2)}, u32[]{:S(2)}) collective-permute-start(bf16[512,1024]{1,0:T(8,128)(2,1)} %collective-permute-done.2.refs_5_), channel_id=1, source_target_pairs={{8,16},{12,20},{16,24},{20,28},{9,17},{13,21},{17,25},{21,29},{10,... | collective-permute-start | bytes 3145736 | tf_op jit(solution)/shard_map/rows_1_0/ppermute | solution.py:289
  175.7 25.8 %collective-permute-start.11 = (bf16[512,1024]{1,0:T(8,128)(2,1)}, bf16[512,1024]{1,0:T(8,128)(2,1)S(1)}, u32[]{:S(2)}, u32[]{:S(2)}) collective-permute-start(bf16[512,1024]{1,0:T(8,128)(2,1)} %collective-permute-done.3.refs_14_), channel_id=1, source_target_pairs={{8,0},{12,4},{16,8},{20,12},{9,1},{13,5},{17,9},{21,13},{10,2},{14... | collective-permute-start | bytes 3145736 | tf_op jit(solution)/shard_map/rows_1_0/ppermute | solution.py:293
  184.7 13.7 %copy-start.25 = (s32[15]{0:T(128)S(1)}, s32[15]{0:T(128)}, u32[]{:S(2)}) copy-start(s32[15]{0:T(128)} %copy-done.24) | copy-start | bytes 184
  193.1 28.2 %collective-permute-start.7 = (bf16[512,1024]{1,0:T(8,128)(2,1)}, bf16[512,1024]{1,0:T(8,128)(2,1)}, u32[]{:S(2)}, u32[]{:S(2)}) collective-permute-start(bf16[512,1024]{1,0:T(8,128)(2,1)} %sums_1_1.1), channel_id=1, source_target_pairs={{0,8},{4,12},{24,16},{28,20},{1,9},{5,13},{25,17},{29,21},{2,10},{... | collective-permute-start | bytes 3145736 | tf_op jit(solution)/shard_map/sums_1_1/ppermute | solution.py:506
  201.5 26.1 %copy-start.10 = (bf16[512,1024]{1,0:T(8,128)(2,1)}, bf16[512,1024]{1,0:T(8,128)(2,1)S(1)}, u32[]{:S(2)}) copy-start(bf16[512,1024]{1,0:T(8,128)(2,1)S(1)} %collective-permute-done.10.up_ref.refs_9_) | copy-start | bytes 3145732
  202.5 23.5 %collective-permute-start.12 = (bf16[512,1024]{1,0:T(8,128)(2,1)}, bf16[512,1024]{1,0:T(8,128)(2,1)S(1)}, u32[]{:S(2)}, u32[]{:S(2)}) collective-permute-start(bf16[512,1024]{1,0:T(8,128)(2,1)} %collective-permute-done.8.refs_5_), channel_id=1, source_target_pairs={{8,16},{12,20},{16,24},{20,28},{9,17},{13,21},{17,25},{21,29},{10,... | collective-permute-start | bytes 3145736 | tf_op jit(solution)/shard_map/rows_1_1/ppermute | solution.py:289
  203.2 24.4 %collective-permute-start.13 = (bf16[512,1024]{1,0:T(8,128)(2,1)}, bf16[512,1024]{1,0:T(8,128)(2,1)S(1)}, u32[]{:S(2)}, u32[]{:S(2)}) collective-permute-start(bf16[512,1024]{1,0:T(8,128)(2,1)} %collective-permute-done.9.refs_14_), channel_id=1, source_target_pairs={{8,0},{12,4},{16,8},{20,12},{9,1},{13,5},{17,9},{21,13},{10,2},{14... | collective-permute-start | bytes 3145736 | tf_op jit(solution)/shard_map/rows_1_1/ppermute | solution.py:293
  204.5 40.5 %collective-permute-start.14 = (bf16[512,1024]{1,0:T(8,128)(2,1)}, bf16[512,1024]{1,0:T(8,128)(2,1)}, u32[]{:S(2)}, u32[]{:S(2)}) collective-permute-start(bf16[512,1024]{1,0:T(8,128)(2,1)} %sums_2_0.1), channel_id=1, source_target_pairs={{0,8},{4,12},{8,16},{12,20},{1,9},{5,13},{9,17},{13,21},{2,10},{6,... | collective-permute-start | bytes 3145736 | tf_op jit(solution)/shard_map/sums_2_0/ppermute | solution.py:508
  210.1 35.0 %collective-permute-start.15 = (bf16[512,1024]{1,0:T(8,128)(2,1)}, bf16[512,1024]{1,0:T(8,128)(2,1)}, u32[]{:S(2)}, u32[]{:S(2)}) collective-permute-start(bf16[512,1024]{1,0:T(8,128)(2,1)} %sums_2_0.1), channel_id=1, source_target_pairs={{16,8},{20,12},{24,16},{28,20},{17,9},{21,13},{25,17},{29,21},{18,... | collective-permute-start | bytes 3145736 | tf_op jit(solution)/shard_map/sums_2_0/ppermute | solution.py:509
  226.0 28.1 %copy-start.8 = (bf16[512,1024]{1,0:T(8,128)(2,1)}, bf16[512,1024]{1,0:T(8,128)(2,1)S(1)}, u32[]{:S(2)}) copy-start(bf16[512,1024]{1,0:T(8,128)(2,1)S(1)} %collective-permute-done.12.up_ref.refs_9_) | copy-start | bytes 3145732
  228.8 25.3 %copy-start.9 = (bf16[512,1024]{1,0:T(8,128)(2,1)}, bf16[512,1024]{1,0:T(8,128)(2,1)S(1)}, u32[]{:S(2)}) copy-start(bf16[512,1024]{1,0:T(8,128)(2,1)S(1)} %collective-permute-done.13.down_ref.refs_10_) | copy-start | bytes 3145732
  230.6 23.5 %collective-permute-start.16 = (bf16[512,1024]{1,0:T(8,128)(2,1)}, bf16[512,1024]{1,0:T(8,128)(2,1)}, u32[]{:S(2)}, u32[]{:S(2)}) collective-permute-start(bf16[512,1024]{1,0:T(8,128)(2,1)} %rows_2_0.1), channel_id=1, source_target_pairs={{16,24},{20,28},{8,0},{12,4},{17,25},{21,29},{9,1},{13,5},{18,26},... | collective-permute-start | bytes 3145736 | tf_op jit(solution)/shard_map/rows_2_0/ppermute | solution.py:464
  234.7 19.5 %copy-start.27 = (s32[15]{0:T(128)S(1)}, s32[15]{0:T(128)}, u32[]{:S(2)}) copy-start(s32[15]{0:T(128)} %copy-done.24) | copy-start | bytes 184
  234.7 46.4 %collective-permute-start.18 = (bf16[512,1024]{1,0:T(8,128)(2,1)}, bf16[512,1024]{1,0:T(8,128)(2,1)}, u32[]{:S(2)}, u32[]{:S(2)}) collective-permute-start(bf16[512,1024]{1,0:T(8,128)(2,1)} %sums_2_1.1), channel_id=1, source_target_pairs={{0,8},{4,12},{8,16},{12,20},{1,9},{5,13},{9,17},{13,21},{2,10},{6,... | collective-permute-start | bytes 3145736 | tf_op jit(solution)/shard_map/sums_2_1/ppermute | solution.py:508
  243.4 38.2 %collective-permute-start.19 = (bf16[512,1024]{1,0:T(8,128)(2,1)}, bf16[512,1024]{1,0:T(8,128)(2,1)}, u32[]{:S(2)}, u32[]{:S(2)}) collective-permute-start(bf16[512,1024]{1,0:T(8,128)(2,1)} %sums_2_1.1), channel_id=1, source_target_pairs={{16,8},{20,12},{24,16},{28,20},{17,9},{21,13},{25,17},{29,21},{18,... | collective-permute-start | bytes 3145736 | tf_op jit(solution)/shard_map/sums_2_1/ppermute | solution.py:509
  255.9 33.7 %collective-permute-start.20 = (bf16[512,1024]{1,0:T(8,128)(2,1)}, bf16[512,1024]{1,0:T(8,128)(2,1)}, u32[]{:S(2)}, u32[]{:S(2)}) collective-permute-start(bf16[512,1024]{1,0:T(8,128)(2,1)} %rows_2_1.1), channel_id=1, source_target_pairs={{16,24},{20,28},{8,0},{12,4},{17,25},{21,29},{9,1},{13,5},{18,26},... | collective-permute-start | bytes 3145736 | tf_op jit(solution)/shard_map/rows_2_1/ppermute | solution.py:464
  260.5 40.9 %collective-permute-start.21 = (bf16[512,1024]{1,0:T(8,128)(2,1)}, bf16[512,1024]{1,0:T(8,128)(2,1)}, u32[]{:S(2)}, u32[]{:S(2)}) collective-permute-start(bf16[512,1024]{1,0:T(8,128)(2,1)} %get-tuple-element.114), channel_id=1, source_target_pairs={{0,8},{4,12},{8,16},{12,20},{16,24},{20,28},{1,9},{5,13},{9,17},{1... | collective-permute-start | bytes 3145736 | tf_op jit(solution)/shard_map/sums_3_0/ppermute | solution.py:508
  269.6 12.0 %copy-start.17 = (bf16[512,1024]{1,0:T(8,128)(2,1)S(1)}, bf16[512,1024]{1,0:T(8,128)(2,1)}, u32[]{:S(2)}) copy-start(bf16[512,1024]{1,0:T(8,128)(2,1)} %get-tuple-element.89.refs_1_) | copy-start | bytes 3145732
  269.6 12.0 %copy-start.28 = (s32[15]{0:T(128)S(1)}, s32[15]{0:T(128)}, u32[]{:S(2)}) copy-start(s32[15]{0:T(128)} %copy-done.24) | copy-start | bytes 184
  269.6 39.7 %collective-permute-start.22 = (bf16[512,1024]{1,0:T(8,128)(2,1)}, bf16[512,1024]{1,0:T(8,128)(2,1)}, u32[]{:S(2)}, u32[]{:S(2)}) collective-permute-start(bf16[512,1024]{1,0:T(8,128)(2,1)} %get-tuple-element.102), channel_id=1, source_target_pairs={{8,0},{12,4},{16,8},{20,12},{24,16},{28,20},{9,1},{13,5},{17,9},{2... | collective-permute-start | bytes 3145736 | tf_op jit(solution)/shard_map/sums_3_0/ppermute | solution.py:509
  281.1 31.2 %collective-permute-start.23 = (bf16[512,1024]{1,0:T(8,128)(2,1)}, bf16[512,1024]{1,0:T(8,128)(2,1)S(1)}, u32[]{:S(2)}, u32[]{:S(2)}) collective-permute-start(bf16[512,1024]{1,0:T(8,128)(2,1)} %get-tuple-element.117), channel_id=1, source_target_pairs={{0,4},{4,0},{8,12},{12,8},{16,20},{20,16},{24,28},{28,24},{1,5},{5... | collective-permute-start | bytes 3145736 | tf_op jit(solution)/shard_map/even_0/ppermute | solution.py:297
  285.0 29.1 %collective-permute-start.24 = (bf16[512,1024]{1,0:T(8,128)(2,1)}, bf16[512,1024]{1,0:T(8,128)(2,1)S(1)}, u32[]{:S(2)}, u32[]{:S(2)}) collective-permute-start(bf16[512,1024]{1,0:T(8,128)(2,1)} %get-tuple-element.121), channel_id=1, source_target_pairs={{0,8},{4,12},{8,16},{12,20},{16,24},{20,28},{1,9},{5,13},{9,17},{1... | collective-permute-start | bytes 3145736 | tf_op jit(solution)/shard_map/sums_3_1/ppermute | solution.py:508
  289.6 13.5 %copy-start.31 = (bf16[256,512]{1,0:T(8,128)(2,1)S(1)}, bf16[256,512]{1,0:T(8,128)(2,1)}, u32[]{:S(2)}) copy-start(bf16[256,512]{1,0:T(8,128)(2,1)} %copy-done.30) | copy-start | bytes 786436
  289.6 13.5 %copy-start.33 = (bf16[256,512]{1,0:T(8,128)(2,1)S(1)}, bf16[256,512]{1,0:T(8,128)(2,1)}, u32[]{:S(2)}) copy-start(bf16[256,512]{1,0:T(8,128)(2,1)} %copy-done.32) | copy-start | bytes 786436
  289.6 32.4 %collective-permute-start.25 = (bf16[512,1024]{1,0:T(8,128)(2,1)}, bf16[512,1024]{1,0:T(8,128)(2,1)S(1)}, u32[]{:S(2)}, u32[]{:S(2)}) collective-permute-start(bf16[512,1024]{1,0:T(8,128)(2,1)} %get-tuple-element.110), channel_id=1, source_target_pairs={{8,0},{12,4},{16,8},{20,12},{24,16},{28,20},{9,1},{13,5},{17,9},{2... | collective-permute-start | bytes 3145736 | tf_op jit(solution)/shard_map/sums_3_1/ppermute | solution.py:509
  301.4 22.5 %collective-permute-start.26 = (bf16[512,1024]{1,0:T(8,128)(2,1)}, bf16[512,1024]{1,0:T(8,128)(2,1)S(1)}, u32[]{:S(2)}, u32[]{:S(2)}) collective-permute-start(bf16[512,1024]{1,0:T(8,128)(2,1)} %get-tuple-element.125), channel_id=1, source_target_pairs={{0,4},{4,0},{8,12},{12,8},{16,20},{20,16},{24,28},{28,24},{1,5},{5... | collective-permute-start | bytes 3145736 | tf_op jit(solution)/shard_map/even_1/ppermute | solution.py:297
  (25 other events, 112.0 us)
Sparse Core Ops, SparseCore 0:
  36.8 21.6 all-gather.4
  60.6 22.5 all-gather.6
  84.8 22.5 all-gather.8
  108.9 34.4 all-gather.10

commit v4 on v3

--- a/solution.py
+++ b/solution.py
@@ -12,6 +12,7 @@
 
 def cost(rank):
     return pl.CostEstimate(flops=0, bytes_accessed=rank * 2**19, transcendentals=0)
+LOG2_E = 1.4426950408889634
 LOW = jnp.bfloat16
 WIDE = jnp.float32
 
@@ -41,25 +42,39 @@
         lax.broadcasted_iota(jnp.int32, (query_count, 1), 0) + (offset + 1), length
     )
     visible = position < limit
-    for head in range(block // HEAD_DIM):
-        columns = slice(head * HEAD_DIM, (head + 1) * HEAD_DIM)
-        query, grad = query_ref[:, columns], grad_ref[:, columns]
-        key, value = key_rows[:, columns], value_rows[:, columns]
-        scores = lax.dot_general(query, key, across, preferred_element_type=WIDE) * scale
-        scores = jnp.where(visible, scores, -1e30)
-        weights = jnp.exp(scores - jnp.max(scores, axis=-1, keepdims=True))
-        probs = weights * (1.0 / jnp.sum(weights, axis=-1, keepdims=True))
-        probs_low = probs.astype(LOW)
-        context = jnp.dot(probs_low, value, preferred_element_type=WIDE)
-        delta = jnp.sum(grad.astype(WIDE) * context, axis=-1, keepdims=True)
-        prob_grad = lax.dot_general(grad, value, across, preferred_element_type=WIDE)
-        score_grad = (probs * (prob_grad - delta) * scale).astype(LOW)
-        query_grad_ref[:, columns] = jnp.dot(score_grad, key, preferred_element_type=WIDE).astype(LOW)
-        key_grad = lax.dot_general(score_grad, query, down, preferred_element_type=WIDE)
-        value_grad = lax.dot_general(probs_low, grad, down, preferred_element_type=WIDE)
-        rows_grad_ref[:, columns] = key_grad.astype(LOW)
+    heads = range(block // HEAD_DIM)
+    columns = [slice(head * HEAD_DIM, (head + 1) * HEAD_DIM) for head in heads]
+    query = [query_ref[:, part] for part in columns]
+    grad = [grad_ref[:, part] for part in columns]
+    key = [key_rows[:, part] for part in columns]
+    value = [value_rows[:, part] for part in columns]
+
+    def dots(left, right, dims):
+        return [
+            lax.dot_general(left[head], right[head], dims, preferred_element_type=WIDE) for head in heads
+        ]
+
+    scores = [jnp.where(visible, one, -1e30) for one in dots(query, key, across)]
+    prob_grad = dots(grad, value, across)
+    weights = [
+        jnp.exp2((one - jnp.max(one, axis=-1, keepdims=True)) * (scale * LOG2_E)) for one in scores
+    ]
+    probs = [one * (1.0 / jnp.sum(one, axis=-1, keepdims=True)) for one in weights]
+    probs_low = [one.astype(LOW) for one in probs]
+    delta = [
+        jnp.sum(probs_low[head].astype(WIDE) * prob_grad[head], axis=-1, keepdims=True) for head in heads
+    ]
+    score_grad = [
+        (probs[head] * (prob_grad[head] - delta[head]) * scale).astype(LOW) for head in heads
+    ]
+    query_grads = dots(score_grad, key, (((1,), (0,)), ((), ())))
+    key_grads = dots(query, score_grad, down)
+    value_grads = dots(grad, probs_low, down)
+    for head in heads:
+        query_grad_ref[:, columns[head]] = query_grads[head].astype(LOW)
+        rows_grad_ref[:, columns[head]] = key_grads[head].T.astype(LOW)
         value_columns = slice(block + head * HEAD_DIM, block + (head + 1) * HEAD_DIM)
-        rows_grad_ref[:, value_columns] = value_grad.astype(LOW)
+        rows_grad_ref[:, value_columns] = value_grads[head].T.astype(LOW)
 
 
 def attend(rank, info, doc_states, key_weight, value_weight, queries, grads, first, heads):
@@ -350,10 +365,9 @@
             for i in range(major):
                 for j in range(minor):
                     for t in range(tp_count):
-                        if slots[t // ratio]:
-                            to = at((i + slots[t // ratio]) % major, j)
-                            pairs.append((at(i, j) * tp_count + t, to * tp_count + t))
-            return rows, lax.ppermute(rows, ("seq", "tp"), pairs)
+                        to = at((i + slots[t // ratio]) % major, j)
+                        pairs.append((at(i, j) * tp_count + t, to * tp_count + t))
+            return lax.ppermute(rows, ("seq", "tp"), pairs)
 
     side_parts = []
     if ratio == 1:
@@ -366,15 +380,15 @@
     with jax.named_scope("gather_states"):
         doc_states = [lax.all_gather(piece, "tp", axis=1, tiled=True) for piece in doc_pieces]
     found = [send_line(doc_states[piece], piece) for piece in range(pieces - 1)]
-    joined = lax.optimization_barrier((*doc_states, *[got for _, got in found], *side_parts))
-    doc_states, side_parts = list(joined[:pieces]), joined[2 * pieces - 1 :]
-    found = [(rows, got) for (rows, _), got in zip(found, joined[pieces : 2 * pieces - 1])]
+    joined = lax.optimization_barrier((*doc_states, *found, *side_parts))
+    doc_states, found, side_parts = (
+        list(joined[:pieces]), list(joined[pieces : 2 * pieces - 1]), joined[2 * pieces - 1 :]
+    )
     found.append(send_line(doc_states[-1], pieces - 1))
 
     def gather_line(after):
         with jax.named_scope("line_states"):
-            arrived = lax.optimization_barrier((*[got for _, got in found], after))[:-1]
-            pieces_found = [jnp.where(distance == 0, rows, got) for (rows, _), got in zip(found, arrived)]
+            pieces_found = lax.optimization_barrier((*found, after))[:-1]
             if 1 < pieces < minor:
                 rows = [rows.reshape(piece_rows, minor // pieces, 1, slice_width) for rows in pieces_found]
                 rows = jnp.concatenate(rows, axis=2).reshape(piece_rows, minor * slice_width)

time: 334 us -> 329 us (0.985)
  Pallas kernels: 123 us -> 116 us
    pallas_call x4, Pallas kernels: 46.3 us -> 39.8 us  [attend(): pl.pallas_call(lambda *refs: attend_kernel(pieces, *refs), grid=(heads //...]
    ppermute x4, waiting for transfers between devices: 1.56 us -> 5.9 us  [step_down(): return lax.ppermute(value, 'seq', pairs)]
  transfers between devices with their start and end apart: 32 -> 32, of which waited for: 10 -> 12; matrix products, arithmetic and copies ran while one was open for 6% -> 5% of each run, Pallas kernels for 36% -> 35%
where the time goes in v4:
time: 329 us; the launch traced here: 327 us
  Pallas kernels  116 us (35%)
  starting transfers between devices  84 us (26%)
  waiting for transfers between devices  55.8 us (17%)
  blocking collectives  21.4 us (7%)
  local copies, waits for them, and re-layouts  20.4 us (6%)
  between operations  15.1 us (5%)
  other arithmetic  8.29 us (3%)
  matrix products  5.85 us (2%)
    pallas_call x8, Pallas kernels, products(): pl.pallas_call(body, grid_spec=pltpu.PrefetchScalarGridSpec(num_scalar_pr...  53.4 us
    pallas_call x4, Pallas kernels, attend(): pl.pallas_call(lambda *refs: attend_kernel(pieces, *refs), grid=(heads //...  39.8 us
    ppermute x4, starting transfers between devices, send_sums(): sums_up[index] = lax.ppermute(up, 'seq', up_pairs)  30.9 us
    all_to_all x1, blocking collectives, route(): lax.all_to_all(sent, 'seq', split_axis=0, concat_axis=0, tiled=True)  21.4 us
    all_to_all x1, waiting for transfers between devices, route(): lax.all_to_all(sent, 'seq', split_axis=0, concat_axis=0, tiled=True)  14.2 us
    unnamed x82, local copies, waits for them, and re-layouts  13.3 us
    ppermute x4, waiting for transfers between devices, send_sums(): sums_down[index] = lax.ppermute(down, 'seq', down_pairs)  13 us
    pallas_call x4, Pallas kernels, add_arrivals(): pl.pallas_call(body, grid_spec=pltpu.PrefetchScalarGridSpec(num_scalar_pr...  11.3 us
  transfers between devices with their start and end apart: 32, of which 12 were waited for; matrix products, arithmetic and copies ran while one was open for 5% of the time, Pallas kernels for 35%

profile of v4, /device:TPU:0, one launch (start us, length us, event | category | flops | bytes accessed | tf_op | source)
XLA Modules:
  0.0 327.4 jit_solution(3870482658377602066)
XLA Ops:
  8.2 2.4 convolution_convert_fusion.1
  10.6 7.4 %all-to-all-start = ((bf16[8,80,512]{2,1,0:T(8,128)(2,1)}), bf16[8,80,512]{2,1,0:T(8,128)(2,1)S(1)}, u32[]{:S(2)}, u32[]{:S(2)}) async-start(bf16[8,80,512]{2,1,0:T(8,128)(2,1)} %bitcast.3), calls=%async_computation | async-start | bytes 1310720 | tf_op jit(solution)/shard_map/route/all_to_all | solution.py:270
  21.0 14.2 %all-to-all-done = bf16[8,80,512]{2,1,0:T(8,128)(2,1)S(1)} async-done(((bf16[8,80,512]{2,1,0:T(8,128)(2,1)}), bf16[8,80,512]{2,1,0:T(8,128)(2,1)S(1)}, u32[]{:S(2)}, u32[]{:S(2)}) %all-to-all-start) | async-done | bytes 655392 | tf_op jit(solution)/shard_map/route/all_to_all | solution.py:270
  37.3 21.4 %all_to_all.24 = bf16[8,80,512]{2,1,0:T(8,128)(2,1)S(1)} all-to-all(bf16[8,80,512]{2,1,0:T(8,128)(2,1)S(1)} %bitcast.42), channel_id=1, replica_groups=mesh['seq'=8,'tp'=4] {'seq'}, dimensions={0} | all-to-all | bytes 1310720 | tf_op jit(solution)/shard_map/route/all_to_all | solution.py:270
  61.5 2.1 fusion.8
  63.6 2.0 constant_dynamic-slice_fusion
  65.6 2.8 collective-permute-start
  68.4 7.6 %collective-permute-done.1 = bf16[512,512]{1,0:T(8,128)(2,1)} collective-permute-done((bf16[512,512]{1,0:T(8,128)(2,1)}, bf16[512,512]{1,0:T(8,128)(2,1)}, u32[]{:S(2)}, u32[]{:S(2)}) %collective-permute-start.1) | collective-permute-done | bytes 524320 | tf_op jit(solution)/shard_map/side_states/ppermute | solution.py:312
  76.0 7.3 %all-gather.7.cloned.1.call-done.refs_2_ = bf16[512,2048]{1,0:T(8,128)(2,1)} async-done(((bf16[512,512]{1,0:T(8,128)(2,1)}), bf16[512,2048]{1,0:T(8,128)(2,1)}) %all-gather.7.cloned.1.call-update) | async-done | bytes 2097168 | tf_op jit(solution)/shard_map/gather_states/all_gather | solution.py:381
  84.5 3.4 %collective-permute-start.17 = (bf16[512,512]{1,0:T(8,128)(2,1)S(1)}, bf16[512,512]{1,0:T(8,128)(2,1)S(1)}, u32[]{:S(2)}, u32[]{:S(2)}) collective-permute-start(bf16[512,512]{1,0:T(8,128)(2,1)S(1)} %constant_dynamic-slice_fusion.1), channel_id=1, source_target_pairs={{0,8},{1,25},{2,18},{3,3},{4,12},{5,29},{6,22},{7,7},{8,16},{9,1},... | collective-permute-start | bytes 1572872 | tf_op jit(solution)/shard_map/line_states_1/ppermute | solution.py:370
  90.7 9.7 %attend_0.1 = (bf16[256,512]{1,0:T(8,128)(2,1)S(1)}, bf16[512,1024]{1,0:T(8,128)(2,1)S(1)}) custom-call(s32[15]{0:T(128)S(1)} %stack.54.refs_0_.scalar_ref, bf16[512,2048]{1,0:T(8,128)(2,1)S(1)} %copy-done, bf16[512,2048]{1,0:T(8,128)(2,1)S(1)} %copy-done.1, bf16[4,2,512,2048]{3,2,1,0:T(8,128)(2,1)} %bitcast.24, bf16[4,2,512,2048]{3,2,1,0:T(8,128)(2,1)} %bitcast.25, ...), custom_call_target="tpu_custom_call" | custom-call | bytes 524288 | tf_op jit(solution)/shard_map/attend_0/pallas_call | solution.py:97
  102.3 2.2 pad_maximum_fusion.1
  104.5 3.4 %collective-permute-start.2 = (bf16[512,1024]{1,0:T(8,128)(2,1)}, bf16[512,1024]{1,0:T(8,128)(2,1)}, u32[]{:S(2)}, u32[]{:S(2)}) collective-permute-start(bf16[512,1024]{1,0:T(8,128)(2,1)} %copy-done.15), channel_id=1, source_target_pairs={{0,8},{4,12},{8,16},{12,20},{16,24},{20,28},{1,9},{5,13},{9,17},{1... | collective-permute-start | bytes 3145736 | tf_op jit(solution)/shard_map/rows_0_0/ppermute | solution.py:304
  112.2 10.0 %attend_2.1 = (bf16[256,512]{1,0:T(8,128)(2,1)S(1)}, bf16[512,1024]{1,0:T(8,128)(2,1)}) custom-call(s32[15]{0:T(128)S(1)} %stack.54.refs_0_.scalar_ref, bf16[512,2048]{1,0:T(8,128)(2,1)S(1)} %copy-done, bf16[512,2048]{1,0:T(8,128)(2,1)S(1)} %copy-done.2, bf16[4,2,512,2048]{3,2,1,0:T(8,128)(2,1)} %bitcast.26, bf16[4,2,512,2048]{3,2,1,0:T(8,128)(2,1)} %bitcast.27, ...), custom_call_target="tpu_custom_call" | custom-call | bytes 1048576 | tf_op jit(solution)/shard_map/attend_2/pallas_call | solution.py:97
  124.3 10.1 %attend_1.1 = (bf16[256,512]{1,0:T(8,128)(2,1)S(1)}, bf16[512,1024]{1,0:T(8,128)(2,1)}) custom-call(s32[15]{0:T(128)S(1)} %stack.54.refs_0_.scalar_ref, bf16[512,2048]{1,0:T(8,128)(2,1)S(1)} %copy-done, bf16[512,2048]{1,0:T(8,128)(2,1)S(1)} %copy-done.2, bf16[4,2,512,2048]{3,2,1,0:T(8,128)(2,1)} %bitcast.28, bf16[4,2,512,2048]{3,2,1,0:T(8,128)(2,1)} %bitcast.29, ...), custom_call_target="tpu_custom_call" | custom-call | bytes 1572864 | tf_op jit(solution)/shard_map/attend_1/pallas_call | solution.py:97
  135.2 5.7 %collective-permute-start.8 = (bf16[512,1024]{1,0:T(8,128)(2,1)}, bf16[512,1024]{1,0:T(8,128)(2,1)}, u32[]{:S(2)}, u32[]{:S(2)}) collective-permute-start(bf16[512,1024]{1,0:T(8,128)(2,1)} %get-tuple-element.77.refs_2_), channel_id=1, source_target_pairs={{0,8},{4,12},{8,16},{12,20},{16,24},{20,28},{1,9},{5,13},{9,17},{1... | collective-permute-start | bytes 3145736 | tf_op jit(solution)/shard_map/rows_0_1/ppermute | solution.py:304
  144.8 10.0 %attend_3.1 = (bf16[256,512]{1,0:T(8,128)(2,1)S(1)}, bf16[512,1024]{1,0:T(8,128)(2,1)}) custom-call(s32[15]{0:T(128)S(1)} %stack.54.refs_0_.scalar_ref, bf16[512,2048]{1,0:T(8,128)(2,1)S(1)} %copy-done, bf16[512,2048]{1,0:T(8,128)(2,1)S(1)} %copy-done.3, bf16[4,2,512,2048]{3,2,1,0:T(8,128)(2,1)} %bitcast.30, bf16[4,2,512,2048]{3,2,1,0:T(8,128)(2,1)} %bitcast.31, ...), custom_call_target="tpu_custom_call" | custom-call | bytes 2097152 | tf_op jit(solution)/shard_map/attend_3/pallas_call | solution.py:97
  156.9 4.5 %sums_1_0.1 = bf16[512,1024]{1,0:T(8,128)(2,1)} custom-call(s32[15]{0:T(128)} %copy-done.24, bf16[512,2048]{1,0:T(8,128)(2,1)} %broadcast_select_fusion.refs_0_.refs_1_.refs_2_, bf16[512,1024]{1,0:T(8,128)(2,1)} %get-tuple-element.73.refs_1_.refs_3_, bf16[2048,512]{1,0:T(8,128)(2,1)} %all-gather.9.cloned.1.call-done.refs_2_.refs_4_.refs_5_.refs_6_, ...), custom_call_target="tpu_custom_call" | custom-call | bytes 2621440 | tf_op jit(solution)/shard_map/sums_1_0/pallas_call | solution.py:148
  161.4 4.6 %collective-permute-start.6 = (bf16[512,1024]{1,0:T(8,128)(2,1)}, bf16[512,1024]{1,0:T(8,128)(2,1)S(1)}, u32[]{:S(2)}, u32[]{:S(2)}) collective-permute-start(bf16[512,1024]{1,0:T(8,128)(2,1)} %sums_1_0.1), channel_id=1, source_target_pairs={{0,8},{4,12},{24,16},{28,20},{1,9},{5,13},{25,17},{29,21},{2,10},{... | collective-permute-start | bytes 3145736 | tf_op jit(solution)/shard_map/sums_1_0/ppermute | solution.py:520
  169.0 7.4 %side_ahead_0.1 = (bf16[512,1024]{1,0:T(8,128)(2,1)}, bf16[512,1024]{1,0:T(8,128)(2,1)}, bf16[512,1024]{1,0:T(8,128)(2,1)}) custom-call(s32[15]{0:T(128)} %copy-done.24, bf16[512,2048]{1,0:T(8,128)(2,1)} %broadcast_select_fusion.refs_0_.refs_1_.refs_2_, bf16[512,2048]{1,0:T(8,128)(2,1)} %broadcast_select_fusion.refs_0_.refs_1_.refs_2_, ...), custom_call_target="tpu_custom_call" | custom-call | tf_op jit(solution)/shard_map/side_ahead_0/pallas_call | solution.py:148
  176.5 3.3 %collective-permute-done.5.refs_3_.refs_7_ = bf16[512,1024]{1,0:T(8,128)(2,1)} collective-permute-done((bf16[512,1024]{1,0:T(8,128)(2,1)}, bf16[512,1024]{1,0:T(8,128)(2,1)}, u32[]{:S(2)}, u32[]{:S(2)}) %collective-permute-start.5) | collective-permute-done | bytes 1048608 | tf_op jit(solution)/shard_map/side_rows_1/ppermute | solution.py:312
  179.8 4.6 %sums_1_1.1 = bf16[512,1024]{1,0:T(8,128)(2,1)} custom-call(s32[15]{0:T(128)} %copy-done.24, bf16[512,2048]{1,0:T(8,128)(2,1)} %broadcast_select_fusion.refs_0_.refs_1_.refs_2_, bf16[512,1024]{1,0:T(8,128)(2,1)} %get-tuple-element.80.refs_1_.refs_3_, bf16[2048,512]{1,0:T(8,128)(2,1)} %all-gather.9.cloned.1.call-done.refs_2_.refs_4_.refs_5_.refs_6_, ...), custom_call_target="tpu_custom_call" | custom-call | bytes 3670016 | tf_op jit(solution)/shard_map/sums_1_1/pallas_call | solution.py:148
  184.4 5.3 %collective-permute-start.7 = (bf16[512,1024]{1,0:T(8,128)(2,1)}, bf16[512,1024]{1,0:T(8,128)(2,1)}, u32[]{:S(2)}, u32[]{:S(2)}) collective-permute-start(bf16[512,1024]{1,0:T(8,128)(2,1)} %sums_1_1.1), channel_id=1, source_target_pairs={{0,8},{4,12},{24,16},{28,20},{1,9},{5,13},{25,17},{29,21},{2,10},{... | collective-permute-start | bytes 3145736 | tf_op jit(solution)/shard_map/sums_1_1/ppermute | solution.py:520
  190.9 1.9 sums_2_0.1
  197.2 6.1 %collective-permute-start.14 = (bf16[512,1024]{1,0:T(8,128)(2,1)}, bf16[512,1024]{1,0:T(8,128)(2,1)}, u32[]{:S(2)}, u32[]{:S(2)}) collective-permute-start(bf16[512,1024]{1,0:T(8,128)(2,1)} %sums_2_0.1), channel_id=1, source_target_pairs={{0,8},{4,12},{8,16},{12,20},{1,9},{5,13},{9,17},{13,21},{2,10},{6,... | collective-permute-start | bytes 3145736 | tf_op jit(solution)/shard_map/sums_2_0/ppermute | solution.py:522
  203.4 1.7 collective-permute-start.15
  205.0 7.4 %side_ahead_1.1 = (bf16[512,1024]{1,0:T(8,128)(2,1)}, bf16[512,1024]{1,0:T(8,128)(2,1)}, bf16[512,1024]{1,0:T(8,128)(2,1)}) custom-call(s32[15]{0:T(128)} %copy-done.24, bf16[512,2048]{1,0:T(8,128)(2,1)} %broadcast_select_fusion.refs_0_.refs_1_.refs_2_, bf16[512,2048]{1,0:T(8,128)(2,1)} %broadcast_select_fusion.refs_0_.refs_1_.refs_2_, ...), custom_call_target="tpu_custom_call" | custom-call | tf_op jit(solution)/shard_map/side_ahead_1/pallas_call | solution.py:148
  212.6 4.7 %side_own_1.1.refs_0_ = bf16[512,1024]{1,0:T(8,128)(2,1)} custom-call(s32[15]{0:T(128)} %copy-done.24, bf16[512,2048]{1,0:T(8,128)(2,1)} %broadcast_select_fusion.refs_0_.refs_1_.refs_2_, bf16[512,1024]{1,0:T(8,128)(2,1)} %get-tuple-element.80.refs_1_.refs_3_, bf16[2048,512]{1,0:T(8,128)(2,1)} %all-gather.9.cloned.1.call-done.refs_2_.refs_4_.refs_5_.refs_6_, ...), custom_call_target="tpu_custom_call" | custom-call | bytes 5242880 | tf_op jit(solution)/shard_map/side_own_1/pallas_call | solution.py:148
  217.4 3.5 %collective-permute-done.13.down_ref.refs_10_ = bf16[512,1024]{1,0:T(8,128)(2,1)S(1)} collective-permute-done((bf16[512,1024]{1,0:T(8,128)(2,1)}, bf16[512,1024]{1,0:T(8,128)(2,1)S(1)}, u32[]{:S(2)}, u32[]{:S(2)}) %collective-permute-start.13) | collective-permute-done | bytes 1048608 | tf_op jit(solution)/shard_map/rows_1_1/ppermute | solution.py:308
  222.1 1.8 rows_2_0.1
  225.2 2.8 sums_2_1.1
  228.0 9.9 %collective-permute-start.18 = (bf16[512,1024]{1,0:T(8,128)(2,1)}, bf16[512,1024]{1,0:T(8,128)(2,1)}, u32[]{:S(2)}, u32[]{:S(2)}) collective-permute-start(bf16[512,1024]{1,0:T(8,128)(2,1)} %sums_2_1.1), channel_id=1, source_target_pairs={{0,8},{4,12},{8,16},{12,20},{1,9},{5,13},{9,17},{13,21},{2,10},{6,... | collective-permute-start | bytes 3145736 | tf_op jit(solution)/shard_map/sums_2_1/ppermute | solution.py:522
  239.5 4.5 %side_own_0.1.refs_0_ = bf16[512,1024]{1,0:T(8,128)(2,1)} custom-call(s32[15]{0:T(128)} %copy-done.24, bf16[512,2048]{1,0:T(8,128)(2,1)} %broadcast_select_fusion.refs_0_.refs_1_.refs_2_, bf16[512,1024]{1,0:T(8,128)(2,1)} %get-tuple-element.73.refs_1_.refs_3_, bf16[2048,512]{1,0:T(8,128)(2,1)} %all-gather.9.cloned.1.call-done.refs_2_.refs_4_.refs_5_.refs_6_, ...), custom_call_target="tpu_custom_call" | custom-call | bytes 6815744 | tf_op jit(solution)/shard_map/side_own_0/pallas_call | solution.py:148
  244.0 3.4 %collective-permute-done.16.refs_6_.refs_13_ = bf16[512,1024]{1,0:T(8,128)(2,1)} collective-permute-done((bf16[512,1024]{1,0:T(8,128)(2,1)}, bf16[512,1024]{1,0:T(8,128)(2,1)}, u32[]{:S(2)}, u32[]{:S(2)}) %collective-permute-start.16) | collective-permute-done | bytes 1048608 | tf_op jit(solution)/shard_map/rows_2_0/ppermute | solution.py:478
  247.4 1.7 rows_2_1.1
  250.5 3.3 %sums_3_0.1 = (bf16[512,1024]{1,0:T(8,128)(2,1)}, bf16[512,1024]{1,0:T(8,128)(2,1)}) custom-call(s32[15]{0:T(128)S(1)} %copy-done.27, bf16[512,1024]{1,0:T(8,128)(2,1)S(1)} %copy-done.18, bf16[512,1024]{1,0:T(8,128)(2,1)S(1)} %copy-done.19, bf16[512,1024]{1,0:T(8,128)(2,1)} %collective-permute-done.14.refs_2_, bf16[512,1024]{1,0:T(8,128)(2,1)} %collective-permute-done.15.refs_3_), custom_call_target="tpu_custom_call" | custom-call | bytes 7864320 | tf_op jit(solution)/shard_map/sums_3_0/pallas_call | solution.py:171
  253.8 10.3 %collective-permute-start.21 = (bf16[512,1024]{1,0:T(8,128)(2,1)}, bf16[512,1024]{1,0:T(8,128)(2,1)}, u32[]{:S(2)}, u32[]{:S(2)}) collective-permute-start(bf16[512,1024]{1,0:T(8,128)(2,1)} %get-tuple-element.114), channel_id=1, source_target_pairs={{0,8},{4,12},{8,16},{12,20},{16,24},{20,28},{1,9},{5,13},{9,17},{1... | collective-permute-start | bytes 3145736 | tf_op jit(solution)/shard_map/sums_3_0/ppermute | solution.py:522
  265.5 10.1 %even_0.1 = (bf16[512,1024]{1,0:T(8,128)(2,1)}, bf16[512,1024]{1,0:T(8,128)(2,1)}) custom-call(s32[15]{0:T(128)} %copy-done.24, bf16[2048,1024]{1,0:T(8,128)(2,1)} %all-gather.11.cloned.1.call-done.refs_0_.refs_1_.refs_3_.refs_4_.refs_7_.refs_8_.refs_11_.refs_12_, ...), custom_call_target="tpu_custom_call" | custom-call | bytes 8388608 | tf_op jit(solution)/shard_map/even_0/pallas_call | solution.py:148
  276.2 3.4 %sums_3_1.1 = (bf16[512,1024]{1,0:T(8,128)(2,1)}, bf16[512,1024]{1,0:T(8,128)(2,1)}) custom-call(s32[15]{0:T(128)S(1)} %copy-done.28, bf16[512,1024]{1,0:T(8,128)(2,1)S(1)} %copy-done.16, bf16[512,1024]{1,0:T(8,128)(2,1)S(1)} %copy-done.17, bf16[512,1024]{1,0:T(8,128)(2,1)} %collective-permute-done.18.refs_2_, bf16[512,1024]{1,0:T(8,128)(2,1)} %collective-permute-done.19.refs_3_), custom_call_target="tpu_custom_call" | custom-call | bytes 8912896 | tf_op jit(solution)/shard_map/sums_3_1/pallas_call | solution.py:171
  279.5 4.6 %collective-permute-start.24 = (bf16[512,1024]{1,0:T(8,128)(2,1)}, bf16[512,1024]{1,0:T(8,128)(2,1)S(1)}, u32[]{:S(2)}, u32[]{:S(2)}) collective-permute-start(bf16[512,1024]{1,0:T(8,128)(2,1)} %get-tuple-element.121), channel_id=1, source_target_pairs={{0,8},{4,12},{8,16},{12,20},{16,24},{20,28},{1,9},{5,13},{9,17},{1... | collective-permute-start | bytes 3145736 | tf_op jit(solution)/shard_map/sums_3_1/ppermute | solution.py:522
  285.6 10.1 %even_1.1 = (bf16[512,1024]{1,0:T(8,128)(2,1)}, bf16[512,1024]{1,0:T(8,128)(2,1)}) custom-call(s32[15]{0:T(128)} %copy-done.24, bf16[2048,1024]{1,0:T(8,128)(2,1)} %all-gather.11.cloned.1.call-done.refs_0_.refs_1_.refs_3_.refs_4_.refs_7_.refs_8_.refs_11_.refs_12_, ...), custom_call_target="tpu_custom_call" | custom-call | bytes 9437184 | tf_op jit(solution)/shard_map/even_1/pallas_call | solution.py:148
  297.3 2.0 pad_maximum_fusion
  299.4 4.4 %collective-permute-done.22.refs_2_ = bf16[512,1024]{1,0:T(8,128)(2,1)} collective-permute-done((bf16[512,1024]{1,0:T(8,128)(2,1)}, bf16[512,1024]{1,0:T(8,128)(2,1)}, u32[]{:S(2)}, u32[]{:S(2)}) %collective-permute-start.22) | collective-permute-done | bytes 1048608 | tf_op jit(solution)/shard_map/sums_3_0/ppermute | solution.py:523
  303.8 3.0 finish_2.1
  306.8 1.7 finish_0.1
  308.6 8.6 %collective-permute-done.25.refs_2_ = bf16[512,1024]{1,0:T(8,128)(2,1)S(1)} collective-permute-done((bf16[512,1024]{1,0:T(8,128)(2,1)}, bf16[512,1024]{1,0:T(8,128)(2,1)S(1)}, u32[]{:S(2)}, u32[]{:S(2)}) %collective-permute-start.25) | collective-permute-done | bytes 1048608 | tf_op jit(solution)/shard_map/sums_3_1/ppermute | solution.py:523
  317.2 1.9 finish_3.1
  319.1 1.7 finish_1.1
  (148 shorter events, 46.2 us)
Async XLA Ops:
  7.2 12.1 %copy-start.36 = (s32[4096]{0:T(1024)S(1)}, s32[4096]{0:T(1024)}, u32[]{:S(2)}) copy-start(s32[4096]{0:T(1024)} %param.13) | copy-start | bytes 49156
  10.6 26.1 %copy-start.37 = (bf16[512,1024]{1,0:T(8,128)(2,1)S(1)}, bf16[512,1024]{1,0:T(8,128)(2,1)}, u32[]{:S(2)}) copy-start(bf16[512,1024]{1,0:T(8,128)(2,1)} %param.11) | copy-start | bytes 3145732
  10.6 24.7 %all-to-all-start = ((bf16[8,80,512]{2,1,0:T(8,128)(2,1)}), bf16[8,80,512]{2,1,0:T(8,128)(2,1)S(1)}, u32[]{:S(2)}, u32[]{:S(2)}) async-start(bf16[8,80,512]{2,1,0:T(8,128)(2,1)} %bitcast.3), calls=%async_computation | async-start | bytes 1310720 | tf_op jit(solution)/shard_map/route/all_to_all | solution.py:270
  18.0 45.6 %all-gather.5.cloned.1.call-start = ((), (), s32[]{:S(2)}) async-start(), calls=%async_computation.2 | async-start | bytes 2621440 | tf_op jit(solution)/shard_map/gather_states/all_gather | solution.py:381
  21.0 122.8 %copy-start.24 = (s32[15]{0:T(128)}, s32[15]{0:T(128)S(1)}, u32[]{:S(2)}) copy-start(s32[15]{0:T(128)S(1)} %stack.54.refs_0_.scalar_ref) | copy-start | bytes 184
  36.7 46.6 %all-gather.7.cloned.1.call-start = ((), (), s32[]{:S(2)}) async-start(), calls=%async_computation.3 | async-start | bytes 2621440 | tf_op jit(solution)/shard_map/gather_states/all_gather | solution.py:381
  37.3 22.9 %copy-start.40 = (s32[4]{0:T(128)S(1)}, s32[4]{0:T(128)}, u32[]{:S(2)}) copy-start(s32[4]{0:T(128)} %constant.152.clone) | copy-start | bytes 52
  37.3 24.2 %copy-start.35 = (bf16[512,512]{1,0:T(8,128)(2,1)S(1)}, bf16[512,512]{1,0:T(8,128)(2,1)}, u32[]{:S(2)}) copy-start(bf16[512,512]{1,0:T(8,128)(2,1)} %fusion.2) | copy-start | bytes 1572868
  60.1 96.8 %all-gather.9.cloned.1.call-start = ((), (), s32[]{:S(2)}) async-start(), calls=%async_computation.4 | async-start | bytes 2621440 | tf_op jit(solution)/shard_map/side_states/all_gather | solution.py:407
  61.5 26.4 %copy-start.4 = (bf16[256,2048]{1,0:T(8,128)(2,1)S(1)}, bf16[256,2048]{1,0:T(8,128)(2,1)}, u32[]{:S(2)}) copy-start(bf16[256,2048]{1,0:T(8,128)(2,1)} %refs_7_.7) | copy-start | bytes 3145732
  63.6 12.4 %collective-permute-start.1 = (bf16[512,512]{1,0:T(8,128)(2,1)}, bf16[512,512]{1,0:T(8,128)(2,1)}, u32[]{:S(2)}, u32[]{:S(2)}) collective-permute-start(bf16[512,512]{1,0:T(8,128)(2,1)} %fusion.8), channel_id=1, source_target_pairs={{0,4},{4,0},{8,12},{12,8},{16,20},{20,16},{24,28},{28,24},{1,5},{5... | collective-permute-start | bytes 1572872 | tf_op jit(solution)/shard_map/side_states/ppermute | solution.py:312
  63.6 24.3 %copy-start = (bf16[512,2048]{1,0:T(8,128)(2,1)S(1)}, bf16[512,2048]{1,0:T(8,128)(2,1)}, u32[]{:S(2)}) copy-start(bf16[512,2048]{1,0:T(8,128)(2,1)} %all-gather.5.cloned.1.call-done.refs_1_) | copy-start | bytes 6291460
  65.6 17.6 %collective-permute-start = (bf16[512,512]{1,0:T(8,128)(2,1)}, bf16[512,512]{1,0:T(8,128)(2,1)}, u32[]{:S(2)}, u32[]{:S(2)}) collective-permute-start(bf16[512,512]{1,0:T(8,128)(2,1)} %constant_dynamic-slice_fusion), channel_id=1, source_target_pairs={{0,8},{1,25},{2,18},{3,3},{4,12},{5,29},{6,22},{7,7},{8,16},{9,1},... | collective-permute-start | bytes 1572872 | tf_op jit(solution)/shard_map/line_states_0/ppermute | solution.py:370
  83.3 182.2 %all-gather.11.cloned.1.call-start = ((), (), s32[]{:S(2)}) async-start(), calls=%async_computation.5 | async-start | bytes 5242880 | tf_op jit(solution)/shard_map/line_states/all_gather | solution.py:397
  84.5 17.8 %collective-permute-start.17 = (bf16[512,512]{1,0:T(8,128)(2,1)S(1)}, bf16[512,512]{1,0:T(8,128)(2,1)S(1)}, u32[]{:S(2)}, u32[]{:S(2)}) collective-permute-start(bf16[512,512]{1,0:T(8,128)(2,1)S(1)} %constant_dynamic-slice_fusion.1), channel_id=1, source_target_pairs={{0,8},{1,25},{2,18},{3,3},{4,12},{5,29},{6,22},{7,7},{8,16},{9,1},... | collective-permute-start | bytes 1572872 | tf_op jit(solution)/shard_map/line_states_1/ppermute | solution.py:370
  104.5 39.3 %collective-permute-start.2 = (bf16[512,1024]{1,0:T(8,128)(2,1)}, bf16[512,1024]{1,0:T(8,128)(2,1)}, u32[]{:S(2)}, u32[]{:S(2)}) collective-permute-start(bf16[512,1024]{1,0:T(8,128)(2,1)} %copy-done.15), channel_id=1, source_target_pairs={{0,8},{4,12},{8,16},{12,20},{16,24},{20,28},{1,9},{5,13},{9,17},{1... | collective-permute-start | bytes 3145736 | tf_op jit(solution)/shard_map/rows_0_0/ppermute | solution.py:304
  107.9 35.9 %collective-permute-start.3 = (bf16[512,1024]{1,0:T(8,128)(2,1)}, bf16[512,1024]{1,0:T(8,128)(2,1)}, u32[]{:S(2)}, u32[]{:S(2)}) collective-permute-start(bf16[512,1024]{1,0:T(8,128)(2,1)} %copy-done.15), channel_id=1, source_target_pairs={{8,0},{12,4},{16,8},{20,12},{24,16},{28,20},{9,1},{13,5},{17,9},{2... | collective-permute-start | bytes 3145736 | tf_op jit(solution)/shard_map/rows_0_0/ppermute | solution.py:308
  122.9 34.0 %collective-permute-start.4 = (bf16[512,1024]{1,0:T(8,128)(2,1)}, bf16[512,1024]{1,0:T(8,128)(2,1)}, u32[]{:S(2)}, u32[]{:S(2)}) collective-permute-start(bf16[512,1024]{1,0:T(8,128)(2,1)} %get-tuple-element.73.refs_1_.refs_3_), channel_id=1, source_target_pairs={{0,4},{4,0},{8,12},{12,8},{16,20},{20,16},{24,28},{28,24},{1,5},{5... | collective-permute-start | bytes 3145736 | tf_op jit(solution)/shard_map/side_rows_0/ppermute | solution.py:312
  135.2 30.8 %collective-permute-start.8 = (bf16[512,1024]{1,0:T(8,128)(2,1)}, bf16[512,1024]{1,0:T(8,128)(2,1)}, u32[]{:S(2)}, u32[]{:S(2)}) collective-permute-start(bf16[512,1024]{1,0:T(8,128)(2,1)} %get-tuple-element.77.refs_2_), channel_id=1, source_target_pairs={{0,8},{4,12},{8,16},{12,20},{16,24},{20,28},{1,9},{5,13},{9,17},{1... | collective-permute-start | bytes 3145736 | tf_op jit(solution)/shard_map/rows_0_1/ppermute | solution.py:304
  140.8 26.2 %collective-permute-start.9 = (bf16[512,1024]{1,0:T(8,128)(2,1)}, bf16[512,1024]{1,0:T(8,128)(2,1)}, u32[]{:S(2)}, u32[]{:S(2)}) collective-permute-start(bf16[512,1024]{1,0:T(8,128)(2,1)} %get-tuple-element.77.refs_2_), channel_id=1, source_target_pairs={{8,0},{12,4},{16,8},{20,12},{24,16},{28,20},{9,1},{13,5},{17,9},{2... | collective-permute-start | bytes 3145736 | tf_op jit(solution)/shard_map/rows_0_1/ppermute | solution.py:308
  155.5 24.3 %collective-permute-start.5 = (bf16[512,1024]{1,0:T(8,128)(2,1)}, bf16[512,1024]{1,0:T(8,128)(2,1)}, u32[]{:S(2)}, u32[]{:S(2)}) collective-permute-start(bf16[512,1024]{1,0:T(8,128)(2,1)} %get-tuple-element.80.refs_1_.refs_3_), channel_id=1, source_target_pairs={{0,4},{4,0},{8,12},{12,8},{16,20},{20,16},{24,28},{28,24},{1,5},{5... | collective-permute-start | bytes 3145736 | tf_op jit(solution)/shard_map/side_rows_1/ppermute | solution.py:312
  161.4 28.3 %collective-permute-start.6 = (bf16[512,1024]{1,0:T(8,128)(2,1)}, bf16[512,1024]{1,0:T(8,128)(2,1)S(1)}, u32[]{:S(2)}, u32[]{:S(2)}) collective-permute-start(bf16[512,1024]{1,0:T(8,128)(2,1)} %sums_1_0.1), channel_id=1, source_target_pairs={{0,8},{4,12},{24,16},{28,20},{1,9},{5,13},{25,17},{29,21},{2,10},{... | collective-permute-start | bytes 3145736 | tf_op jit(solution)/shard_map/sums_1_0/ppermute | solution.py:520
  167.0 25.8 %collective-permute-start.10 = (bf16[512,1024]{1,0:T(8,128)(2,1)}, bf16[512,1024]{1,0:T(8,128)(2,1)S(1)}, u32[]{:S(2)}, u32[]{:S(2)}) collective-permute-start(bf16[512,1024]{1,0:T(8,128)(2,1)} %collective-permute-done.2.refs_5_), channel_id=1, source_target_pairs={{8,16},{12,20},{16,24},{20,28},{9,17},{13,21},{17,25},{21,29},{10,... | collective-permute-start | bytes 3145736 | tf_op jit(solution)/shard_map/rows_1_0/ppermute | solution.py:304
  167.7 26.5 %collective-permute-start.11 = (bf16[512,1024]{1,0:T(8,128)(2,1)}, bf16[512,1024]{1,0:T(8,128)(2,1)S(1)}, u32[]{:S(2)}, u32[]{:S(2)}) collective-permute-start(bf16[512,1024]{1,0:T(8,128)(2,1)} %collective-permute-done.3.refs_14_), channel_id=1, source_target_pairs={{8,0},{12,4},{16,8},{20,12},{9,1},{13,5},{17,9},{21,13},{10,2},{14... | collective-permute-start | bytes 3145736 | tf_op jit(solution)/shard_map/rows_1_0/ppermute | solution.py:308
  176.5 13.2 %copy-start.25 = (s32[15]{0:T(128)S(1)}, s32[15]{0:T(128)}, u32[]{:S(2)}) copy-start(s32[15]{0:T(128)} %copy-done.24) | copy-start | bytes 184
  184.4 28.2 %collective-permute-start.7 = (bf16[512,1024]{1,0:T(8,128)(2,1)}, bf16[512,1024]{1,0:T(8,128)(2,1)}, u32[]{:S(2)}, u32[]{:S(2)}) collective-permute-start(bf16[512,1024]{1,0:T(8,128)(2,1)} %sums_1_1.1), channel_id=1, source_target_pairs={{0,8},{4,12},{24,16},{28,20},{1,9},{5,13},{25,17},{29,21},{2,10},{... | collective-permute-start | bytes 3145736 | tf_op jit(solution)/shard_map/sums_1_1/ppermute | solution.py:520
  192.8 28.1 %copy-start.10 = (bf16[512,1024]{1,0:T(8,128)(2,1)}, bf16[512,1024]{1,0:T(8,128)(2,1)S(1)}, u32[]{:S(2)}) copy-start(bf16[512,1024]{1,0:T(8,128)(2,1)S(1)} %collective-permute-done.10.up_ref.refs_9_) | copy-start | bytes 3145732
  195.2 22.2 %collective-permute-start.12 = (bf16[512,1024]{1,0:T(8,128)(2,1)}, bf16[512,1024]{1,0:T(8,128)(2,1)S(1)}, u32[]{:S(2)}, u32[]{:S(2)}) collective-permute-start(bf16[512,1024]{1,0:T(8,128)(2,1)} %collective-permute-done.8.refs_5_), channel_id=1, source_target_pairs={{8,16},{12,20},{16,24},{20,28},{9,17},{13,21},{17,25},{21,29},{10,... | collective-permute-start | bytes 3145736 | tf_op jit(solution)/shard_map/rows_1_1/ppermute | solution.py:304
  195.9 24.9 %collective-permute-start.13 = (bf16[512,1024]{1,0:T(8,128)(2,1)}, bf16[512,1024]{1,0:T(8,128)(2,1)S(1)}, u32[]{:S(2)}, u32[]{:S(2)}) collective-permute-start(bf16[512,1024]{1,0:T(8,128)(2,1)} %collective-permute-done.9.refs_14_), channel_id=1, source_target_pairs={{8,0},{12,4},{16,8},{20,12},{9,1},{13,5},{17,9},{21,13},{10,2},{14... | collective-permute-start | bytes 3145736 | tf_op jit(solution)/shard_map/rows_1_1/ppermute | solution.py:308
  197.2 42.3 %collective-permute-start.14 = (bf16[512,1024]{1,0:T(8,128)(2,1)}, bf16[512,1024]{1,0:T(8,128)(2,1)}, u32[]{:S(2)}, u32[]{:S(2)}) collective-permute-start(bf16[512,1024]{1,0:T(8,128)(2,1)} %sums_2_0.1), channel_id=1, source_target_pairs={{0,8},{4,12},{8,16},{12,20},{1,9},{5,13},{9,17},{13,21},{2,10},{6,... | collective-permute-start | bytes 3145736 | tf_op jit(solution)/shard_map/sums_2_0/ppermute | solution.py:522
  203.4 36.2 %collective-permute-start.15 = (bf16[512,1024]{1,0:T(8,128)(2,1)}, bf16[512,1024]{1,0:T(8,128)(2,1)}, u32[]{:S(2)}, u32[]{:S(2)}) collective-permute-start(bf16[512,1024]{1,0:T(8,128)(2,1)} %sums_2_0.1), channel_id=1, source_target_pairs={{16,8},{20,12},{24,16},{28,20},{17,9},{21,13},{25,17},{29,21},{18,... | collective-permute-start | bytes 3145736 | tf_op jit(solution)/shard_map/sums_2_0/ppermute | solution.py:523
  217.4 30.0 %copy-start.8 = (bf16[512,1024]{1,0:T(8,128)(2,1)}, bf16[512,1024]{1,0:T(8,128)(2,1)S(1)}, u32[]{:S(2)}) copy-start(bf16[512,1024]{1,0:T(8,128)(2,1)S(1)} %collective-permute-done.12.up_ref.refs_9_) | copy-start | bytes 3145732
  222.1 25.3 %copy-start.9 = (bf16[512,1024]{1,0:T(8,128)(2,1)}, bf16[512,1024]{1,0:T(8,128)(2,1)S(1)}, u32[]{:S(2)}) copy-start(bf16[512,1024]{1,0:T(8,128)(2,1)S(1)} %collective-permute-done.13.down_ref.refs_10_) | copy-start | bytes 3145732
  223.9 23.5 %collective-permute-start.16 = (bf16[512,1024]{1,0:T(8,128)(2,1)}, bf16[512,1024]{1,0:T(8,128)(2,1)}, u32[]{:S(2)}, u32[]{:S(2)}) collective-permute-start(bf16[512,1024]{1,0:T(8,128)(2,1)} %rows_2_0.1), channel_id=1, source_target_pairs={{16,24},{20,28},{8,0},{12,4},{17,25},{21,29},{9,1},{13,5},{18,26},... | collective-permute-start | bytes 3145736 | tf_op jit(solution)/shard_map/rows_2_0/ppermute | solution.py:478
  228.0 19.4 %copy-start.27 = (s32[15]{0:T(128)S(1)}, s32[15]{0:T(128)}, u32[]{:S(2)}) copy-start(s32[15]{0:T(128)} %copy-done.24) | copy-start | bytes 184
  228.0 47.6 %collective-permute-start.18 = (bf16[512,1024]{1,0:T(8,128)(2,1)}, bf16[512,1024]{1,0:T(8,128)(2,1)}, u32[]{:S(2)}, u32[]{:S(2)}) collective-permute-start(bf16[512,1024]{1,0:T(8,128)(2,1)} %sums_2_1.1), channel_id=1, source_target_pairs={{0,8},{4,12},{8,16},{12,20},{1,9},{5,13},{9,17},{13,21},{2,10},{6,... | collective-permute-start | bytes 3145736 | tf_op jit(solution)/shard_map/sums_2_1/ppermute | solution.py:522
  237.9 38.3 %collective-permute-start.19 = (bf16[512,1024]{1,0:T(8,128)(2,1)}, bf16[512,1024]{1,0:T(8,128)(2,1)}, u32[]{:S(2)}, u32[]{:S(2)}) collective-permute-start(bf16[512,1024]{1,0:T(8,128)(2,1)} %sums_2_1.1), channel_id=1, source_target_pairs={{16,8},{20,12},{24,16},{28,20},{17,9},{21,13},{25,17},{29,21},{18,... | collective-permute-start | bytes 3145736 | tf_op jit(solution)/shard_map/sums_2_1/ppermute | solution.py:523
  249.2 35.0 %collective-permute-start.20 = (bf16[512,1024]{1,0:T(8,128)(2,1)}, bf16[512,1024]{1,0:T(8,128)(2,1)}, u32[]{:S(2)}, u32[]{:S(2)}) collective-permute-start(bf16[512,1024]{1,0:T(8,128)(2,1)} %rows_2_1.1), channel_id=1, source_target_pairs={{16,24},{20,28},{8,0},{12,4},{17,25},{21,29},{9,1},{13,5},{18,26},... | collective-permute-start | bytes 3145736 | tf_op jit(solution)/shard_map/rows_2_1/ppermute | solution.py:478
  253.8 41.9 %collective-permute-start.21 = (bf16[512,1024]{1,0:T(8,128)(2,1)}, bf16[512,1024]{1,0:T(8,128)(2,1)}, u32[]{:S(2)}, u32[]{:S(2)}) collective-permute-start(bf16[512,1024]{1,0:T(8,128)(2,1)} %get-tuple-element.114), channel_id=1, source_target_pairs={{0,8},{4,12},{8,16},{12,20},{16,24},{20,28},{1,9},{5,13},{9,17},{1... | collective-permute-start | bytes 3145736 | tf_op jit(solution)/shard_map/sums_3_0/ppermute | solution.py:522
  264.1 12.1 %copy-start.17 = (bf16[512,1024]{1,0:T(8,128)(2,1)S(1)}, bf16[512,1024]{1,0:T(8,128)(2,1)}, u32[]{:S(2)}) copy-start(bf16[512,1024]{1,0:T(8,128)(2,1)} %get-tuple-element.89.refs_1_) | copy-start | bytes 3145732
  264.1 12.1 %copy-start.28 = (s32[15]{0:T(128)S(1)}, s32[15]{0:T(128)}, u32[]{:S(2)}) copy-start(s32[15]{0:T(128)} %copy-done.24) | copy-start | bytes 184
  264.1 39.7 %collective-permute-start.22 = (bf16[512,1024]{1,0:T(8,128)(2,1)}, bf16[512,1024]{1,0:T(8,128)(2,1)}, u32[]{:S(2)}, u32[]{:S(2)}) collective-permute-start(bf16[512,1024]{1,0:T(8,128)(2,1)} %get-tuple-element.102), channel_id=1, source_target_pairs={{8,0},{12,4},{16,8},{20,12},{24,16},{28,20},{9,1},{13,5},{17,9},{2... | collective-permute-start | bytes 3145736 | tf_op jit(solution)/shard_map/sums_3_0/ppermute | solution.py:523
  275.6 31.2 %collective-permute-start.23 = (bf16[512,1024]{1,0:T(8,128)(2,1)}, bf16[512,1024]{1,0:T(8,128)(2,1)S(1)}, u32[]{:S(2)}, u32[]{:S(2)}) collective-permute-start(bf16[512,1024]{1,0:T(8,128)(2,1)} %get-tuple-element.117), channel_id=1, source_target_pairs={{0,4},{4,0},{8,12},{12,8},{16,20},{20,16},{24,28},{28,24},{1,5},{5... | collective-permute-start | bytes 3145736 | tf_op jit(solution)/shard_map/even_0/ppermute | solution.py:312
  279.5 29.0 %collective-permute-start.24 = (bf16[512,1024]{1,0:T(8,128)(2,1)}, bf16[512,1024]{1,0:T(8,128)(2,1)S(1)}, u32[]{:S(2)}, u32[]{:S(2)}) collective-permute-start(bf16[512,1024]{1,0:T(8,128)(2,1)} %get-tuple-element.121), channel_id=1, source_target_pairs={{0,8},{4,12},{8,16},{12,20},{16,24},{20,28},{1,9},{5,13},{9,17},{1... | collective-permute-start | bytes 3145736 | tf_op jit(solution)/shard_map/sums_3_1/ppermute | solution.py:522
  284.2 13.1 %copy-start.31 = (bf16[256,512]{1,0:T(8,128)(2,1)S(1)}, bf16[256,512]{1,0:T(8,128)(2,1)}, u32[]{:S(2)}) copy-start(bf16[256,512]{1,0:T(8,128)(2,1)} %copy-done.30) | copy-start | bytes 786436
  284.2 13.1 %copy-start.33 = (bf16[256,512]{1,0:T(8,128)(2,1)S(1)}, bf16[256,512]{1,0:T(8,128)(2,1)}, u32[]{:S(2)}) copy-start(bf16[256,512]{1,0:T(8,128)(2,1)} %copy-done.32) | copy-start | bytes 786436
  284.2 33.0 %collective-permute-start.25 = (bf16[512,1024]{1,0:T(8,128)(2,1)}, bf16[512,1024]{1,0:T(8,128)(2,1)S(1)}, u32[]{:S(2)}, u32[]{:S(2)}) collective-permute-start(bf16[512,1024]{1,0:T(8,128)(2,1)} %get-tuple-element.110), channel_id=1, source_target_pairs={{8,0},{12,4},{16,8},{20,12},{24,16},{28,20},{9,1},{13,5},{17,9},{2... | collective-permute-start | bytes 3145736 | tf_op jit(solution)/shard_map/sums_3_1/ppermute | solution.py:523
  295.7 23.4 %collective-permute-start.26 = (bf16[512,1024]{1,0:T(8,128)(2,1)}, bf16[512,1024]{1,0:T(8,128)(2,1)S(1)}, u32[]{:S(2)}, u32[]{:S(2)}) collective-permute-start(bf16[512,1024]{1,0:T(8,128)(2,1)} %get-tuple-element.125), channel_id=1, source_target_pairs={{0,4},{4,0},{8,12},{12,8},{16,20},{20,16},{24,28},{28,24},{1,5},{5... | collective-permute-start | bytes 3145736 | tf_op jit(solution)/shard_map/even_1/ppermute | solution.py:312
  (25 other events, 111.9 us)
Sparse Core Ops, SparseCore 0:
  36.8 21.6 all-gather.4
  60.6 22.5 all-gather.6
  84.8 22.5 all-gather.8
  108.9 34.4 all-gather.10

commit v5 on v4

--- a/solution.py
+++ b/solution.py
@@ -19,7 +19,7 @@
 
 def attend_kernel(pieces, info_ref, *refs):
     states_refs, key_refs, value_refs = refs[:pieces], refs[pieces : 2 * pieces], refs[2 * pieces : 3 * pieces]
-    query_ref, grad_ref, query_grad_ref, rows_grad_ref = refs[3 * pieces :]
+    *partial_refs, query_ref, grad_ref, query_grad_ref, rows_grad_ref = refs[3 * pieces :]
     length = info_ref[0]
     offset = info_ref[1]
     scale = HEAD_DIM ** (-0.5)
@@ -28,15 +28,17 @@
     query_count, block = query_ref.shape
     state_count = states_refs[0].shape[0]
 
-    def project(weight_refs):
+    def project(weight_refs, place):
         total = None
+        for ref in partial_refs:
+            total = ref[:, place * block : (place + 1) * block]
         for states_ref, weight_ref in zip(states_refs, weight_refs):
             weight = weight_ref[...].reshape(-1, block)
             product = jnp.dot(states_ref[...], weight, preferred_element_type=WIDE)
             total = product if total is None else total + product
         return total.astype(LOW)
 
-    key_rows, value_rows = project(key_refs), project(value_refs)
+    key_rows, value_rows = project(key_refs, 0), project(value_refs, 1)
     position = lax.broadcasted_iota(jnp.int32, (query_count, state_count), 1)
     limit = jnp.minimum(
         lax.broadcasted_iota(jnp.int32, (query_count, 1), 0) + (offset + 1), length
@@ -77,10 +79,10 @@
         rows_grad_ref[:, value_columns] = value_grads[head].T.astype(LOW)
 
 
-def attend(rank, info, doc_states, key_weight, value_weight, queries, grads, first, heads):
+def attend(rank, info, states, partial, key_weight, value_weight, queries, grads, first, heads):
     query_count = queries.shape[0]
-    pieces = len(doc_states)
-    state_count, feature_count = doc_states[0].shape
+    numbers = sorted(states)
+    state_count, feature_count = states[numbers[0]].shape
     part_count, _, part_features, _ = key_weight.shape
     pair = 2 if heads % 2 == 0 and first % 2 == 0 else 1
     block = pair * HEAD_DIM
@@ -89,11 +91,15 @@
         pl.BlockSpec(
             (part_count, 1, part_features, block), lambda h, piece=piece: (0, piece, 0, first // pair + h)
         )
-        for piece in range(pieces)
+        for piece in numbers
     ]
     states_spec = pl.BlockSpec(
         (state_count, feature_count), lambda h: (0, 0), pipeline_mode=pl.Buffered(1)
     )
+    pieces = len(numbers)
+    weights = [key_weight] * pieces + [value_weight] * pieces
+    pair_spec = pl.BlockSpec((state_count, 2 * block), lambda h: (0, h))
+    partials = [] if partial is None else [partial]
     return pl.pallas_call(
         lambda *refs: attend_kernel(pieces, *refs),
         grid=(heads // pair,),
@@ -102,20 +108,53 @@
             *[states_spec] * pieces,
             *weight_specs,
             *weight_specs,
+            *[pair_spec] * len(partials),
             pl.BlockSpec((query_count, block), lambda h: (0, first // pair + h)),
             pl.BlockSpec((query_count, block), lambda h: (0, first // pair + h)),
         ],
-        out_specs=[
-            pl.BlockSpec((query_count, block), lambda h: (0, h)),
-            pl.BlockSpec((state_count, 2 * block), lambda h: (0, h)),
-        ],
+        out_specs=[pl.BlockSpec((query_count, block), lambda h: (0, h)), pair_spec],
         out_shape=[
             jax.ShapeDtypeStruct((query_count, width), LOW),
             jax.ShapeDtypeStruct((state_count, 2 * width), LOW),
         ],
         compiler_params=pltpu.CompilerParams(vmem_limit_bytes=40 * 1024 * 1024),
         cost_estimate=cost(rank),
-    )(info, *doc_states, *[key_weight] * pieces, *[value_weight] * pieces, queries, grads)
+    )(info, *[states[number] for number in numbers], *weights, *partials, queries, grads)
+
+
+def project_piece(states, piece, key_weight, value_weight, first, heads):
+    state_count, feature_count = states.shape
+    part_count, _, part_features, _ = key_weight.shape
+    pair = 2 if heads % 2 == 0 and first % 2 == 0 else 1
+    block = pair * HEAD_DIM
+    weight_spec = pl.BlockSpec(
+        (part_count, 1, part_features, block), lambda h: (0, piece, 0, first // pair + h)
+    )
+
+    def body(states_ref, key_ref, value_ref, out_ref):
+        for place, ref in enumerate((key_ref, value_ref)):
+            weight = ref[...].reshape(-1, block)
+            out_ref[:, place * block : (place + 1) * block] = jnp.dot(
+                states_ref[...], weight, preferred_element_type=WIDE
+            )
+
+    return pl.pallas_call(
+        body,
+        grid=(heads // pair,),
+        in_specs=[
+            pl.BlockSpec((state_count, feature_count), lambda h: (0, 0), pipeline_mode=pl.Buffered(1)),
+            weight_spec,
+            weight_spec,
+        ],
+        out_specs=pl.BlockSpec((state_count, 2 * block), lambda h: (0, h)),
+        out_shape=jax.ShapeDtypeStruct((state_count, 2 * heads * HEAD_DIM), WIDE),
+        compiler_params=pltpu.CompilerParams(vmem_limit_bytes=40 * 1024 * 1024),
+        cost_estimate=pl.CostEstimate(
+            flops=4 * state_count * feature_count * heads * HEAD_DIM,
+            bytes_accessed=4 * feature_count * heads * HEAD_DIM,
+            transcendentals=0,
+        ),
+    )(states, key_weight, value_weight)
 
 
 def products(rank, scalars, z_slot, count, terms, rows, slice_width, block):
@@ -379,11 +418,25 @@
                 side_parts.append(turn(wanted, shift))
     with jax.named_scope("gather_states"):
         doc_states = [lax.all_gather(piece, "tp", axis=1, tiled=True) for piece in doc_pieces]
+    weight_shape = (tp_count, pieces, feature_count // (tp_count * pieces), key_weight.shape[1])
+    key_parts, value_parts = key_weight.reshape(weight_shape), value_weight.reshape(weight_shape)
     found = [send_line(doc_states[piece], piece) for piece in range(pieces - 1)]
-    joined = lax.optimization_barrier((*doc_states, *found, *side_parts))
-    doc_states, found, side_parts = (
-        list(joined[:pieces]), list(joined[pieces : 2 * pieces - 1]), joined[2 * pieces - 1 :]
-    )
+    partials = [None] * group_count
+    if pieces == 2:
+        with jax.named_scope("project_first_piece"):
+            for group in range(group_count - 1):
+                partials[group] = project_piece(
+                    doc_states[0], 0, key_parts, value_parts, group * heads, heads
+                )
+    early = [value for value in partials if value is not None]
+    joined = list(lax.optimization_barrier((*doc_states, *found, *side_parts, *early)))
+    doc_states = [joined.pop(0) for _ in doc_states]
+    found = [joined.pop(0) for _ in found]
+    side_parts = [joined.pop(0) for _ in side_parts]
+    if early:
+        partials = [*joined, None]
+    all_states = dict(enumerate(doc_states))
+    late_states = {pieces - 1: doc_states[-1]}
     found.append(send_line(doc_states[-1], pieces - 1))
 
     def gather_line(after):
@@ -431,8 +484,6 @@
         pending.clear()
         return lax.optimization_barrier((table, *others))[0]
 
-    weight_shape = (tp_count, pieces, feature_count // (tp_count * pieces), key_weight.shape[1])
-    key_parts, value_parts = key_weight.reshape(weight_shape), value_weight.reshape(weight_shape)
     query_grads = [None] * group_count
 
     def attend_group(group):
@@ -440,7 +491,8 @@
         with jax.named_scope(f"attend_{group}"):
             info = scalars()
             query_grads[group], latest = attend(
-                rank, info, doc_states, key_parts, value_parts, queries, context_grad,
+                rank, info, all_states if partials[group] is None else late_states, partials[group],
+                key_parts, value_parts, queries, context_grad,
                 group * heads, heads,
             )
             return latest

time: 329 us -> 320 us (0.973)
  waiting for transfers between devices: 55.8 us -> 28.7 us
  starting transfers between devices: 84 us -> 91.9 us
  local copies, waits for them, and re-layouts: 20.4 us -> 26.4 us
  Pallas kernels: 116 us -> 121 us
    pallas_call x0 -> x3, Pallas kernels: none -> 12.8 us  [project_piece(): pl.pallas_call(body, grid=(heads // pair,), in_specs=[pl.BlockSpec((state...]
    pallas_call x4, Pallas kernels: 39.8 us -> 31.2 us  [attend(): pl.pallas_call(lambda *refs: attend_kernel(pieces, *refs), grid=(heads //...]
    ppermute x4, starting transfers between devices: 30.9 us -> 39.1 us  [send_sums(): sums_up[index] = lax.ppermute(up, 'seq', up_pairs)]
    ppermute x5, waiting for transfers between devices: 10.9 us -> 2.98 us  [turn(): return lax.ppermute(value, 'seq', pairs)]
    all_gather x2, waiting for transfers between devices: 7.27 us -> 0.01 us  [shards(): lax.all_gather(piece, 'tp', axis=1, tiled=True)]
    unnamed x82 -> x100, local copies, waits for them, and re-layouts: 13.3 us -> 19.5 us
    ppermute x4, waiting for transfers between devices: 13 us -> 7.91 us  [send_sums(): sums_down[index] = lax.ppermute(down, 'seq', down_pairs)]
    ppermute x4, waiting for transfers between devices: 5.9 us -> 1.29 us  [step_down(): return lax.ppermute(value, 'seq', pairs)]
  transfers between devices with their start and end apart: 32 -> 32, of which waited for: 12 -> 7; matrix products, arithmetic and copies ran while one was open for 5% -> 5% of each run, Pallas kernels for 35% -> 37%
where the time goes in v5:
time: 320 us; the launch traced here: 318 us
  Pallas kernels  121 us (38%)
  starting transfers between devices  91.9 us (29%)
  waiting for transfers between devices  28.7 us (9%)
  local copies, waits for them, and re-layouts  26.4 us (8%)
  blocking collectives  21.4 us (7%)
  between operations  15.2 us (5%)
  other arithmetic  7.38 us (2%)
  matrix products  5.87 us (2%)
    pallas_call x8, Pallas kernels, products(): pl.pallas_call(body, grid_spec=pltpu.PrefetchScalarGridSpec(num_scalar_pr...  53.3 us
    ppermute x4, starting transfers between devices, send_sums(): sums_up[index] = lax.ppermute(up, 'seq', up_pairs)  39.1 us
    pallas_call x4, Pallas kernels, attend(): pl.pallas_call(lambda *refs: attend_kernel(pieces, *refs), grid=(heads //...  31.2 us
    all_to_all x1, blocking collectives, route(): lax.all_to_all(sent, 'seq', split_axis=0, concat_axis=0, tiled=True)  21.4 us
    unnamed x100, local copies, waits for them, and re-layouts  19.5 us
    all_to_all x1, waiting for transfers between devices, route(): lax.all_to_all(sent, 'seq', split_axis=0, concat_axis=0, tiled=True)  14.2 us
    pallas_call x3, Pallas kernels, project_piece(): pl.pallas_call(body, grid=(heads // pair,), in_specs=[pl.BlockSpec((state...  12.8 us
    pallas_call x4, Pallas kernels, add_arrivals(): pl.pallas_call(body, grid_spec=pltpu.PrefetchScalarGridSpec(num_scalar_pr...  11.4 us
  transfers between devices with their start and end apart: 32, of which 7 were waited for; matrix products, arithmetic and copies ran while one was open for 5% of the time, Pallas kernels for 37%

profile of v5, /device:TPU:0, one launch (start us, length us, event | category | flops | bytes accessed | tf_op | source)
XLA Modules:
  0.0 317.6 jit_solution(18170314169591768253)
XLA Ops:
  8.2 2.4 convolution_convert_fusion.1
  10.6 7.4 %all-to-all-start = ((bf16[8,80,512]{2,1,0:T(8,128)(2,1)}), bf16[8,80,512]{2,1,0:T(8,128)(2,1)S(1)}, u32[]{:S(2)}, u32[]{:S(2)}) async-start(bf16[8,80,512]{2,1,0:T(8,128)(2,1)} %bitcast.3), calls=%async_computation | async-start | bytes 1310720 | tf_op jit(solution)/shard_map/route/all_to_all | solution.py:309
  21.0 14.2 %all-to-all-done = bf16[8,80,512]{2,1,0:T(8,128)(2,1)S(1)} async-done(((bf16[8,80,512]{2,1,0:T(8,128)(2,1)}), bf16[8,80,512]{2,1,0:T(8,128)(2,1)S(1)}, u32[]{:S(2)}, u32[]{:S(2)}) %all-to-all-start) | async-done | bytes 655392 | tf_op jit(solution)/shard_map/route/all_to_all | solution.py:309
  37.3 21.4 %all_to_all.24 = bf16[8,80,512]{2,1,0:T(8,128)(2,1)S(1)} all-to-all(bf16[8,80,512]{2,1,0:T(8,128)(2,1)S(1)} %bitcast.42), channel_id=1, replica_groups=mesh['seq'=8,'tp'=4] {'seq'}, dimensions={0} | all-to-all | bytes 1310720 | tf_op jit(solution)/shard_map/route/all_to_all | solution.py:309
  62.8 1.9 constant_dynamic-slice_fusion
  64.7 2.8 collective-permute-start
  67.5 1.7 copy-done
  69.3 4.2 %project_first_piece.3.refs_4_ = f32[512,1024]{1,0:T(8,128)S(1)} custom-call(bf16[512,2048]{1,0:T(8,128)(2,1)S(1)} %copy-done, bf16[4,2,512,2048]{3,2,1,0:T(8,128)(2,1)} %bitcast.24, bf16[4,2,512,2048]{3,2,1,0:T(8,128)(2,1)} %bitcast.32), custom_call_target="tpu_custom_call" | custom-call | flops 2147483648 | bytes 4194304 | tf_op jit(solution)/shard_map/project_first_piece/pallas_call | solution.py:141
  74.8 4.2 %project_first_piece.4.refs_4_ = f32[512,1024]{1,0:T(8,128)S(1)} custom-call(bf16[512,2048]{1,0:T(8,128)(2,1)S(1)} %copy-done, bf16[4,2,512,2048]{3,2,1,0:T(8,128)(2,1)} %bitcast.25, bf16[4,2,512,2048]{3,2,1,0:T(8,128)(2,1)} %bitcast.33), custom_call_target="tpu_custom_call" | custom-call | flops 2147483648 | bytes 4194304 | tf_op jit(solution)/shard_map/project_first_piece/pallas_call | solution.py:141
  80.4 4.3 %project_first_piece.5.refs_4_ = f32[512,1024]{1,0:T(8,128)S(1)} custom-call(bf16[512,2048]{1,0:T(8,128)(2,1)S(1)} %copy-done, bf16[4,2,512,2048]{3,2,1,0:T(8,128)(2,1)} %bitcast.26, bf16[4,2,512,2048]{3,2,1,0:T(8,128)(2,1)} %bitcast.34), custom_call_target="tpu_custom_call" | custom-call | flops 2147483648 | bytes 4194304 | tf_op jit(solution)/shard_map/project_first_piece/pallas_call | solution.py:141
  88.0 2.5 collective-permute-start.17
  92.1 1.7 copy-done.15
  93.8 6.6 %attend_0.1 = (bf16[256,512]{1,0:T(8,128)(2,1)S(1)}, bf16[512,1024]{1,0:T(8,128)(2,1)S(1)}) custom-call(s32[15]{0:T(128)S(1)} %stack.54.refs_0_.scalar_ref, bf16[512,2048]{1,0:T(8,128)(2,1)S(1)} %copy-done.2, bf16[4,2,512,2048]{3,2,1,0:T(8,128)(2,1)} %bitcast.27, bf16[4,2,512,2048]{3,2,1,0:T(8,128)(2,1)} %bitcast.35, f32[512,1024]{1,0:T(8,128)S(1)} %copy-done.15, ...), custom_call_target="tpu_custom_call" | custom-call | bytes 524288 | tf_op jit(solution)/shard_map/attend_0/pallas_call | solution.py:103
  101.4 2.1 collective-permute-done.17
  103.5 2.2 pad_maximum_fusion.1
  105.7 3.7 %collective-permute-start.2 = (bf16[512,1024]{1,0:T(8,128)(2,1)}, bf16[512,1024]{1,0:T(8,128)(2,1)}, u32[]{:S(2)}, u32[]{:S(2)}) collective-permute-start(bf16[512,1024]{1,0:T(8,128)(2,1)} %copy-done.23), channel_id=1, source_target_pairs={{0,8},{4,12},{8,16},{12,20},{16,24},{20,28},{1,9},{5,13},{9,17},{1... | collective-permute-start | bytes 3145736 | tf_op jit(solution)/shard_map/rows_0_0/ppermute | solution.py:343
  113.7 7.4 %attend_2.1 = (bf16[256,512]{1,0:T(8,128)(2,1)S(1)}, bf16[512,1024]{1,0:T(8,128)(2,1)}) custom-call(s32[15]{0:T(128)S(1)} %stack.54.refs_0_.scalar_ref, bf16[512,2048]{1,0:T(8,128)(2,1)S(1)} %copy-done.3, bf16[4,2,512,2048]{3,2,1,0:T(8,128)(2,1)} %bitcast.28, bf16[4,2,512,2048]{3,2,1,0:T(8,128)(2,1)} %bitcast.36, f32[512,1024]{1,0:T(8,128)S(1)} %copy-done.13, ...), custom_call_target="tpu_custom_call" | custom-call | bytes 1048576 | tf_op jit(solution)/shard_map/attend_2/pallas_call | solution.py:103
  121.1 1.7 collective-permute-start.4
  122.8 7.2 %attend_1.1 = (bf16[256,512]{1,0:T(8,128)(2,1)S(1)}, bf16[512,1024]{1,0:T(8,128)(2,1)}) custom-call(s32[15]{0:T(128)S(1)} %stack.54.refs_0_.scalar_ref, bf16[512,2048]{1,0:T(8,128)(2,1)S(1)} %copy-done.4, bf16[4,2,512,2048]{3,2,1,0:T(8,128)(2,1)} %bitcast.29, bf16[4,2,512,2048]{3,2,1,0:T(8,128)(2,1)} %bitcast.37, f32[512,1024]{1,0:T(8,128)S(1)} %copy-done.11, ...), custom_call_target="tpu_custom_call" | custom-call | bytes 1572864 | tf_op jit(solution)/shard_map/attend_1/pallas_call | solution.py:103
  130.7 5.6 %collective-permute-start.8 = (bf16[512,1024]{1,0:T(8,128)(2,1)}, bf16[512,1024]{1,0:T(8,128)(2,1)}, u32[]{:S(2)}, u32[]{:S(2)}) collective-permute-start(bf16[512,1024]{1,0:T(8,128)(2,1)} %get-tuple-element.82.refs_2_), channel_id=1, source_target_pairs={{0,8},{4,12},{8,16},{12,20},{16,24},{20,28},{1,9},{5,13},{9,17},{1... | collective-permute-start | bytes 3145736 | tf_op jit(solution)/shard_map/rows_0_1/ppermute | solution.py:343
  140.2 10.0 %attend_3.1 = (bf16[256,512]{1,0:T(8,128)(2,1)S(1)}, bf16[512,1024]{1,0:T(8,128)(2,1)}) custom-call(s32[15]{0:T(128)S(1)} %stack.54.refs_0_.scalar_ref, bf16[512,2048]{1,0:T(8,128)(2,1)S(1)} %copy-done.1, bf16[512,2048]{1,0:T(8,128)(2,1)S(1)} %copy-done.5, bf16[4,2,512,2048]{3,2,1,0:T(8,128)(2,1)} %bitcast.30, bf16[4,2,512,2048]{3,2,1,0:T(8,128)(2,1)} %bitcast.31, ...), custom_call_target="tpu_custom_call" | custom-call | bytes 2097152 | tf_op jit(solution)/shard_map/attend_3/pallas_call | solution.py:103
  152.4 4.5 %sums_1_0.1 = bf16[512,1024]{1,0:T(8,128)(2,1)} custom-call(s32[15]{0:T(128)} %copy-done.32, bf16[512,2048]{1,0:T(8,128)(2,1)} %broadcast_select_fusion.refs_0_.refs_1_.refs_2_, bf16[512,1024]{1,0:T(8,128)(2,1)} %get-tuple-element.77.refs_1_.refs_3_, bf16[2048,512]{1,0:T(8,128)(2,1)} %all-gather.9.cloned.1.call-done.refs_2_.refs_4_.refs_5_.refs_6_, ...), custom_call_target="tpu_custom_call" | custom-call | bytes 2621440 | tf_op jit(solution)/shard_map/sums_1_0/pallas_call | solution.py:187
  156.9 4.6 %collective-permute-start.6 = (bf16[512,1024]{1,0:T(8,128)(2,1)}, bf16[512,1024]{1,0:T(8,128)(2,1)S(1)}, u32[]{:S(2)}, u32[]{:S(2)}) collective-permute-start(bf16[512,1024]{1,0:T(8,128)(2,1)} %sums_1_0.1), channel_id=1, source_target_pairs={{0,8},{4,12},{24,16},{28,20},{1,9},{5,13},{25,17},{29,21},{2,10},{... | collective-permute-start | bytes 3145736 | tf_op jit(solution)/shard_map/sums_1_0/ppermute | solution.py:572
  163.6 7.4 %side_ahead_0.1 = (bf16[512,1024]{1,0:T(8,128)(2,1)}, bf16[512,1024]{1,0:T(8,128)(2,1)}, bf16[512,1024]{1,0:T(8,128)(2,1)}) custom-call(s32[15]{0:T(128)} %copy-done.32, bf16[512,2048]{1,0:T(8,128)(2,1)} %broadcast_select_fusion.refs_0_.refs_1_.refs_2_, bf16[512,2048]{1,0:T(8,128)(2,1)} %broadcast_select_fusion.refs_0_.refs_1_.refs_2_, ...), custom_call_target="tpu_custom_call" | custom-call | tf_op jit(solution)/shard_map/side_ahead_0/pallas_call | solution.py:187
  171.0 3.0 collective-permute-done.5.refs_3_.refs_7_
  174.0 4.6 %sums_1_1.1 = bf16[512,1024]{1,0:T(8,128)(2,1)} custom-call(s32[15]{0:T(128)} %copy-done.32, bf16[512,2048]{1,0:T(8,128)(2,1)} %broadcast_select_fusion.refs_0_.refs_1_.refs_2_, bf16[512,1024]{1,0:T(8,128)(2,1)} %get-tuple-element.86.refs_1_.refs_3_, bf16[2048,512]{1,0:T(8,128)(2,1)} %all-gather.9.cloned.1.call-done.refs_2_.refs_4_.refs_5_.refs_6_, ...), custom_call_target="tpu_custom_call" | custom-call | bytes 3670016 | tf_op jit(solution)/shard_map/sums_1_1/pallas_call | solution.py:187
  178.6 5.3 %collective-permute-start.7 = (bf16[512,1024]{1,0:T(8,128)(2,1)}, bf16[512,1024]{1,0:T(8,128)(2,1)}, u32[]{:S(2)}, u32[]{:S(2)}) collective-permute-start(bf16[512,1024]{1,0:T(8,128)(2,1)} %sums_1_1.1), channel_id=1, source_target_pairs={{0,8},{4,12},{24,16},{28,20},{1,9},{5,13},{25,17},{29,21},{2,10},{... | collective-permute-start | bytes 3145736 | tf_op jit(solution)/shard_map/sums_1_1/ppermute | solution.py:572
  185.1 1.9 sums_2_0.1
  190.0 8.5 %collective-permute-start.14 = (bf16[512,1024]{1,0:T(8,128)(2,1)}, bf16[512,1024]{1,0:T(8,128)(2,1)}, u32[]{:S(2)}, u32[]{:S(2)}) collective-permute-start(bf16[512,1024]{1,0:T(8,128)(2,1)} %sums_2_0.1), channel_id=1, source_target_pairs={{0,8},{4,12},{8,16},{12,20},{1,9},{5,13},{9,17},{13,21},{2,10},{6,... | collective-permute-start | bytes 3145736 | tf_op jit(solution)/shard_map/sums_2_0/ppermute | solution.py:574
  200.2 7.4 %side_ahead_1.1 = (bf16[512,1024]{1,0:T(8,128)(2,1)}, bf16[512,1024]{1,0:T(8,128)(2,1)}, bf16[512,1024]{1,0:T(8,128)(2,1)}) custom-call(s32[15]{0:T(128)} %copy-done.32, bf16[512,2048]{1,0:T(8,128)(2,1)} %broadcast_select_fusion.refs_0_.refs_1_.refs_2_, bf16[512,2048]{1,0:T(8,128)(2,1)} %broadcast_select_fusion.refs_0_.refs_1_.refs_2_, ...), custom_call_target="tpu_custom_call" | custom-call | tf_op jit(solution)/shard_map/side_ahead_1/pallas_call | solution.py:187
  207.6 4.7 %side_own_1.1.refs_0_ = bf16[512,1024]{1,0:T(8,128)(2,1)} custom-call(s32[15]{0:T(128)} %copy-done.32, bf16[512,2048]{1,0:T(8,128)(2,1)} %broadcast_select_fusion.refs_0_.refs_1_.refs_2_, bf16[512,1024]{1,0:T(8,128)(2,1)} %get-tuple-element.86.refs_1_.refs_3_, bf16[2048,512]{1,0:T(8,128)(2,1)} %all-gather.9.cloned.1.call-done.refs_2_.refs_4_.refs_5_.refs_6_, ...), custom_call_target="tpu_custom_call" | custom-call | bytes 5242880 | tf_op jit(solution)/shard_map/side_own_1/pallas_call | solution.py:187
  214.8 1.8 rows_2_0.1
  217.9 2.8 sums_2_1.1
  220.6 12.4 %collective-permute-start.18 = (bf16[512,1024]{1,0:T(8,128)(2,1)}, bf16[512,1024]{1,0:T(8,128)(2,1)}, u32[]{:S(2)}, u32[]{:S(2)}) collective-permute-start(bf16[512,1024]{1,0:T(8,128)(2,1)} %sums_2_1.1), channel_id=1, source_target_pairs={{0,8},{4,12},{8,16},{12,20},{1,9},{5,13},{9,17},{13,21},{2,10},{6,... | collective-permute-start | bytes 3145736 | tf_op jit(solution)/shard_map/sums_2_1/ppermute | solution.py:574
  234.7 4.5 %side_own_0.1.refs_0_ = bf16[512,1024]{1,0:T(8,128)(2,1)} custom-call(s32[15]{0:T(128)} %copy-done.32, bf16[512,2048]{1,0:T(8,128)(2,1)} %broadcast_select_fusion.refs_0_.refs_1_.refs_2_, bf16[512,1024]{1,0:T(8,128)(2,1)} %get-tuple-element.77.refs_1_.refs_3_, bf16[2048,512]{1,0:T(8,128)(2,1)} %all-gather.9.cloned.1.call-done.refs_2_.refs_4_.refs_5_.refs_6_, ...), custom_call_target="tpu_custom_call" | custom-call | bytes 6815744 | tf_op jit(solution)/shard_map/side_own_0/pallas_call | solution.py:187
  239.3 1.7 rows_2_1.1
  242.3 3.4 %sums_3_0.1 = (bf16[512,1024]{1,0:T(8,128)(2,1)}, bf16[512,1024]{1,0:T(8,128)(2,1)}) custom-call(s32[15]{0:T(128)S(1)} %copy-done.35, bf16[512,1024]{1,0:T(8,128)(2,1)S(1)} %copy-done.26, bf16[512,1024]{1,0:T(8,128)(2,1)S(1)} %copy-done.27, bf16[512,1024]{1,0:T(8,128)(2,1)} %collective-permute-done.14.refs_2_, bf16[512,1024]{1,0:T(8,128)(2,1)} %collective-permute-done.15.refs_3_), custom_call_target="tpu_custom_call" | custom-call | bytes 7864320 | tf_op jit(solution)/shard_map/sums_3_0/pallas_call | solution.py:210
  245.7 13.6 %collective-permute-start.21 = (bf16[512,1024]{1,0:T(8,128)(2,1)}, bf16[512,1024]{1,0:T(8,128)(2,1)}, u32[]{:S(2)}, u32[]{:S(2)}) collective-permute-start(bf16[512,1024]{1,0:T(8,128)(2,1)} %get-tuple-element.120), channel_id=1, source_target_pairs={{0,8},{4,12},{8,16},{12,20},{16,24},{20,28},{1,9},{5,13},{9,17},{1... | collective-permute-start | bytes 3145736 | tf_op jit(solution)/shard_map/sums_3_0/ppermute | solution.py:574
  260.8 10.1 %even_0.1 = (bf16[512,1024]{1,0:T(8,128)(2,1)}, bf16[512,1024]{1,0:T(8,128)(2,1)}) custom-call(s32[15]{0:T(128)} %copy-done.32, bf16[2048,1024]{1,0:T(8,128)(2,1)} %all-gather.11.cloned.1.call-done.refs_0_.refs_1_.refs_3_.refs_4_.refs_7_.refs_8_.refs_11_.refs_12_, ...), custom_call_target="tpu_custom_call" | custom-call | bytes 8388608 | tf_op jit(solution)/shard_map/even_0/pallas_call | solution.py:187
  271.5 3.4 %sums_3_1.1 = (bf16[512,1024]{1,0:T(8,128)(2,1)}, bf16[512,1024]{1,0:T(8,128)(2,1)}) custom-call(s32[15]{0:T(128)S(1)} %copy-done.36, bf16[512,1024]{1,0:T(8,128)(2,1)S(1)} %copy-done.24, bf16[512,1024]{1,0:T(8,128)(2,1)S(1)} %copy-done.25, bf16[512,1024]{1,0:T(8,128)(2,1)} %collective-permute-done.18.refs_2_, bf16[512,1024]{1,0:T(8,128)(2,1)} %collective-permute-done.19.refs_3_), custom_call_target="tpu_custom_call" | custom-call | bytes 8912896 | tf_op jit(solution)/shard_map/sums_3_1/pallas_call | solution.py:210
  274.9 4.6 %collective-permute-start.24 = (bf16[512,1024]{1,0:T(8,128)(2,1)}, bf16[512,1024]{1,0:T(8,128)(2,1)S(1)}, u32[]{:S(2)}, u32[]{:S(2)}) collective-permute-start(bf16[512,1024]{1,0:T(8,128)(2,1)} %get-tuple-element.127), channel_id=1, source_target_pairs={{0,8},{4,12},{8,16},{12,20},{16,24},{20,28},{1,9},{5,13},{9,17},{1... | collective-permute-start | bytes 3145736 | tf_op jit(solution)/shard_map/sums_3_1/ppermute | solution.py:574
  281.0 10.0 %even_1.1 = (bf16[512,1024]{1,0:T(8,128)(2,1)}, bf16[512,1024]{1,0:T(8,128)(2,1)}) custom-call(s32[15]{0:T(128)} %copy-done.32, bf16[2048,1024]{1,0:T(8,128)(2,1)} %all-gather.11.cloned.1.call-done.refs_0_.refs_1_.refs_3_.refs_4_.refs_7_.refs_8_.refs_11_.refs_12_, ...), custom_call_target="tpu_custom_call" | custom-call | bytes 9437184 | tf_op jit(solution)/shard_map/even_1/pallas_call | solution.py:187
  292.6 2.0 pad_maximum_fusion
  296.3 3.0 finish_2.1
  299.3 1.7 finish_0.1
  301.1 6.3 %collective-permute-done.25.refs_2_ = bf16[512,1024]{1,0:T(8,128)(2,1)S(1)} collective-permute-done((bf16[512,1024]{1,0:T(8,128)(2,1)}, bf16[512,1024]{1,0:T(8,128)(2,1)S(1)}, u32[]{:S(2)}, u32[]{:S(2)}) %collective-permute-start.25) | collective-permute-done | bytes 1048608 | tf_op jit(solution)/shard_map/sums_3_1/ppermute | solution.py:575
  307.4 1.9 finish_3.1
  309.3 1.7 finish_1.1
  (169 shorter events, 50.1 us)
Async XLA Ops:
  10.6 26.1 %copy-start.46 = (bf16[512,1024]{1,0:T(8,128)(2,1)S(1)}, bf16[512,1024]{1,0:T(8,128)(2,1)}, u32[]{:S(2)}) copy-start(bf16[512,1024]{1,0:T(8,128)(2,1)} %param.11) | copy-start | bytes 3145732
  10.6 24.7 %all-to-all-start = ((bf16[8,80,512]{2,1,0:T(8,128)(2,1)}), bf16[8,80,512]{2,1,0:T(8,128)(2,1)S(1)}, u32[]{:S(2)}, u32[]{:S(2)}) async-start(bf16[8,80,512]{2,1,0:T(8,128)(2,1)} %bitcast.3), calls=%async_computation | async-start | bytes 1310720 | tf_op jit(solution)/shard_map/route/all_to_all | solution.py:309
  18.0 44.9 %all-gather.5.cloned.1.call-start = ((), (), s32[]{:S(2)}) async-start(), calls=%async_computation.2 | async-start | bytes 2621440 | tf_op jit(solution)/shard_map/gather_states/all_gather | solution.py:420
  21.0 118.2 %copy-start.32 = (s32[15]{0:T(128)}, s32[15]{0:T(128)S(1)}, u32[]{:S(2)}) copy-start(s32[15]{0:T(128)S(1)} %stack.54.refs_0_.scalar_ref) | copy-start | bytes 184
  36.7 49.4 %all-gather.7.cloned.1.call-start = ((), (), s32[]{:S(2)}) async-start(), calls=%async_computation.3 | async-start | bytes 2621440 | tf_op jit(solution)/shard_map/gather_states/all_gather | solution.py:420
  37.3 22.9 %copy-start.49 = (s32[4]{0:T(128)S(1)}, s32[4]{0:T(128)}, u32[]{:S(2)}) copy-start(s32[4]{0:T(128)} %constant.152.clone) | copy-start | bytes 52
  37.3 24.2 %copy-start.43 = (bf16[512,512]{1,0:T(8,128)(2,1)S(1)}, bf16[512,512]{1,0:T(8,128)(2,1)}, u32[]{:S(2)}) copy-start(bf16[512,512]{1,0:T(8,128)(2,1)} %fusion.2) | copy-start | bytes 1572868
  60.1 92.2 %all-gather.9.cloned.1.call-start = ((), (), s32[]{:S(2)}) async-start(), calls=%async_computation.4 | async-start | bytes 2621440 | tf_op jit(solution)/shard_map/side_states/all_gather | solution.py:460
  62.7 23.3 %collective-permute-start.1 = (bf16[512,512]{1,0:T(8,128)(2,1)S(1)}, bf16[512,512]{1,0:T(8,128)(2,1)S(1)}, u32[]{:S(2)}, u32[]{:S(2)}) collective-permute-start(bf16[512,512]{1,0:T(8,128)(2,1)S(1)} %fusion.8), channel_id=1, source_target_pairs={{0,4},{4,0},{8,12},{12,8},{16,20},{20,16},{24,28},{28,24},{1,5},{5... | collective-permute-start | bytes 1572872 | tf_op jit(solution)/shard_map/side_states/ppermute | solution.py:351
  64.7 21.4 %collective-permute-start = (bf16[512,512]{1,0:T(8,128)(2,1)}, bf16[512,512]{1,0:T(8,128)(2,1)}, u32[]{:S(2)}, u32[]{:S(2)}) collective-permute-start(bf16[512,512]{1,0:T(8,128)(2,1)} %constant_dynamic-slice_fusion), channel_id=1, source_target_pairs={{0,8},{1,25},{2,18},{3,3},{4,12},{5,29},{6,22},{7,7},{8,16},{9,1},... | collective-permute-start | bytes 1572872 | tf_op jit(solution)/shard_map/line_states_0/ppermute | solution.py:409
  86.9 173.9 %all-gather.11.cloned.1.call-start = ((), (), s32[]{:S(2)}) async-start(), calls=%async_computation.5 | async-start | bytes 5242880 | tf_op jit(solution)/shard_map/line_states/all_gather | solution.py:450
  88.0 15.4 %collective-permute-start.17 = (bf16[512,512]{1,0:T(8,128)(2,1)S(1)}, bf16[512,512]{1,0:T(8,128)(2,1)S(1)}, u32[]{:S(2)}, u32[]{:S(2)}) collective-permute-start(bf16[512,512]{1,0:T(8,128)(2,1)S(1)} %constant_dynamic-slice_fusion.1), channel_id=1, source_target_pairs={{0,8},{1,25},{2,18},{3,3},{4,12},{5,29},{6,22},{7,7},{8,16},{9,1},... | collective-permute-start | bytes 1572872 | tf_op jit(solution)/shard_map/line_states_1/ppermute | solution.py:409
  105.7 17.2 %copy-start.4 = (bf16[512,2048]{1,0:T(8,128)(2,1)S(1)}, bf16[512,2048]{1,0:T(8,128)(2,1)}, u32[]{:S(2)}) copy-start(bf16[512,2048]{1,0:T(8,128)(2,1)} %all-gather.7.cloned.1.call-done.refs_1_.refs_2_) | copy-start | bytes 6291460
  105.7 33.6 %collective-permute-start.2 = (bf16[512,1024]{1,0:T(8,128)(2,1)}, bf16[512,1024]{1,0:T(8,128)(2,1)}, u32[]{:S(2)}, u32[]{:S(2)}) collective-permute-start(bf16[512,1024]{1,0:T(8,128)(2,1)} %copy-done.23), channel_id=1, source_target_pairs={{0,8},{4,12},{8,16},{12,20},{16,24},{20,28},{1,9},{5,13},{9,17},{1... | collective-permute-start | bytes 3145736 | tf_op jit(solution)/shard_map/rows_0_0/ppermute | solution.py:343
  109.4 29.9 %collective-permute-start.3 = (bf16[512,1024]{1,0:T(8,128)(2,1)}, bf16[512,1024]{1,0:T(8,128)(2,1)}, u32[]{:S(2)}, u32[]{:S(2)}) collective-permute-start(bf16[512,1024]{1,0:T(8,128)(2,1)} %copy-done.23), channel_id=1, source_target_pairs={{8,0},{12,4},{16,8},{20,12},{24,16},{28,20},{9,1},{13,5},{17,9},{2... | collective-permute-start | bytes 3145736 | tf_op jit(solution)/shard_map/rows_0_0/ppermute | solution.py:347
  121.1 16.5 %copy-start.1 = (bf16[512,2048]{1,0:T(8,128)(2,1)S(1)}, bf16[512,2048]{1,0:T(8,128)(2,1)}, u32[]{:S(2)}) copy-start(bf16[512,2048]{1,0:T(8,128)(2,1)} %all-gather.5.cloned.1.call-done.states_ref.refs_1_) | copy-start | bytes 6291460
  121.1 31.2 %collective-permute-start.4 = (bf16[512,1024]{1,0:T(8,128)(2,1)}, bf16[512,1024]{1,0:T(8,128)(2,1)}, u32[]{:S(2)}, u32[]{:S(2)}) collective-permute-start(bf16[512,1024]{1,0:T(8,128)(2,1)} %get-tuple-element.77.refs_1_.refs_3_), channel_id=1, source_target_pairs={{0,4},{4,0},{8,12},{12,8},{16,20},{20,16},{24,28},{28,24},{1,5},{5... | collective-permute-start | bytes 3145736 | tf_op jit(solution)/shard_map/side_rows_0/ppermute | solution.py:351
  130.7 30.8 %collective-permute-start.8 = (bf16[512,1024]{1,0:T(8,128)(2,1)}, bf16[512,1024]{1,0:T(8,128)(2,1)}, u32[]{:S(2)}, u32[]{:S(2)}) collective-permute-start(bf16[512,1024]{1,0:T(8,128)(2,1)} %get-tuple-element.82.refs_2_), channel_id=1, source_target_pairs={{0,8},{4,12},{8,16},{12,20},{16,24},{20,28},{1,9},{5,13},{9,17},{1... | collective-permute-start | bytes 3145736 | tf_op jit(solution)/shard_map/rows_0_1/ppermute | solution.py:343
  136.3 25.2 %collective-permute-start.9 = (bf16[512,1024]{1,0:T(8,128)(2,1)}, bf16[512,1024]{1,0:T(8,128)(2,1)}, u32[]{:S(2)}, u32[]{:S(2)}) collective-permute-start(bf16[512,1024]{1,0:T(8,128)(2,1)} %get-tuple-element.82.refs_2_), channel_id=1, source_target_pairs={{8,0},{12,4},{16,8},{20,12},{24,16},{28,20},{9,1},{13,5},{17,9},{2... | collective-permute-start | bytes 3145736 | tf_op jit(solution)/shard_map/rows_0_1/ppermute | solution.py:347
  151.0 23.0 %collective-permute-start.5 = (bf16[512,1024]{1,0:T(8,128)(2,1)}, bf16[512,1024]{1,0:T(8,128)(2,1)}, u32[]{:S(2)}, u32[]{:S(2)}) collective-permute-start(bf16[512,1024]{1,0:T(8,128)(2,1)} %get-tuple-element.86.refs_1_.refs_3_), channel_id=1, source_target_pairs={{0,4},{4,0},{8,12},{12,8},{16,20},{20,16},{24,28},{28,24},{1,5},{5... | collective-permute-start | bytes 3145736 | tf_op jit(solution)/shard_map/side_rows_1/ppermute | solution.py:351
  156.9 27.0 %collective-permute-start.6 = (bf16[512,1024]{1,0:T(8,128)(2,1)}, bf16[512,1024]{1,0:T(8,128)(2,1)S(1)}, u32[]{:S(2)}, u32[]{:S(2)}) collective-permute-start(bf16[512,1024]{1,0:T(8,128)(2,1)} %sums_1_0.1), channel_id=1, source_target_pairs={{0,8},{4,12},{24,16},{28,20},{1,9},{5,13},{25,17},{29,21},{2,10},{... | collective-permute-start | bytes 3145736 | tf_op jit(solution)/shard_map/sums_1_0/ppermute | solution.py:572
  161.5 25.4 %collective-permute-start.10 = (bf16[512,1024]{1,0:T(8,128)(2,1)}, bf16[512,1024]{1,0:T(8,128)(2,1)S(1)}, u32[]{:S(2)}, u32[]{:S(2)}) collective-permute-start(bf16[512,1024]{1,0:T(8,128)(2,1)} %collective-permute-done.2.refs_5_), channel_id=1, source_target_pairs={{8,16},{12,20},{16,24},{20,28},{9,17},{13,21},{17,25},{21,29},{10,... | collective-permute-start | bytes 3145736 | tf_op jit(solution)/shard_map/rows_1_0/ppermute | solution.py:343
  162.3 24.7 %collective-permute-start.11 = (bf16[512,1024]{1,0:T(8,128)(2,1)}, bf16[512,1024]{1,0:T(8,128)(2,1)S(1)}, u32[]{:S(2)}, u32[]{:S(2)}) collective-permute-start(bf16[512,1024]{1,0:T(8,128)(2,1)} %collective-permute-done.3.refs_14_), channel_id=1, source_target_pairs={{8,0},{12,4},{16,8},{20,12},{9,1},{13,5},{17,9},{21,13},{10,2},{14... | collective-permute-start | bytes 3145736 | tf_op jit(solution)/shard_map/rows_1_0/ppermute | solution.py:347
  171.0 12.9 %copy-start.33 = (s32[15]{0:T(128)S(1)}, s32[15]{0:T(128)}, u32[]{:S(2)}) copy-start(s32[15]{0:T(128)} %copy-done.32) | copy-start | bytes 184
  178.6 29.0 %collective-permute-start.7 = (bf16[512,1024]{1,0:T(8,128)(2,1)}, bf16[512,1024]{1,0:T(8,128)(2,1)}, u32[]{:S(2)}, u32[]{:S(2)}) collective-permute-start(bf16[512,1024]{1,0:T(8,128)(2,1)} %sums_1_1.1), channel_id=1, source_target_pairs={{0,8},{4,12},{24,16},{28,20},{1,9},{5,13},{25,17},{29,21},{2,10},{... | collective-permute-start | bytes 3145736 | tf_op jit(solution)/shard_map/sums_1_1/ppermute | solution.py:572
  187.0 26.6 %copy-start.18 = (bf16[512,1024]{1,0:T(8,128)(2,1)}, bf16[512,1024]{1,0:T(8,128)(2,1)S(1)}, u32[]{:S(2)}) copy-start(bf16[512,1024]{1,0:T(8,128)(2,1)S(1)} %collective-permute-done.10.up_ref.refs_9_) | copy-start | bytes 3145732
  188.0 24.3 %collective-permute-start.12 = (bf16[512,1024]{1,0:T(8,128)(2,1)}, bf16[512,1024]{1,0:T(8,128)(2,1)S(1)}, u32[]{:S(2)}, u32[]{:S(2)}) collective-permute-start(bf16[512,1024]{1,0:T(8,128)(2,1)} %collective-permute-done.8.refs_5_), channel_id=1, source_target_pairs={{8,16},{12,20},{16,24},{20,28},{9,17},{13,21},{17,25},{21,29},{10,... | collective-permute-start | bytes 3145736 | tf_op jit(solution)/shard_map/rows_1_1/ppermute | solution.py:343
  188.7 24.8 %collective-permute-start.13 = (bf16[512,1024]{1,0:T(8,128)(2,1)}, bf16[512,1024]{1,0:T(8,128)(2,1)S(1)}, u32[]{:S(2)}, u32[]{:S(2)}) collective-permute-start(bf16[512,1024]{1,0:T(8,128)(2,1)} %collective-permute-done.9.refs_14_), channel_id=1, source_target_pairs={{8,0},{12,4},{16,8},{20,12},{9,1},{13,5},{17,9},{21,13},{10,2},{14... | collective-permute-start | bytes 3145736 | tf_op jit(solution)/shard_map/rows_1_1/ppermute | solution.py:347
  190.0 44.6 %collective-permute-start.14 = (bf16[512,1024]{1,0:T(8,128)(2,1)}, bf16[512,1024]{1,0:T(8,128)(2,1)}, u32[]{:S(2)}, u32[]{:S(2)}) collective-permute-start(bf16[512,1024]{1,0:T(8,128)(2,1)} %sums_2_0.1), channel_id=1, source_target_pairs={{0,8},{4,12},{8,16},{12,20},{1,9},{5,13},{9,17},{13,21},{2,10},{6,... | collective-permute-start | bytes 3145736 | tf_op jit(solution)/shard_map/sums_2_0/ppermute | solution.py:574
  198.5 36.1 %collective-permute-start.15 = (bf16[512,1024]{1,0:T(8,128)(2,1)}, bf16[512,1024]{1,0:T(8,128)(2,1)}, u32[]{:S(2)}, u32[]{:S(2)}) collective-permute-start(bf16[512,1024]{1,0:T(8,128)(2,1)} %sums_2_0.1), channel_id=1, source_target_pairs={{16,8},{20,12},{24,16},{28,20},{17,9},{21,13},{25,17},{29,21},{18,... | collective-permute-start | bytes 3145736 | tf_op jit(solution)/shard_map/sums_2_0/ppermute | solution.py:575
  212.3 27.0 %copy-start.16 = (bf16[512,1024]{1,0:T(8,128)(2,1)}, bf16[512,1024]{1,0:T(8,128)(2,1)S(1)}, u32[]{:S(2)}) copy-start(bf16[512,1024]{1,0:T(8,128)(2,1)S(1)} %collective-permute-done.12.up_ref.refs_9_) | copy-start | bytes 3145732
  214.8 24.5 %copy-start.17 = (bf16[512,1024]{1,0:T(8,128)(2,1)}, bf16[512,1024]{1,0:T(8,128)(2,1)S(1)}, u32[]{:S(2)}) copy-start(bf16[512,1024]{1,0:T(8,128)(2,1)S(1)} %collective-permute-done.13.down_ref.refs_10_) | copy-start | bytes 3145732
  216.6 22.7 %collective-permute-start.16 = (bf16[512,1024]{1,0:T(8,128)(2,1)}, bf16[512,1024]{1,0:T(8,128)(2,1)}, u32[]{:S(2)}, u32[]{:S(2)}) collective-permute-start(bf16[512,1024]{1,0:T(8,128)(2,1)} %rows_2_0.1), channel_id=1, source_target_pairs={{16,24},{20,28},{8,0},{12,4},{17,25},{21,29},{9,1},{13,5},{18,26},... | collective-permute-start | bytes 3145736 | tf_op jit(solution)/shard_map/rows_2_0/ppermute | solution.py:530
  220.6 18.7 %copy-start.35 = (s32[15]{0:T(128)S(1)}, s32[15]{0:T(128)}, u32[]{:S(2)}) copy-start(s32[15]{0:T(128)} %copy-done.32) | copy-start | bytes 184
  220.6 50.3 %collective-permute-start.18 = (bf16[512,1024]{1,0:T(8,128)(2,1)}, bf16[512,1024]{1,0:T(8,128)(2,1)}, u32[]{:S(2)}, u32[]{:S(2)}) collective-permute-start(bf16[512,1024]{1,0:T(8,128)(2,1)} %sums_2_1.1), channel_id=1, source_target_pairs={{0,8},{4,12},{8,16},{12,20},{1,9},{5,13},{9,17},{13,21},{2,10},{6,... | collective-permute-start | bytes 3145736 | tf_op jit(solution)/shard_map/sums_2_1/ppermute | solution.py:574
  233.0 38.5 %collective-permute-start.19 = (bf16[512,1024]{1,0:T(8,128)(2,1)}, bf16[512,1024]{1,0:T(8,128)(2,1)}, u32[]{:S(2)}, u32[]{:S(2)}) collective-permute-start(bf16[512,1024]{1,0:T(8,128)(2,1)} %sums_2_1.1), channel_id=1, source_target_pairs={{16,8},{20,12},{24,16},{28,20},{17,9},{21,13},{25,17},{29,21},{18,... | collective-permute-start | bytes 3145736 | tf_op jit(solution)/shard_map/sums_2_1/ppermute | solution.py:575
  241.0 38.5 %collective-permute-start.20 = (bf16[512,1024]{1,0:T(8,128)(2,1)}, bf16[512,1024]{1,0:T(8,128)(2,1)}, u32[]{:S(2)}, u32[]{:S(2)}) collective-permute-start(bf16[512,1024]{1,0:T(8,128)(2,1)} %rows_2_1.1), channel_id=1, source_target_pairs={{16,24},{20,28},{8,0},{12,4},{17,25},{21,29},{9,1},{13,5},{18,26},... | collective-permute-start | bytes 3145736 | tf_op jit(solution)/shard_map/rows_2_1/ppermute | solution.py:530
  245.7 45.3 %collective-permute-start.21 = (bf16[512,1024]{1,0:T(8,128)(2,1)}, bf16[512,1024]{1,0:T(8,128)(2,1)}, u32[]{:S(2)}, u32[]{:S(2)}) collective-permute-start(bf16[512,1024]{1,0:T(8,128)(2,1)} %get-tuple-element.120), channel_id=1, source_target_pairs={{0,8},{4,12},{8,16},{12,20},{16,24},{20,28},{1,9},{5,13},{9,17},{1... | collective-permute-start | bytes 3145736 | tf_op jit(solution)/shard_map/sums_3_0/ppermute | solution.py:574
  259.3 12.2 %copy-start.24 = (bf16[512,1024]{1,0:T(8,128)(2,1)S(1)}, bf16[512,1024]{1,0:T(8,128)(2,1)}, u32[]{:S(2)}) copy-start(bf16[512,1024]{1,0:T(8,128)(2,1)} %get-tuple-element.115.refs_0_) | copy-start | bytes 3145732
  259.3 12.2 %copy-start.25 = (bf16[512,1024]{1,0:T(8,128)(2,1)S(1)}, bf16[512,1024]{1,0:T(8,128)(2,1)}, u32[]{:S(2)}) copy-start(bf16[512,1024]{1,0:T(8,128)(2,1)} %get-tuple-element.95.refs_1_) | copy-start | bytes 3145732
  259.3 12.2 %copy-start.36 = (s32[15]{0:T(128)S(1)}, s32[15]{0:T(128)}, u32[]{:S(2)}) copy-start(s32[15]{0:T(128)} %copy-done.32) | copy-start | bytes 184
  259.4 36.9 %collective-permute-start.22 = (bf16[512,1024]{1,0:T(8,128)(2,1)}, bf16[512,1024]{1,0:T(8,128)(2,1)}, u32[]{:S(2)}, u32[]{:S(2)}) collective-permute-start(bf16[512,1024]{1,0:T(8,128)(2,1)} %get-tuple-element.108), channel_id=1, source_target_pairs={{8,0},{12,4},{16,8},{20,12},{24,16},{28,20},{9,1},{13,5},{17,9},{2... | collective-permute-start | bytes 3145736 | tf_op jit(solution)/shard_map/sums_3_0/ppermute | solution.py:575
  270.9 28.4 %collective-permute-start.23 = (bf16[512,1024]{1,0:T(8,128)(2,1)}, bf16[512,1024]{1,0:T(8,128)(2,1)S(1)}, u32[]{:S(2)}, u32[]{:S(2)}) collective-permute-start(bf16[512,1024]{1,0:T(8,128)(2,1)} %get-tuple-element.123), channel_id=1, source_target_pairs={{0,4},{4,0},{8,12},{12,8},{16,20},{20,16},{24,28},{28,24},{1,5},{5... | collective-permute-start | bytes 3145736 | tf_op jit(solution)/shard_map/even_0/ppermute | solution.py:351
  274.9 26.2 %collective-permute-start.24 = (bf16[512,1024]{1,0:T(8,128)(2,1)}, bf16[512,1024]{1,0:T(8,128)(2,1)S(1)}, u32[]{:S(2)}, u32[]{:S(2)}) collective-permute-start(bf16[512,1024]{1,0:T(8,128)(2,1)} %get-tuple-element.127), channel_id=1, source_target_pairs={{0,8},{4,12},{8,16},{12,20},{16,24},{20,28},{1,9},{5,13},{9,17},{1... | collective-permute-start | bytes 3145736 | tf_op jit(solution)/shard_map/sums_3_1/ppermute | solution.py:574
  279.5 13.1 %copy-start.39 = (bf16[256,512]{1,0:T(8,128)(2,1)S(1)}, bf16[256,512]{1,0:T(8,128)(2,1)}, u32[]{:S(2)}) copy-start(bf16[256,512]{1,0:T(8,128)(2,1)} %copy-done.38) | copy-start | bytes 786436
  279.5 13.1 %copy-start.41 = (bf16[256,512]{1,0:T(8,128)(2,1)S(1)}, bf16[256,512]{1,0:T(8,128)(2,1)}, u32[]{:S(2)}) copy-start(bf16[256,512]{1,0:T(8,128)(2,1)} %copy-done.40) | copy-start | bytes 786436
  279.5 27.9 %collective-permute-start.25 = (bf16[512,1024]{1,0:T(8,128)(2,1)}, bf16[512,1024]{1,0:T(8,128)(2,1)S(1)}, u32[]{:S(2)}, u32[]{:S(2)}) collective-permute-start(bf16[512,1024]{1,0:T(8,128)(2,1)} %get-tuple-element.116), channel_id=1, source_target_pairs={{8,0},{12,4},{16,8},{20,12},{24,16},{28,20},{9,1},{13,5},{17,9},{2... | collective-permute-start | bytes 3145736 | tf_op jit(solution)/shard_map/sums_3_1/ppermute | solution.py:575
  291.0 18.3 %collective-permute-start.26 = (bf16[512,1024]{1,0:T(8,128)(2,1)}, bf16[512,1024]{1,0:T(8,128)(2,1)S(1)}, u32[]{:S(2)}, u32[]{:S(2)}) collective-permute-start(bf16[512,1024]{1,0:T(8,128)(2,1)} %get-tuple-element.131), channel_id=1, source_target_pairs={{0,4},{4,0},{8,12},{12,8},{16,20},{20,16},{24,28},{28,24},{1,5},{5... | collective-permute-start | bytes 3145736 | tf_op jit(solution)/shard_map/even_1/ppermute | solution.py:351
  (34 other events, 140.6 us)
Sparse Core Ops, SparseCore 0:
  36.8 21.6 all-gather.4
  60.2 22.4 all-gather.6
  87.0 23.1 all-gather.8
  111.6 34.4 all-gather.10

commit v6 on v5

--- a/solution.py
+++ b/solution.py
@@ -6,7 +6,7 @@
 from jax.sharding import PartitionSpec as P
 
 HEAD_DIM = 128
-VMEM_LIMIT = 60 * 1024 * 1024
+VMEM_LIMIT = 40 * 1024 * 1024
 SMALL_LIMIT = 16 * 1024 * 1024
 
 

time: 320 us -> 315 us (0.984)
  Pallas kernels: 121 us -> 102 us
  waiting for transfers between devices: 28.7 us -> 44.8 us
  starting transfers between devices: 91.9 us -> 85.1 us
  local copies, waits for them, and re-layouts: 26.4 us -> 32.4 us
    pallas_call x8, Pallas kernels: 53.3 us -> 38.6 us  [products(): pl.pallas_call(body, grid_spec=pltpu.PrefetchScalarGridSpec(num_scalar_pr...]
    ppermute x2, waiting for transfers between devices: 0.01 us -> 7.75 us  [send_sums(): lax.ppermute(up, 'seq', up_pairs + down_pairs)]
    unnamed x100 -> x98, local copies, waits for them, and re-layouts: 19.5 us -> 25.5 us
    ppermute x4, starting transfers between devices: 39.1 us -> 35.1 us  [send_sums(): sums_up[index] = lax.ppermute(up, 'seq', up_pairs)]
    ppermute x4, waiting for transfers between devices: 7.91 us -> 11.5 us  [send_sums(): sums_down[index] = lax.ppermute(down, 'seq', down_pairs)]
    pallas_call x4, Pallas kernels: 11.4 us -> 8.07 us  [add_arrivals(): pl.pallas_call(body, grid_spec=pltpu.PrefetchScalarGridSpec(num_scalar_pr...]
  transfers between devices with their start and end apart: 32 -> 32, of which waited for: 7 -> 11; matrix products, arithmetic and copies ran while one was open for 5% -> 5% of each run, Pallas kernels for 37% -> 32%
where the time goes in v6:
time: 315 us; the launch traced here: 313 us
  Pallas kernels  102 us (32%)
  starting transfers between devices  85.1 us (27%)
  waiting for transfers between devices  44.8 us (14%)
  local copies, waits for them, and re-layouts  32.4 us (10%)
  blocking collectives  21.4 us (7%)
  between operations  15.4 us (5%)
  other arithmetic  6.8 us (2%)
  matrix products  5.88 us (2%)
    pallas_call x8, Pallas kernels, products(): pl.pallas_call(body, grid_spec=pltpu.PrefetchScalarGridSpec(num_scalar_pr...  38.6 us
    ppermute x4, starting transfers between devices, send_sums(): sums_up[index] = lax.ppermute(up, 'seq', up_pairs)  35.1 us
    pallas_call x4, Pallas kernels, attend(): pl.pallas_call(lambda *refs: attend_kernel(pieces, *refs), grid=(heads //...  31.1 us
    unnamed x98, local copies, waits for them, and re-layouts  25.5 us
    all_to_all x1, blocking collectives, route(): lax.all_to_all(sent, 'seq', split_axis=0, concat_axis=0, tiled=True)  21.4 us
    all_to_all x1, waiting for transfers between devices, route(): lax.all_to_all(sent, 'seq', split_axis=0, concat_axis=0, tiled=True)  14.2 us
    pallas_call x3, Pallas kernels, project_piece(): pl.pallas_call(body, grid=(heads // pair,), in_specs=[pl.BlockSpec((state...  12.8 us
    ppermute x4, waiting for transfers between devices, send_sums(): sums_down[index] = lax.ppermute(down, 'seq', down_pairs)  11.5 us
  transfers between devices with their start and end apart: 32, of which 11 were waited for; matrix products, arithmetic and copies ran while one was open for 5% of the time, Pallas kernels for 32%

profile of v6, /device:TPU:0, one launch (start us, length us, event | category | flops | bytes accessed | tf_op | source)
XLA Modules:
  0.0 313.3 jit_solution(27361983918925994)
XLA Ops:
  8.2 2.4 convolution_convert_fusion.1
  10.6 7.4 %all-to-all-start = ((bf16[8,80,512]{2,1,0:T(8,128)(2,1)}), bf16[8,80,512]{2,1,0:T(8,128)(2,1)S(1)}, u32[]{:S(2)}, u32[]{:S(2)}) async-start(bf16[8,80,512]{2,1,0:T(8,128)(2,1)} %bitcast.3), calls=%async_computation | async-start | bytes 1310720 | tf_op jit(solution)/shard_map/route/all_to_all | solution.py:309
  21.0 14.2 %all-to-all-done = bf16[8,80,512]{2,1,0:T(8,128)(2,1)S(1)} async-done(((bf16[8,80,512]{2,1,0:T(8,128)(2,1)}), bf16[8,80,512]{2,1,0:T(8,128)(2,1)S(1)}, u32[]{:S(2)}, u32[]{:S(2)}) %all-to-all-start) | async-done | bytes 655392 | tf_op jit(solution)/shard_map/route/all_to_all | solution.py:309
  37.3 21.4 %all_to_all.24 = bf16[8,80,512]{2,1,0:T(8,128)(2,1)S(1)} all-to-all(bf16[8,80,512]{2,1,0:T(8,128)(2,1)S(1)} %bitcast.42), channel_id=1, replica_groups=mesh['seq'=8,'tp'=4] {'seq'}, dimensions={0} | all-to-all | bytes 1310720 | tf_op jit(solution)/shard_map/route/all_to_all | solution.py:309
  62.9 1.9 constant_dynamic-slice_fusion
  64.7 2.8 collective-permute-start
  69.3 4.2 %project_first_piece.3.refs_4_ = f32[512,1024]{1,0:T(8,128)S(1)} custom-call(bf16[512,2048]{1,0:T(8,128)(2,1)S(1)} %copy-done.3, bf16[4,2,512,2048]{3,2,1,0:T(8,128)(2,1)} %bitcast.24, bf16[4,2,512,2048]{3,2,1,0:T(8,128)(2,1)} %bitcast.32), custom_call_target="tpu_custom_call" | custom-call | flops 2147483648 | bytes 4194304 | tf_op jit(solution)/shard_map/project_first_piece/pallas_call | solution.py:141
  74.8 4.2 %project_first_piece.4.refs_4_ = f32[512,1024]{1,0:T(8,128)S(1)} custom-call(bf16[512,2048]{1,0:T(8,128)(2,1)S(1)} %copy-done.3, bf16[4,2,512,2048]{3,2,1,0:T(8,128)(2,1)} %bitcast.25, bf16[4,2,512,2048]{3,2,1,0:T(8,128)(2,1)} %bitcast.33), custom_call_target="tpu_custom_call" | custom-call | flops 2147483648 | bytes 4194304 | tf_op jit(solution)/shard_map/project_first_piece/pallas_call | solution.py:141
  80.4 4.3 %project_first_piece.5.refs_4_ = f32[512,1024]{1,0:T(8,128)S(1)} custom-call(bf16[512,2048]{1,0:T(8,128)(2,1)S(1)} %copy-done.3, bf16[4,2,512,2048]{3,2,1,0:T(8,128)(2,1)} %bitcast.26, bf16[4,2,512,2048]{3,2,1,0:T(8,128)(2,1)} %bitcast.34), custom_call_target="tpu_custom_call" | custom-call | flops 2147483648 | bytes 4194304 | tf_op jit(solution)/shard_map/project_first_piece/pallas_call | solution.py:141
  88.0 2.5 collective-permute-start.17
  93.8 6.6 %attend_0.1 = (bf16[256,512]{1,0:T(8,128)(2,1)S(1)}, bf16[512,1024]{1,0:T(8,128)(2,1)S(1)}) custom-call(s32[15]{0:T(128)S(1)} %stack.54.refs_0_.scalar_ref, bf16[512,2048]{1,0:T(8,128)(2,1)S(1)} %copy-done.5, bf16[4,2,512,2048]{3,2,1,0:T(8,128)(2,1)} %bitcast.27, bf16[4,2,512,2048]{3,2,1,0:T(8,128)(2,1)} %bitcast.35, f32[512,1024]{1,0:T(8,128)S(1)} %copy-done.17, ...), custom_call_target="tpu_custom_call" | custom-call | bytes 524288 | tf_op jit(solution)/shard_map/attend_0/pallas_call | solution.py:103
  101.4 2.1 collective-permute-done.17
  103.4 2.2 pad_maximum_fusion.1
  105.6 3.7 %collective-permute-start.2 = (bf16[512,1024]{1,0:T(8,128)(2,1)}, bf16[512,1024]{1,0:T(8,128)(2,1)}, u32[]{:S(2)}, u32[]{:S(2)}) collective-permute-start(bf16[512,1024]{1,0:T(8,128)(2,1)} %copy-done.30), channel_id=1, source_target_pairs={{0,8},{4,12},{8,16},{12,20},{16,24},{20,28},{1,9},{5,13},{9,17},{1... | collective-permute-start | bytes 3145736 | tf_op jit(solution)/shard_map/rows_0_0/ppermute | solution.py:343
  113.6 7.3 %attend_2.1 = (bf16[256,512]{1,0:T(8,128)(2,1)S(1)}, bf16[512,1024]{1,0:T(8,128)(2,1)}) custom-call(s32[15]{0:T(128)S(1)} %stack.54.refs_0_.scalar_ref, bf16[512,2048]{1,0:T(8,128)(2,1)S(1)} %copy-done.6, bf16[4,2,512,2048]{3,2,1,0:T(8,128)(2,1)} %bitcast.28, bf16[4,2,512,2048]{3,2,1,0:T(8,128)(2,1)} %bitcast.36, f32[512,1024]{1,0:T(8,128)S(1)} %copy-done.15, ...), custom_call_target="tpu_custom_call" | custom-call | bytes 1048576 | tf_op jit(solution)/shard_map/attend_2/pallas_call | solution.py:103
  122.6 7.2 %attend_1.1 = (bf16[256,512]{1,0:T(8,128)(2,1)S(1)}, bf16[512,1024]{1,0:T(8,128)(2,1)}) custom-call(s32[15]{0:T(128)S(1)} %stack.54.refs_0_.scalar_ref, bf16[512,2048]{1,0:T(8,128)(2,1)S(1)} %copy-done.6, bf16[4,2,512,2048]{3,2,1,0:T(8,128)(2,1)} %bitcast.29, bf16[4,2,512,2048]{3,2,1,0:T(8,128)(2,1)} %bitcast.37, f32[512,1024]{1,0:T(8,128)S(1)} %copy-done.13, ...), custom_call_target="tpu_custom_call" | custom-call | bytes 1572864 | tf_op jit(solution)/shard_map/attend_1/pallas_call | solution.py:103
  130.5 5.6 %collective-permute-start.8 = (bf16[512,1024]{1,0:T(8,128)(2,1)}, bf16[512,1024]{1,0:T(8,128)(2,1)}, u32[]{:S(2)}, u32[]{:S(2)}) collective-permute-start(bf16[512,1024]{1,0:T(8,128)(2,1)} %get-tuple-element.82.refs_2_), channel_id=1, source_target_pairs={{0,8},{4,12},{8,16},{12,20},{16,24},{20,28},{1,9},{5,13},{9,17},{1... | collective-permute-start | bytes 3145736 | tf_op jit(solution)/shard_map/rows_0_1/ppermute | solution.py:343
  137.4 2.0 broadcast_select_fusion.refs_0_.refs_1_.refs_2_
  140.5 10.0 %attend_3.1 = (bf16[256,512]{1,0:T(8,128)(2,1)S(1)}, bf16[512,1024]{1,0:T(8,128)(2,1)}) custom-call(s32[15]{0:T(128)S(1)} %stack.54.refs_0_.scalar_ref, bf16[512,2048]{1,0:T(8,128)(2,1)S(1)} %copy-done.4, bf16[512,2048]{1,0:T(8,128)(2,1)S(1)} %copy-done.7, bf16[4,2,512,2048]{3,2,1,0:T(8,128)(2,1)} %bitcast.30, bf16[4,2,512,2048]{3,2,1,0:T(8,128)(2,1)} %bitcast.31, ...), custom_call_target="tpu_custom_call" | custom-call | bytes 2097152 | tf_op jit(solution)/shard_map/attend_3/pallas_call | solution.py:103
  153.2 3.3 %sums_1_0.1 = bf16[512,1024]{1,0:T(8,128)(2,1)S(1)} custom-call(s32[15]{0:T(128)S(1)} %stack.54.refs_0_.scalar_ref, bf16[512,2048]{1,0:T(8,128)(2,1)S(1)} %broadcast_select_fusion.refs_0_.refs_1_.refs_2_, bf16[512,1024]{1,0:T(8,128)(2,1)} %get-tuple-element.77.refs_1_.refs_3_, bf16[2048,512]{1,0:T(8,128)(2,1)S(1)} %copy-done.2, ...), custom_call_target="tpu_custom_call" | custom-call | bytes 2621440 | tf_op jit(solution)/shard_map/sums_1_0/pallas_call | solution.py:187
  156.5 4.6 %collective-permute-start.6 = (bf16[512,1024]{1,0:T(8,128)(2,1)S(1)}, bf16[512,1024]{1,0:T(8,128)(2,1)S(1)}, u32[]{:S(2)}, u32[]{:S(2)}) collective-permute-start(bf16[512,1024]{1,0:T(8,128)(2,1)S(1)} %sums_1_0.1), channel_id=1, source_target_pairs={{0,8},{4,12},{24,16},{28,20},{1,9},{5,13},{25,17},{29,21},{2,10},{... | collective-permute-start | bytes 3145736 | tf_op jit(solution)/shard_map/sums_1_0/ppermute | solution.py:572
  163.2 5.7 %side_ahead_0.1 = (bf16[512,1024]{1,0:T(8,128)(2,1)S(1)}, bf16[512,1024]{1,0:T(8,128)(2,1)S(1)}, bf16[512,1024]{1,0:T(8,128)(2,1)S(1)}) custom-call(s32[15]{0:T(128)S(1)} %stack.54.refs_0_.scalar_ref, bf16[512,2048]{1,0:T(8,128)(2,1)S(1)} %broadcast_select_fusion.refs_0_.refs_1_.refs_2_, bf16[512,2048]{1,0:T(8,128)(2,1)S(1)} %broadcast_select_fusion.refs_0_.refs_1_.refs_2_, ...), custom_call_target="tpu_custom_call" | custom-call | tf_op jit(solution)/shard_map/side_ahead_0/pallas_call | solution.py:187
  168.9 4.6 %collective-permute-done.5.refs_3_.refs_7_ = bf16[512,1024]{1,0:T(8,128)(2,1)S(1)} collective-permute-done((bf16[512,1024]{1,0:T(8,128)(2,1)}, bf16[512,1024]{1,0:T(8,128)(2,1)S(1)}, u32[]{:S(2)}, u32[]{:S(2)}) %collective-permute-start.5) | collective-permute-done | bytes 1048608 | tf_op jit(solution)/shard_map/side_rows_1/ppermute | solution.py:351
  173.5 3.2 %sums_1_1.1 = bf16[512,1024]{1,0:T(8,128)(2,1)S(1)} custom-call(s32[15]{0:T(128)S(1)} %stack.54.refs_0_.scalar_ref, bf16[512,2048]{1,0:T(8,128)(2,1)S(1)} %broadcast_select_fusion.refs_0_.refs_1_.refs_2_, bf16[512,1024]{1,0:T(8,128)(2,1)} %get-tuple-element.86.refs_1_.refs_3_, bf16[2048,512]{1,0:T(8,128)(2,1)S(1)} %copy-done.2, ...), custom_call_target="tpu_custom_call" | custom-call | bytes 3670016 | tf_op jit(solution)/shard_map/sums_1_1/pallas_call | solution.py:187
  176.6 4.4 %collective-permute-start.7 = (bf16[512,1024]{1,0:T(8,128)(2,1)S(1)}, bf16[512,1024]{1,0:T(8,128)(2,1)S(1)}, u32[]{:S(2)}, u32[]{:S(2)}) collective-permute-start(bf16[512,1024]{1,0:T(8,128)(2,1)S(1)} %sums_1_1.1), channel_id=1, source_target_pairs={{0,8},{4,12},{24,16},{28,20},{1,9},{5,13},{25,17},{29,21},{2,10},{... | collective-permute-start | bytes 3145736 | tf_op jit(solution)/shard_map/sums_1_1/ppermute | solution.py:572
  181.0 3.6 %collective-permute-done.6.refs_1_ = bf16[512,1024]{1,0:T(8,128)(2,1)S(1)} collective-permute-done((bf16[512,1024]{1,0:T(8,128)(2,1)S(1)}, bf16[512,1024]{1,0:T(8,128)(2,1)S(1)}, u32[]{:S(2)}, u32[]{:S(2)}) %collective-permute-start.6) | collective-permute-done | bytes 1048608 | tf_op jit(solution)/shard_map/sums_1_0/ppermute | solution.py:572
  188.5 5.9 %collective-permute-start.14 = (bf16[512,1024]{1,0:T(8,128)(2,1)S(1)}, bf16[512,1024]{1,0:T(8,128)(2,1)S(1)}, u32[]{:S(2)}, u32[]{:S(2)}) collective-permute-start(bf16[512,1024]{1,0:T(8,128)(2,1)S(1)} %sums_2_0.1), channel_id=1, source_target_pairs={{0,8},{4,12},{8,16},{12,20},{1,9},{5,13},{9,17},{13,21},{2,10},{6,... | collective-permute-start | bytes 3145736 | tf_op jit(solution)/shard_map/sums_2_0/ppermute | solution.py:574
  195.4 5.5 %side_ahead_1.1 = (bf16[512,1024]{1,0:T(8,128)(2,1)S(1)}, bf16[512,1024]{1,0:T(8,128)(2,1)S(1)}, bf16[512,1024]{1,0:T(8,128)(2,1)S(1)}) custom-call(s32[15]{0:T(128)S(1)} %stack.54.refs_0_.scalar_ref, bf16[512,2048]{1,0:T(8,128)(2,1)S(1)} %broadcast_select_fusion.refs_0_.refs_1_.refs_2_, bf16[512,2048]{1,0:T(8,128)(2,1)S(1)} %broadcast_select_fusion.refs_0_.refs_1_.refs_2_, ...), custom_call_target="tpu_custom_call" | custom-call | tf_op jit(solution)/shard_map/side_ahead_1/pallas_call | solution.py:187
  202.9 4.2 %collective-permute-done.7.refs_1_ = bf16[512,1024]{1,0:T(8,128)(2,1)S(1)} collective-permute-done((bf16[512,1024]{1,0:T(8,128)(2,1)S(1)}, bf16[512,1024]{1,0:T(8,128)(2,1)S(1)}, u32[]{:S(2)}, u32[]{:S(2)}) %collective-permute-start.7) | collective-permute-done | bytes 1048608 | tf_op jit(solution)/shard_map/sums_1_1/ppermute | solution.py:572
  207.1 3.2 %side_own_1.1.refs_0_ = bf16[512,1024]{1,0:T(8,128)(2,1)S(1)} custom-call(s32[15]{0:T(128)S(1)} %stack.54.refs_0_.scalar_ref, bf16[512,2048]{1,0:T(8,128)(2,1)S(1)} %broadcast_select_fusion.refs_0_.refs_1_.refs_2_, bf16[512,1024]{1,0:T(8,128)(2,1)} %get-tuple-element.86.refs_1_.refs_3_, bf16[2048,512]{1,0:T(8,128)(2,1)S(1)} %copy-done.2, ...), custom_call_target="tpu_custom_call" | custom-call | bytes 5242880 | tf_op jit(solution)/shard_map/side_own_1/pallas_call | solution.py:187
  213.4 1.9 sums_2_1.1
  215.3 10.6 %collective-permute-start.18 = (bf16[512,1024]{1,0:T(8,128)(2,1)}, bf16[512,1024]{1,0:T(8,128)(2,1)}, u32[]{:S(2)}, u32[]{:S(2)}) collective-permute-start(bf16[512,1024]{1,0:T(8,128)(2,1)} %sums_2_1.1), channel_id=1, source_target_pairs={{0,8},{4,12},{8,16},{12,20},{1,9},{5,13},{9,17},{13,21},{2,10},{6,... | collective-permute-start | bytes 3145736 | tf_op jit(solution)/shard_map/sums_2_1/ppermute | solution.py:574
  227.5 2.0 collective-permute-done.14.refs_2_
  229.6 3.3 %side_own_0.1.refs_0_ = bf16[512,1024]{1,0:T(8,128)(2,1)S(1)} custom-call(s32[15]{0:T(128)S(1)} %stack.54.refs_0_.scalar_ref, bf16[512,2048]{1,0:T(8,128)(2,1)S(1)} %broadcast_select_fusion.refs_0_.refs_1_.refs_2_, bf16[512,1024]{1,0:T(8,128)(2,1)} %get-tuple-element.77.refs_1_.refs_3_, bf16[2048,512]{1,0:T(8,128)(2,1)S(1)} %copy-done.2, ...), custom_call_target="tpu_custom_call" | custom-call | bytes 6815744 | tf_op jit(solution)/shard_map/side_own_0/pallas_call | solution.py:187
  236.8 2.4 sums_3_0.1
  239.2 13.9 %collective-permute-start.21 = (bf16[512,1024]{1,0:T(8,128)(2,1)}, bf16[512,1024]{1,0:T(8,128)(2,1)}, u32[]{:S(2)}, u32[]{:S(2)}) collective-permute-start(bf16[512,1024]{1,0:T(8,128)(2,1)} %get-tuple-element.120), channel_id=1, source_target_pairs={{0,8},{4,12},{8,16},{12,20},{16,24},{20,28},{1,9},{5,13},{9,17},{1... | collective-permute-start | bytes 3145736 | tf_op jit(solution)/shard_map/sums_3_0/ppermute | solution.py:574
  254.4 2.2 copy-done
  260.3 7.4 %even_0.1 = (bf16[512,1024]{1,0:T(8,128)(2,1)S(1)}, bf16[512,1024]{1,0:T(8,128)(2,1)S(1)}) custom-call(s32[15]{0:T(128)S(1)} %stack.54.refs_0_.scalar_ref, bf16[2048,1024]{1,0:T(8,128)(2,1)S(1)} %copy-done, bf16[2048,1024]{1,0:T(8,128)(2,1)S(1)} %copy-done, bf16[512,1024]{1,0:T(8,128)(2,1)S(1)} %copy-done.31, bf16[2048,1024]{1,0:T(8,128)(2,1)S(1)} %copy-done, ...), custom_call_target="tpu_custom_call" | custom-call | bytes 8388608 | tf_op jit(solution)/shard_map/even_0/pallas_call | solution.py:187
  267.7 1.9 collective-permute-start.23
  269.6 2.8 sums_3_1.1
  272.4 4.6 %collective-permute-start.24 = (bf16[512,1024]{1,0:T(8,128)(2,1)S(1)}, bf16[512,1024]{1,0:T(8,128)(2,1)S(1)}, u32[]{:S(2)}, u32[]{:S(2)}) collective-permute-start(bf16[512,1024]{1,0:T(8,128)(2,1)S(1)} %get-tuple-element.127), channel_id=1, source_target_pairs={{0,8},{4,12},{8,16},{12,20},{16,24},{20,28},{1,9},{5,13},{9,17},{1... | collective-permute-start | bytes 3145736 | tf_op jit(solution)/shard_map/sums_3_1/ppermute | solution.py:574
  278.5 6.9 %even_1.1 = (bf16[512,1024]{1,0:T(8,128)(2,1)S(1)}, bf16[512,1024]{1,0:T(8,128)(2,1)S(1)}) custom-call(s32[15]{0:T(128)S(1)} %stack.54.refs_0_.scalar_ref, bf16[2048,1024]{1,0:T(8,128)(2,1)S(1)} %copy-done.1, bf16[2048,1024]{1,0:T(8,128)(2,1)S(1)} %copy-done.1, bf16[512,1024]{1,0:T(8,128)(2,1)} %get-tuple-element.82.refs_2_, ...), custom_call_target="tpu_custom_call" | custom-call | bytes 9437184 | tf_op jit(solution)/shard_map/even_1/pallas_call | solution.py:187
  286.9 5.1 %collective-permute-done.22.refs_2_ = bf16[512,1024]{1,0:T(8,128)(2,1)} collective-permute-done((bf16[512,1024]{1,0:T(8,128)(2,1)}, bf16[512,1024]{1,0:T(8,128)(2,1)}, u32[]{:S(2)}, u32[]{:S(2)}) %collective-permute-start.22) | collective-permute-done | bytes 1048608 | tf_op jit(solution)/shard_map/sums_3_0/ppermute | solution.py:575
  292.0 3.0 finish_2.1
  295.0 1.7 finish_0.1
  296.8 6.3 %collective-permute-done.25.refs_2_ = bf16[512,1024]{1,0:T(8,128)(2,1)S(1)} collective-permute-done((bf16[512,1024]{1,0:T(8,128)(2,1)S(1)}, bf16[512,1024]{1,0:T(8,128)(2,1)S(1)}, u32[]{:S(2)}, u32[]{:S(2)}) %collective-permute-start.25) | collective-permute-done | bytes 1048608 | tf_op jit(solution)/shard_map/sums_3_1/ppermute | solution.py:575
  303.1 1.9 finish_3.1
  305.0 1.7 finish_1.1
  (167 shorter events, 58.1 us)
Async XLA Ops:
  7.2 11.0 %copy-start.46 = (s32[8]{0:T(128)S(1)}, s32[8]{0:T(128)}, u32[]{:S(2)}) copy-start(s32[8]{0:T(128)} %param.14) | copy-start | bytes 100
  7.2 11.5 %copy-start.47 = (s32[8]{0:T(128)S(1)}, s32[8]{0:T(128)}, u32[]{:S(2)}) copy-start(s32[8]{0:T(128)} %param.15) | copy-start | bytes 100
  7.2 12.1 %copy-start.44 = (s32[4096]{0:T(1024)S(1)}, s32[4096]{0:T(1024)}, u32[]{:S(2)}) copy-start(s32[4096]{0:T(1024)} %param.13) | copy-start | bytes 49156
  10.6 26.1 %copy-start.45 = (bf16[512,1024]{1,0:T(8,128)(2,1)S(1)}, bf16[512,1024]{1,0:T(8,128)(2,1)}, u32[]{:S(2)}) copy-start(bf16[512,1024]{1,0:T(8,128)(2,1)} %param.11) | copy-start | bytes 3145732
  10.6 24.7 %all-to-all-start = ((bf16[8,80,512]{2,1,0:T(8,128)(2,1)}), bf16[8,80,512]{2,1,0:T(8,128)(2,1)S(1)}, u32[]{:S(2)}, u32[]{:S(2)}) async-start(bf16[8,80,512]{2,1,0:T(8,128)(2,1)} %bitcast.3), calls=%async_computation | async-start | bytes 1310720 | tf_op jit(solution)/shard_map/route/all_to_all | solution.py:309
  18.0 44.9 %all-gather.5.cloned.1.call-start = ((), (), s32[]{:S(2)}) async-start(), calls=%async_computation.2 | async-start | bytes 2621440 | tf_op jit(solution)/shard_map/gather_states/all_gather | solution.py:420
  36.7 49.4 %all-gather.7.cloned.1.call-start = ((), (), s32[]{:S(2)}) async-start(), calls=%async_computation.3 | async-start | bytes 2621440 | tf_op jit(solution)/shard_map/gather_states/all_gather | solution.py:420
  37.3 22.9 %copy-start.48 = (s32[4]{0:T(128)S(1)}, s32[4]{0:T(128)}, u32[]{:S(2)}) copy-start(s32[4]{0:T(128)} %constant.152.clone) | copy-start | bytes 52
  37.3 24.2 %copy-start.42 = (bf16[512,512]{1,0:T(8,128)(2,1)S(1)}, bf16[512,512]{1,0:T(8,128)(2,1)}, u32[]{:S(2)}) copy-start(bf16[512,512]{1,0:T(8,128)(2,1)} %fusion.2) | copy-start | bytes 1572868
  60.1 91.5 %all-gather.9.cloned.1.call-start = ((), (), s32[]{:S(2)}) async-start(), calls=%async_computation.4 | async-start | bytes 2621440 | tf_op jit(solution)/shard_map/side_states/all_gather | solution.py:460
  62.7 23.3 %collective-permute-start.1 = (bf16[512,512]{1,0:T(8,128)(2,1)S(1)}, bf16[512,512]{1,0:T(8,128)(2,1)S(1)}, u32[]{:S(2)}, u32[]{:S(2)}) collective-permute-start(bf16[512,512]{1,0:T(8,128)(2,1)S(1)} %fusion.8), channel_id=1, source_target_pairs={{0,4},{4,0},{8,12},{12,8},{16,20},{20,16},{24,28},{28,24},{1,5},{5... | collective-permute-start | bytes 1572872 | tf_op jit(solution)/shard_map/side_states/ppermute | solution.py:351
  64.7 21.3 %collective-permute-start = (bf16[512,512]{1,0:T(8,128)(2,1)}, bf16[512,512]{1,0:T(8,128)(2,1)}, u32[]{:S(2)}, u32[]{:S(2)}) collective-permute-start(bf16[512,512]{1,0:T(8,128)(2,1)} %constant_dynamic-slice_fusion), channel_id=1, source_target_pairs={{0,8},{1,25},{2,18},{3,3},{4,12},{5,29},{6,22},{7,7},{8,16},{9,1},... | collective-permute-start | bytes 1572872 | tf_op jit(solution)/shard_map/line_states_0/ppermute | solution.py:409
  80.4 10.1 %copy-start.9 = (bf16[256,2048]{1,0:T(8,128)(2,1)S(1)}, bf16[256,2048]{1,0:T(8,128)(2,1)}, u32[]{:S(2)}) copy-start(bf16[256,2048]{1,0:T(8,128)(2,1)} %refs_8_.1) | copy-start | bytes 3145732
  86.9 167.5 %all-gather.11.cloned.1.call-start = ((), (), s32[]{:S(2)}) async-start(), calls=%async_computation.5 | async-start | bytes 5242880 | tf_op jit(solution)/shard_map/line_states/all_gather | solution.py:450
  88.0 15.4 %collective-permute-start.17 = (bf16[512,512]{1,0:T(8,128)(2,1)S(1)}, bf16[512,512]{1,0:T(8,128)(2,1)S(1)}, u32[]{:S(2)}, u32[]{:S(2)}) collective-permute-start(bf16[512,512]{1,0:T(8,128)(2,1)S(1)} %constant_dynamic-slice_fusion.1), channel_id=1, source_target_pairs={{0,8},{1,25},{2,18},{3,3},{4,12},{5,29},{6,22},{7,7},{8,16},{9,1},... | collective-permute-start | bytes 1572872 | tf_op jit(solution)/shard_map/line_states_1/ppermute | solution.py:409
  101.4 9.4 %copy-start.6 = (bf16[512,2048]{1,0:T(8,128)(2,1)S(1)}, bf16[512,2048]{1,0:T(8,128)(2,1)}, u32[]{:S(2)}) copy-start(bf16[512,2048]{1,0:T(8,128)(2,1)} %all-gather.7.cloned.1.call-done.refs_1_.refs_2_) | copy-start | bytes 6291460
  105.6 33.8 %collective-permute-start.2 = (bf16[512,1024]{1,0:T(8,128)(2,1)}, bf16[512,1024]{1,0:T(8,128)(2,1)}, u32[]{:S(2)}, u32[]{:S(2)}) collective-permute-start(bf16[512,1024]{1,0:T(8,128)(2,1)} %copy-done.30), channel_id=1, source_target_pairs={{0,8},{4,12},{8,16},{12,20},{16,24},{20,28},{1,9},{5,13},{9,17},{1... | collective-permute-start | bytes 3145736 | tf_op jit(solution)/shard_map/rows_0_0/ppermute | solution.py:343
  109.3 30.1 %collective-permute-start.3 = (bf16[512,1024]{1,0:T(8,128)(2,1)}, bf16[512,1024]{1,0:T(8,128)(2,1)}, u32[]{:S(2)}, u32[]{:S(2)}) collective-permute-start(bf16[512,1024]{1,0:T(8,128)(2,1)} %copy-done.30), channel_id=1, source_target_pairs={{8,0},{12,4},{16,8},{20,12},{24,16},{28,20},{9,1},{13,5},{17,9},{2... | collective-permute-start | bytes 3145736 | tf_op jit(solution)/shard_map/rows_0_0/ppermute | solution.py:347
  120.9 30.7 %collective-permute-start.4 = (bf16[512,1024]{1,0:T(8,128)(2,1)}, bf16[512,1024]{1,0:T(8,128)(2,1)}, u32[]{:S(2)}, u32[]{:S(2)}) collective-permute-start(bf16[512,1024]{1,0:T(8,128)(2,1)} %get-tuple-element.77.refs_1_.refs_3_), channel_id=1, source_target_pairs={{0,4},{4,0},{8,12},{12,8},{16,20},{20,16},{24,28},{28,24},{1,5},{5... | collective-permute-start | bytes 3145736 | tf_op jit(solution)/shard_map/side_rows_0/ppermute | solution.py:351
  130.5 30.6 %collective-permute-start.8 = (bf16[512,1024]{1,0:T(8,128)(2,1)}, bf16[512,1024]{1,0:T(8,128)(2,1)}, u32[]{:S(2)}, u32[]{:S(2)}) collective-permute-start(bf16[512,1024]{1,0:T(8,128)(2,1)} %get-tuple-element.82.refs_2_), channel_id=1, source_target_pairs={{0,8},{4,12},{8,16},{12,20},{16,24},{20,28},{1,9},{5,13},{9,17},{1... | collective-permute-start | bytes 3145736 | tf_op jit(solution)/shard_map/rows_0_1/ppermute | solution.py:343
  136.1 25.0 %collective-permute-start.9 = (bf16[512,1024]{1,0:T(8,128)(2,1)}, bf16[512,1024]{1,0:T(8,128)(2,1)}, u32[]{:S(2)}, u32[]{:S(2)}) collective-permute-start(bf16[512,1024]{1,0:T(8,128)(2,1)} %get-tuple-element.82.refs_2_), channel_id=1, source_target_pairs={{8,0},{12,4},{16,8},{20,12},{24,16},{28,20},{9,1},{13,5},{17,9},{2... | collective-permute-start | bytes 3145736 | tf_op jit(solution)/shard_map/rows_0_1/ppermute | solution.py:347
  151.2 22.2 %collective-permute-start.5 = (bf16[512,1024]{1,0:T(8,128)(2,1)}, bf16[512,1024]{1,0:T(8,128)(2,1)S(1)}, u32[]{:S(2)}, u32[]{:S(2)}) collective-permute-start(bf16[512,1024]{1,0:T(8,128)(2,1)} %get-tuple-element.86.refs_1_.refs_3_), channel_id=1, source_target_pairs={{0,4},{4,0},{8,12},{12,8},{16,20},{20,16},{24,28},{28,24},{1,5},{5... | collective-permute-start | bytes 3145736 | tf_op jit(solution)/shard_map/side_rows_1/ppermute | solution.py:351
  156.5 28.1 %collective-permute-start.6 = (bf16[512,1024]{1,0:T(8,128)(2,1)S(1)}, bf16[512,1024]{1,0:T(8,128)(2,1)S(1)}, u32[]{:S(2)}, u32[]{:S(2)}) collective-permute-start(bf16[512,1024]{1,0:T(8,128)(2,1)S(1)} %sums_1_0.1), channel_id=1, source_target_pairs={{0,8},{4,12},{24,16},{28,20},{1,9},{5,13},{25,17},{29,21},{2,10},{... | collective-permute-start | bytes 3145736 | tf_op jit(solution)/shard_map/sums_1_0/ppermute | solution.py:572
  161.1 24.6 %collective-permute-start.10 = (bf16[512,1024]{1,0:T(8,128)(2,1)}, bf16[512,1024]{1,0:T(8,128)(2,1)S(1)}, u32[]{:S(2)}, u32[]{:S(2)}) collective-permute-start(bf16[512,1024]{1,0:T(8,128)(2,1)} %collective-permute-done.2.refs_5_), channel_id=1, source_target_pairs={{8,16},{12,20},{16,24},{20,28},{9,17},{13,21},{17,25},{21,29},{10,... | collective-permute-start | bytes 3145736 | tf_op jit(solution)/shard_map/rows_1_0/ppermute | solution.py:343
  161.9 24.7 %collective-permute-start.11 = (bf16[512,1024]{1,0:T(8,128)(2,1)}, bf16[512,1024]{1,0:T(8,128)(2,1)S(1)}, u32[]{:S(2)}, u32[]{:S(2)}) collective-permute-start(bf16[512,1024]{1,0:T(8,128)(2,1)} %collective-permute-done.3.refs_14_), channel_id=1, source_target_pairs={{8,0},{12,4},{16,8},{20,12},{9,1},{13,5},{17,9},{21,13},{10,2},{14... | collective-permute-start | bytes 3145736 | tf_op jit(solution)/shard_map/rows_1_0/ppermute | solution.py:347
  176.6 30.5 %collective-permute-start.7 = (bf16[512,1024]{1,0:T(8,128)(2,1)S(1)}, bf16[512,1024]{1,0:T(8,128)(2,1)S(1)}, u32[]{:S(2)}, u32[]{:S(2)}) collective-permute-start(bf16[512,1024]{1,0:T(8,128)(2,1)S(1)} %sums_1_1.1), channel_id=1, source_target_pairs={{0,8},{4,12},{24,16},{28,20},{1,9},{5,13},{25,17},{29,21},{2,10},{... | collective-permute-start | bytes 3145736 | tf_op jit(solution)/shard_map/sums_1_1/ppermute | solution.py:572
  185.7 25.4 %copy-start.22 = (bf16[512,1024]{1,0:T(8,128)(2,1)}, bf16[512,1024]{1,0:T(8,128)(2,1)S(1)}, u32[]{:S(2)}) copy-start(bf16[512,1024]{1,0:T(8,128)(2,1)S(1)} %collective-permute-done.10.up_ref.refs_9_) | copy-start | bytes 3145732
  186.5 24.6 %copy-start.24 = (bf16[512,1024]{1,0:T(8,128)(2,1)}, bf16[512,1024]{1,0:T(8,128)(2,1)S(1)}, u32[]{:S(2)}) copy-start(bf16[512,1024]{1,0:T(8,128)(2,1)S(1)} %collective-permute-done.11.down_ref.refs_10_) | copy-start | bytes 3145732
  186.5 23.8 %collective-permute-start.12 = (bf16[512,1024]{1,0:T(8,128)(2,1)}, bf16[512,1024]{1,0:T(8,128)(2,1)S(1)}, u32[]{:S(2)}, u32[]{:S(2)}) collective-permute-start(bf16[512,1024]{1,0:T(8,128)(2,1)} %collective-permute-done.8.refs_5_), channel_id=1, source_target_pairs={{8,16},{12,20},{16,24},{20,28},{9,17},{13,21},{17,25},{21,29},{10,... | collective-permute-start | bytes 3145736 | tf_op jit(solution)/shard_map/rows_1_1/ppermute | solution.py:343
  187.2 23.9 %collective-permute-start.13 = (bf16[512,1024]{1,0:T(8,128)(2,1)}, bf16[512,1024]{1,0:T(8,128)(2,1)S(1)}, u32[]{:S(2)}, u32[]{:S(2)}) collective-permute-start(bf16[512,1024]{1,0:T(8,128)(2,1)} %collective-permute-done.9.refs_14_), channel_id=1, source_target_pairs={{8,0},{12,4},{16,8},{20,12},{9,1},{13,5},{17,9},{21,13},{10,2},{14... | collective-permute-start | bytes 3145736 | tf_op jit(solution)/shard_map/rows_1_1/ppermute | solution.py:347
  188.5 41.0 %collective-permute-start.14 = (bf16[512,1024]{1,0:T(8,128)(2,1)S(1)}, bf16[512,1024]{1,0:T(8,128)(2,1)S(1)}, u32[]{:S(2)}, u32[]{:S(2)}) collective-permute-start(bf16[512,1024]{1,0:T(8,128)(2,1)S(1)} %sums_2_0.1), channel_id=1, source_target_pairs={{0,8},{4,12},{8,16},{12,20},{1,9},{5,13},{9,17},{13,21},{2,10},{6,... | collective-permute-start | bytes 3145736 | tf_op jit(solution)/shard_map/sums_2_0/ppermute | solution.py:574
  194.5 35.1 %collective-permute-start.15 = (bf16[512,1024]{1,0:T(8,128)(2,1)S(1)}, bf16[512,1024]{1,0:T(8,128)(2,1)S(1)}, u32[]{:S(2)}, u32[]{:S(2)}) collective-permute-start(bf16[512,1024]{1,0:T(8,128)(2,1)S(1)} %sums_2_0.1), channel_id=1, source_target_pairs={{16,8},{20,12},{24,16},{28,20},{17,9},{21,13},{25,17},{29,21},{18,... | collective-permute-start | bytes 3145736 | tf_op jit(solution)/shard_map/sums_2_0/ppermute | solution.py:575
  210.3 23.5 %copy-start.18 = (bf16[512,1024]{1,0:T(8,128)(2,1)}, bf16[512,1024]{1,0:T(8,128)(2,1)S(1)}, u32[]{:S(2)}) copy-start(bf16[512,1024]{1,0:T(8,128)(2,1)S(1)} %collective-permute-done.12.up_ref.refs_9_) | copy-start | bytes 3145732
  211.1 22.6 %copy-start.20 = (bf16[512,1024]{1,0:T(8,128)(2,1)}, bf16[512,1024]{1,0:T(8,128)(2,1)S(1)}, u32[]{:S(2)}) copy-start(bf16[512,1024]{1,0:T(8,128)(2,1)S(1)} %collective-permute-done.13.down_ref.refs_10_) | copy-start | bytes 3145732
  212.1 21.7 %collective-permute-start.16 = (bf16[512,1024]{1,0:T(8,128)(2,1)S(1)}, bf16[512,1024]{1,0:T(8,128)(2,1)S(1)}, u32[]{:S(2)}, u32[]{:S(2)}) collective-permute-start(bf16[512,1024]{1,0:T(8,128)(2,1)S(1)} %rows_2_0.1), channel_id=1, source_target_pairs={{16,24},{20,28},{8,0},{12,4},{17,25},{21,29},{9,1},{13,5},{18,26},... | collective-permute-start | bytes 3145736 | tf_op jit(solution)/shard_map/rows_2_0/ppermute | solution.py:530
  215.3 52.4 %collective-permute-start.18 = (bf16[512,1024]{1,0:T(8,128)(2,1)}, bf16[512,1024]{1,0:T(8,128)(2,1)}, u32[]{:S(2)}, u32[]{:S(2)}) collective-permute-start(bf16[512,1024]{1,0:T(8,128)(2,1)} %sums_2_1.1), channel_id=1, source_target_pairs={{0,8},{4,12},{8,16},{12,20},{1,9},{5,13},{9,17},{13,21},{2,10},{6,... | collective-permute-start | bytes 3145736 | tf_op jit(solution)/shard_map/sums_2_1/ppermute | solution.py:574
  225.9 43.7 %collective-permute-start.19 = (bf16[512,1024]{1,0:T(8,128)(2,1)}, bf16[512,1024]{1,0:T(8,128)(2,1)}, u32[]{:S(2)}, u32[]{:S(2)}) collective-permute-start(bf16[512,1024]{1,0:T(8,128)(2,1)} %sums_2_1.1), channel_id=1, source_target_pairs={{16,8},{20,12},{24,16},{28,20},{17,9},{21,13},{25,17},{29,21},{18,... | collective-permute-start | bytes 3145736 | tf_op jit(solution)/shard_map/sums_2_1/ppermute | solution.py:575
  235.5 41.5 %collective-permute-start.20 = (bf16[512,1024]{1,0:T(8,128)(2,1)}, bf16[512,1024]{1,0:T(8,128)(2,1)S(1)}, u32[]{:S(2)}, u32[]{:S(2)}) collective-permute-start(bf16[512,1024]{1,0:T(8,128)(2,1)} %rows_2_1.1), channel_id=1, source_target_pairs={{16,24},{20,28},{8,0},{12,4},{17,25},{21,29},{9,1},{13,5},{18,26},... | collective-permute-start | bytes 3145736 | tf_op jit(solution)/shard_map/rows_2_1/ppermute | solution.py:530
  239.2 46.3 %collective-permute-start.21 = (bf16[512,1024]{1,0:T(8,128)(2,1)}, bf16[512,1024]{1,0:T(8,128)(2,1)}, u32[]{:S(2)}, u32[]{:S(2)}) collective-permute-start(bf16[512,1024]{1,0:T(8,128)(2,1)} %get-tuple-element.120), channel_id=1, source_target_pairs={{0,8},{4,12},{8,16},{12,20},{16,24},{20,28},{1,9},{5,13},{9,17},{1... | collective-permute-start | bytes 3145736 | tf_op jit(solution)/shard_map/sums_3_0/ppermute | solution.py:574
  253.1 38.9 %collective-permute-start.22 = (bf16[512,1024]{1,0:T(8,128)(2,1)}, bf16[512,1024]{1,0:T(8,128)(2,1)}, u32[]{:S(2)}, u32[]{:S(2)}) collective-permute-start(bf16[512,1024]{1,0:T(8,128)(2,1)} %get-tuple-element.108), channel_id=1, source_target_pairs={{8,0},{12,4},{16,8},{20,12},{24,16},{28,20},{9,1},{13,5},{17,9},{2... | collective-permute-start | bytes 3145736 | tf_op jit(solution)/shard_map/sums_3_0/ppermute | solution.py:575
  260.2 9.3 %copy-start.33 = (bf16[512,1024]{1,0:T(8,128)(2,1)S(1)}, bf16[512,1024]{1,0:T(8,128)(2,1)}, u32[]{:S(2)}) copy-start(bf16[512,1024]{1,0:T(8,128)(2,1)} %copy-done.32) | copy-start | bytes 3145732
  260.2 9.3 %copy-start.35 = (bf16[512,1024]{1,0:T(8,128)(2,1)S(1)}, bf16[512,1024]{1,0:T(8,128)(2,1)}, u32[]{:S(2)}) copy-start(bf16[512,1024]{1,0:T(8,128)(2,1)} %copy-done.34) | copy-start | bytes 3145732
  260.3 18.2 %copy-start.19 = (bf16[512,1024]{1,0:T(8,128)(2,1)S(1)}, bf16[512,1024]{1,0:T(8,128)(2,1)}, u32[]{:S(2)}) copy-start(bf16[512,1024]{1,0:T(8,128)(2,1)} %copy-done.18) | copy-start | bytes 3145732
  260.3 18.2 %copy-start.21 = (bf16[512,1024]{1,0:T(8,128)(2,1)S(1)}, bf16[512,1024]{1,0:T(8,128)(2,1)}, u32[]{:S(2)}) copy-start(bf16[512,1024]{1,0:T(8,128)(2,1)} %copy-done.20) | copy-start | bytes 3145732
  267.7 27.4 %collective-permute-start.23 = (bf16[512,1024]{1,0:T(8,128)(2,1)S(1)}, bf16[512,1024]{1,0:T(8,128)(2,1)S(1)}, u32[]{:S(2)}, u32[]{:S(2)}) collective-permute-start(bf16[512,1024]{1,0:T(8,128)(2,1)S(1)} %get-tuple-element.123), channel_id=1, source_target_pairs={{0,4},{4,0},{8,12},{12,8},{16,20},{20,16},{24,28},{28,24},{1,5},{5... | collective-permute-start | bytes 3145736 | tf_op jit(solution)/shard_map/even_0/ppermute | solution.py:351
  272.4 24.4 %collective-permute-start.24 = (bf16[512,1024]{1,0:T(8,128)(2,1)S(1)}, bf16[512,1024]{1,0:T(8,128)(2,1)S(1)}, u32[]{:S(2)}, u32[]{:S(2)}) collective-permute-start(bf16[512,1024]{1,0:T(8,128)(2,1)S(1)} %get-tuple-element.127), channel_id=1, source_target_pairs={{0,8},{4,12},{8,16},{12,20},{16,24},{20,28},{1,9},{5,13},{9,17},{1... | collective-permute-start | bytes 3145736 | tf_op jit(solution)/shard_map/sums_3_1/ppermute | solution.py:574
  277.0 26.1 %collective-permute-start.25 = (bf16[512,1024]{1,0:T(8,128)(2,1)S(1)}, bf16[512,1024]{1,0:T(8,128)(2,1)S(1)}, u32[]{:S(2)}, u32[]{:S(2)}) collective-permute-start(bf16[512,1024]{1,0:T(8,128)(2,1)S(1)} %get-tuple-element.116), channel_id=1, source_target_pairs={{8,0},{12,4},{16,8},{20,12},{24,16},{28,20},{9,1},{13,5},{17,9},{2... | collective-permute-start | bytes 3145736 | tf_op jit(solution)/shard_map/sums_3_1/ppermute | solution.py:575
  285.5 19.6 %collective-permute-start.26 = (bf16[512,1024]{1,0:T(8,128)(2,1)S(1)}, bf16[512,1024]{1,0:T(8,128)(2,1)S(1)}, u32[]{:S(2)}, u32[]{:S(2)}) collective-permute-start(bf16[512,1024]{1,0:T(8,128)(2,1)S(1)} %get-tuple-element.131), channel_id=1, source_target_pairs={{0,4},{4,0},{8,12},{12,8},{16,20},{20,16},{24,28},{28,24},{1,5},{5... | collective-permute-start | bytes 3145736 | tf_op jit(solution)/shard_map/even_1/ppermute | solution.py:351
  (33 other events, 112.9 us)
Sparse Core Ops, SparseCore 0:
  36.8 21.6 all-gather.4
  60.3 22.3 all-gather.6
  87.0 23.1 all-gather.8
  111.6 34.4 all-gather.10

commit v7 on v6

--- a/solution.py
+++ b/solution.py
@@ -412,9 +412,12 @@
     if ratio == 1:
         with jax.named_scope("side_states"):
             for shift in range(1, minor):
-                wanted = lax.dynamic_slice_in_dim(
-                    doc_part, ((x + shift) % minor) * slice_width, slice_width, 1
-                )
+                if pieces == minor == 2:
+                    wanted = jnp.where((x + shift) % minor == 1, doc_pieces[1], doc_pieces[0])
+                else:
+                    wanted = lax.dynamic_slice_in_dim(
+                        doc_part, ((x + shift) % minor) * slice_width, slice_width, 1
+                    )
                 side_parts.append(turn(wanted, shift))
     with jax.named_scope("gather_states"):
         doc_states = [lax.all_gather(piece, "tp", axis=1, tiled=True) for piece in doc_pieces]

time: 315 us -> 316 us (level)
  blocking collectives: 21.4 us -> 0 us
  waiting for transfers between devices: 44.8 us -> 61.5 us
  starting transfers between devices: 85.1 us -> 91.5 us
    all_to_all x1 -> x0, blocking collectives: 21.4 us -> none  [route(): lax.all_to_all(sent, 'seq', split_axis=0, concat_axis=0, tiled=True)]
    all_to_all x1 -> x2, waiting for transfers between devices: 14.2 us -> 31.7 us  [route(): lax.all_to_all(sent, 'seq', split_axis=0, concat_axis=0, tiled=True)]
    all_to_all x1 -> x2, starting transfers between devices: 7.38 us -> 11.2 us  [route(): lax.all_to_all(sent, 'seq', split_axis=0, concat_axis=0, tiled=True)]
  transfers between devices with their start and end apart: 32 -> 33, of which waited for: 11 -> 13; matrix products, arithmetic and copies ran while one was open for 5% -> 4% of each run, Pallas kernels for 32% -> 32%
where the time goes in v7:
time: 316 us; the launch traced here: 314 us
  Pallas kernels  102 us (32%)
  starting transfers between devices  91.5 us (29%)
  waiting for transfers between devices  61.5 us (19%)
  local copies, waits for them, and re-layouts  31.7 us (10%)
  between operations  15.3 us (5%)
  matrix products  6.86 us (2%)
  other arithmetic  5.56 us (2%)
    pallas_call x8, Pallas kernels, products(): pl.pallas_call(body, grid_spec=pltpu.PrefetchScalarGridSpec(num_scalar_pr...  38.6 us
    ppermute x4, starting transfers between devices, send_sums(): sums_up[index] = lax.ppermute(up, 'seq', up_pairs)  36.2 us
    all_to_all x2, waiting for transfers between devices, route(): lax.all_to_all(sent, 'seq', split_axis=0, concat_axis=0, tiled=True)  31.7 us
    pallas_call x4, Pallas kernels, attend(): pl.pallas_call(lambda *refs: attend_kernel(pieces, *refs), grid=(heads //...  31.3 us
    unnamed x98, local copies, waits for them, and re-layouts  25.6 us
    pallas_call x3, Pallas kernels, project_piece(): pl.pallas_call(body, grid=(heads // pair,), in_specs=[pl.BlockSpec((state...  12.8 us
    ppermute x4, starting transfers between devices, step_up(): return lax.ppermute(value, 'seq', pairs)  11.7 us
    all_to_all x2, starting transfers between devices, route(): lax.all_to_all(sent, 'seq', split_axis=0, concat_axis=0, tiled=True)  11.2 us
  transfers between devices with their start and end apart: 33, of which 13 were waited for; matrix products, arithmetic and copies ran while one was open for 4% of the time, Pallas kernels for 32%

profile of v7, /device:TPU:0, one launch (start us, length us, event | category | flops | bytes accessed | tf_op | source)
XLA Modules:
  0.0 314.3 jit_solution(9329800339598585602)
XLA Ops:
  8.2 2.4 convolution_convert_fusion.1
  10.6 7.4 %all-to-all-start = ((bf16[8,80,512]{2,1,0:T(8,128)(2,1)}), bf16[8,80,512]{2,1,0:T(8,128)(2,1)S(1)}, u32[]{:S(2)}, u32[]{:S(2)}) async-start(bf16[8,80,512]{2,1,0:T(8,128)(2,1)} %bitcast.3), calls=%async_computation | async-start | bytes 1310720 | tf_op jit(solution)/shard_map/route/all_to_all | solution.py:309
  21.0 14.2 %all-to-all-done = bf16[8,80,512]{2,1,0:T(8,128)(2,1)S(1)} async-done(((bf16[8,80,512]{2,1,0:T(8,128)(2,1)}), bf16[8,80,512]{2,1,0:T(8,128)(2,1)S(1)}, u32[]{:S(2)}, u32[]{:S(2)}) %all-to-all-start) | async-done | bytes 655392 | tf_op jit(solution)/shard_map/route/all_to_all | solution.py:309
  38.0 3.8 %all-to-all-start.1 = ((bf16[8,80,512]{2,1,0:T(8,128)(2,1)}), bf16[8,80,512]{2,1,0:T(8,128)(2,1)S(1)}, u32[]{:S(2)}, u32[]{:S(2)}) async-start(bf16[8,80,512]{2,1,0:T(8,128)(2,1)} %bitcast.17), calls=%async_computation.1 | async-start | bytes 1310720 | tf_op jit(solution)/shard_map/route/all_to_all | solution.py:309
  41.9 17.4 %all-to-all-done.1 = bf16[8,80,512]{2,1,0:T(8,128)(2,1)S(1)} async-done(((bf16[8,80,512]{2,1,0:T(8,128)(2,1)}), bf16[8,80,512]{2,1,0:T(8,128)(2,1)S(1)}, u32[]{:S(2)}, u32[]{:S(2)}) %all-to-all-start.1) | async-done | bytes 655392 | tf_op jit(solution)/shard_map/route/all_to_all | solution.py:309
  64.8 1.9 collective-permute-start
  66.8 1.7 copy-done.3
  68.5 4.2 %project_first_piece.3.refs_4_ = f32[512,1024]{1,0:T(8,128)S(1)} custom-call(bf16[512,2048]{1,0:T(8,128)(2,1)S(1)} %copy-done.3, bf16[4,2,512,2048]{3,2,1,0:T(8,128)(2,1)} %bitcast.24, bf16[4,2,512,2048]{3,2,1,0:T(8,128)(2,1)} %bitcast.32), custom_call_target="tpu_custom_call" | custom-call | flops 2147483648 | bytes 4194304 | tf_op jit(solution)/shard_map/project_first_piece/pallas_call | solution.py:141
  74.0 4.2 %project_first_piece.4.refs_4_ = f32[512,1024]{1,0:T(8,128)S(1)} custom-call(bf16[512,2048]{1,0:T(8,128)(2,1)S(1)} %copy-done.3, bf16[4,2,512,2048]{3,2,1,0:T(8,128)(2,1)} %bitcast.25, bf16[4,2,512,2048]{3,2,1,0:T(8,128)(2,1)} %bitcast.33), custom_call_target="tpu_custom_call" | custom-call | flops 2147483648 | bytes 4194304 | tf_op jit(solution)/shard_map/project_first_piece/pallas_call | solution.py:141
  79.6 4.3 %project_first_piece.5.refs_4_ = f32[512,1024]{1,0:T(8,128)S(1)} custom-call(bf16[512,2048]{1,0:T(8,128)(2,1)S(1)} %copy-done.3, bf16[4,2,512,2048]{3,2,1,0:T(8,128)(2,1)} %bitcast.26, bf16[4,2,512,2048]{3,2,1,0:T(8,128)(2,1)} %bitcast.34), custom_call_target="tpu_custom_call" | custom-call | flops 2147483648 | bytes 4194304 | tf_op jit(solution)/shard_map/project_first_piece/pallas_call | solution.py:141
  87.2 2.3 collective-permute-start.17
  92.9 6.8 %attend_0.1 = (bf16[256,512]{1,0:T(8,128)(2,1)S(1)}, bf16[512,1024]{1,0:T(8,128)(2,1)S(1)}) custom-call(s32[15]{0:T(128)S(1)} %stack.54.refs_0_.scalar_ref, bf16[512,2048]{1,0:T(8,128)(2,1)S(1)} %copy-done.5, bf16[4,2,512,2048]{3,2,1,0:T(8,128)(2,1)} %bitcast.27, bf16[4,2,512,2048]{3,2,1,0:T(8,128)(2,1)} %bitcast.35, f32[512,1024]{1,0:T(8,128)S(1)} %copy-done.17, ...), custom_call_target="tpu_custom_call" | custom-call | bytes 524288 | tf_op jit(solution)/shard_map/attend_0/pallas_call | solution.py:103
  100.7 1.9 collective-permute-done.17
  102.6 2.2 pad_maximum_fusion.1
  104.8 4.7 %collective-permute-start.2 = (bf16[512,1024]{1,0:T(8,128)(2,1)}, bf16[512,1024]{1,0:T(8,128)(2,1)}, u32[]{:S(2)}, u32[]{:S(2)}) collective-permute-start(bf16[512,1024]{1,0:T(8,128)(2,1)} %copy-done.30), channel_id=1, source_target_pairs={{0,8},{4,12},{8,16},{12,20},{16,24},{20,28},{1,9},{5,13},{9,17},{1... | collective-permute-start | bytes 3145736 | tf_op jit(solution)/shard_map/rows_0_0/ppermute | solution.py:343
  113.7 7.3 %attend_2.1 = (bf16[256,512]{1,0:T(8,128)(2,1)S(1)}, bf16[512,1024]{1,0:T(8,128)(2,1)}) custom-call(s32[15]{0:T(128)S(1)} %stack.54.refs_0_.scalar_ref, bf16[512,2048]{1,0:T(8,128)(2,1)S(1)} %copy-done.6, bf16[4,2,512,2048]{3,2,1,0:T(8,128)(2,1)} %bitcast.28, bf16[4,2,512,2048]{3,2,1,0:T(8,128)(2,1)} %bitcast.36, f32[512,1024]{1,0:T(8,128)S(1)} %copy-done.15, ...), custom_call_target="tpu_custom_call" | custom-call | bytes 1048576 | tf_op jit(solution)/shard_map/attend_2/pallas_call | solution.py:103
  121.4 7.2 %attend_1.1 = (bf16[256,512]{1,0:T(8,128)(2,1)S(1)}, bf16[512,1024]{1,0:T(8,128)(2,1)}) custom-call(s32[15]{0:T(128)S(1)} %stack.54.refs_0_.scalar_ref, bf16[512,2048]{1,0:T(8,128)(2,1)S(1)} %copy-done.6, bf16[4,2,512,2048]{3,2,1,0:T(8,128)(2,1)} %bitcast.29, bf16[4,2,512,2048]{3,2,1,0:T(8,128)(2,1)} %bitcast.37, f32[512,1024]{1,0:T(8,128)S(1)} %copy-done.13, ...), custom_call_target="tpu_custom_call" | custom-call | bytes 1572864 | tf_op jit(solution)/shard_map/attend_1/pallas_call | solution.py:103
  129.2 5.6 %collective-permute-start.8 = (bf16[512,1024]{1,0:T(8,128)(2,1)}, bf16[512,1024]{1,0:T(8,128)(2,1)}, u32[]{:S(2)}, u32[]{:S(2)}) collective-permute-start(bf16[512,1024]{1,0:T(8,128)(2,1)} %get-tuple-element.82.refs_2_), channel_id=1, source_target_pairs={{0,8},{4,12},{8,16},{12,20},{16,24},{20,28},{1,9},{5,13},{9,17},{1... | collective-permute-start | bytes 3145736 | tf_op jit(solution)/shard_map/rows_0_1/ppermute | solution.py:343
  136.2 2.0 broadcast_select_fusion.refs_0_.refs_1_.refs_2_
  139.3 10.0 %attend_3.1 = (bf16[256,512]{1,0:T(8,128)(2,1)S(1)}, bf16[512,1024]{1,0:T(8,128)(2,1)}) custom-call(s32[15]{0:T(128)S(1)} %stack.54.refs_0_.scalar_ref, bf16[512,2048]{1,0:T(8,128)(2,1)S(1)} %copy-done.4, bf16[512,2048]{1,0:T(8,128)(2,1)S(1)} %copy-done.7, bf16[4,2,512,2048]{3,2,1,0:T(8,128)(2,1)} %bitcast.30, bf16[4,2,512,2048]{3,2,1,0:T(8,128)(2,1)} %bitcast.31, ...), custom_call_target="tpu_custom_call" | custom-call | bytes 2097152 | tf_op jit(solution)/shard_map/attend_3/pallas_call | solution.py:103
  150.0 1.9 collective-permute-start.5
  153.5 3.3 %sums_1_0.1 = bf16[512,1024]{1,0:T(8,128)(2,1)S(1)} custom-call(s32[15]{0:T(128)S(1)} %stack.54.refs_0_.scalar_ref, bf16[512,2048]{1,0:T(8,128)(2,1)S(1)} %broadcast_select_fusion.refs_0_.refs_1_.refs_2_, bf16[512,1024]{1,0:T(8,128)(2,1)} %get-tuple-element.77.refs_1_.refs_3_, bf16[2048,512]{1,0:T(8,128)(2,1)S(1)} %copy-done.2, ...), custom_call_target="tpu_custom_call" | custom-call | bytes 2621440 | tf_op jit(solution)/shard_map/sums_1_0/pallas_call | solution.py:187
  156.8 4.6 %collective-permute-start.6 = (bf16[512,1024]{1,0:T(8,128)(2,1)S(1)}, bf16[512,1024]{1,0:T(8,128)(2,1)S(1)}, u32[]{:S(2)}, u32[]{:S(2)}) collective-permute-start(bf16[512,1024]{1,0:T(8,128)(2,1)S(1)} %sums_1_0.1), channel_id=1, source_target_pairs={{0,8},{4,12},{24,16},{28,20},{1,9},{5,13},{25,17},{29,21},{2,10},{... | collective-permute-start | bytes 3145736 | tf_op jit(solution)/shard_map/sums_1_0/ppermute | solution.py:575
  163.5 5.7 %side_ahead_0.1 = (bf16[512,1024]{1,0:T(8,128)(2,1)S(1)}, bf16[512,1024]{1,0:T(8,128)(2,1)S(1)}, bf16[512,1024]{1,0:T(8,128)(2,1)S(1)}) custom-call(s32[15]{0:T(128)S(1)} %stack.54.refs_0_.scalar_ref, bf16[512,2048]{1,0:T(8,128)(2,1)S(1)} %broadcast_select_fusion.refs_0_.refs_1_.refs_2_, bf16[512,2048]{1,0:T(8,128)(2,1)S(1)} %broadcast_select_fusion.refs_0_.refs_1_.refs_2_, ...), custom_call_target="tpu_custom_call" | custom-call | tf_op jit(solution)/shard_map/side_ahead_0/pallas_call | solution.py:187
  169.2 4.7 %collective-permute-done.5.refs_3_.refs_7_ = bf16[512,1024]{1,0:T(8,128)(2,1)S(1)} collective-permute-done((bf16[512,1024]{1,0:T(8,128)(2,1)}, bf16[512,1024]{1,0:T(8,128)(2,1)S(1)}, u32[]{:S(2)}, u32[]{:S(2)}) %collective-permute-start.5) | collective-permute-done | bytes 1048608 | tf_op jit(solution)/shard_map/side_rows_1/ppermute | solution.py:351
  173.9 3.2 %sums_1_1.1 = bf16[512,1024]{1,0:T(8,128)(2,1)S(1)} custom-call(s32[15]{0:T(128)S(1)} %stack.54.refs_0_.scalar_ref, bf16[512,2048]{1,0:T(8,128)(2,1)S(1)} %broadcast_select_fusion.refs_0_.refs_1_.refs_2_, bf16[512,1024]{1,0:T(8,128)(2,1)} %get-tuple-element.86.refs_1_.refs_3_, bf16[2048,512]{1,0:T(8,128)(2,1)S(1)} %copy-done.2, ...), custom_call_target="tpu_custom_call" | custom-call | bytes 3670016 | tf_op jit(solution)/shard_map/sums_1_1/pallas_call | solution.py:187
  177.1 4.3 %collective-permute-start.7 = (bf16[512,1024]{1,0:T(8,128)(2,1)S(1)}, bf16[512,1024]{1,0:T(8,128)(2,1)S(1)}, u32[]{:S(2)}, u32[]{:S(2)}) collective-permute-start(bf16[512,1024]{1,0:T(8,128)(2,1)S(1)} %sums_1_1.1), channel_id=1, source_target_pairs={{0,8},{4,12},{24,16},{28,20},{1,9},{5,13},{25,17},{29,21},{2,10},{... | collective-permute-start | bytes 3145736 | tf_op jit(solution)/shard_map/sums_1_1/ppermute | solution.py:575
  181.4 3.2 %collective-permute-done.6.refs_1_ = bf16[512,1024]{1,0:T(8,128)(2,1)S(1)} collective-permute-done((bf16[512,1024]{1,0:T(8,128)(2,1)S(1)}, bf16[512,1024]{1,0:T(8,128)(2,1)S(1)}, u32[]{:S(2)}, u32[]{:S(2)}) %collective-permute-start.6) | collective-permute-done | bytes 1048608 | tf_op jit(solution)/shard_map/sums_1_0/ppermute | solution.py:575
  188.9 6.4 %collective-permute-start.14 = (bf16[512,1024]{1,0:T(8,128)(2,1)S(1)}, bf16[512,1024]{1,0:T(8,128)(2,1)S(1)}, u32[]{:S(2)}, u32[]{:S(2)}) collective-permute-start(bf16[512,1024]{1,0:T(8,128)(2,1)S(1)} %sums_2_0.1), channel_id=1, source_target_pairs={{0,8},{4,12},{8,16},{12,20},{1,9},{5,13},{9,17},{13,21},{2,10},{6,... | collective-permute-start | bytes 3145736 | tf_op jit(solution)/shard_map/sums_2_0/ppermute | solution.py:577
  196.3 5.5 %side_ahead_1.1 = (bf16[512,1024]{1,0:T(8,128)(2,1)S(1)}, bf16[512,1024]{1,0:T(8,128)(2,1)S(1)}, bf16[512,1024]{1,0:T(8,128)(2,1)S(1)}) custom-call(s32[15]{0:T(128)S(1)} %stack.54.refs_0_.scalar_ref, bf16[512,2048]{1,0:T(8,128)(2,1)S(1)} %broadcast_select_fusion.refs_0_.refs_1_.refs_2_, bf16[512,2048]{1,0:T(8,128)(2,1)S(1)} %broadcast_select_fusion.refs_0_.refs_1_.refs_2_, ...), custom_call_target="tpu_custom_call" | custom-call | tf_op jit(solution)/shard_map/side_ahead_1/pallas_call | solution.py:187
  203.8 3.3 %collective-permute-done.7.refs_1_ = bf16[512,1024]{1,0:T(8,128)(2,1)S(1)} collective-permute-done((bf16[512,1024]{1,0:T(8,128)(2,1)S(1)}, bf16[512,1024]{1,0:T(8,128)(2,1)S(1)}, u32[]{:S(2)}, u32[]{:S(2)}) %collective-permute-start.7) | collective-permute-done | bytes 1048608 | tf_op jit(solution)/shard_map/sums_1_1/ppermute | solution.py:575
  207.1 3.2 %side_own_1.1.refs_0_ = bf16[512,1024]{1,0:T(8,128)(2,1)S(1)} custom-call(s32[15]{0:T(128)S(1)} %stack.54.refs_0_.scalar_ref, bf16[512,2048]{1,0:T(8,128)(2,1)S(1)} %broadcast_select_fusion.refs_0_.refs_1_.refs_2_, bf16[512,1024]{1,0:T(8,128)(2,1)} %get-tuple-element.86.refs_1_.refs_3_, bf16[2048,512]{1,0:T(8,128)(2,1)S(1)} %copy-done.2, ...), custom_call_target="tpu_custom_call" | custom-call | bytes 5242880 | tf_op jit(solution)/shard_map/side_own_1/pallas_call | solution.py:187
  213.7 1.9 sums_2_1.1
  215.5 11.2 %collective-permute-start.18 = (bf16[512,1024]{1,0:T(8,128)(2,1)}, bf16[512,1024]{1,0:T(8,128)(2,1)}, u32[]{:S(2)}, u32[]{:S(2)}) collective-permute-start(bf16[512,1024]{1,0:T(8,128)(2,1)} %sums_2_1.1), channel_id=1, source_target_pairs={{0,8},{4,12},{8,16},{12,20},{1,9},{5,13},{9,17},{13,21},{2,10},{6,... | collective-permute-start | bytes 3145736 | tf_op jit(solution)/shard_map/sums_2_1/ppermute | solution.py:577
  229.6 3.3 %side_own_0.1.refs_0_ = bf16[512,1024]{1,0:T(8,128)(2,1)S(1)} custom-call(s32[15]{0:T(128)S(1)} %stack.54.refs_0_.scalar_ref, bf16[512,2048]{1,0:T(8,128)(2,1)S(1)} %broadcast_select_fusion.refs_0_.refs_1_.refs_2_, bf16[512,1024]{1,0:T(8,128)(2,1)} %get-tuple-element.77.refs_1_.refs_3_, bf16[2048,512]{1,0:T(8,128)(2,1)S(1)} %copy-done.2, ...), custom_call_target="tpu_custom_call" | custom-call | bytes 6815744 | tf_op jit(solution)/shard_map/side_own_0/pallas_call | solution.py:187
  237.7 2.4 sums_3_0.1
  240.1 14.0 %collective-permute-start.21 = (bf16[512,1024]{1,0:T(8,128)(2,1)}, bf16[512,1024]{1,0:T(8,128)(2,1)}, u32[]{:S(2)}, u32[]{:S(2)}) collective-permute-start(bf16[512,1024]{1,0:T(8,128)(2,1)} %get-tuple-element.120), channel_id=1, source_target_pairs={{0,8},{4,12},{8,16},{12,20},{16,24},{20,28},{1,9},{5,13},{9,17},{1... | collective-permute-start | bytes 3145736 | tf_op jit(solution)/shard_map/sums_3_0/ppermute | solution.py:577
  255.4 2.2 copy-done
  261.2 7.4 %even_0.1 = (bf16[512,1024]{1,0:T(8,128)(2,1)S(1)}, bf16[512,1024]{1,0:T(8,128)(2,1)S(1)}) custom-call(s32[15]{0:T(128)S(1)} %stack.54.refs_0_.scalar_ref, bf16[2048,1024]{1,0:T(8,128)(2,1)S(1)} %copy-done, bf16[2048,1024]{1,0:T(8,128)(2,1)S(1)} %copy-done, bf16[512,1024]{1,0:T(8,128)(2,1)S(1)} %copy-done.31, bf16[2048,1024]{1,0:T(8,128)(2,1)S(1)} %copy-done, ...), custom_call_target="tpu_custom_call" | custom-call | bytes 8388608 | tf_op jit(solution)/shard_map/even_0/pallas_call | solution.py:187
  268.8 2.8 sums_3_1.1
  271.7 4.6 %collective-permute-start.24 = (bf16[512,1024]{1,0:T(8,128)(2,1)S(1)}, bf16[512,1024]{1,0:T(8,128)(2,1)S(1)}, u32[]{:S(2)}, u32[]{:S(2)}) collective-permute-start(bf16[512,1024]{1,0:T(8,128)(2,1)S(1)} %get-tuple-element.127), channel_id=1, source_target_pairs={{0,8},{4,12},{8,16},{12,20},{16,24},{20,28},{1,9},{5,13},{9,17},{1... | collective-permute-start | bytes 3145736 | tf_op jit(solution)/shard_map/sums_3_1/ppermute | solution.py:577
  277.8 6.9 %even_1.1 = (bf16[512,1024]{1,0:T(8,128)(2,1)S(1)}, bf16[512,1024]{1,0:T(8,128)(2,1)S(1)}) custom-call(s32[15]{0:T(128)S(1)} %stack.54.refs_0_.scalar_ref, bf16[2048,1024]{1,0:T(8,128)(2,1)S(1)} %copy-done.1, bf16[2048,1024]{1,0:T(8,128)(2,1)S(1)} %copy-done.1, bf16[512,1024]{1,0:T(8,128)(2,1)} %get-tuple-element.82.refs_2_, ...), custom_call_target="tpu_custom_call" | custom-call | bytes 9437184 | tf_op jit(solution)/shard_map/even_1/pallas_call | solution.py:187
  284.7 2.0 collective-permute-start.26
  287.9 3.1 collective-permute-done.22.refs_2_
  290.9 3.0 finish_2.1
  294.0 1.7 finish_0.1
  295.7 7.2 %collective-permute-done.25.refs_2_ = bf16[512,1024]{1,0:T(8,128)(2,1)S(1)} collective-permute-done((bf16[512,1024]{1,0:T(8,128)(2,1)S(1)}, bf16[512,1024]{1,0:T(8,128)(2,1)S(1)}, u32[]{:S(2)}, u32[]{:S(2)}) %collective-permute-start.25) | collective-permute-done | bytes 1048608 | tf_op jit(solution)/shard_map/sums_3_1/ppermute | solution.py:578
  302.9 1.9 finish_3.1
  (167 shorter events, 62.4 us)
Async XLA Ops:
  7.2 11.0 %copy-start.46 = (s32[8]{0:T(128)S(1)}, s32[8]{0:T(128)}, u32[]{:S(2)}) copy-start(s32[8]{0:T(128)} %param.14) | copy-start | bytes 100
  7.2 11.5 %copy-start.47 = (s32[8]{0:T(128)S(1)}, s32[8]{0:T(128)}, u32[]{:S(2)}) copy-start(s32[8]{0:T(128)} %param.15) | copy-start | bytes 100
  7.2 12.1 %copy-start.44 = (s32[4096]{0:T(1024)S(1)}, s32[4096]{0:T(1024)}, u32[]{:S(2)}) copy-start(s32[4096]{0:T(1024)} %param.13) | copy-start | bytes 49156
  10.6 26.1 %copy-start.45 = (bf16[512,1024]{1,0:T(8,128)(2,1)S(1)}, bf16[512,1024]{1,0:T(8,128)(2,1)}, u32[]{:S(2)}) copy-start(bf16[512,1024]{1,0:T(8,128)(2,1)} %param.11) | copy-start | bytes 3145732
  10.6 24.7 %all-to-all-start = ((bf16[8,80,512]{2,1,0:T(8,128)(2,1)}), bf16[8,80,512]{2,1,0:T(8,128)(2,1)S(1)}, u32[]{:S(2)}, u32[]{:S(2)}) async-start(bf16[8,80,512]{2,1,0:T(8,128)(2,1)} %bitcast.3), calls=%async_computation | async-start | bytes 1310720 | tf_op jit(solution)/shard_map/route/all_to_all | solution.py:309
  18.0 45.8 %all-gather.5.cloned.1.call-start = ((), (), s32[]{:S(2)}) async-start(), calls=%async_computation.2 | async-start | bytes 2621440 | tf_op jit(solution)/shard_map/gather_states/all_gather | solution.py:423
  36.7 22.6 %copy-start.43 = (bf16[512,512]{1,0:T(8,128)(2,1)S(1)}, bf16[512,512]{1,0:T(8,128)(2,1)}, u32[]{:S(2)}) copy-start(bf16[512,512]{1,0:T(8,128)(2,1)} %fusion.2) | copy-start | bytes 1572868
  38.0 22.9 %copy-start.48 = (s32[4]{0:T(128)S(1)}, s32[4]{0:T(128)}, u32[]{:S(2)}) copy-start(s32[4]{0:T(128)} %constant.150.clone) | copy-start | bytes 52
  38.0 21.2 %all-to-all-start.1 = ((bf16[8,80,512]{2,1,0:T(8,128)(2,1)}), bf16[8,80,512]{2,1,0:T(8,128)(2,1)S(1)}, u32[]{:S(2)}, u32[]{:S(2)}) async-start(bf16[8,80,512]{2,1,0:T(8,128)(2,1)} %bitcast.17), calls=%async_computation.1 | async-start | bytes 1310720 | tf_op jit(solution)/shard_map/route/all_to_all | solution.py:309
  41.8 43.5 %all-gather.7.cloned.1.call-start = ((), (), s32[]{:S(2)}) async-start(), calls=%async_computation.3 | async-start | bytes 2621440 | tf_op jit(solution)/shard_map/gather_states/all_gather | solution.py:423
  60.9 91.0 %all-gather.9.cloned.1.call-start = ((), (), s32[]{:S(2)}) async-start(), calls=%async_computation.4 | async-start | bytes 2621440 | tf_op jit(solution)/shard_map/side_states/all_gather | solution.py:463
  62.2 23.1 %collective-permute-start.1 = (bf16[512,512]{1,0:T(8,128)(2,1)}, bf16[512,512]{1,0:T(8,128)(2,1)S(1)}, u32[]{:S(2)}, u32[]{:S(2)}) collective-permute-start(bf16[512,512]{1,0:T(8,128)(2,1)} %get-tuple-element.137), channel_id=1, source_target_pairs={{0,4},{4,0},{8,12},{12,8},{16,20},{20,16},{24,28},{28,24},{1,5},{5... | collective-permute-start | bytes 1572872 | tf_op jit(solution)/shard_map/side_states/ppermute | solution.py:351
  64.8 20.5 %collective-permute-start = (bf16[512,512]{1,0:T(8,128)(2,1)S(1)}, bf16[512,512]{1,0:T(8,128)(2,1)}, u32[]{:S(2)}, u32[]{:S(2)}) collective-permute-start(bf16[512,512]{1,0:T(8,128)(2,1)S(1)} %constant_dynamic-slice_fusion), channel_id=1, source_target_pairs={{0,8},{1,25},{2,18},{3,3},{4,12},{5,29},{6,22},{7,7},{8,16},{9,1},... | collective-permute-start | bytes 1572872 | tf_op jit(solution)/shard_map/line_states_0/ppermute | solution.py:409
  86.1 169.3 %all-gather.11.cloned.1.call-start = ((), (), s32[]{:S(2)}) async-start(), calls=%async_computation.5 | async-start | bytes 5242880 | tf_op jit(solution)/shard_map/line_states/all_gather | solution.py:453
  87.2 15.3 %collective-permute-start.17 = (bf16[512,512]{1,0:T(8,128)(2,1)S(1)}, bf16[512,512]{1,0:T(8,128)(2,1)S(1)}, u32[]{:S(2)}, u32[]{:S(2)}) collective-permute-start(bf16[512,512]{1,0:T(8,128)(2,1)S(1)} %constant_dynamic-slice_fusion.1), channel_id=1, source_target_pairs={{0,8},{1,25},{2,18},{3,3},{4,12},{5,29},{6,22},{7,7},{8,16},{9,1},... | collective-permute-start | bytes 1572872 | tf_op jit(solution)/shard_map/line_states_1/ppermute | solution.py:409
  104.8 33.4 %collective-permute-start.2 = (bf16[512,1024]{1,0:T(8,128)(2,1)}, bf16[512,1024]{1,0:T(8,128)(2,1)}, u32[]{:S(2)}, u32[]{:S(2)}) collective-permute-start(bf16[512,1024]{1,0:T(8,128)(2,1)} %copy-done.30), channel_id=1, source_target_pairs={{0,8},{4,12},{8,16},{12,20},{16,24},{20,28},{1,9},{5,13},{9,17},{1... | collective-permute-start | bytes 3145736 | tf_op jit(solution)/shard_map/rows_0_0/ppermute | solution.py:343
  109.4 28.7 %collective-permute-start.3 = (bf16[512,1024]{1,0:T(8,128)(2,1)}, bf16[512,1024]{1,0:T(8,128)(2,1)}, u32[]{:S(2)}, u32[]{:S(2)}) collective-permute-start(bf16[512,1024]{1,0:T(8,128)(2,1)} %copy-done.30), channel_id=1, source_target_pairs={{8,0},{12,4},{16,8},{20,12},{24,16},{28,20},{9,1},{13,5},{17,9},{2... | collective-permute-start | bytes 3145736 | tf_op jit(solution)/shard_map/rows_0_0/ppermute | solution.py:347
  121.1 30.8 %collective-permute-start.4 = (bf16[512,1024]{1,0:T(8,128)(2,1)}, bf16[512,1024]{1,0:T(8,128)(2,1)}, u32[]{:S(2)}, u32[]{:S(2)}) collective-permute-start(bf16[512,1024]{1,0:T(8,128)(2,1)} %get-tuple-element.77.refs_1_.refs_3_), channel_id=1, source_target_pairs={{0,4},{4,0},{8,12},{12,8},{16,20},{20,16},{24,28},{28,24},{1,5},{5... | collective-permute-start | bytes 3145736 | tf_op jit(solution)/shard_map/side_rows_0/ppermute | solution.py:351
  129.2 32.2 %collective-permute-start.8 = (bf16[512,1024]{1,0:T(8,128)(2,1)}, bf16[512,1024]{1,0:T(8,128)(2,1)}, u32[]{:S(2)}, u32[]{:S(2)}) collective-permute-start(bf16[512,1024]{1,0:T(8,128)(2,1)} %get-tuple-element.82.refs_2_), channel_id=1, source_target_pairs={{0,8},{4,12},{8,16},{12,20},{16,24},{20,28},{1,9},{5,13},{9,17},{1... | collective-permute-start | bytes 3145736 | tf_op jit(solution)/shard_map/rows_0_1/ppermute | solution.py:343
  134.8 26.6 %collective-permute-start.9 = (bf16[512,1024]{1,0:T(8,128)(2,1)}, bf16[512,1024]{1,0:T(8,128)(2,1)}, u32[]{:S(2)}, u32[]{:S(2)}) collective-permute-start(bf16[512,1024]{1,0:T(8,128)(2,1)} %get-tuple-element.82.refs_2_), channel_id=1, source_target_pairs={{8,0},{12,4},{16,8},{20,12},{24,16},{28,20},{9,1},{13,5},{17,9},{2... | collective-permute-start | bytes 3145736 | tf_op jit(solution)/shard_map/rows_0_1/ppermute | solution.py:347
  150.0 23.9 %collective-permute-start.5 = (bf16[512,1024]{1,0:T(8,128)(2,1)}, bf16[512,1024]{1,0:T(8,128)(2,1)S(1)}, u32[]{:S(2)}, u32[]{:S(2)}) collective-permute-start(bf16[512,1024]{1,0:T(8,128)(2,1)} %get-tuple-element.86.refs_1_.refs_3_), channel_id=1, source_target_pairs={{0,4},{4,0},{8,12},{12,8},{16,20},{20,16},{24,28},{28,24},{1,5},{5... | collective-permute-start | bytes 3145736 | tf_op jit(solution)/shard_map/side_rows_1/ppermute | solution.py:351
  156.8 27.8 %collective-permute-start.6 = (bf16[512,1024]{1,0:T(8,128)(2,1)S(1)}, bf16[512,1024]{1,0:T(8,128)(2,1)S(1)}, u32[]{:S(2)}, u32[]{:S(2)}) collective-permute-start(bf16[512,1024]{1,0:T(8,128)(2,1)S(1)} %sums_1_0.1), channel_id=1, source_target_pairs={{0,8},{4,12},{24,16},{28,20},{1,9},{5,13},{25,17},{29,21},{2,10},{... | collective-permute-start | bytes 3145736 | tf_op jit(solution)/shard_map/sums_1_0/ppermute | solution.py:575
  161.5 24.2 %collective-permute-start.10 = (bf16[512,1024]{1,0:T(8,128)(2,1)}, bf16[512,1024]{1,0:T(8,128)(2,1)S(1)}, u32[]{:S(2)}, u32[]{:S(2)}) collective-permute-start(bf16[512,1024]{1,0:T(8,128)(2,1)} %collective-permute-done.2.refs_5_), channel_id=1, source_target_pairs={{8,16},{12,20},{16,24},{20,28},{9,17},{13,21},{17,25},{21,29},{10,... | collective-permute-start | bytes 3145736 | tf_op jit(solution)/shard_map/rows_1_0/ppermute | solution.py:343
  162.2 24.7 %collective-permute-start.11 = (bf16[512,1024]{1,0:T(8,128)(2,1)}, bf16[512,1024]{1,0:T(8,128)(2,1)S(1)}, u32[]{:S(2)}, u32[]{:S(2)}) collective-permute-start(bf16[512,1024]{1,0:T(8,128)(2,1)} %collective-permute-done.3.refs_14_), channel_id=1, source_target_pairs={{8,0},{12,4},{16,8},{20,12},{9,1},{13,5},{17,9},{21,13},{10,2},{14... | collective-permute-start | bytes 3145736 | tf_op jit(solution)/shard_map/rows_1_0/ppermute | solution.py:347
  177.1 30.0 %collective-permute-start.7 = (bf16[512,1024]{1,0:T(8,128)(2,1)S(1)}, bf16[512,1024]{1,0:T(8,128)(2,1)S(1)}, u32[]{:S(2)}, u32[]{:S(2)}) collective-permute-start(bf16[512,1024]{1,0:T(8,128)(2,1)S(1)} %sums_1_1.1), channel_id=1, source_target_pairs={{0,8},{4,12},{24,16},{28,20},{1,9},{5,13},{25,17},{29,21},{2,10},{... | collective-permute-start | bytes 3145736 | tf_op jit(solution)/shard_map/sums_1_1/ppermute | solution.py:575
  185.7 25.8 %copy-start.22 = (bf16[512,1024]{1,0:T(8,128)(2,1)}, bf16[512,1024]{1,0:T(8,128)(2,1)S(1)}, u32[]{:S(2)}) copy-start(bf16[512,1024]{1,0:T(8,128)(2,1)S(1)} %collective-permute-done.10.up_ref.refs_9_) | copy-start | bytes 3145732
  186.9 24.5 %copy-start.24 = (bf16[512,1024]{1,0:T(8,128)(2,1)}, bf16[512,1024]{1,0:T(8,128)(2,1)S(1)}, u32[]{:S(2)}) copy-start(bf16[512,1024]{1,0:T(8,128)(2,1)S(1)} %collective-permute-done.11.down_ref.refs_10_) | copy-start | bytes 3145732
  186.9 23.4 %collective-permute-start.12 = (bf16[512,1024]{1,0:T(8,128)(2,1)}, bf16[512,1024]{1,0:T(8,128)(2,1)S(1)}, u32[]{:S(2)}, u32[]{:S(2)}) collective-permute-start(bf16[512,1024]{1,0:T(8,128)(2,1)} %collective-permute-done.8.refs_5_), channel_id=1, source_target_pairs={{8,16},{12,20},{16,24},{20,28},{9,17},{13,21},{17,25},{21,29},{10,... | collective-permute-start | bytes 3145736 | tf_op jit(solution)/shard_map/rows_1_1/ppermute | solution.py:343
  187.6 23.8 %collective-permute-start.13 = (bf16[512,1024]{1,0:T(8,128)(2,1)}, bf16[512,1024]{1,0:T(8,128)(2,1)S(1)}, u32[]{:S(2)}, u32[]{:S(2)}) collective-permute-start(bf16[512,1024]{1,0:T(8,128)(2,1)} %collective-permute-done.9.refs_14_), channel_id=1, source_target_pairs={{8,0},{12,4},{16,8},{20,12},{9,1},{13,5},{17,9},{21,13},{10,2},{14... | collective-permute-start | bytes 3145736 | tf_op jit(solution)/shard_map/rows_1_1/ppermute | solution.py:347
  188.9 40.6 %collective-permute-start.14 = (bf16[512,1024]{1,0:T(8,128)(2,1)S(1)}, bf16[512,1024]{1,0:T(8,128)(2,1)S(1)}, u32[]{:S(2)}, u32[]{:S(2)}) collective-permute-start(bf16[512,1024]{1,0:T(8,128)(2,1)S(1)} %sums_2_0.1), channel_id=1, source_target_pairs={{0,8},{4,12},{8,16},{12,20},{1,9},{5,13},{9,17},{13,21},{2,10},{6,... | collective-permute-start | bytes 3145736 | tf_op jit(solution)/shard_map/sums_2_0/ppermute | solution.py:577
  195.4 34.2 %collective-permute-start.15 = (bf16[512,1024]{1,0:T(8,128)(2,1)S(1)}, bf16[512,1024]{1,0:T(8,128)(2,1)S(1)}, u32[]{:S(2)}, u32[]{:S(2)}) collective-permute-start(bf16[512,1024]{1,0:T(8,128)(2,1)S(1)} %sums_2_0.1), channel_id=1, source_target_pairs={{16,8},{20,12},{24,16},{28,20},{17,9},{21,13},{25,17},{29,21},{18,... | collective-permute-start | bytes 3145736 | tf_op jit(solution)/shard_map/sums_2_0/ppermute | solution.py:578
  210.3 24.4 %copy-start.18 = (bf16[512,1024]{1,0:T(8,128)(2,1)}, bf16[512,1024]{1,0:T(8,128)(2,1)S(1)}, u32[]{:S(2)}) copy-start(bf16[512,1024]{1,0:T(8,128)(2,1)S(1)} %collective-permute-done.12.up_ref.refs_9_) | copy-start | bytes 3145732
  211.4 23.2 %copy-start.20 = (bf16[512,1024]{1,0:T(8,128)(2,1)}, bf16[512,1024]{1,0:T(8,128)(2,1)S(1)}, u32[]{:S(2)}) copy-start(bf16[512,1024]{1,0:T(8,128)(2,1)S(1)} %collective-permute-done.13.down_ref.refs_10_) | copy-start | bytes 3145732
  212.4 22.3 %collective-permute-start.16 = (bf16[512,1024]{1,0:T(8,128)(2,1)S(1)}, bf16[512,1024]{1,0:T(8,128)(2,1)S(1)}, u32[]{:S(2)}, u32[]{:S(2)}) collective-permute-start(bf16[512,1024]{1,0:T(8,128)(2,1)S(1)} %rows_2_0.1), channel_id=1, source_target_pairs={{16,24},{20,28},{8,0},{12,4},{17,25},{21,29},{9,1},{13,5},{18,26},... | collective-permute-start | bytes 3145736 | tf_op jit(solution)/shard_map/rows_2_0/ppermute | solution.py:533
  215.5 53.1 %collective-permute-start.18 = (bf16[512,1024]{1,0:T(8,128)(2,1)}, bf16[512,1024]{1,0:T(8,128)(2,1)}, u32[]{:S(2)}, u32[]{:S(2)}) collective-permute-start(bf16[512,1024]{1,0:T(8,128)(2,1)} %sums_2_1.1), channel_id=1, source_target_pairs={{0,8},{4,12},{8,16},{12,20},{1,9},{5,13},{9,17},{13,21},{2,10},{6,... | collective-permute-start | bytes 3145736 | tf_op jit(solution)/shard_map/sums_2_1/ppermute | solution.py:577
  226.7 42.1 %collective-permute-start.19 = (bf16[512,1024]{1,0:T(8,128)(2,1)}, bf16[512,1024]{1,0:T(8,128)(2,1)}, u32[]{:S(2)}, u32[]{:S(2)}) collective-permute-start(bf16[512,1024]{1,0:T(8,128)(2,1)} %sums_2_1.1), channel_id=1, source_target_pairs={{16,8},{20,12},{24,16},{28,20},{17,9},{21,13},{25,17},{29,21},{18,... | collective-permute-start | bytes 3145736 | tf_op jit(solution)/shard_map/sums_2_1/ppermute | solution.py:578
  236.4 39.9 %collective-permute-start.20 = (bf16[512,1024]{1,0:T(8,128)(2,1)}, bf16[512,1024]{1,0:T(8,128)(2,1)S(1)}, u32[]{:S(2)}, u32[]{:S(2)}) collective-permute-start(bf16[512,1024]{1,0:T(8,128)(2,1)} %rows_2_1.1), channel_id=1, source_target_pairs={{16,24},{20,28},{8,0},{12,4},{17,25},{21,29},{9,1},{13,5},{18,26},... | collective-permute-start | bytes 3145736 | tf_op jit(solution)/shard_map/rows_2_1/ppermute | solution.py:533
  240.1 44.7 %collective-permute-start.21 = (bf16[512,1024]{1,0:T(8,128)(2,1)}, bf16[512,1024]{1,0:T(8,128)(2,1)}, u32[]{:S(2)}, u32[]{:S(2)}) collective-permute-start(bf16[512,1024]{1,0:T(8,128)(2,1)} %get-tuple-element.120), channel_id=1, source_target_pairs={{0,8},{4,12},{8,16},{12,20},{16,24},{20,28},{1,9},{5,13},{9,17},{1... | collective-permute-start | bytes 3145736 | tf_op jit(solution)/shard_map/sums_3_0/ppermute | solution.py:577
  254.0 36.9 %collective-permute-start.22 = (bf16[512,1024]{1,0:T(8,128)(2,1)}, bf16[512,1024]{1,0:T(8,128)(2,1)}, u32[]{:S(2)}, u32[]{:S(2)}) collective-permute-start(bf16[512,1024]{1,0:T(8,128)(2,1)} %get-tuple-element.108), channel_id=1, source_target_pairs={{8,0},{12,4},{16,8},{20,12},{24,16},{28,20},{9,1},{13,5},{17,9},{2... | collective-permute-start | bytes 3145736 | tf_op jit(solution)/shard_map/sums_3_0/ppermute | solution.py:578
  261.2 16.5 %copy-start.19 = (bf16[512,1024]{1,0:T(8,128)(2,1)S(1)}, bf16[512,1024]{1,0:T(8,128)(2,1)}, u32[]{:S(2)}) copy-start(bf16[512,1024]{1,0:T(8,128)(2,1)} %copy-done.18) | copy-start | bytes 3145732
  261.2 16.5 %copy-start.21 = (bf16[512,1024]{1,0:T(8,128)(2,1)S(1)}, bf16[512,1024]{1,0:T(8,128)(2,1)}, u32[]{:S(2)}) copy-start(bf16[512,1024]{1,0:T(8,128)(2,1)} %copy-done.20) | copy-start | bytes 3145732
  268.6 25.3 %collective-permute-start.23 = (bf16[512,1024]{1,0:T(8,128)(2,1)S(1)}, bf16[512,1024]{1,0:T(8,128)(2,1)S(1)}, u32[]{:S(2)}, u32[]{:S(2)}) collective-permute-start(bf16[512,1024]{1,0:T(8,128)(2,1)S(1)} %get-tuple-element.123), channel_id=1, source_target_pairs={{0,4},{4,0},{8,12},{12,8},{16,20},{20,16},{24,28},{28,24},{1,5},{5... | collective-permute-start | bytes 3145736 | tf_op jit(solution)/shard_map/even_0/ppermute | solution.py:351
  271.7 24.1 %collective-permute-start.24 = (bf16[512,1024]{1,0:T(8,128)(2,1)S(1)}, bf16[512,1024]{1,0:T(8,128)(2,1)S(1)}, u32[]{:S(2)}, u32[]{:S(2)}) collective-permute-start(bf16[512,1024]{1,0:T(8,128)(2,1)S(1)} %get-tuple-element.127), channel_id=1, source_target_pairs={{0,8},{4,12},{8,16},{12,20},{16,24},{20,28},{1,9},{5,13},{9,17},{1... | collective-permute-start | bytes 3145736 | tf_op jit(solution)/shard_map/sums_3_1/ppermute | solution.py:577
  276.3 10.5 %copy-start.37 = (bf16[256,512]{1,0:T(8,128)(2,1)S(1)}, bf16[256,512]{1,0:T(8,128)(2,1)}, u32[]{:S(2)}) copy-start(bf16[256,512]{1,0:T(8,128)(2,1)} %copy-done.36) | copy-start | bytes 786436
  276.3 10.4 %copy-start.39 = (bf16[256,512]{1,0:T(8,128)(2,1)S(1)}, bf16[256,512]{1,0:T(8,128)(2,1)}, u32[]{:S(2)}) copy-start(bf16[256,512]{1,0:T(8,128)(2,1)} %copy-done.38) | copy-start | bytes 786436
  276.3 10.4 %copy-start.41 = (bf16[256,512]{1,0:T(8,128)(2,1)S(1)}, bf16[256,512]{1,0:T(8,128)(2,1)}, u32[]{:S(2)}) copy-start(bf16[256,512]{1,0:T(8,128)(2,1)} %copy-done.40) | copy-start | bytes 786436
  276.3 26.6 %collective-permute-start.25 = (bf16[512,1024]{1,0:T(8,128)(2,1)S(1)}, bf16[512,1024]{1,0:T(8,128)(2,1)S(1)}, u32[]{:S(2)}, u32[]{:S(2)}) collective-permute-start(bf16[512,1024]{1,0:T(8,128)(2,1)S(1)} %get-tuple-element.116), channel_id=1, source_target_pairs={{8,0},{12,4},{16,8},{20,12},{24,16},{28,20},{9,1},{13,5},{17,9},{2... | collective-permute-start | bytes 3145736 | tf_op jit(solution)/shard_map/sums_3_1/ppermute | solution.py:578
  284.7 21.2 %collective-permute-start.26 = (bf16[512,1024]{1,0:T(8,128)(2,1)S(1)}, bf16[512,1024]{1,0:T(8,128)(2,1)S(1)}, u32[]{:S(2)}, u32[]{:S(2)}) collective-permute-start(bf16[512,1024]{1,0:T(8,128)(2,1)S(1)} %get-tuple-element.131), channel_id=1, source_target_pairs={{0,4},{4,0},{8,12},{12,8},{16,20},{20,16},{24,28},{28,24},{1,5},{5... | collective-permute-start | bytes 3145736 | tf_op jit(solution)/shard_map/even_1/ppermute | solution.py:351
  (34 other events, 120.9 us)
Sparse Core Ops, SparseCore 0:
  36.8 21.6 all-gather.4
  61.0 21.6 all-gather.6
  86.2 22.4 all-gather.8
  110.1 34.4 all-gather.10
